TPU v7x, 32 devices: a whole 2x2x4 slice. The times are simulated.
32 devices in a mesh: dp: 16 (over z, y, x), tensor: 2 (over core).
Axes of the slice: x: 2, y: 2, z: 4, core: 2. Of those that a mesh axis runs over, the one named last changes fastest.
Arguments:
- inputs: bfloat16 [12288, 2048], P(('dp', 'tensor')), may hold values from -6 to 6
- cotangent: bfloat16 [12288, 2048], P(('dp', 'tensor')), may hold values from -6 to 6
- seq_lengths: int32 [16, 5], P('dp'), may hold values from 0 to 768, as said below
- attn_gain: bfloat16 [2048], P('dp'), may hold values from 0.25 to 1.75
- w_query: bfloat16 [2048, 2048], P('dp', 'tensor'), may hold values from -0.125 to 0.125
- w_key: bfloat16 [2048, 256], P('dp', 'tensor'), may hold values from -0.125 to 0.125
- w_value: bfloat16 [2048, 256], P('dp', 'tensor'), may hold values from -0.125 to 0.125
- w_out: bfloat16 [2048, 2048], P('tensor', 'dp'), may hold values from -1 to 1
- mlp_gain: bfloat16 [2048], P('dp'), may hold values from 0.25 to 1.75
- w_gate: bfloat16 [2048, 5632], P('dp', 'tensor'), may hold values from -0.125 to 0.125
- w_up: bfloat16 [2048, 5632], P('dp', 'tensor'), may hold values from -0.125 to 0.125
- w_down: bfloat16 [5632, 2048], P('tensor', 'dp'), may hold values from -0.078125 to 0.078125
Outputs:
- output: bfloat16 [12288, 2048], P(('dp', 'tensor'))
- grad_inputs: float32 [12288, 2048], P(('dp', 'tensor'))
- grad_attn_gain: float32 [2048], P('dp')
- grad_w_query: float32 [2048, 2048], P('dp', 'tensor')
- grad_w_key: float32 [2048, 256], P('dp', 'tensor')
- grad_w_value: float32 [2048, 256], P('dp', 'tensor')
- grad_w_out: float32 [2048, 2048], P('tensor', 'dp')
- grad_mlp_gain: float32 [2048], P('dp')
- grad_w_gate: float32 [2048, 5632], P('dp', 'tensor')
- grad_w_up: float32 [2048, 5632], P('dp', 'tensor')
- grad_w_down: float32 [5632, 2048], P('tensor', 'dp')
Inputs may be any that keep to these rules, and one draw needn't show every extreme that they name: `seq_lengths`: row g lists the lengths of the sequences of index g of dp in order, nonzero ones first, zeros for unused slots; their blocks, ceil(length / 128) each, number more than 3 and at most 6; in every row some sequence holds rows on both sides of row 384; one sequence in every draw has length 768.
All inputs are finite; a program needn't handle non-finite values.
Results may differ from a plain program's by a relative error of at most 0.015.
Values may be sent and summed in bfloat16 or wider, within the bound.
No kernel may reach another device: no remote copies, remote signals or barrier semaphores. Data moves between devices by JAX's collectives and lax.ppermute only.
A program may use at most 256 MiB of HBM per device.

v0:
```python
import jax
import jax.numpy as jnp
from jax import lax
from jax.sharding import PartitionSpec as P

HEAD_DIM = 64
BLOCK = 128


norm_epsilon = 1e-05
rope_base = 10000.0
masked_score = -1e30


def build_layout(lengths, total_rows):
    block_counts = (lengths + BLOCK - 1) // BLOCK
    seq_ends = jnp.cumsum(block_counts, dtype=jnp.int32) * BLOCK
    seq_starts = seq_ends - block_counts * BLOCK
    row_ids = jnp.arange(total_rows, dtype=jnp.int32)
    membership = (
        (row_ids[:, None] >= seq_starts[None, :]) & (row_ids[:, None] < seq_ends[None, :])
    ).astype(jnp.int32)
    slot_ids = jnp.arange(lengths.shape[0], dtype=jnp.int32)
    segment = jnp.sum(membership * (slot_ids[None, :] + 1), axis=1, dtype=jnp.int32) - 1
    first_row = jnp.sum(membership * seq_starts[None, :], axis=1, dtype=jnp.int32)
    seq_limit = jnp.sum(membership * lengths[None, :], axis=1, dtype=jnp.int32)
    position = row_ids - first_row
    is_valid = (segment >= 0) & (position < seq_limit)
    allowed = (
        (segment[:, None] == segment[None, :])
        & (segment[:, None] >= 0)
        & (position[None, :] <= position[:, None])
        & is_valid[None, :]
    )
    allowed = allowed | (row_ids[:, None] == row_ids[None, :])
    return (position, is_valid, allowed)


def rotate_heads(values, position, direction):
    row_count = values.shape[0]
    head_count = values.shape[1] // HEAD_DIM
    half_dim = HEAD_DIM // 2
    frequency = rope_base ** (-2.0 * jnp.arange(half_dim, dtype=jnp.float32) / HEAD_DIM)
    angles = position.astype(jnp.float32)[:, None] * frequency[None, :]
    cosine = jnp.cos(angles)[:, None, :]
    sine_part = direction * jnp.sin(angles)[:, None, :]
    shaped = values.reshape(row_count, head_count, 2, half_dim)
    first_half = shaped[:, :, 0, :]
    second_half = shaped[:, :, 1, :]
    turned = jnp.stack(
        [
            first_half * cosine - second_half * sine_part,
            second_half * cosine + first_half * sine_part,
        ],
        axis=2,
    )
    return turned.reshape(row_count, head_count * HEAD_DIM)


def matmul(left, right):
    return jnp.dot(left, right, preferred_element_type=jnp.float32)


def contract_rows(left, right):
    return lax.dot_general(
        left, right, (((0,), (0,)), ((), ())), preferred_element_type=jnp.float32
    )


def contract_cols(left, right):
    return lax.dot_general(
        left, right, (((1,), (1,)), ((), ())), preferred_element_type=jnp.float32
    )


def rms_scale(values):
    return lax.rsqrt(jnp.mean(values * values, axis=-1, keepdims=True) + norm_epsilon)


def norm_back(grad_normed, unit_rows, row_scale, gain):
    scaled = grad_normed * gain.astype(jnp.float32)
    grad_gain = jnp.sum(grad_normed * unit_rows, axis=0)
    grad_rows = row_scale * (
        scaled - unit_rows * jnp.mean(scaled * unit_rows, axis=-1, keepdims=True)
    )
    return (grad_gain, grad_rows)


def head_blocks(queries, key_rows, values, kv_index):
    row_count = queries.shape[0]
    kv_local = key_rows.shape[1] // HEAD_DIM
    per_group = queries.shape[1] // (kv_local * HEAD_DIM)
    width = per_group * HEAD_DIM
    query_block = queries[:, kv_index * width : (kv_index + 1) * width].reshape(
        row_count, per_group, HEAD_DIM
    )
    key_block = key_rows[:, kv_index * HEAD_DIM : (kv_index + 1) * HEAD_DIM]
    value_block = values[:, kv_index * HEAD_DIM : (kv_index + 1) * HEAD_DIM]
    return (query_block, key_block, value_block)


def masked_scores(query_block, key_block, allowed):
    scores = jnp.einsum(
        "qzd,kd->zqk", query_block, key_block, preferred_element_type=jnp.float32
    ) * HEAD_DIM ** (-0.5)
    return jnp.where(allowed[None], scores, masked_score)


def attend_forward(queries, key_rows, values, allowed):
    row_count = queries.shape[0]
    kv_local = key_rows.shape[1] // HEAD_DIM
    outputs = []
    totals = []
    for kv_index in range(kv_local):
        query_block, key_block, value_block = head_blocks(queries, key_rows, values, kv_index)
        scores = masked_scores(query_block, key_block, allowed)
        row_max = jnp.max(scores, axis=-1, keepdims=True)
        exponent = jnp.exp(scores - row_max)
        row_sum = jnp.sum(exponent, axis=-1, keepdims=True)
        weights = (exponent / row_sum).astype(jnp.bfloat16)
        mixed = jnp.einsum("zqk,kd->qzd", weights, value_block, preferred_element_type=jnp.float32)
        outputs.append(mixed.reshape(row_count, -1))
        totals.append(row_max[..., 0] + jnp.log(row_sum[..., 0]))
    return (jnp.concatenate(outputs, axis=1).astype(jnp.bfloat16), totals)


def attend_backward(queries, key_rows, values, allowed, totals, grad_mixed):
    row_count = queries.shape[0]
    kv_local = key_rows.shape[1] // HEAD_DIM
    per_group = queries.shape[1] // (kv_local * HEAD_DIM)
    width = per_group * HEAD_DIM
    grads_query = []
    grads_key = []
    grads_value = []
    for kv_index in range(kv_local):
        query_block, key_block, value_block = head_blocks(queries, key_rows, values, kv_index)
        scores = masked_scores(query_block, key_block, allowed)
        probs = jnp.exp(scores - totals[kv_index][..., None])
        grad_out = grad_mixed[:, kv_index * width : (kv_index + 1) * width].reshape(
            row_count, per_group, HEAD_DIM
        )
        grads_value.append(
            jnp.einsum(
                "zqk,qzd->kd",
                probs.astype(jnp.bfloat16),
                grad_out,
                preferred_element_type=jnp.float32,
            )
        )
        grad_prob = jnp.einsum(
            "qzd,kd->zqk", grad_out, value_block, preferred_element_type=jnp.float32
        )
        center = jnp.sum(probs * grad_prob, axis=-1, keepdims=True)
        grad_score = (probs * (grad_prob - center)).astype(jnp.bfloat16)
        grad_query = jnp.einsum(
            "zqk,kd->qzd", grad_score, key_block, preferred_element_type=jnp.float32
        ) * HEAD_DIM ** (-0.5)
        grads_query.append(grad_query.reshape(row_count, width))
        grads_key.append(
            jnp.einsum("zqk,qzd->kd", grad_score, query_block, preferred_element_type=jnp.float32)
            * HEAD_DIM ** (-0.5)
        )
    return (
        jnp.concatenate(grads_query, axis=1),
        jnp.concatenate(grads_key, axis=1),
        jnp.concatenate(grads_value, axis=1),
    )


def body(
    inputs,
    cotangent,
    seq_lengths,
    attn_gain,
    w_query,
    w_key,
    w_value,
    w_out,
    mlp_gain,
    w_gate,
    w_up,
    w_down,
):
    own_rows = inputs.shape[0]
    group_rows = own_rows * lax.axis_size("tensor")
    row_start = lax.axis_index("tensor") * own_rows
    position, is_valid, allowed = build_layout(seq_lengths[0], group_rows)
    own_valid = lax.dynamic_slice_in_dim(is_valid, row_start, own_rows, 0)
    gain_one, query_w, key_w, value_w, out_w = (
        lax.all_gather(attn_gain, "dp", axis=0, tiled=True),
        lax.all_gather(w_query, "dp", axis=0, tiled=True),
        lax.all_gather(w_key, "dp", axis=0, tiled=True),
        lax.all_gather(w_value, "dp", axis=0, tiled=True),
        lax.all_gather(w_out, "dp", axis=1, tiled=True),
    )
    inputs_wide = inputs.astype(jnp.float32)
    scale_one = rms_scale(inputs_wide)
    unit_one = inputs_wide * scale_one
    normed_own = (unit_one * gain_one.astype(jnp.float32)).astype(jnp.bfloat16)
    normed = lax.all_gather(normed_own, "tensor", axis=0, tiled=True)
    queries = rotate_heads(matmul(normed, query_w), position, 1.0).astype(jnp.bfloat16)
    key_rows = rotate_heads(matmul(normed, key_w), position, 1.0).astype(jnp.bfloat16)
    values = matmul(normed, value_w).astype(jnp.bfloat16)
    mixed, totals = attend_forward(queries, key_rows, values, allowed)
    attended = lax.psum_scatter(matmul(mixed, out_w), "tensor", scatter_dimension=0, tiled=True)
    residual = inputs_wide + attended
    gain_two, gate_w, up_w, down_w = (
        lax.all_gather(mlp_gain, "dp", axis=0, tiled=True),
        lax.all_gather(w_gate, "dp", axis=0, tiled=True),
        lax.all_gather(w_up, "dp", axis=0, tiled=True),
        lax.all_gather(w_down, "dp", axis=1, tiled=True),
    )
    scale_two = rms_scale(residual)
    unit_two = residual * scale_two
    normed_mlp_own = (unit_two * gain_two.astype(jnp.float32)).astype(jnp.bfloat16)
    normed_mlp = lax.all_gather(normed_mlp_own, "tensor", axis=0, tiled=True)
    gate_act = matmul(normed_mlp, gate_w)
    up_act = matmul(normed_mlp, up_w)
    hidden = (jax.nn.silu(gate_act) * up_act).astype(jnp.bfloat16)
    branch = lax.psum_scatter(
        matmul(hidden, down_w).astype(jnp.bfloat16), "tensor", scatter_dimension=0, tiled=True
    ).astype(jnp.float32)
    output = jnp.where(own_valid[:, None], residual + branch, 0.0).astype(jnp.bfloat16)
    grad_branch_own = jnp.where(own_valid[:, None], cotangent, jnp.zeros_like(cotangent))
    grad_branch = lax.all_gather(grad_branch_own, "tensor", axis=0, tiled=True)
    grad_hidden = contract_cols(grad_branch, down_w)
    grad_down = contract_rows(hidden, grad_branch)
    sigmoid_gate = jax.nn.sigmoid(gate_act)
    grad_gate = (
        grad_hidden * up_act * sigmoid_gate * (1.0 + gate_act * (1.0 - sigmoid_gate))
    ).astype(jnp.bfloat16)
    grad_up = (grad_hidden * gate_act * sigmoid_gate).astype(jnp.bfloat16)
    grad_gate_w = contract_rows(normed_mlp, grad_gate)
    grad_up_w = contract_rows(normed_mlp, grad_up)
    grad_normed_mlp = lax.psum_scatter(
        contract_cols(grad_gate, gate_w) + contract_cols(grad_up, up_w),
        "tensor",
        scatter_dimension=0,
        tiled=True,
    )
    grad_gain_two, grad_norm_two = norm_back(grad_normed_mlp, unit_two, scale_two, gain_two)
    grad_residual = grad_branch_own.astype(jnp.float32) + grad_norm_two
    grad_attended = lax.all_gather(grad_residual.astype(jnp.bfloat16), "tensor", axis=0, tiled=True)
    grad_mixed = contract_cols(grad_attended, out_w).astype(jnp.bfloat16)
    grad_out_w = contract_rows(mixed, grad_attended)
    grad_query_rot, grad_key_rot, grad_value_wide = attend_backward(
        queries, key_rows, values, allowed, totals, grad_mixed
    )
    grad_query = rotate_heads(grad_query_rot, position, -1.0).astype(jnp.bfloat16)
    grad_key = rotate_heads(grad_key_rot, position, -1.0).astype(jnp.bfloat16)
    grad_value = grad_value_wide.astype(jnp.bfloat16)
    grad_query_w = contract_rows(normed, grad_query)
    grad_key_w = contract_rows(normed, grad_key)
    grad_value_w = contract_rows(normed, grad_value)
    grad_normed_part = (
        contract_cols(grad_query, query_w)
        + contract_cols(grad_key, key_w)
        + contract_cols(grad_value, value_w)
    )
    grad_normed = lax.psum_scatter(
        grad_normed_part.astype(jnp.bfloat16), "tensor", scatter_dimension=0, tiled=True
    ).astype(jnp.float32)
    grad_gain_one, grad_norm_one = norm_back(grad_normed, unit_one, scale_one, gain_one)
    grad_rows = grad_residual + grad_norm_one
    (
        sum_gain_one,
        sum_query,
        sum_key,
        sum_value,
        sum_out,
        sum_gain_two,
        sum_gate,
        sum_up,
        sum_down,
    ) = (
        lax.psum_scatter(grad_gain_one, "dp", scatter_dimension=0, tiled=True),
        lax.psum_scatter(grad_query_w, "dp", scatter_dimension=0, tiled=True),
        lax.psum_scatter(grad_key_w, "dp", scatter_dimension=0, tiled=True),
        lax.psum_scatter(grad_value_w, "dp", scatter_dimension=0, tiled=True),
        lax.psum_scatter(grad_out_w, "dp", scatter_dimension=1, tiled=True),
        lax.psum_scatter(grad_gain_two, "dp", scatter_dimension=0, tiled=True),
        lax.psum_scatter(grad_gate_w, "dp", scatter_dimension=0, tiled=True),
        lax.psum_scatter(grad_up_w, "dp", scatter_dimension=0, tiled=True),
        lax.psum_scatter(grad_down, "dp", scatter_dimension=1, tiled=True),
    )
    total_gain_one, total_gain_two = lax.psum((sum_gain_one, sum_gain_two), "tensor")
    return (
        output,
        grad_rows,
        total_gain_one,
        sum_query,
        sum_key,
        sum_value,
        sum_out,
        total_gain_two,
        sum_gate,
        sum_up,
        sum_down,
    )


def solution(mesh):
    placed = (
        P(("dp", "tensor"), None),
        P(("dp", "tensor"), None),
        P("dp", None),
        P("dp"),
        P("dp", "tensor"),
        P("dp", "tensor"),
        P("dp", "tensor"),
        P("tensor", "dp"),
        P("dp"),
        P("dp", "tensor"),
        P("dp", "tensor"),
        P("tensor", "dp"),
    )
    return jax.shard_map(
        body,
        mesh=mesh,
        in_specs=placed,
        out_specs=(
            P(("dp", "tensor"), None),
            P(("dp", "tensor"), None),
            P("dp"),
            P("dp", "tensor"),
            P("dp", "tensor"),
            P("dp", "tensor"),
            P("tensor", "dp"),
            P("dp"),
            P("dp", "tensor"),
            P("dp", "tensor"),
            P("tensor", "dp"),
        ),
        check_vma=False,
    )
```

profile of v0, /device:TPU:0, one launch (start us, length us, event | category | flops | bytes accessed | tf_op | source)
XLA Modules:
  0.0 2939.7 jit_solution(2686038016169371139)
XLA Ops:
  7.2 1.8 fusion.28
  9.1 42.4 %all-gather = bf16[16,1,128]{2,1,0:T(2,128)(2,1)S(1)} all-gather(bf16[1,1,128]{2,1,0:T(2,128)(2,1)} %bitcast.186), channel_id=1, replica_groups=mesh['dp'=16,'tensor'=2] {'dp'}, dimensions={0}, use_global_device_ids=true | all-gather | bytes 4352 | tf_op jit(solution)/shard_map/all_gather | solution.py:190
  52.0 3.0 fusion.25
  57.0 42.1 %all_gather.42 = bf16[2048,128]{1,0:T(8,128)(2,1)} all-gather(bf16[128,128]{1,0:T(8,128)(2,1)S(1)} %copy-done.31), channel_id=1, replica_groups=mesh['dp'=16,'tensor'=2] {'dp'}, dimensions={0}, use_global_device_ids=true | all-gather | bytes 557056 | tf_op jit(solution)/shard_map/all_gather | solution.py:192
  99.1 46.0 %all_gather.41 = bf16[2048,128]{1,0:T(8,128)(2,1)} all-gather(bf16[128,128]{1,0:T(8,128)(2,1)S(1)} %copy-done.32), channel_id=1, replica_groups=mesh['dp'=16,'tensor'=2] {'dp'}, dimensions={0}, use_global_device_ids=true | all-gather | bytes 557056 | tf_op jit(solution)/shard_map/all_gather | solution.py:193
  146.1 1.9 fusion.29
  148.1 3.3 fusion.64
  151.5 1.9 convolution_convert_fusion.2
  153.4 5.3 fusion.65
  160.3 8.1 fusion.62
  168.5 8.7 fusion.63
  177.2 8.9 fusion.7
  186.1 9.0 fusion.6
  195.1 8.5 fusion.31
  203.7 8.7 fusion.32
  212.4 27.6 all-gather.16.cloned.1.call-done
  240.0 7.5 fusion.48
  248.2 37.7 %all-gather.1 = bf16[16,1,128]{2,1,0:T(2,128)(2,1)S(1)} all-gather(bf16[1,1,128]{2,1,0:T(2,128)(2,1)S(1)} %bitcast.188), channel_id=1, replica_groups=mesh['dp'=16,'tensor'=2] {'dp'}, dimensions={0}, use_global_device_ids=true | all-gather | bytes 4352 | tf_op jit(solution)/shard_map/all_gather | solution.py:208
  286.0 2.9 multiply_reduce_fusion.2
  291.5 2.7 broadcast_select_fusion
  295.0 111.7 %all-gather.22.cloned.1.call-done = bf16[2048,2816]{1,0:T(8,128)(2,1)} async-done(((bf16[128,2816]{1,0:T(8,128)(2,1)}), bf16[2048,2816]{1,0:T(8,128)(2,1)}) %all-gather.22.cloned.1.call-update) | async-done | bytes 11534352 | tf_op jit(solution)/shard_map/all_gather | solution.py:210
  406.7 12.4 all-gather.18.cloned.1.call-done
  419.1 15.8 fusion.67
  435.0 130.6 %all-gather.20.cloned.1.call-done = bf16[2048,2816]{1,0:T(8,128)(2,1)} async-done(((bf16[128,2816]{1,0:T(8,128)(2,1)}), bf16[2048,2816]{1,0:T(8,128)(2,1)}) %all-gather.20.cloned.1.call-update) | async-done | bytes 11534352 | tf_op jit(solution)/shard_map/all_gather | solution.py:209
  565.6 15.7 fusion.66
  581.3 183.7 %all-gather.24.cloned.1.call-done = bf16[2816,2048]{1,0:T(8,128)(2,1)} async-done(((bf16[2816,128]{1,0:T(8,128)(2,1)}), bf16[2816,2048]{1,0:T(8,128)(2,1)}) %all-gather.24.cloned.1.call-update) | async-done | bytes 11534352 | tf_op jit(solution)/shard_map/all_gather | solution.py:211
  765.0 23.1 multiply_convert_fusion
  788.1 13.6 fusion.68
  801.7 13.6 convolution_add_fusion
  815.4 12.8 reduce-scatter.16.cloned.1.call-done
  828.2 3.4 multiply_reduce_fusion
  831.6 2.2 fusion.59
  834.6 12.7 all-gather.28.cloned.1.call-done
  847.4 6.6 convolution_convert_fusion.1
  854.3 9.4 fusion.41
  863.7 12.3 fusion
  875.9 12.9 fusion.2
  888.9 3.6 fusion.33
  894.6 9.4 fusion.44
  904.0 11.8 fusion.3
  915.8 13.1 fusion.5
  928.9 2.9 fusion.34
  931.9 1.8 convolution_multiply_fusion.1
  937.6 3.5 fusion.69
  941.1 2.7 add_convert_fusion
  943.9 14.4 convolution_convert_fusion
  960.1 2.0 fusion.49
  962.2 2.0 fusion.72
  964.2 10.2 fusion.47
  974.5 7.1 fusion.71
  981.6 1.8 copy-done.42
  983.5 14.6 fusion.74
  998.1 14.6 fusion.73
  1014.6 14.6 fusion.75
  1031.2 3.0 fusion.27
  1034.1 77.3 %all-reduce.2 = (f32[2048]{0:T(1024)S(1)}, f32[2048]{0:T(1024)S(1)}) all-reduce(f32[2048]{0:T(1024)S(1)} %get-tuple-element.13, f32[2048]{0:T(1024)S(1)} %copy-done.30), channel_id=6, replica_groups=mesh['dp'=16,'tensor'=2] {'dp'}, use_global_device_ids=true, to_apply=%region_19.20.clone | all-reduce | flops 4096 | bytes 32768
  1111.6 3.0 all-reduce.3
  1114.6 6.2 fusion.24
  1120.8 8.2 reduce-scatter.22.cloned.1.call-done
  1129.1 177.0 %reduce-scatter.26.cloned.1.call-done = f32[1024,128]{1,0:T(8,128)} async-done(((f32[1024,2048]{1,0:T(8,128)}), f32[1024,128]{1,0:T(8,128)}) %reduce-scatter.26.cloned.1.call-update) | async-done | bytes 524304 | tf_op jit(solution)/shard_map/reduce_scatter | solution.py:280
  1306.1 183.0 %reduce-scatter.20.cloned.1.call-done = f32[128,1024]{1,0:T(8,128)} async-done(((f32[2048,1024]{1,0:T(8,128)}), f32[128,1024]{1,0:T(8,128)}) %reduce-scatter.20.cloned.1.call-update) | async-done | bytes 524304 | tf_op jit(solution)/shard_map/reduce_scatter | solution.py:277
  1489.1 478.2 %reduce-scatter.30.cloned.1.call-done = f32[128,2816]{1,0:T(8,128)} async-done(((f32[2048,2816]{1,0:T(8,128)}), f32[128,2816]{1,0:T(8,128)}) %reduce-scatter.30.cloned.1.call-update) | async-done | bytes 1441808 | tf_op jit(solution)/shard_map/reduce_scatter | solution.py:283
  1967.3 482.7 %reduce-scatter.28.cloned.1.call-done = f32[128,2816]{1,0:T(8,128)} async-done(((f32[2048,2816]{1,0:T(8,128)}), f32[128,2816]{1,0:T(8,128)}) %reduce-scatter.28.cloned.1.call-update) | async-done | bytes 1441808 | tf_op jit(solution)/shard_map/reduce_scatter | solution.py:282
  2449.9 482.5 %reduce-scatter.32.cloned.1.call-done = f32[2816,128]{1,0:T(8,128)} async-done(((f32[2816,2048]{1,0:T(8,128)}), f32[2816,128]{1,0:T(8,128)}) %reduce-scatter.32.cloned.1.call-update) | async-done | bytes 1441808 | tf_op jit(solution)/shard_map/reduce_scatter | solution.py:284
  (180 shorter events, 21.8 us)
Async XLA Ops:
  7.2 140.9 %all-gather.12.cloned.1.call-start = ((), (), s32[]{:S(2)}) async-start(), calls=%async_computation.11 | async-start | bytes 4718592 | tf_op jit(solution)/shard_map/all_gather | solution.py:200
  7.2 49.3 %copy-start.39 = (s32[1,5]{1,0:T(1,128)S(1)}, s32[1,5]{1,0:T(1,128)}, u32[]{:S(2)}) copy-start(s32[1,5]{1,0:T(1,128)} %param.14) | copy-start | bytes 64
  7.2 49.7 %copy-start.31 = (bf16[128,128]{1,0:T(8,128)(2,1)S(1)}, bf16[128,128]{1,0:T(8,128)(2,1)}, u32[]{:S(2)}) copy-start(bf16[128,128]{1,0:T(8,128)(2,1)} %param.17) | copy-start | bytes 98308
  9.0 90.0 %copy-start.32 = (bf16[128,128]{1,0:T(8,128)(2,1)S(1)}, bf16[128,128]{1,0:T(8,128)(2,1)}, u32[]{:S(2)}) copy-start(bf16[128,128]{1,0:T(8,128)(2,1)} %param.18) | copy-start | bytes 98308
  9.1 42.4 %copy-start.33 = (f32[384]{0:T(512)}, f32[384]{0:T(512)S(1)}, u32[]{:S(2)}) copy-start(f32[384]{0:T(512)S(1)} %add_rsqrt_fusion.1) | copy-start | bytes 4612
  55.0 98.4 %all-gather.14.cloned.1.call-start = ((), (), s32[]{:S(2)}) async-start(), calls=%async_computation.12 | async-start | bytes 4456448 | tf_op jit(solution)/shard_map/all_gather | solution.py:191
  55.8 184.2 %all-gather.16.cloned.1.call-start = ((), (), s32[]{:S(2)}) async-start(), calls=%async_computation.13 | async-start | bytes 4456448 | tf_op jit(solution)/shard_map/all_gather | solution.py:194
  56.5 229.4 %reduce-scatter.12.cloned.1.call-start = ((), (), s32[]{:S(2)}) async-start(), calls=%async_computation.14 | async-start | bytes 9437184 | tf_op jit(solution)/shard_map/reduce_scatter | solution.py:205
  146.1 12.6 copy-start.14
  148.1 3.4 copy-start.2
  148.1 3.4 copy-start.11
  151.5 16.9 copy-start.16
  159.5 8.9 copy-start.8
  159.5 8.9 copy-start.6
  186.1 9.0 copy-start.21
  203.6 36.3 %copy-start.44 = (bf16[64,8,768]{2,0,1:T(8,128)(2,1)}, bf16[64,8,768]{2,0,1:T(8,128)(2,1)S(1)}, u32[]{:S(2)}) copy-start(bf16[64,8,768]{2,0,1:T(8,128)(2,1)S(1)} %fusion.31) | copy-start | bytes 2359300
  212.3 35.2 %copy-start.45 = (bf16[64,8,768]{2,0,1:T(8,128)(2,1)}, bf16[64,8,768]{2,0,1:T(8,128)(2,1)S(1)}, u32[]{:S(2)}) copy-start(bf16[64,8,768]{2,0,1:T(8,128)(2,1)S(1)} %fusion.32) | copy-start | bytes 2359300
  247.5 159.2 %all-gather.22.cloned.1.call-start = ((), (), s32[]{:S(2)}) async-start(), calls=%async_computation.17 | async-start | bytes 12255232 | tf_op jit(solution)/shard_map/all_gather | solution.py:210
  248.1 171.0 %all-gather.18.cloned.1.call-start = ((), (), s32[]{:S(2)}) async-start(), calls=%async_computation.15 | async-start | bytes 4718592 | tf_op jit(solution)/shard_map/all_gather | solution.py:216
  285.9 545.7 %copy-start.24 = (f32[16,1,128]{2,1,0:T(1,128)}, f32[16,1,128]{2,1,0:T(1,128)S(1)}, u32[]{:S(2)}) copy-start(f32[16,1,128]{2,1,0:T(1,128)S(1)} %convert_element_type.129) | copy-start | bytes 24580
  288.8 542.8 %copy-start = (f32[384,2048]{1,0:T(8,128)}, f32[384,2048]{1,0:T(8,128)S(1)}, u32[]{:S(2)}) copy-start(f32[384,2048]{1,0:T(8,128)S(1)} %get-tuple-element.23) | copy-start | bytes 9437188
  288.9 542.8 %copy-start.28 = (f32[384]{0:T(512)}, f32[384]{0:T(512)S(1)}, u32[]{:S(2)}) copy-start(f32[384]{0:T(512)S(1)} %add_rsqrt_fusion) | copy-start | bytes 4612
  290.6 275.0 %all-gather.20.cloned.1.call-start = ((), (), s32[]{:S(2)}) async-start(), calls=%async_computation.16 | async-start | bytes 12255232 | tf_op jit(solution)/shard_map/all_gather | solution.py:209
  291.4 289.9 %all-gather.26.cloned.1.call-start = ((), (), s32[]{:S(2)}) async-start(), calls=%async_computation.20 | async-start | bytes 4718592 | tf_op jit(solution)/shard_map/all_gather | solution.py:225
  291.5 540.1 %copy-start.37 = (pred[384]{0:T(512)(128)(4,1)}, pred[384]{0:T(512)(128)(4,1)S(1)}, u32[]{:S(2)}) copy-start(pred[384]{0:T(512)(128)(4,1)S(1)} %dynamic_slice.3) | copy-start | bytes 1156
  294.2 470.8 %all-gather.24.cloned.1.call-start = ((), (), s32[]{:S(2)}) async-start(), calls=%async_computation.18 | async-start | bytes 12255232 | tf_op jit(solution)/shard_map/all_gather | solution.py:211
  295.0 533.2 %reduce-scatter.16.cloned.1.call-start = ((), (), s32[]{:S(2)}) async-start(), calls=%async_computation.21 | async-start | bytes 9437184 | tf_op jit(solution)/shard_map/reduce_scatter | solution.py:235
  788.1 13.6 copy-start.47
  815.3 32.0 %all-gather.28.cloned.1.call-start = ((), (), s32[]{:S(2)}) async-start(), calls=%async_computation.22 | async-start | bytes 4718592 | tf_op jit(solution)/shard_map/all_gather | solution.py:243
  828.2 3.4 copy-start.4
  828.2 3.4 copy-start.5
  831.6 2.3 copy-start.35
  833.9 197.2 %reduce-scatter.18.cloned.1.call-start = ((), (), s32[]{:S(2)}) async-start(), calls=%async_computation.23 | async-start | bytes 4718592 | tf_op jit(solution)/shard_map/reduce_scatter | solution.py:260
  875.9 12.9 copy-start.9
  888.8 3.6 copy-start.17
  894.5 9.4 copy-start.22
  894.6 9.4 copy-start.23
  915.8 13.1 copy-start.7
  931.8 1.8 copy-start.20
  931.8 1.9 copy-start.15
  931.8 1.9 copy-start.19
  931.9 2.0 copy-start.13
  934.8 2.8 copy-start.41
  935.5 1.1 copy-start.18
  937.6 3.5 copy-start.12
  943.8 170.7 %reduce-scatter.14.cloned.1.call-start = ((), (), s32[]{:S(2)}) async-start(), calls=%async_computation.19 | async-start | bytes 4718592 | tf_op jit(solution)/shard_map/reduce_scatter | solution.py:220
  958.2 1.9 copy-start.3
  958.3 162.5 %reduce-scatter.24.cloned.1.call-start = ((), (), s32[]{:S(2)}) async-start(), calls=%async_computation.26 | async-start | bytes 1114112 | tf_op jit(solution)/shard_map/reduce_scatter | solution.py:279
  962.1 166.9 %reduce-scatter.22.cloned.1.call-start = ((), (), s32[]{:S(2)}) async-start(), calls=%async_computation.25 | async-start | bytes 1114112 | tf_op jit(solution)/shard_map/reduce_scatter | solution.py:278
  964.2 341.9 %reduce-scatter.26.cloned.1.call-start = ((), (), s32[]{:S(2)}) async-start(), calls=%async_computation.27 | async-start | bytes 8912896 | tf_op jit(solution)/shard_map/reduce_scatter | solution.py:280
  974.4 514.7 %reduce-scatter.20.cloned.1.call-start = ((), (), s32[]{:S(2)}) async-start(), calls=%async_computation.24 | async-start | bytes 8912896 | tf_op jit(solution)/shard_map/reduce_scatter | solution.py:277
  981.6 1.9 copy-start.42
  981.6 985.7 %reduce-scatter.30.cloned.1.call-start = ((), (), s32[]{:S(2)}) async-start(), calls=%async_computation.29 | async-start | bytes 24510464 | tf_op jit(solution)/shard_map/reduce_scatter | solution.py:283
  998.0 1451.9 %reduce-scatter.28.cloned.1.call-start = ((), (), s32[]{:S(2)}) async-start(), calls=%async_computation.28 | async-start | bytes 24510464 | tf_op jit(solution)/shard_map/reduce_scatter | solution.py:282
  1012.7 1.9 copy-start.43
  1012.8 1919.7 %reduce-scatter.32.cloned.1.call-start = ((), (), s32[]{:S(2)}) async-start(), calls=%async_computation.30 | async-start | bytes 24510464 | tf_op jit(solution)/shard_map/reduce_scatter | solution.py:284
  1029.2 1.9 copy-start.27
  1029.2 1.9 copy-start.34
  1029.2 4.9 copy-start.30
  1029.3 85.3 %copy-start.1 = (f32[384,2048]{1,0:T(8,128)S(1)}, f32[384,2048]{1,0:T(8,128)}, u32[]{:S(2)}) copy-start(f32[384,2048]{1,0:T(8,128)} %copy-done) | copy-start | bytes 9437188
  1029.3 85.3 %copy-start.25 = (f32[16,1,128]{2,1,0:T(1,128)S(1)}, f32[16,1,128]{2,1,0:T(1,128)}, u32[]{:S(2)}) copy-start(f32[16,1,128]{2,1,0:T(1,128)} %copy-done.24) | copy-start | bytes 24580
  1029.3 85.3 %copy-start.29 = (f32[384]{0:T(512)S(1)}, f32[384]{0:T(512)}, u32[]{:S(2)}) copy-start(f32[384]{0:T(512)} %copy-done.28) | copy-start | bytes 4612
  1029.3 85.3 %copy-start.36 = (f32[384]{0:T(512)S(1)}, f32[384]{0:T(512)}, u32[]{:S(2)}) copy-start(f32[384]{0:T(512)} %copy-done.35) | copy-start | bytes 4612
  1029.3 85.3 %copy-start.38 = (pred[384]{0:T(512)(128)(4,1)S(1)}, pred[384]{0:T(512)(128)(4,1)}, u32[]{:S(2)}) copy-start(pred[384]{0:T(512)(128)(4,1)} %copy-done.37) | copy-start | bytes 1156
  (4 other events, 3.0 us)
Sparse Core Ops, SparseCore 0:
  55.2 7.9 all-gather.11
  65.9 82.6 all-gather.13
  151.4 88.5 all-gather.15
  247.6 12.6 reduce-scatter.11
  263.3 143.3 all-gather.21
  408.8 10.3 all-gather.17
  422.2 143.3 all-gather.19
  567.8 10.3 all-gather.25
  581.2 183.7 all-gather.23
  815.4 12.6 reduce-scatter.15
  834.0 13.2 all-gather.27
  944.0 12.0 reduce-scatter.17
  958.4 12.0 reduce-scatter.13
  973.2 78.9 reduce-scatter.23
  1054.9 74.0 reduce-scatter.21
  1131.8 174.2 reduce-scatter.25
  1308.8 180.2 reduce-scatter.19
  1491.8 475.3 reduce-scatter.29
  1970.2 479.7 reduce-scatter.27
  2452.7 479.7 reduce-scatter.31
where the time goes:
time: 2950 us; the launch traced here: 2940 us
  waiting for transfers between devices  2310 us (78%)
  matrix products  280 us (9%)
  blocking collectives  248 us (8%)
  other arithmetic  76.3 us (3%)
    reduce_scatter x1, waiting for transfers between devices, body(): lax.psum_scatter(grad_gate_w, 'dp', scatter_dimension=0, tiled=True)  483 us
    reduce_scatter x1, waiting for transfers between devices, body(): lax.psum_scatter(grad_down, 'dp', scatter_dimension=1, tiled=True)  483 us
    reduce_scatter x1, waiting for transfers between devices, body(): lax.psum_scatter(grad_up_w, 'dp', scatter_dimension=0, tiled=True)  478 us
    all_gather x1, waiting for transfers between devices, body(): lax.all_gather(w_down, 'dp', axis=1, tiled=True)  184 us
    reduce_scatter x1, waiting for transfers between devices, body(): lax.psum_scatter(grad_query_w, 'dp', scatter_dimension=0, tiled=True)  183 us
    reduce_scatter x1, waiting for transfers between devices, body(): lax.psum_scatter(grad_out_w, 'dp', scatter_dimension=1, tiled=True)  177 us
    all_gather x1, waiting for transfers between devices, body(): lax.all_gather(w_gate, 'dp', axis=0, tiled=True)  131 us
    all_gather x1, waiting for transfers between devices, body(): lax.all_gather(w_up, 'dp', axis=0, tiled=True)  112 us
  transfers between devices with their start and end apart: 20, of which 13 were waited for; matrix products, arithmetic and copies ran while one was open for 7% of the time, Pallas kernels for 0%

commit v1 on v0

v1 whole, which is shorter than its diff:
```python
import functools

import jax
import jax.numpy as jnp
from jax import lax
from jax.experimental import pallas as pl
from jax.experimental.layout import Layout, with_layout_constraint
from jax.experimental.pallas import tpu as pltpu
from jax.sharding import PartitionSpec as P

HEAD_DIM = 64
BLOCK = 128
LANES = 128

norm_epsilon = 1e-05
rope_base = 10000.0
masked_score = -1e30

bf16 = jnp.bfloat16
f32 = jnp.float32

X, Y, T, Z = 0, 1, 2, 3


def nbits():
    return lax.axis_size("dp").bit_length() - 1


def block_axes():
    return [T] + list(range(nbits() - 1, Z - 1, -1)) + [Y, X]


def rest_bits():
    return list(range(Z, nbits()))


def exchange(values, bit):
    size = lax.axis_size("dp")
    return lax.ppermute(values, "dp", [(i, i ^ (1 << bit)) for i in range(size)])


def core_exchange(values):
    return lax.ppermute(values, "tensor", [(0, 1), (1, 0)])


def as_block(values):
    return values.reshape((1,) * nbits() + values.shape)


def after(values, *others):
    return lax.optimization_barrier((values,) + others)[0] if others else values


def row_major(values):
    return with_layout_constraint(values, Layout(major_to_minor=tuple(range(values.ndim))))


def gather_step(values, bit, *others):
    came = exchange(after(values, *others), bit)
    return jnp.concatenate([values, came], axis=block_axes().index(bit)), came


def gather_bits(values, bits):
    for bit in bits:
        values, _ = gather_step(values, bit)
    return values


def scatter_step(values, bit, kind, *others):
    axis = block_axes().index(bit)
    kept = lax.slice_in_dim(values, 0, 1, axis=axis)
    sent = lax.slice_in_dim(values, 1, 2, axis=axis)
    came = exchange(row_major(after(sent.astype(bf16), *others)), bit)
    total = kept.astype(f32) + came.astype(f32)
    return row_major(total.astype(kind)), came


def flat(blocks):
    return blocks.reshape(-1, blocks.shape[-1])


def as_blocks(rows):
    return rows.reshape((2,) * nbits() + (rows.shape[0] // lax.axis_size("dp"), rows.shape[1]))


def block_mask(place):
    axes = block_axes()
    mask = 0
    for level, bit in enumerate(axes):
        mask |= ((place >> (len(axes) - 1 - level)) & 1) << bit
    return mask


def block_place(mask):
    axes = block_axes()
    place = 0
    for level, bit in enumerate(axes):
        place = place + (((mask >> bit) & 1) << (len(axes) - 1 - level))
    return place


def reorder_kernel(count, offsets, *refs):
    half = len(refs) // 2
    for source, target in zip(refs[:half], refs[half:]):
        for place in range(count):
            start = pl.multiple_of(offsets[place], LANES)
            target[:, place * LANES : (place + 1) * LANES] = source[:, pl.ds(start, LANES)]


def reorder(arrays, places):
    count = len(places)
    rows, columns = arrays[0].shape
    width = columns // count
    if width % LANES:
        return [
            jnp.concatenate(
                [lax.dynamic_slice_in_dim(v, p * width, width, 1) for p in places], axis=1
            )
            for v in arrays
        ]
    spec = pl.BlockSpec((BLOCK, columns), lambda i, offsets: (i, 0))
    return pl.pallas_call(
        functools.partial(reorder_kernel, count),
        grid_spec=pltpu.PrefetchScalarGridSpec(
            num_scalar_prefetch=1,
            grid=(rows // BLOCK,),
            in_specs=[spec] * len(arrays),
            out_specs=[spec] * len(arrays),
        ),
        out_shape=[jax.ShapeDtypeStruct(v.shape, v.dtype) for v in arrays],
        compiler_params=pltpu.CompilerParams(vmem_limit_bytes=32 * 1024 * 1024),
        cost_estimate=pl.CostEstimate(
            flops=0, bytes_accessed=sum(2 * v.size * v.dtype.itemsize for v in arrays), transcendentals=0
        ),
        name="reorder",
    )(jnp.stack(places).astype(jnp.int32) * width, *arrays)


def to_relative(*arrays):
    me = lax.axis_index("dp")
    return reorder(arrays, [me ^ block_mask(place) for place in range(lax.axis_size("dp"))])


def from_relative(*arrays):
    me = lax.axis_index("dp")
    return reorder(arrays, [block_place(me ^ index) for index in range(lax.axis_size("dp"))])


def swap_halves(values):
    half = values.shape[1] // 2
    return jnp.concatenate([values[:, half:], values[:, :half]], axis=1)


def pick_first(flag, first, second, axis):
    return jnp.concatenate(
        [jnp.where(flag, first, second), jnp.where(flag, second, first)], axis=axis
    )


def build_layout(lengths, total_rows):
    block_counts = (lengths + BLOCK - 1) // BLOCK
    seq_ends = jnp.cumsum(block_counts, dtype=jnp.int32) * BLOCK
    seq_starts = seq_ends - block_counts * BLOCK
    row_ids = jnp.arange(total_rows, dtype=jnp.int32)
    membership = (
        (row_ids[:, None] >= seq_starts[None, :]) & (row_ids[:, None] < seq_ends[None, :])
    ).astype(jnp.int32)
    slot_ids = jnp.arange(lengths.shape[0], dtype=jnp.int32)
    segment = jnp.sum(membership * (slot_ids[None, :] + 1), axis=1, dtype=jnp.int32) - 1
    first_row = jnp.sum(membership * seq_starts[None, :], axis=1, dtype=jnp.int32)
    seq_limit = jnp.sum(membership * lengths[None, :], axis=1, dtype=jnp.int32)
    position = row_ids - first_row
    is_valid = (segment >= 0) & (position < seq_limit)
    allowed = (
        (segment[:, None] == segment[None, :])
        & (segment[:, None] >= 0)
        & (position[:, None] <= position[None, :])
        & is_valid[:, None]
    )
    allowed = allowed | (row_ids[:, None] == row_ids[None, :])
    bias = jnp.where(allowed, 0.0, masked_score).astype(f32)
    return position, is_valid, bias


def rotation_tables(position):
    half_dim = HEAD_DIM // 2
    lane = jnp.arange(LANES, dtype=jnp.int32)
    frequency = rope_base ** (-2.0 * (lane % half_dim).astype(f32) / HEAD_DIM)
    angles = position.astype(f32)[:, None] * frequency[None, :]
    sign = jnp.where(lane % HEAD_DIM < half_dim, -1.0, 1.0).astype(f32)
    return jnp.cos(angles), jnp.sin(angles) * sign[None, :]


def matmul(left, right):
    return jnp.dot(left, right, preferred_element_type=f32)


def contract_rows(left, right):
    return lax.dot_general(left, right, (((0,), (0,)), ((), ())), preferred_element_type=f32)


def contract_cols(left, right):
    return lax.dot_general(left, right, (((1,), (1,)), ((), ())), preferred_element_type=f32)


def rms_scale(values):
    return lax.rsqrt(jnp.mean(values * values, axis=-1, keepdims=True) + norm_epsilon)


def norm_back(grad_normed, unit_rows, row_scale, gain):
    scaled = grad_normed * gain
    grad_gain = jnp.sum(grad_normed * unit_rows, axis=0)
    grad_rows = row_scale * (
        scaled - unit_rows * jnp.mean(scaled * unit_rows, axis=-1, keepdims=True)
    )
    return grad_gain, grad_rows


def turn(values, cosine, sine):
    lane = lax.broadcasted_iota(jnp.int32, values.shape, 1)
    half_dim = HEAD_DIM // 2
    partner = jnp.where(
        lane % HEAD_DIM < half_dim,
        pltpu.roll(values, LANES - half_dim, 1),
        pltpu.roll(values, half_dim, 1),
    )
    return values * cosine + partner * sine


def doubled(values, second):
    lane = lax.broadcasted_iota(jnp.int32, values.shape, 1)
    rolled = pltpu.roll(values, HEAD_DIM, 1)
    low = lane < HEAD_DIM
    return jnp.where(second, jnp.where(low, rolled, values), jnp.where(low, values, rolled))


def split_heads(pair):
    lane = lax.broadcasted_iota(jnp.int32, pair.shape, 1)
    zero = jnp.zeros_like(pair)
    return jnp.concatenate(
        [jnp.where(lane < HEAD_DIM, pair, zero), jnp.where(lane < HEAD_DIM, zero, pair)], axis=0
    )


def join_heads(wide):
    row = lax.broadcasted_iota(jnp.int32, (LANES, BLOCK), 0)
    return jnp.where(row < HEAD_DIM, wide[:, :BLOCK], wide[:, BLOCK:]).T


def forward_kernel(
    pairs_per_kv, q_ref, k_ref, v_ref, bias_ref, cos_ref, sin_ref,
    out_ref, turned_ref, keys_ref, values_ref, total_ref, k2, v2t,
):
    pair = pl.program_id(0)
    rows = q_ref.shape[0]
    cosine, sine = cos_ref[...], sin_ref[...]

    @pl.when(pair == 0)
    def _():
        keys_ref[...] = turn(k_ref[...], cosine, sine).astype(bf16)
        values_ref[...] = v_ref[...].astype(bf16)

    @pl.when(lax.rem(pair, pairs_per_kv) == 0)
    def _():
        second = pair >= pairs_per_kv
        k2[...] = doubled(keys_ref[...].astype(f32), second).astype(bf16)
        v2t[...] = doubled(values_ref[...].astype(f32), second).T.astype(bf16)

    turned_ref[...] = (turn(q_ref[...], cosine, sine) * HEAD_DIM ** (-0.5)).astype(bf16)
    for index in range(rows // BLOCK):
        span = (index + 1) * BLOCK
        here = slice(index * BLOCK, span)
        queries = split_heads(turned_ref[here, :])
        scores = lax.dot_general(
            k2[:span, :], queries, (((1,), (1,)), ((), ())), preferred_element_type=f32
        )
        bias = bias_ref[:span, here]
        scores = scores + jnp.concatenate([bias, bias], axis=1)
        top = jnp.max(scores, axis=0, keepdims=True)
        weights = jnp.exp(scores - top)
        total = jnp.sum(weights, axis=0, keepdims=True)
        weights = (weights * (1.0 / total)).astype(bf16)
        mixed = jnp.dot(v2t[:, :span], weights, preferred_element_type=f32)
        out_ref[here, :] = join_heads(mixed).astype(bf16)
        total_ref[:, 2 * index * BLOCK : 2 * span] = top + jnp.log(total)


def backward_kernel(
    pairs_per_kv, q_ref, k_ref, v_ref, grad_ref, bias_ref, cos_ref, sin_ref, total_ref,
    dq_ref, dk_ref, dv_ref, k2, k2t, v2, dk_sum, dv_sum, dk_first, dv_first,
):
    pair = pl.program_id(0)
    rows = q_ref.shape[0]
    cosine, sine = cos_ref[...], sin_ref[...]

    @pl.when(lax.rem(pair, pairs_per_kv) == 0)
    def _():
        second = pair >= pairs_per_kv
        keys = doubled(k_ref[...].astype(f32), second)
        k2[...] = keys.astype(bf16)
        k2t[...] = keys.T.astype(bf16)
        v2[...] = doubled(v_ref[...].astype(f32), second).astype(bf16)
        dk_sum[...] = jnp.zeros_like(dk_sum)
        dv_sum[...] = jnp.zeros_like(dv_sum)

    for index in range(rows // BLOCK):
        span = (index + 1) * BLOCK
        here = slice(index * BLOCK, span)
        queries = split_heads(q_ref[here, :])
        grads = split_heads(grad_ref[here, :])
        scores = lax.dot_general(
            k2[:span, :], queries, (((1,), (1,)), ((), ())), preferred_element_type=f32
        )
        bias = bias_ref[:span, here]
        scores = scores + jnp.concatenate([bias, bias], axis=1)
        probs = jnp.exp(scores - total_ref[:, 2 * index * BLOCK : 2 * span])
        grad_prob = lax.dot_general(
            v2[:span, :], grads, (((1,), (1,)), ((), ())), preferred_element_type=f32
        )
        center = jnp.sum(probs * grad_prob, axis=0, keepdims=True)
        grad_score = (probs * (grad_prob - center)).astype(bf16)
        dv_sum[:span, :] += jnp.dot(probs.astype(bf16), grads, preferred_element_type=f32)
        dk_sum[:span, :] += jnp.dot(grad_score, queries, preferred_element_type=f32)
        wide = jnp.dot(k2t[:, :span], grad_score, preferred_element_type=f32)
        grad_query = join_heads(wide) * HEAD_DIM ** (-0.5)
        dq_ref[here, :] = turn(grad_query, cosine[here, :], -sine[here, :]).astype(bf16)

    @pl.when(pair == pairs_per_kv - 1)
    def _():
        dk_first[...] = dk_sum[...] + pltpu.roll(dk_sum[...], HEAD_DIM, 1)
        dv_first[...] = dv_sum[...] + pltpu.roll(dv_sum[...], HEAD_DIM, 1)

    @pl.when(pair == pl.num_programs(0) - 1)
    def _():
        lane = lax.broadcasted_iota(jnp.int32, dk_first.shape, 1)
        low = lane < HEAD_DIM
        keys = jnp.where(low, dk_first[...], dk_sum[...] + pltpu.roll(dk_sum[...], HEAD_DIM, 1))
        dk_ref[...] = turn(keys, cosine, -sine).astype(bf16)
        dv_ref[...] = jnp.where(
            low, dv_first[...], dv_sum[...] + pltpu.roll(dv_sum[...], HEAD_DIM, 1)
        ).astype(bf16)


def attend_forward(raw, heads_width, bias, cosine, sine):
    rows = raw.shape[0]
    pairs = heads_width // LANES
    whole = lambda shape: pl.BlockSpec(shape, lambda i: (0, 0))
    column = pl.BlockSpec((rows, LANES), lambda i: (0, i))
    return pl.pallas_call(
        functools.partial(forward_kernel, pairs // 2),
        grid=(pairs,),
        in_specs=[
            column,
            pl.BlockSpec((rows, LANES), lambda i: (0, pairs)),
            pl.BlockSpec((rows, LANES), lambda i: (0, pairs + 1)),
            whole((rows, rows)),
            whole((rows, LANES)),
            whole((rows, LANES)),
        ],
        out_specs=[
            column,
            column,
            whole((rows, LANES)),
            whole((rows, LANES)),
            pl.BlockSpec((None, 1, 2 * rows), lambda i: (i, 0, 0)),
        ],
        out_shape=[
            jax.ShapeDtypeStruct((rows, heads_width), bf16),
            jax.ShapeDtypeStruct((rows, heads_width), bf16),
            jax.ShapeDtypeStruct((rows, LANES), bf16),
            jax.ShapeDtypeStruct((rows, LANES), bf16),
            jax.ShapeDtypeStruct((pairs, 1, 2 * rows), f32),
        ],
        scratch_shapes=[pltpu.VMEM((rows, LANES), bf16), pltpu.VMEM((LANES, rows), bf16)],
        compiler_params=pltpu.CompilerParams(vmem_limit_bytes=40 * 1024 * 1024),
        cost_estimate=pl.CostEstimate(
            flops=12 * rows * rows * heads_width,
            bytes_accessed=16 * rows * heads_width,
            transcendentals=rows * rows * heads_width // HEAD_DIM,
        ),
        name="attend_forward",
    )(raw, raw, raw, bias, cosine, sine)


def attend_backward(queries, keys, values, grads, bias, cosine, sine, totals):
    rows, heads_width = queries.shape
    pairs = heads_width // LANES
    whole = lambda shape: pl.BlockSpec(shape, lambda i: (0, 0))
    column = pl.BlockSpec((rows, LANES), lambda i: (0, i))
    return pl.pallas_call(
        functools.partial(backward_kernel, pairs // 2),
        grid=(pairs,),
        in_specs=[
            column,
            whole((rows, LANES)),
            whole((rows, LANES)),
            column,
            whole((rows, rows)),
            whole((rows, LANES)),
            whole((rows, LANES)),
            pl.BlockSpec((None, 1, 2 * rows), lambda i: (i, 0, 0)),
        ],
        out_specs=[column, whole((rows, LANES)), whole((rows, LANES))],
        out_shape=[
            jax.ShapeDtypeStruct((rows, heads_width), bf16),
            jax.ShapeDtypeStruct((rows, LANES), bf16),
            jax.ShapeDtypeStruct((rows, LANES), bf16),
        ],
        scratch_shapes=[
            pltpu.VMEM((rows, LANES), bf16),
            pltpu.VMEM((LANES, rows), bf16),
            pltpu.VMEM((rows, LANES), bf16),
            pltpu.VMEM((rows, LANES), f32),
            pltpu.VMEM((rows, LANES), f32),
            pltpu.VMEM((rows, LANES), f32),
            pltpu.VMEM((rows, LANES), f32),
        ],
        compiler_params=pltpu.CompilerParams(vmem_limit_bytes=40 * 1024 * 1024),
        cost_estimate=pl.CostEstimate(
            flops=30 * rows * rows * heads_width,
            bytes_accessed=16 * rows * heads_width,
            transcendentals=rows * rows * heads_width // HEAD_DIM,
        ),
        name="attend_backward",
    )(queries, keys, values, grads, bias, cosine, sine, totals)


def own_columns(weight):
    t = (lax.axis_index("dp") >> T) & 1
    half = weight.shape[1] // 2
    own = lax.dynamic_slice_in_dim(weight, t * half, half, 1)
    other = lax.dynamic_slice_in_dim(weight, (1 - t) * half, half, 1)
    return as_block(own), as_block(other)


def finish_kernel(turned, t_ref, own_ref, came_ref, out_ref):
    half = own_ref.shape[1]
    first = t_ref[0] == 0
    own = own_ref[...]
    came = came_ref[...].astype(f32)
    low, high = jnp.where(first, own, came), jnp.where(first, came, own)
    if turned:
        out_ref[:half, :] = low.T
        out_ref[half:, :] = high.T
    else:
        out_ref[:, :half] = low
        out_ref[:, half:] = high


def finish_columns(own, came, turned):
    rows, half = own.shape
    t = (lax.axis_index("dp") >> T) & 1
    shape = (2 * half, rows) if turned else (rows, 2 * half)
    if rows % LANES:
        joined = pick_first(t == 0, own, came.astype(f32), 1)
        return joined.T if turned else joined
    return pl.pallas_call(
        functools.partial(finish_kernel, turned),
        in_specs=[
            pl.BlockSpec(memory_space=pltpu.SMEM),
            pl.BlockSpec(memory_space=pltpu.VMEM),
            pl.BlockSpec(memory_space=pltpu.VMEM),
        ],
        out_specs=pl.BlockSpec(memory_space=pltpu.VMEM),
        out_shape=jax.ShapeDtypeStruct(shape, f32),
        compiler_params=pltpu.CompilerParams(vmem_limit_bytes=32 * 1024 * 1024),
        cost_estimate=pl.CostEstimate(
            flops=0, bytes_accessed=14 * rows * half, transcendentals=0
        ),
        name="finish_columns",
    )(t.reshape(1).astype(jnp.int32), own, came)


def body(
    inputs, cotangent, seq_lengths, attn_gain, w_query, w_key, w_value, w_out,
    mlp_gain, w_gate, w_up, w_down,
):
    own_rows = inputs.shape[0]
    core = lax.axis_index("tensor")
    rest = rest_bits()
    heads_width = w_query.shape[1]
    kv_width = w_key.shape[1]
    cut = (heads_width + 2 * kv_width) // 2
    cut_out = heads_width // 2

    def along(blocks, bits, *others):
        for bit in bits:
            blocks, came = gather_step(blocks, bit, *others)
            others = ()
        return blocks, came

    deep = rest + [T]
    out_t = w_out.T
    qa, qa_z = along(as_block(w_query[:, :cut]), deep)
    qb, qb_z = along(as_block(jnp.concatenate([w_query[:, cut:], w_key, w_value], axis=1)), deep)
    gains = flat(gather_bits(as_block(jnp.stack([attn_gain, mlp_gain])), deep + [X, Y]))
    gains = gains.reshape(-1, 2, attn_gain.shape[0]).transpose(1, 0, 2).reshape(2, -1).astype(f32)
    gain_one, gain_two = gains[0], gains[1]
    oa, oa_z = along(as_block(out_t[:, :cut_out]), deep, qa_z)
    ob, ob_z = along(as_block(out_t[:, cut_out:]), deep, qb_z)
    qa, qa_x = gather_step(qa, X)
    qb, qb_y = gather_step(qb, Y)
    qa, qa_y = gather_step(qa, Y)
    qb, qb_x = gather_step(qb, X)
    query_w = jnp.concatenate([flat(qa), flat(qb)], axis=1)

    def swapped(weight, *others):
        own, other = own_columns(weight)
        return jnp.concatenate([own, exchange(after(other, *others), T)], axis=0)

    gate, gate_z = along(swapped(w_gate, qa_z), rest, oa_z)
    up, up_z = along(swapped(w_up, qb_z), rest, ob_z)
    down, down_z = along(swapped(w_down.T, oa_z, ob_z), rest, gate_z)

    oa, oa_x = gather_step(oa, X, qa_x)
    ob, ob_y = gather_step(ob, Y, qb_y)
    oa, oa_y = gather_step(oa, Y, qa_y)
    ob, ob_x = gather_step(ob, X, qb_x)
    out_w = jnp.concatenate([flat(oa), flat(ob)], axis=1)

    gate, gate_x = gather_step(gate, X, oa_x, qb_x)
    up, up_y = gather_step(up, Y, ob_y, qa_y)
    gate, gate_y = gather_step(gate, Y, oa_y)
    up, up_x = gather_step(up, X, ob_x)
    gate_w, up_w = flat(gate), flat(up)
    cut_down = down.shape[-1] // 2 // LANES * LANES
    down_a, down_ax = gather_step(down[..., :cut_down], X, gate_x, ob_x)
    down_b, down_by = gather_step(down[..., cut_down:], Y, up_y, oa_y)
    down_a, _ = gather_step(down_a, Y, gate_y)
    down_b, _ = gather_step(down_b, X, up_x)
    down_w = jnp.concatenate([flat(down_a), flat(down_b)], axis=1)

    position, is_valid, bias = build_layout(seq_lengths[0], 2 * own_rows)
    cosine, sine = rotation_tables(position)
    own_valid = lax.dynamic_slice_in_dim(is_valid, core * own_rows, own_rows, 0)[:, None]

    inputs_rel, cotangent_rel = to_relative(inputs, cotangent)
    inputs_wide = inputs_rel.astype(f32)
    scale_one = rms_scale(inputs_wide)
    unit_one = inputs_wide * scale_one
    normed_own = (unit_one * gain_one).astype(bf16)
    normed = pick_first(core == 0, normed_own, core_exchange(normed_own), 0)
    raw = matmul(normed, query_w)
    mixed, queries, keys, values, totals = attend_forward(raw, heads_width, bias, cosine, sine)
    mixed_own = lax.dynamic_slice_in_dim(mixed, core * own_rows, own_rows, 0)
    mixed_other = lax.dynamic_slice_in_dim(mixed, (1 - core) * own_rows, own_rows, 0)
    came = core_exchange(contract_cols(mixed_other, out_w).astype(bf16))
    residual = inputs_wide + (contract_cols(mixed_own, out_w) + came.astype(f32))

    scale_two = rms_scale(residual)
    unit_two = residual * scale_two
    normed_mlp_own = (unit_two * gain_two).astype(bf16)
    far_own = exchange(swap_halves(normed_mlp_own), T)
    near = jnp.concatenate([normed_mlp_own, core_exchange(normed_mlp_own)], axis=0)
    far = jnp.concatenate([far_own, core_exchange(far_own)], axis=0)
    grad_branch_own = jnp.where(own_valid, cotangent_rel, jnp.zeros_like(cotangent_rel))
    grad_far_own = exchange(after(swap_halves(grad_branch_own), far_own), T)
    grad_near = jnp.concatenate([grad_branch_own, core_exchange(grad_branch_own)], axis=0)
    grad_far = jnp.concatenate([grad_far_own, core_exchange(grad_far_own)], axis=0)
    parts = []
    for rows, grads in ((near, grad_near), (far, grad_far)):
        gate_act = matmul(rows, gate_w)
        up_act = matmul(rows, up_w)
        sigmoid_gate = jax.nn.sigmoid(gate_act)
        hidden = (gate_act * sigmoid_gate * up_act).astype(bf16)
        parts.append((rows, grads, gate_act, up_act, sigmoid_gate, hidden))
    grad_branch = jnp.concatenate([grad_near, grad_far], axis=0)
    grad_down = contract_rows(
        grad_branch, jnp.concatenate([parts[0][5], parts[1][5]], axis=0)
    ).astype(bf16)
    grads_gate, grads_up = [], []
    for rows, grads, gate_act, up_act, sigmoid_gate, hidden in parts:
        grad_hidden = matmul(grads, down_w)
        grads_gate.append(
            (
                grad_hidden * up_act * sigmoid_gate * (1.0 + gate_act * (1.0 - sigmoid_gate))
            ).astype(bf16)
        )
        grads_up.append((grad_hidden * gate_act * sigmoid_gate).astype(bf16))

    def to_owners(near_part, far_part, *others):
        far_sum = far_part[:own_rows] + core_exchange(far_part[own_rows:].astype(bf16)).astype(f32)
        came = exchange(after(swap_halves(far_sum).astype(bf16), *others), T)
        other = core_exchange(near_part[own_rows:].astype(bf16))
        return near_part[:own_rows] + other.astype(f32) + came.astype(f32), came

    far_part = contract_cols(grads_gate[1], gate_w) + contract_cols(grads_up[1], up_w)
    near_part = contract_cols(grads_gate[0], gate_w) + contract_cols(grads_up[0], up_w)
    grad_normed_mlp, grad_z = to_owners(near_part, far_part)
    normed_mlp = jnp.concatenate([near, far], axis=0)
    grad_gate_w = contract_rows(normed_mlp, jnp.concatenate(grads_gate, axis=0)).astype(bf16)
    grad_up_w = contract_rows(normed_mlp, jnp.concatenate(grads_up, axis=0)).astype(bf16)
    branch, _ = to_owners(
        contract_cols(parts[0][5], down_w), contract_cols(parts[1][5], down_w), grad_z
    )
    output = jnp.where(own_valid, residual + branch, 0.0).astype(bf16)

    def back_along(blocks, bits, last_type, *others):
        for step, bit in enumerate(bits):
            kind = last_type if step == len(bits) - 1 else bf16
            blocks, came = scatter_step(blocks, bit, kind, *others)
            others = ()
        return blocks, came

    shallow = rest[::-1]
    down_blocks = as_blocks(grad_down)
    down_a, down_ay = scatter_step(down_blocks[..., :cut_down], Y, bf16)
    down_b, down_bx = scatter_step(down_blocks[..., cut_down:], X, bf16)
    down_a, down_ax = scatter_step(down_a, X, bf16)
    down_b, down_by = scatter_step(down_b, Y, bf16)
    down_sum, _ = back_along(jnp.concatenate([down_a, down_b], axis=-1), shallow, f32)
    gate_sum, gate_y = scatter_step(as_blocks(grad_gate_w), Y, bf16, down_ay)
    up_sum, up_x = scatter_step(as_blocks(grad_up_w), X, bf16, down_bx)
    gate_sum, gate_x = scatter_step(gate_sum, X, bf16, down_ax)
    up_sum, up_y = scatter_step(up_sum, Y, bf16, down_by)
    gate_sum, _ = back_along(gate_sum, shallow, f32, grad_z)
    up_sum, _ = back_along(up_sum, shallow, f32, grad_z)

    def finish(total, turned):
        own = flat(lax.slice_in_dim(total, 0, 1, axis=0))
        sent = lax.slice_in_dim(total, 1, 2, axis=0).astype(bf16)
        return finish_columns(own, flat(exchange(sent, T)), turned)

    sum_down, sum_gate, sum_up = finish(down_sum, True), finish(gate_sum, False), finish(up_sum, False)

    grad_gain_two, grad_norm_two = norm_back(grad_normed_mlp, unit_two, scale_two, gain_two)
    grad_residual = grad_branch_own.astype(f32) + grad_norm_two
    grad_att_own = grad_residual.astype(bf16)
    grad_attended = pick_first(core == 0, grad_att_own, core_exchange(grad_att_own), 0)
    grad_mixed = matmul(grad_attended, out_w).astype(bf16)
    grad_out_w = contract_rows(grad_attended, mixed).astype(bf16)
    out_blocks = as_blocks(grad_out_w)
    out_a, out_ay = scatter_step(out_blocks[..., :cut_out], Y, bf16, gate_y)
    out_b, out_bx = scatter_step(out_blocks[..., cut_out:], X, bf16, up_x)
    out_a, out_ax = scatter_step(out_a, X, bf16, gate_x)
    out_b, out_by = scatter_step(out_b, Y, bf16, up_y)
    deep_back = [T] + shallow
    out_a, _ = back_along(out_a, deep_back, f32)
    out_b, _ = back_along(out_b, deep_back, f32)
    sum_out = jnp.concatenate([flat(out_a), flat(out_b)], axis=1).T
    d_query, d_key, d_value = attend_backward(
        queries, keys, values, grad_mixed, bias, cosine, sine, totals
    )
    d_qkv = jnp.concatenate([d_query, d_key, d_value], axis=1)
    grad_qkv_w = as_blocks(contract_rows(normed, d_qkv).astype(bf16))
    sums = []
    for blocks, bits in ((grad_qkv_w[..., :cut], [Y, X]), (grad_qkv_w[..., cut:], [X, Y])):
        blocks, _ = back_along(blocks, bits + deep_back, f32)
        sums.append(flat(blocks))
    d_own = lax.dynamic_slice_in_dim(d_qkv, core * own_rows, own_rows, 0)
    d_other = lax.dynamic_slice_in_dim(d_qkv, (1 - core) * own_rows, own_rows, 0)
    came = core_exchange(contract_cols(d_other, query_w).astype(bf16))
    grad_normed = contract_cols(d_own, query_w) + came.astype(f32)
    grad_gain_one, grad_norm_one = norm_back(grad_normed, unit_one, scale_one, gain_one)
    grad_rows = grad_residual + grad_norm_one

    def sum_gain(grad):
        grad = grad + core_exchange(grad)
        blocks = as_blocks(grad.reshape(lax.axis_size("dp"), -1))
        for bit in [Y, X] + deep_back:
            axis = block_axes().index(bit)
            kept = lax.slice_in_dim(blocks, 0, 1, axis=axis)
            blocks = kept + exchange(lax.slice_in_dim(blocks, 1, 2, axis=axis), bit)
        return blocks.reshape(-1)

    return (
        from_relative(output)[0],
        from_relative(grad_rows)[0],
        sum_gain(grad_gain_one),
        jnp.concatenate([sums[0], sums[1][:, : heads_width - cut]], axis=1),
        sums[1][:, heads_width - cut : heads_width + kv_width - cut],
        sums[1][:, heads_width + kv_width - cut :],
        sum_out,
        sum_gain(grad_gain_two),
        sum_gate,
        sum_up,
        sum_down,
    )


def solution(mesh):
    placed = (
        P(("dp", "tensor"), None),
        P(("dp", "tensor"), None),
        P("dp", None),
        P("dp"),
        P("dp", "tensor"),
        P("dp", "tensor"),
        P("dp", "tensor"),
        P("tensor", "dp"),
        P("dp"),
        P("dp", "tensor"),
        P("dp", "tensor"),
        P("tensor", "dp"),
    )
    return jax.shard_map(
        body,
        mesh=mesh,
        in_specs=placed,
        out_specs=(
            P(("dp", "tensor"), None),
            P(("dp", "tensor"), None),
            P("dp"),
            P("dp", "tensor"),
            P("dp", "tensor"),
            P("dp", "tensor"),
            P("tensor", "dp"),
            P("dp"),
            P("dp", "tensor"),
            P("dp", "tensor"),
            P("tensor", "dp"),
        ),
        check_vma=False,
    )
```

time: 2950 us -> 865 us (0.29)
  waiting for transfers between devices: 2310 us -> 369 us
  blocking collectives: 248 us -> 0 us
  matrix products: 280 us -> 177 us
  starting transfers between devices: 1.28 us -> 93.1 us
  Pallas kernels: 0 us -> 63.6 us
  local copies, waits for them, and re-layouts: 10.8 us -> 56.1 us
    reduce_scatter x11 -> x0, waiting for transfers between devices: 1820 us -> none  [the longest x1 483 us: body(): lax.psum_scatter(grad_gate_w, 'dp', scatter_dimension=0, tiled=True)]
    all_gather x9 -> x0, waiting for transfers between devices: 479 us -> none  [the longest x1 184 us: body(): lax.all_gather(w_down, 'dp', axis=1, tiled=True)]
    ppermute x0 -> x90, waiting for transfers between devices: none -> 369 us  [the longest x76 368 us: exchange(): return lax.ppermute(values, 'dp', [(i, i ^ 1 << bit) for i in range(size)])]
    all_gather x4 -> x0, blocking collectives: 168 us -> none  [the longest x1 46 us: body(): lax.all_gather(w_value, 'dp', axis=0, tiled=True)]
    ppermute x0 -> x90, starting transfers between devices: none -> 93.1 us  [the longest x76 91.6 us: exchange(): return lax.ppermute(values, 'dp', [(i, i ^ 1 << bit) for i in range(size)])]
    dot_general x19 -> x8, matrix products: 151 us -> 64.3 us  [matmul(): return jnp.dot(left, right, preferred_element_type=f32)]
    unnamed x1 -> x0, blocking collectives: 77.3 us -> none
    pallas_call x0 -> x8, Pallas kernels: none -> 63.6 us  [the longest x1 26.5 us: attend_forward(): pl.pallas_call(functools.partial(forward_kernel, pairs // 2), grid=(pairs...]
  transfers between devices with their start and end apart: 20 -> 90, of which waited for: 13 -> 36; matrix products, arithmetic and copies ran while one was open for 7% -> 36% of each run, Pallas kernels for 0% -> 7%
where the time goes in v1:
time: 865 us; the launch traced here: 855 us
  waiting for transfers between devices  369 us (43%)
  matrix products  177 us (20%)
  other arithmetic  94 us (11%)
  starting transfers between devices  93.1 us (11%)
  Pallas kernels  63.6 us (7%)
  local copies, waits for them, and re-layouts  56.1 us (6%)
    ppermute x76, waiting for transfers between devices, exchange(): return lax.ppermute(values, 'dp', [(i, i ^ 1 << bit) for i in range(size)])  368 us
    ppermute x76, starting transfers between devices, exchange(): return lax.ppermute(values, 'dp', [(i, i ^ 1 << bit) for i in range(size)])  91.6 us
    dot_general x8, matrix products, matmul(): return jnp.dot(left, right, preferred_element_type=f32)  64.3 us
    dot_general x10, matrix products, contract_cols(): lax.dot_general(left, right, (((1,), (1,)), ((), ())), preferred_element_...  58.6 us
    dot_general x5, matrix products, contract_rows(): lax.dot_general(left, right, (((0,), (0,)), ((), ())), preferred_element_...  53.7 us
    concatenate x31, other arithmetic, gather_step(): return (jnp.concatenate([values, came], axis=block_axes().index(bit)), came)  38.5 us
    unnamed x211, local copies, waits for them, and re-layouts  27 us
    pallas_call x1, Pallas kernels, attend_forward(): pl.pallas_call(functools.partial(forward_kernel, pairs // 2), grid=(pairs...  26.5 us
  transfers between devices with their start and end apart: 90, of which 36 were waited for; matrix products, arithmetic and copies ran while one was open for 36% of the time, Pallas kernels for 7%

profile of v1, /device:TPU:0, one launch (start us, length us, event | category | flops | bytes accessed | tf_op | source)
XLA Modules:
  0.0 855.1 jit_solution(423831542804683724)
XLA Ops:
  3.1 4.0 collective-permute-start.9
  9.4 2.9 collective-permute-start
  45.9 4.0 collective-permute-done.10
  54.9 4.0 collective-permute-start.13
  67.3 3.6 collective-permute-done.23
  73.3 5.3 collective-permute-done.27
  81.2 5.1 collective-permute-done.14
  86.3 4.7 collective-permute-start.24
  99.8 48.6 %collective-permute-done.28 = bf16[2,1,1,1,128,1408]{5,4,3,2,1,0:T(8,128)(2,1)S(1)} collective-permute-done((bf16[2,1,1,1,128,1408]{5,4,3,2,1,0:T(8,128)(2,1)S(1)}, bf16[2,1,1,1,128,1408]{5,4,3,2,1,0:T(8,128)(2,1)S(1)}, u32[]{:S(2)}, u32[]{:S(2)}) %collective-permute-start.28) | collective-permute-done | bytes 720928 | tf_op jit(solution)/shard_map/ppermute | solution.py:39
  153.5 6.9 collective-permute-done.15
  169.1 4.2 fusion.47.q_ref.k_ref.v_ref
  173.3 26.5 %attend_forward.1 = (bf16[768,1024]{1,0:T(8,128)(2,1)S(1)}, bf16[768,1024]{1,0:T(8,128)(2,1)S(1)}, bf16[768,128]{1,0:T(8,128)(2,1)S(1)}, bf16[768,128]{1,0:T(8,128)(2,1)S(1)}, f32[8,1,1536]{2,1,0:T(1,128)S(1)}) custom-call(f32[768,1280]{1,0:T(8,128)S(1)} %fusion.47.q_ref.k_ref.v_ref, f32[768,1280]{1,0:T(8,128)S(1)} %fusion.47.q_ref.k_ref.v_ref, ...), custom_call_target="tpu_custom_call" | custom-call | flops 7247757312 | bytes 12582912 | tf_op jit(solution)/shard_map/attend_forward/pallas_call | solution.py:349
  204.4 3.0 convolution_convert_fusion.6
  212.8 8.6 %collective-permute-done.31 = bf16[1,1,1,1,128,1408]{5,4,3,2,1,0:T(8,128)(2,1)} collective-permute-done((bf16[1,1,1,1,128,1408]{5,4,3,2,1,0:T(8,128)(2,1)}, bf16[1,1,1,1,128,1408]{5,4,3,2,1,0:T(8,128)(2,1)}, u32[]{:S(2)}, u32[]{:S(2)}) %collective-permute-start.31) | collective-permute-done | bytes 360480 | tf_op jit(solution)/shard_map/ppermute | solution.py:39
  224.9 3.1 pad_maximum_fusion.11
  229.5 3.1 pad_maximum_fusion.10
  234.6 3.5 multiply_reduce_fusion.2
  244.3 13.6 %collective-permute-done.32 = bf16[2,1,1,1,128,1408]{5,4,3,2,1,0:T(8,128)(2,1)} collective-permute-done((bf16[2,1,1,1,128,1408]{5,4,3,2,1,0:T(8,128)(2,1)}, bf16[2,1,1,1,128,1408]{5,4,3,2,1,0:T(8,128)(2,1)}, u32[]{:S(2)}, u32[]{:S(2)}) %collective-permute-start.32) | collective-permute-done | bytes 720928 | tf_op jit(solution)/shard_map/ppermute | solution.py:39
  263.1 43.2 %collective-permute-done.33 = bf16[2,2,1,1,128,640]{5,4,3,2,1,0:T(8,128)(2,1)S(1)} collective-permute-done((bf16[2,2,1,1,128,640]{5,4,3,2,1,0:T(8,128)(2,1)S(1)}, bf16[2,2,1,1,128,640]{5,4,3,2,1,0:T(8,128)(2,1)S(1)}, u32[]{:S(2)}, u32[]{:S(2)}) %collective-permute-start.33) | collective-permute-done | bytes 655392 | tf_op jit(solution)/shard_map/ppermute | solution.py:39
  306.5 7.4 collective-permute-done.35
  317.9 3.3 pad_maximum_fusion.2
  323.1 7.9 fusion.45
  331.0 3.4 pad_maximum_fusion.1
  334.5 17.6 %collective-permute-done.34 = bf16[2,2,1,2,128,640]{5,4,3,2,1,0:T(8,128)(2,1)S(1)} collective-permute-done((bf16[2,2,1,2,128,640]{5,4,3,2,1,0:T(8,128)(2,1)S(1)}, bf16[2,2,1,2,128,640]{5,4,3,2,1,0:T(8,128)(2,1)S(1)}, u32[]{:S(2)}, u32[]{:S(2)}) %collective-permute-start.34) | collective-permute-done | bytes 1310752 | tf_op jit(solution)/shard_map/ppermute | solution.py:39
  352.6 6.7 fusion.93
  359.7 9.7 %fusion.38 = f32[768,1408]{1,0:T(8,128)} fusion(bf16[384,2048]{1,0:T(8,128)(2,1)} %collective-permute-done.46, bf16[384,2048]{1,0:T(8,128)(2,1)S(1)} %copy-done.33, bf16[2048,768]{1,0:T(8,128)(2,1)S(1)} %bitcast.174, bf16[2048,640]{1,0:T(8,128)(2,1)S(1)} %bitcast.184), kind=kOutput, calls=%fused_computation.75 | convolution fusion | flops 4447010816 | bytes 13238272 | tf_op jit(solution)/shard_map/dot_general | solution.py:195
  369.4 11.2 %multiply_convert_fusion.1 = (bf16[768,1408]{1,0:T(8,128)(2,1)}, bf16[768,1408]{1,0:T(8,128)(2,1)}, bf16[768,1408]{1,0:T(8,128)(2,1)S(1)}) fusion(f32[768,1408]{1,0:T(8,128)} %fusion.38, f32[768,1408]{1,0:T(8,128)} %fusion.45, bf16[2048,1408]{1,0:T(8,128)(2,1)S(1)} %bitcast.151, bf16[384,2048]{1,0:T(8,128)(2,1)S(1)} %copy-done.92, ...), kind=kOutput, calls=%fused_computation.35 | convolution fusion | flops 4452777984 | bytes 24051712 | tf_op jit(solution)/shard_map/dot_general | solution.py:195
  380.6 7.2 fusion.95
  387.9 7.4 convolution_add_fusion
  397.7 5.1 fusion.85
  407.3 10.5 %fusion.34 = f32[768,1408]{1,0:T(8,128)} fusion(bf16[384,2048]{1,0:T(8,128)(2,1)} %collective-permute-done.42, bf16[384,2048]{1,0:T(8,128)(2,1)} %collective-permute-done.41, bf16[2048,768]{1,0:T(8,128)(2,1)S(1)} %bitcast.176, bf16[2048,640]{1,0:T(8,128)(2,1)} %bitcast.185), kind=kOutput, calls=%fused_computation.71 | convolution fusion | flops 4447010816 | bytes 13238272 | tf_op jit(solution)/shard_map/dot_general | solution.py:195
  417.8 10.7 %multiply_convert_fusion.3 = (bf16[768,1408]{1,0:T(8,128)(2,1)}, bf16[768,1408]{1,0:T(8,128)(2,1)}, bf16[768,1408]{1,0:T(8,128)(2,1)}) fusion(f32[768,1408]{1,0:T(8,128)} %fusion.34, f32[768,1408]{1,0:T(8,128)} %fusion.93, bf16[768,2048]{1,0:T(8,128)(2,1)S(1)} %copy-done.76, bf16[2048,1408]{1,0:T(8,128)(2,1)S(1)} %bitcast.155), kind=kOutput, calls=%fused_computation.37 | convolution fusion | flops 4446486528 | bytes 24051712 | tf_op jit(solution)/shard_map/dot_general | solution.py:195
  428.5 15.1 %convolution_convert_fusion.1 = bf16[2048,1408]{1,0:T(8,128)(2,1)} fusion(bf16[384,2048]{1,0:T(8,128)(2,1)} %collective-permute-done.42, bf16[384,2048]{1,0:T(8,128)(2,1)} %collective-permute-done.41, bf16[384,2048]{1,0:T(8,128)(2,1)} %collective-permute-done.46, bf16[384,2048]{1,0:T(8,128)(2,1)S(1)} %copy-done.33, ...), kind=kOutput, calls=%fused_computation.1 | convolution fusion | flops 8895070208 | bytes 16384000 | tf_op jit(solution)/shard_map/dot_general | solution.py:199
  447.9 9.8 %fusion.94 = f32[768,2048]{1,0:T(8,128)} fusion(bf16[768,1408]{1,0:T(8,128)(2,1)S(1)} %copy-done.96, bf16[2048,1408]{1,0:T(8,128)(2,1)} %bitcast.150), kind=kOutput, calls=%fused_computation.276 | convolution fusion | flops 4429185024 | bytes 14221312 | tf_op jit(solution)/shard_map/dot_general | solution.py:203
  457.8 7.2 convolution_add_fusion.1
  472.5 15.1 %convolution_convert_fusion = bf16[2048,1408]{1,0:T(8,128)(2,1)} fusion(bf16[768,1408]{1,0:T(8,128)(2,1)} %get-tuple-element.144, bf16[768,1408]{1,0:T(8,128)(2,1)} %copy-done.95, bf16[384,2048]{1,0:T(8,128)(2,1)S(1)} %copy-done.65, bf16[384,2048]{1,0:T(8,128)(2,1)} %collective-permute-done.38, bf16[384,2048]{1,0:T(8,128)(2,1)} %copy-done.91, ...), kind=kOutput, calls=%fused_computation | convolution fusion | flops 8895070208 | bytes 16384000 | tf_op jit(solution)/shard_map/dot_general | solution.py:199
  487.6 14.9 %convolution_convert_fusion.2 = bf16[2048,1408]{1,0:T(8,128)(2,1)} fusion(bf16[768,1408]{1,0:T(8,128)(2,1)} %get-tuple-element.142, bf16[768,1408]{1,0:T(8,128)(2,1)} %get-tuple-element.139, bf16[384,2048]{1,0:T(8,128)(2,1)S(1)} %copy-done.65, bf16[384,2048]{1,0:T(8,128)(2,1)} %collective-permute-done.38, bf16[384,2048]{1,0:T(8,128)(2,1)} %copy-done.91, ...), kind=kOutput, calls=%fused_computation.2 | convolution fusion | flops 8895070208 | bytes 16384000 | tf_op jit(solution)/shard_map/dot_general | solution.py:199
  502.5 7.6 fusion.84
  518.2 2.8 add_convert_fusion.5
  529.6 8.5 collective-permute-done.66
  538.5 8.7 %collective-permute-done.74 = bf16[2,2,1,1,128,768]{5,4,3,2,1,0:T(8,128)(2,1)S(1)} collective-permute-done((bf16[2,2,1,1,128,768]{5,4,3,2,1,0:T(8,128)(2,1)S(1)}, bf16[2,2,1,1,128,768]{5,4,3,2,1,0:T(8,128)(2,1)S(1)}, u32[]{:S(2)}, u32[]{:S(2)}) %collective-permute-start.74) | collective-permute-done | bytes 786464 | tf_op jit(solution)/shard_map/ppermute | solution.py:39
  549.6 20.6 %collective-permute-done.44 = bf16[384,2048]{1,0:T(8,128)(2,1)S(1)} collective-permute-done((bf16[384,2048]{1,0:T(8,128)(2,1)S(1)}, bf16[384,2048]{1,0:T(8,128)(2,1)S(1)}, u32[]{:S(2)}, u32[]{:S(2)}) %collective-permute-start.44) | collective-permute-done | bytes 1572896 | tf_op jit(solution)/shard_map/ppermute | solution.py:39
  574.3 33.6 %collective-permute-done.80 = f32[2,2,1,2,1,128]{5,4,3,2,1,0:T(1,128)S(1)} collective-permute-done((f32[2,2,1,2,1,128]{5,4,3,2,1,0:T(1,128)S(1)}, f32[2,2,1,2,1,128]{5,4,3,2,1,0:T(1,128)S(1)}, u32[]{:S(2)}, u32[]{:S(2)}) %collective-permute-start.80) | collective-permute-done | bytes 4128 | tf_op jit(solution)/shard_map/ppermute | solution.py:39
  613.1 5.8 collective-permute-done.82
  629.5 23.6 %collective-permute-done.45 = bf16[384,2048]{1,0:T(8,128)(2,1)} collective-permute-done((bf16[384,2048]{1,0:T(8,128)(2,1)}, bf16[384,2048]{1,0:T(8,128)(2,1)}, u32[]{:S(2)}, u32[]{:S(2)}) %collective-permute-start.45) | collective-permute-done | bytes 1572896 | tf_op jit(solution)/shard_map/ppermute | solution.py:39
  653.1 5.0 fusion.86
  671.2 3.4 fusion.48.grad_ref
  674.7 26.3 %attend_backward.1 = (bf16[768,1024]{1,0:T(8,128)(2,1)S(1)}, bf16[768,128]{1,0:T(8,128)(2,1)S(1)}, bf16[768,128]{1,0:T(8,128)(2,1)S(1)}) custom-call(bf16[768,1024]{1,0:T(8,128)(2,1)S(1)} %copy-done.14, bf16[768,128]{1,0:T(8,128)(2,1)S(1)} %copy-done.16, bf16[768,128]{1,0:T(8,128)(2,1)S(1)} %copy-done.18, bf16[768,1024]{1,0:T(8,128)(2,1)S(1)} %fusion.48.grad_ref, ...), custom_call_target="tpu_custom_call" | custom-call | flops 18119393280 | bytes 12582912 | tf_op jit(solution)/shard_map/attend_backward/pallas_call | solution.py:390
  703.0 4.7 convolution_convert_fusion.3
  710.0 4.0 convolution_convert_fusion.4
  716.2 3.4 convolution_convert_fusion.5
  723.5 8.0 collective-permute-done.86
  732.8 8.7 %collective-permute-done.85 = bf16[1,1,1,1,128,1408]{5,4,3,2,1,0:T(8,128)(2,1)S(1)} collective-permute-done((bf16[1,1,1,1,128,1408]{5,4,3,2,1,0:T(8,128)(2,1)S(1)}, bf16[1,1,1,1,128,1408]{5,4,3,2,1,0:T(8,128)(2,1)S(1)}, u32[]{:S(2)}, u32[]{:S(2)}) %collective-permute-start.85) | collective-permute-done | bytes 360480 | tf_op jit(solution)/shard_map/ppermute | solution.py:39
  743.1 7.6 collective-permute-done.87
  752.2 21.1 %collective-permute-done.73 = bf16[2,2,2,1,128,512]{5,4,3,2,1,0:T(8,128)(2,1)S(1)} collective-permute-done((bf16[2,2,2,1,128,512]{5,4,3,2,1,0:T(8,128)(2,1)}, bf16[2,2,2,1,128,512]{5,4,3,2,1,0:T(8,128)(2,1)S(1)}, u32[]{:S(2)}, u32[]{:S(2)}) %collective-permute-start.73) | collective-permute-done | bytes 1048608 | tf_op jit(solution)/shard_map/ppermute | solution.py:39
  777.2 4.4 fusion.25
  784.3 9.5 %collective-permute-done.76 = bf16[2,2,1,1,128,512]{5,4,3,2,1,0:T(8,128)(2,1)S(1)} collective-permute-done((bf16[2,2,1,1,128,512]{5,4,3,2,1,0:T(8,128)(2,1)S(1)}, bf16[2,2,1,1,128,512]{5,4,3,2,1,0:T(8,128)(2,1)S(1)}, u32[]{:S(2)}, u32[]{:S(2)}) %collective-permute-start.76) | collective-permute-done | bytes 524320 | tf_op jit(solution)/shard_map/ppermute | solution.py:39
  793.9 10.9 %collective-permute-done.51 = f32[2,2,1,2,1,128]{5,4,3,2,1,0:T(1,128)S(1)} collective-permute-done((f32[2,2,1,2,1,128]{5,4,3,2,1,0:T(1,128)S(1)}, f32[2,2,1,2,1,128]{5,4,3,2,1,0:T(1,128)S(1)}, u32[]{:S(2)}, u32[]{:S(2)}) %collective-permute-start.51) | collective-permute-done | bytes 4128 | tf_op jit(solution)/shard_map/ppermute | solution.py:39
  814.1 2.8 reorder.5
  819.6 8.0 collective-permute-done.69
  830.4 5.3 collective-permute-done.70
  836.7 3.2 collective-permute-done.61
  841.1 5.0 collective-permute-done.57
  849.1 4.7 collective-permute-done.58
  (533 shorter events, 227.0 us)
Async XLA Ops:
  3.1 34.3 %collective-permute-start.9 = (bf16[1,1,1,1,128,640]{5,4,3,2,1,0:T(8,128)(2,1)}, bf16[1,1,1,1,128,640]{5,4,3,2,1,0:T(8,128)(2,1)}, u32[]{:S(2)}, u32[]{:S(2)}) collective-permute-start(bf16[1,1,1,1,128,640]{5,4,3,2,1,0:T(8,128)(2,1)} %maximum_bitcast_fusion.1), channel_id=1, source_target_pairs={{0,16},{2,18},{4,20},{6,22},{8,24},{10,26},{12,28},{14,30},{16,0},... | collective-permute-start | bytes 491528 | tf_op jit(solution)/shard_map/ppermute | solution.py:39
  8.7 30.9 %collective-permute-start.5 = (bf16[1,1,1,1,128,640]{5,4,3,2,1,0:T(8,128)(2,1)}, bf16[1,1,1,1,128,640]{5,4,3,2,1,0:T(8,128)(2,1)}, u32[]{:S(2)}, u32[]{:S(2)}) collective-permute-start(bf16[1,1,1,1,128,640]{5,4,3,2,1,0:T(8,128)(2,1)} %slice_bitcast_fusion.3), channel_id=1, source_target_pairs={{0,16},{2,18},{4,20},{6,22},{8,24},{10,26},{12,28},{14,30},{16,0},... | collective-permute-start | bytes 491528 | tf_op jit(solution)/shard_map/ppermute | solution.py:39
  9.4 13.0 %collective-permute-start = (bf16[1,1,1,1,2,128]{5,4,3,2,1,0:T(2,128)(2,1)S(1)}, bf16[1,1,1,1,2,128]{5,4,3,2,1,0:T(2,128)(2,1)S(1)}, u32[]{:S(2)}, u32[]{:S(2)}) collective-permute-start(bf16[1,1,1,1,2,128]{5,4,3,2,1,0:T(2,128)(2,1)S(1)} %maximum_bitcast_fusion.2), channel_id=1, source_target_pairs={{0,16},{2,18},{4,20},{6,22},{8,24},{10,26},{12,28},{14,30},{16,0},... | collective-permute-start | bytes 1544 | tf_op jit(solution)/shard_map/ppermute | solution.py:39
  41.4 13.5 %collective-permute-start.6 = (bf16[1,2,1,1,128,640]{5,4,3,2,1,0:T(8,128)(2,1)}, bf16[1,2,1,1,128,640]{5,4,3,2,1,0:T(8,128)(2,1)}, u32[]{:S(2)}, u32[]{:S(2)}) collective-permute-start(bf16[1,2,1,1,128,640]{5,4,3,2,1,0:T(8,128)(2,1)} %pad_maximum_fusion.61), channel_id=1, source_target_pairs={{0,8},{2,10},{4,12},{6,14},{8,0},{10,2},{12,4},{14,6},{16,24},{18,... | collective-permute-start | bytes 983048 | tf_op jit(solution)/shard_map/ppermute | solution.py:39
  45.2 50.1 %collective-permute-start.4 = (bf16[384,2048]{1,0:T(8,128)(2,1)}, bf16[384,2048]{1,0:T(8,128)(2,1)}, u32[]{:S(2)}, u32[]{:S(2)}) collective-permute-start(bf16[384,2048]{1,0:T(8,128)(2,1)} %fusion.20), channel_id=1, source_target_pairs={{0,1},{1,0},{2,3},{3,2},{4,5},{5,4},{6,7},{7,6},{8,9},{9,8},{10,11... | collective-permute-start | bytes 4718600 | tf_op jit(solution)/shard_map/ppermute | solution.py:43
  49.9 13.5 %collective-permute-start.17 = (bf16[1,1,1,1,128,512]{5,4,3,2,1,0:T(8,128)(2,1)}, bf16[1,1,1,1,128,512]{5,4,3,2,1,0:T(8,128)(2,1)S(1)}, u32[]{:S(2)}, u32[]{:S(2)}) collective-permute-start(bf16[1,1,1,1,128,512]{5,4,3,2,1,0:T(8,128)(2,1)} %get-tuple-element.58), channel_id=1, source_target_pairs={{0,16},{2,18},{4,20},{6,22},{8,24},{10,26},{12,28},{14,30},{16,0},... | collective-permute-start | bytes 393224 | tf_op jit(solution)/shard_map/ppermute | solution.py:39
  60.6 18.0 %collective-permute-start.27 = (bf16[1,1,1,1,128,1408]{5,4,3,2,1,0:T(8,128)(2,1)}, bf16[1,1,1,1,128,1408]{5,4,3,2,1,0:T(8,128)(2,1)S(1)}, u32[]{:S(2)}, u32[]{:S(2)}) collective-permute-start(bf16[1,1,1,1,128,1408]{5,4,3,2,1,0:T(8,128)(2,1)} %get-tuple-element.65), channel_id=1, source_target_pairs={{0,8},{2,10},{4,12},{6,14},{8,0},{10,2},{12,4},{14,6},{16,24},{18,... | collective-permute-start | bytes 1081352 | tf_op jit(solution)/shard_map/ppermute | solution.py:39
  63.4 27.9 %collective-permute-start.11 = (bf16[2,2,1,1,128,640]{5,4,3,2,1,0:T(8,128)(2,1)S(1)}, bf16[2,2,1,1,128,640]{5,4,3,2,1,0:T(8,128)(2,1)S(1)}, u32[]{:S(2)}, u32[]{:S(2)}) collective-permute-start(bf16[2,2,1,1,128,640]{5,4,3,2,1,0:T(8,128)(2,1)S(1)} %pad_maximum_fusion.57), channel_id=1, source_target_pairs={{0,4},{2,6},{4,0},{6,2},{8,12},{10,14},{12,8},{14,10},{16,20},{18,... | collective-permute-start | bytes 1966088 | tf_op jit(solution)/shard_map/ppermute | solution.py:39
  65.8 26.7 %collective-permute-start.7 = (bf16[2,2,1,1,128,640]{5,4,3,2,1,0:T(8,128)(2,1)S(1)}, bf16[2,2,1,1,128,640]{5,4,3,2,1,0:T(8,128)(2,1)S(1)}, u32[]{:S(2)}, u32[]{:S(2)}) collective-permute-start(bf16[2,2,1,1,128,640]{5,4,3,2,1,0:T(8,128)(2,1)S(1)} %pad_maximum_fusion.56), channel_id=1, source_target_pairs={{0,2},{2,0},{4,6},{6,4},{8,10},{10,8},{12,14},{14,12},{16,18},{18,... | collective-permute-start | bytes 1966088 | tf_op jit(solution)/shard_map/ppermute | solution.py:39
  70.9 20.1 %collective-permute-start.18 = (bf16[1,2,1,1,128,512]{5,4,3,2,1,0:T(8,128)(2,1)S(1)}, bf16[1,2,1,1,128,512]{5,4,3,2,1,0:T(8,128)(2,1)S(1)}, u32[]{:S(2)}, u32[]{:S(2)}) collective-permute-start(bf16[1,2,1,1,128,512]{5,4,3,2,1,0:T(8,128)(2,1)S(1)} %pad_maximum_fusion.64), channel_id=1, source_target_pairs={{0,8},{2,10},{4,12},{6,14},{8,0},{10,2},{12,4},{14,6},{16,24},{18,... | collective-permute-start | bytes 786440 | tf_op jit(solution)/shard_map/ppermute | solution.py:39
  86.3 64.7 %collective-permute-start.24 = (bf16[2,1,1,1,128,1408]{5,4,3,2,1,0:T(8,128)(2,1)S(1)}, bf16[2,1,1,1,128,1408]{5,4,3,2,1,0:T(8,128)(2,1)S(1)}, u32[]{:S(2)}, u32[]{:S(2)}) collective-permute-start(bf16[2,1,1,1,128,1408]{5,4,3,2,1,0:T(8,128)(2,1)S(1)} %pad_maximum_fusion.52), channel_id=1, source_target_pairs={{0,16},{2,18},{4,20},{6,22},{8,24},{10,26},{12,28},{14,30},{16,0},... | collective-permute-start | bytes 2162696 | tf_op jit(solution)/shard_map/ppermute | solution.py:39
  91.0 57.3 %collective-permute-start.28 = (bf16[2,1,1,1,128,1408]{5,4,3,2,1,0:T(8,128)(2,1)S(1)}, bf16[2,1,1,1,128,1408]{5,4,3,2,1,0:T(8,128)(2,1)S(1)}, u32[]{:S(2)}, u32[]{:S(2)}) collective-permute-start(bf16[2,1,1,1,128,1408]{5,4,3,2,1,0:T(8,128)(2,1)S(1)} %pad_maximum_fusion.53), channel_id=1, source_target_pairs={{0,16},{2,18},{4,20},{6,22},{8,24},{10,26},{12,28},{14,30},{16,0},... | collective-permute-start | bytes 2162696 | tf_op jit(solution)/shard_map/ppermute | solution.py:39
  91.2 61.2 %collective-permute-start.19 = (bf16[2,2,1,1,128,512]{5,4,3,2,1,0:T(8,128)(2,1)S(1)}, bf16[2,2,1,1,128,512]{5,4,3,2,1,0:T(8,128)(2,1)S(1)}, u32[]{:S(2)}, u32[]{:S(2)}) collective-permute-start(bf16[2,2,1,1,128,512]{5,4,3,2,1,0:T(8,128)(2,1)S(1)} %pad_maximum_fusion.59), channel_id=1, source_target_pairs={{0,4},{2,6},{4,0},{6,2},{8,12},{10,14},{12,8},{14,10},{16,20},{18,... | collective-permute-start | bytes 1572872 | tf_op jit(solution)/shard_map/ppermute | solution.py:39
  92.6 68.9 %collective-permute-start.12 = (bf16[2,2,2,1,128,640]{5,4,3,2,1,0:T(8,128)(2,1)S(1)}, bf16[2,2,2,1,128,640]{5,4,3,2,1,0:T(8,128)(2,1)S(1)}, u32[]{:S(2)}, u32[]{:S(2)}) collective-permute-start(bf16[2,2,2,1,128,640]{5,4,3,2,1,0:T(8,128)(2,1)S(1)} %pad_maximum_fusion.38), channel_id=1, source_target_pairs={{0,2},{2,0},{4,6},{6,4},{8,10},{10,8},{12,14},{14,12},{16,18},{18,... | collective-permute-start | bytes 3932168 | tf_op jit(solution)/shard_map/ppermute | solution.py:39
  95.3 67.5 %collective-permute-start.8 = (bf16[2,2,1,2,128,640]{5,4,3,2,1,0:T(8,128)(2,1)S(1)}, bf16[2,2,1,2,128,640]{5,4,3,2,1,0:T(8,128)(2,1)S(1)}, u32[]{:S(2)}, u32[]{:S(2)}) collective-permute-start(bf16[2,2,1,2,128,640]{5,4,3,2,1,0:T(8,128)(2,1)S(1)} %pad_maximum_fusion.37), channel_id=1, source_target_pairs={{0,4},{2,6},{4,0},{6,2},{8,12},{10,14},{12,8},{14,10},{16,20},{18,... | collective-permute-start | bytes 3932168 | tf_op jit(solution)/shard_map/ppermute | solution.py:39
  161.4 38.5 %collective-permute-start.20 = (bf16[2,2,2,1,128,512]{5,4,3,2,1,0:T(8,128)(2,1)}, bf16[2,2,2,1,128,512]{5,4,3,2,1,0:T(8,128)(2,1)}, u32[]{:S(2)}, u32[]{:S(2)}) collective-permute-start(bf16[2,2,2,1,128,512]{5,4,3,2,1,0:T(8,128)(2,1)} %pad_maximum_fusion.48), channel_id=1, source_target_pairs={{0,2},{2,0},{4,6},{6,4},{8,10},{10,8},{12,14},{14,12},{16,18},{18,... | collective-permute-start | bytes 3145736 | tf_op jit(solution)/shard_map/ppermute | solution.py:39
  162.8 39.3 %collective-permute-start.16 = (bf16[2,2,1,2,128,512]{5,4,3,2,1,0:T(8,128)(2,1)}, bf16[2,2,1,2,128,512]{5,4,3,2,1,0:T(8,128)(2,1)}, u32[]{:S(2)}, u32[]{:S(2)}) collective-permute-start(bf16[2,2,1,2,128,512]{5,4,3,2,1,0:T(8,128)(2,1)} %pad_maximum_fusion.47), channel_id=1, source_target_pairs={{0,4},{2,6},{4,0},{6,2},{8,12},{10,14},{12,8},{14,10},{16,20},{18,... | collective-permute-start | bytes 3145736 | tf_op jit(solution)/shard_map/ppermute | solution.py:39
  163.9 61.0 %collective-permute-start.29 = (bf16[2,2,1,1,128,1408]{5,4,3,2,1,0:T(8,128)(2,1)}, bf16[2,2,1,1,128,1408]{5,4,3,2,1,0:T(8,128)(2,1)}, u32[]{:S(2)}, u32[]{:S(2)}) collective-permute-start(bf16[2,2,1,1,128,1408]{5,4,3,2,1,0:T(8,128)(2,1)} %pad_maximum_fusion.36), channel_id=1, source_target_pairs={{0,4},{2,6},{4,0},{6,2},{8,12},{10,14},{12,8},{14,10},{16,20},{18,... | collective-permute-start | bytes 4325384 | tf_op jit(solution)/shard_map/ppermute | solution.py:39
  164.8 64.7 %collective-permute-start.25 = (bf16[2,2,1,1,128,1408]{5,4,3,2,1,0:T(8,128)(2,1)}, bf16[2,2,1,1,128,1408]{5,4,3,2,1,0:T(8,128)(2,1)}, u32[]{:S(2)}, u32[]{:S(2)}) collective-permute-start(bf16[2,2,1,1,128,1408]{5,4,3,2,1,0:T(8,128)(2,1)} %pad_maximum_fusion.35), channel_id=1, source_target_pairs={{0,2},{2,0},{4,6},{6,4},{8,10},{10,8},{12,14},{14,12},{16,18},{18,... | collective-permute-start | bytes 4325384 | tf_op jit(solution)/shard_map/ppermute | solution.py:39
  207.4 27.2 %collective-permute-start.21 = (bf16[384,2048]{1,0:T(8,128)(2,1)}, bf16[384,2048]{1,0:T(8,128)(2,1)}, u32[]{:S(2)}, u32[]{:S(2)}) collective-permute-start(bf16[384,2048]{1,0:T(8,128)(2,1)} %convolution_convert_fusion.6), channel_id=1, source_target_pairs={{0,1},{1,0},{2,3},{3,2},{4,5},{5,4},{6,7},{7,6},{8,9},{9,8},{10,11... | collective-permute-start | bytes 4718600 | tf_op jit(solution)/shard_map/ppermute | solution.py:43
  223.4 34.5 %collective-permute-start.32 = (bf16[2,1,1,1,128,1408]{5,4,3,2,1,0:T(8,128)(2,1)}, bf16[2,1,1,1,128,1408]{5,4,3,2,1,0:T(8,128)(2,1)}, u32[]{:S(2)}, u32[]{:S(2)}) collective-permute-start(bf16[2,1,1,1,128,1408]{5,4,3,2,1,0:T(8,128)(2,1)} %pad_maximum_fusion.54), channel_id=1, source_target_pairs={{0,16},{2,18},{4,20},{6,22},{8,24},{10,26},{12,28},{14,30},{16,0},... | collective-permute-start | bytes 2162696 | tf_op jit(solution)/shard_map/ppermute | solution.py:39
  228.0 89.2 %collective-permute-start.30 = (bf16[2,2,2,1,128,1408]{5,4,3,2,1,0:T(8,128)(2,1)}, bf16[2,2,2,1,128,1408]{5,4,3,2,1,0:T(8,128)(2,1)}, u32[]{:S(2)}, u32[]{:S(2)}) collective-permute-start(bf16[2,2,2,1,128,1408]{5,4,3,2,1,0:T(8,128)(2,1)} %pad_maximum_fusion.11), channel_id=1, source_target_pairs={{0,2},{2,0},{4,6},{6,4},{8,10},{10,8},{12,14},{14,12},{16,18},{18,... | collective-permute-start | bytes 8650760 | tf_op jit(solution)/shard_map/ppermute | solution.py:39
  232.6 84.9 %collective-permute-start.26 = (bf16[2,2,1,2,128,1408]{5,4,3,2,1,0:T(8,128)(2,1)}, bf16[2,2,1,2,128,1408]{5,4,3,2,1,0:T(8,128)(2,1)}, u32[]{:S(2)}, u32[]{:S(2)}) collective-permute-start(bf16[2,2,1,2,128,1408]{5,4,3,2,1,0:T(8,128)(2,1)} %pad_maximum_fusion.10), channel_id=1, source_target_pairs={{0,4},{2,6},{4,0},{6,2},{8,12},{10,14},{12,8},{14,10},{16,20},{18,... | collective-permute-start | bytes 8650760 | tf_op jit(solution)/shard_map/ppermute | solution.py:39
  241.1 73.0 %collective-permute-start.38 = (bf16[384,2048]{1,0:T(8,128)(2,1)}, bf16[384,2048]{1,0:T(8,128)(2,1)}, u32[]{:S(2)}, u32[]{:S(2)}) collective-permute-start(bf16[384,2048]{1,0:T(8,128)(2,1)} %pad_maximum_fusion.26), channel_id=1, source_target_pairs={{0,8},{2,10},{4,12},{6,14},{8,0},{10,2},{12,4},{14,6},{16,24},{18,... | collective-permute-start | bytes 4718600 | tf_op jit(solution)/shard_map/ppermute | solution.py:39
  259.1 47.3 %collective-permute-start.33 = (bf16[2,2,1,1,128,640]{5,4,3,2,1,0:T(8,128)(2,1)S(1)}, bf16[2,2,1,1,128,640]{5,4,3,2,1,0:T(8,128)(2,1)S(1)}, u32[]{:S(2)}, u32[]{:S(2)}) collective-permute-start(bf16[2,2,1,1,128,640]{5,4,3,2,1,0:T(8,128)(2,1)S(1)} %pad_maximum_fusion.55), channel_id=1, source_target_pairs={{0,2},{2,0},{4,6},{6,4},{8,10},{10,8},{12,14},{14,12},{16,18},{18,... | collective-permute-start | bytes 1966088 | tf_op jit(solution)/shard_map/ppermute | solution.py:39
  261.7 52.2 %collective-permute-start.35 = (bf16[2,2,1,1,128,768]{5,4,3,2,1,0:T(8,128)(2,1)S(1)}, bf16[2,2,1,1,128,768]{5,4,3,2,1,0:T(8,128)(2,1)S(1)}, u32[]{:S(2)}, u32[]{:S(2)}) collective-permute-start(bf16[2,2,1,1,128,768]{5,4,3,2,1,0:T(8,128)(2,1)S(1)} %pad_maximum_fusion.49), channel_id=1, source_target_pairs={{0,4},{2,6},{4,0},{6,2},{8,12},{10,14},{12,8},{14,10},{16,20},{18,... | collective-permute-start | bytes 2359304 | tf_op jit(solution)/shard_map/ppermute | solution.py:39
  306.3 14.9 %collective-permute-start.22 = (bf16[384,2048]{1,0:T(8,128)(2,1)S(1)}, bf16[384,2048]{1,0:T(8,128)(2,1)S(1)}, u32[]{:S(2)}, u32[]{:S(2)}) collective-permute-start(bf16[384,2048]{1,0:T(8,128)(2,1)S(1)} %multiply_convert_fusion.6), channel_id=1, source_target_pairs={{0,1},{1,0},{2,3},{3,2},{4,5},{5,4},{6,7},{7,6},{8,9},{9,8},{10,11... | collective-permute-start | bytes 4718600 | tf_op jit(solution)/shard_map/ppermute | solution.py:43
  313.9 45.7 %collective-permute-start.46 = (bf16[384,2048]{1,0:T(8,128)(2,1)S(1)}, bf16[384,2048]{1,0:T(8,128)(2,1)}, u32[]{:S(2)}, u32[]{:S(2)}) collective-permute-start(bf16[384,2048]{1,0:T(8,128)(2,1)S(1)} %copy-done.33), channel_id=1, source_target_pairs={{0,1},{1,0},{2,3},{3,2},{4,5},{5,4},{6,7},{7,6},{8,9},{9,8},{10,11... | collective-permute-start | bytes 4718600 | tf_op jit(solution)/shard_map/ppermute | solution.py:43
  314.1 38.3 %collective-permute-start.41 = (bf16[384,2048]{1,0:T(8,128)(2,1)S(1)}, bf16[384,2048]{1,0:T(8,128)(2,1)}, u32[]{:S(2)}, u32[]{:S(2)}) collective-permute-start(bf16[384,2048]{1,0:T(8,128)(2,1)S(1)} %pad_maximum_fusion.28), channel_id=1, source_target_pairs={{0,8},{2,10},{4,12},{6,14},{8,0},{10,2},{12,4},{14,6},{16,24},{18,... | collective-permute-start | bytes 4718600 | tf_op jit(solution)/shard_map/ppermute | solution.py:39
  317.2 35.2 %collective-permute-start.39 = (bf16[384,2048]{1,0:T(8,128)(2,1)}, bf16[384,2048]{1,0:T(8,128)(2,1)S(1)}, u32[]{:S(2)}, u32[]{:S(2)}) collective-permute-start(bf16[384,2048]{1,0:T(8,128)(2,1)} %collective-permute-done.38), channel_id=1, source_target_pairs={{0,1},{1,0},{2,3},{3,2},{4,5},{5,4},{6,7},{7,6},{8,9},{9,8},{10,11... | collective-permute-start | bytes 4718600 | tf_op jit(solution)/shard_map/ppermute | solution.py:43
  317.5 41.8 %collective-permute-start.36 = (bf16[2,2,2,1,128,768]{5,4,3,2,1,0:T(8,128)(2,1)S(1)}, bf16[2,2,2,1,128,768]{5,4,3,2,1,0:T(8,128)(2,1)S(1)}, u32[]{:S(2)}, u32[]{:S(2)}) collective-permute-start(bf16[2,2,2,1,128,768]{5,4,3,2,1,0:T(8,128)(2,1)S(1)} %pad_maximum_fusion.25), channel_id=1, source_target_pairs={{0,2},{2,0},{4,6},{6,4},{8,10},{10,8},{12,14},{14,12},{16,18},{18,... | collective-permute-start | bytes 4718600 | tf_op jit(solution)/shard_map/ppermute | solution.py:39
  321.3 30.8 %collective-permute-start.34 = (bf16[2,2,1,2,128,640]{5,4,3,2,1,0:T(8,128)(2,1)S(1)}, bf16[2,2,1,2,128,640]{5,4,3,2,1,0:T(8,128)(2,1)S(1)}, u32[]{:S(2)}, u32[]{:S(2)}) collective-permute-start(bf16[2,2,1,2,128,640]{5,4,3,2,1,0:T(8,128)(2,1)S(1)} %pad_maximum_fusion.39), channel_id=1, source_target_pairs={{0,4},{2,6},{4,0},{6,2},{8,12},{10,14},{12,8},{14,10},{16,20},{18,... | collective-permute-start | bytes 3932168 | tf_op jit(solution)/shard_map/ppermute | solution.py:39
  352.4 54.9 %collective-permute-start.42 = (bf16[384,2048]{1,0:T(8,128)(2,1)}, bf16[384,2048]{1,0:T(8,128)(2,1)}, u32[]{:S(2)}, u32[]{:S(2)}) collective-permute-start(bf16[384,2048]{1,0:T(8,128)(2,1)} %collective-permute-done.41), channel_id=1, source_target_pairs={{0,1},{1,0},{2,3},{3,2},{4,5},{5,4},{6,7},{7,6},{8,9},{9,8},{10,11... | collective-permute-start | bytes 4718600 | tf_op jit(solution)/shard_map/ppermute | solution.py:43
  396.6 152.5 %collective-permute-start.47 = (bf16[384,2048]{1,0:T(8,128)(2,1)}, bf16[384,2048]{1,0:T(8,128)(2,1)S(1)}, u32[]{:S(2)}, u32[]{:S(2)}) collective-permute-start(bf16[384,2048]{1,0:T(8,128)(2,1)} %slice.625), channel_id=1, source_target_pairs={{0,1},{1,0},{2,3},{3,2},{4,5},{5,4},{6,7},{7,6},{8,9},{9,8},{10,11... | collective-permute-start | bytes 4718600 | tf_op jit(solution)/shard_map/ppermute | solution.py:43
  406.8 222.4 %collective-permute-start.37 = (bf16[384,2048]{1,0:T(8,128)(2,1)}, bf16[384,2048]{1,0:T(8,128)(2,1)}, u32[]{:S(2)}, u32[]{:S(2)}) collective-permute-start(bf16[384,2048]{1,0:T(8,128)(2,1)} %slice.628), channel_id=1, source_target_pairs={{0,1},{1,0},{2,3},{3,2},{4,5},{5,4},{6,7},{7,6},{8,9},{9,8},{10,11... | collective-permute-start | bytes 4718600 | tf_op jit(solution)/shard_map/ppermute | solution.py:43
  469.0 52.0 %collective-permute-start.43 = (bf16[384,2048]{1,0:T(8,128)(2,1)}, bf16[384,2048]{1,0:T(8,128)(2,1)}, u32[]{:S(2)}, u32[]{:S(2)}) collective-permute-start(bf16[384,2048]{1,0:T(8,128)(2,1)} %slice.626), channel_id=1, source_target_pairs={{0,1},{1,0},{2,3},{3,2},{4,5},{5,4},{6,7},{7,6},{8,9},{9,8},{10,11... | collective-permute-start | bytes 4718600 | tf_op jit(solution)/shard_map/ppermute | solution.py:43
  469.1 54.7 %collective-permute-start.71 = (bf16[2,2,2,1,128,768]{5,4,3,2,1,0:T(8,128)(2,1)S(1)}, bf16[2,2,2,1,128,768]{5,4,3,2,1,0:T(8,128)(2,1)}, u32[]{:S(2)}, u32[]{:S(2)}) collective-permute-start(bf16[2,2,2,1,128,768]{5,4,3,2,1,0:T(8,128)(2,1)S(1)} %slice.507), channel_id=1, source_target_pairs={{0,2},{2,0},{4,6},{6,4},{8,10},{10,8},{12,14},{14,12},{16,18},{18,... | collective-permute-start | bytes 4718600 | tf_op jit(solution)/shard_map/ppermute | solution.py:39
  470.7 47.5 %collective-permute-start.63 = (bf16[2,2,1,2,128,640]{5,4,3,2,1,0:T(8,128)(2,1)}, bf16[2,2,1,2,128,640]{5,4,3,2,1,0:T(8,128)(2,1)}, u32[]{:S(2)}, u32[]{:S(2)}) collective-permute-start(bf16[2,2,1,2,128,640]{5,4,3,2,1,0:T(8,128)(2,1)} %slice.493), channel_id=1, source_target_pairs={{0,4},{2,6},{4,0},{6,2},{8,12},{10,14},{12,8},{14,10},{16,20},{18,... | collective-permute-start | bytes 3932168 | tf_op jit(solution)/shard_map/ppermute | solution.py:39
  521.1 17.0 %collective-permute-start.66 = (bf16[2,2,1,1,128,640]{5,4,3,2,1,0:T(8,128)(2,1)S(1)}, bf16[2,2,1,1,128,640]{5,4,3,2,1,0:T(8,128)(2,1)S(1)}, u32[]{:S(2)}, u32[]{:S(2)}) collective-permute-start(bf16[2,2,1,1,128,640]{5,4,3,2,1,0:T(8,128)(2,1)S(1)} %slice.499), channel_id=1, source_target_pairs={{0,2},{2,0},{4,6},{6,4},{8,10},{10,8},{12,14},{14,12},{16,18},{18,... | collective-permute-start | bytes 1966088 | tf_op jit(solution)/shard_map/ppermute | solution.py:39
  523.8 46.4 %collective-permute-start.44 = (bf16[384,2048]{1,0:T(8,128)(2,1)S(1)}, bf16[384,2048]{1,0:T(8,128)(2,1)S(1)}, u32[]{:S(2)}, u32[]{:S(2)}) collective-permute-start(bf16[384,2048]{1,0:T(8,128)(2,1)S(1)} %pad_maximum_fusion.29), channel_id=1, source_target_pairs={{0,8},{2,10},{4,12},{6,14},{8,0},{10,2},{12,4},{14,6},{16,24},{18,... | collective-permute-start | bytes 4718600 | tf_op jit(solution)/shard_map/ppermute | solution.py:39
  526.7 20.5 %collective-permute-start.74 = (bf16[2,2,1,1,128,768]{5,4,3,2,1,0:T(8,128)(2,1)S(1)}, bf16[2,2,1,1,128,768]{5,4,3,2,1,0:T(8,128)(2,1)S(1)}, u32[]{:S(2)}, u32[]{:S(2)}) collective-permute-start(bf16[2,2,1,1,128,768]{5,4,3,2,1,0:T(8,128)(2,1)S(1)} %slice.513), channel_id=1, source_target_pairs={{0,4},{2,6},{4,0},{6,2},{8,12},{10,14},{12,8},{14,10},{16,20},{18,... | collective-permute-start | bytes 2359304 | tf_op jit(solution)/shard_map/ppermute | solution.py:39
  538.0 82.3 %collective-permute-start.64 = (bf16[2,2,1,2,128,1408]{5,4,3,2,1,0:T(8,128)(2,1)}, bf16[2,2,1,2,128,1408]{5,4,3,2,1,0:T(8,128)(2,1)}, u32[]{:S(2)}, u32[]{:S(2)}) collective-permute-start(bf16[2,2,1,2,128,1408]{5,4,3,2,1,0:T(8,128)(2,1)} %slice.492), channel_id=1, source_target_pairs={{0,4},{2,6},{4,0},{6,2},{8,12},{10,14},{12,8},{14,10},{16,20},{18,... | collective-permute-start | bytes 8650760 | tf_op jit(solution)/shard_map/ppermute | solution.py:39
  547.2 76.3 %collective-permute-start.72 = (bf16[2,2,2,1,128,1408]{5,4,3,2,1,0:T(8,128)(2,1)}, bf16[2,2,2,1,128,1408]{5,4,3,2,1,0:T(8,128)(2,1)S(1)}, u32[]{:S(2)}, u32[]{:S(2)}) collective-permute-start(bf16[2,2,2,1,128,1408]{5,4,3,2,1,0:T(8,128)(2,1)} %slice.506), channel_id=1, source_target_pairs={{0,2},{2,0},{4,6},{6,4},{8,10},{10,8},{12,14},{14,12},{16,18},{18,... | collective-permute-start | bytes 8650760 | tf_op jit(solution)/shard_map/ppermute | solution.py:39
  549.2 60.5 %collective-permute-start.88 = (bf16[2,1,1,1,128,1408]{5,4,3,2,1,0:T(8,128)(2,1)S(1)}, bf16[2,1,1,1,128,1408]{5,4,3,2,1,0:T(8,128)(2,1)S(1)}, u32[]{:S(2)}, u32[]{:S(2)}) collective-permute-start(bf16[2,1,1,1,128,1408]{5,4,3,2,1,0:T(8,128)(2,1)S(1)} %pad_maximum_fusion.51), channel_id=1, source_target_pairs={{0,16},{2,18},{4,20},{6,22},{8,24},{10,26},{12,28},{14,30},{16,0},... | collective-permute-start | bytes 2162696 | tf_op jit(solution)/shard_map/ppermute | solution.py:39
  572.7 35.1 %collective-permute-start.80 = (f32[2,2,1,2,1,128]{5,4,3,2,1,0:T(1,128)S(1)}, f32[2,2,1,2,1,128]{5,4,3,2,1,0:T(1,128)S(1)}, u32[]{:S(2)}, u32[]{:S(2)}) collective-permute-start(f32[2,2,1,2,1,128]{5,4,3,2,1,0:T(1,128)S(1)} %slice.519), channel_id=1, source_target_pairs={{0,4},{2,6},{4,0},{6,2},{8,12},{10,14},{12,8},{14,10},{16,20},{18,... | collective-permute-start | bytes 12296 | tf_op jit(solution)/shard_map/ppermute | solution.py:39
  609.8 48.9 %collective-permute-start.89 = (bf16[1,1,1,1,128,1408]{5,4,3,2,1,0:T(8,128)(2,1)S(1)}, bf16[1,1,1,1,128,1408]{5,4,3,2,1,0:T(8,128)(2,1)S(1)}, u32[]{:S(2)}, u32[]{:S(2)}) collective-permute-start(bf16[1,1,1,1,128,1408]{5,4,3,2,1,0:T(8,128)(2,1)S(1)} %slice.629), channel_id=1, source_target_pairs={{0,8},{2,10},{4,12},{6,14},{8,0},{10,2},{12,4},{14,6},{16,24},{18,... | collective-permute-start | bytes 1081352 | tf_op jit(solution)/shard_map/ppermute | solution.py:39
  618.8 34.2 %collective-permute-start.45 = (bf16[384,2048]{1,0:T(8,128)(2,1)}, bf16[384,2048]{1,0:T(8,128)(2,1)}, u32[]{:S(2)}, u32[]{:S(2)}) collective-permute-start(bf16[384,2048]{1,0:T(8,128)(2,1)} %pad_maximum_fusion.27), channel_id=1, source_target_pairs={{0,8},{2,10},{4,12},{6,14},{8,0},{10,2},{12,4},{14,6},{16,24},{18,... | collective-permute-start | bytes 4718600 | tf_op jit(solution)/shard_map/ppermute | solution.py:39
  620.4 37.8 %collective-permute-start.83 = (f32[1,1,1,1,1,128]{5,4,3,2,1,0:T(1,128)S(1)}, f32[1,1,1,1,1,128]{5,4,3,2,1,0:T(1,128)S(1)}, u32[]{:S(2)}, u32[]{:S(2)}) collective-permute-start(f32[1,1,1,1,1,128]{5,4,3,2,1,0:T(1,128)S(1)} %slice.525), channel_id=1, source_target_pairs={{0,16},{2,18},{4,20},{6,22},{8,24},{10,26},{12,28},{14,30},{16,0},... | collective-permute-start | bytes 1544 | tf_op jit(solution)/shard_map/ppermute | solution.py:39
  625.1 37.6 %collective-permute-start.67 = (bf16[2,2,1,1,128,1408]{5,4,3,2,1,0:T(8,128)(2,1)S(1)}, bf16[2,2,1,1,128,1408]{5,4,3,2,1,0:T(8,128)(2,1)}, u32[]{:S(2)}, u32[]{:S(2)}) collective-permute-start(bf16[2,2,1,1,128,1408]{5,4,3,2,1,0:T(8,128)(2,1)S(1)} %slice.497), channel_id=1, source_target_pairs={{0,2},{2,0},{4,6},{6,4},{8,10},{10,8},{12,14},{14,12},{16,18},{18,... | collective-permute-start | bytes 4325384 | tf_op jit(solution)/shard_map/ppermute | solution.py:39
  629.2 36.6 %collective-permute-start.75 = (bf16[2,2,1,1,128,1408]{5,4,3,2,1,0:T(8,128)(2,1)}, bf16[2,2,1,1,128,1408]{5,4,3,2,1,0:T(8,128)(2,1)}, u32[]{:S(2)}, u32[]{:S(2)}) collective-permute-start(bf16[2,2,1,1,128,1408]{5,4,3,2,1,0:T(8,128)(2,1)} %slice.511), channel_id=1, source_target_pairs={{0,4},{2,6},{4,0},{6,2},{8,12},{10,14},{12,8},{14,10},{16,20},{18,... | collective-permute-start | bytes 4325384 | tf_op jit(solution)/shard_map/ppermute | solution.py:39
  665.4 56.3 %collective-permute-start.84 = (bf16[2,1,1,1,128,1408]{5,4,3,2,1,0:T(8,128)(2,1)}, bf16[2,1,1,1,128,1408]{5,4,3,2,1,0:T(8,128)(2,1)}, u32[]{:S(2)}, u32[]{:S(2)}) collective-permute-start(bf16[2,1,1,1,128,1408]{5,4,3,2,1,0:T(8,128)(2,1)} %slice.528), channel_id=1, source_target_pairs={{0,16},{2,18},{4,20},{6,22},{8,24},{10,26},{12,28},{14,30},{16,0},... | collective-permute-start | bytes 2162696 | tf_op jit(solution)/shard_map/ppermute | solution.py:39
  668.4 63.0 %collective-permute-start.86 = (bf16[2,1,1,1,128,1408]{5,4,3,2,1,0:T(8,128)(2,1)}, bf16[2,1,1,1,128,1408]{5,4,3,2,1,0:T(8,128)(2,1)}, u32[]{:S(2)}, u32[]{:S(2)}) collective-permute-start(bf16[2,1,1,1,128,1408]{5,4,3,2,1,0:T(8,128)(2,1)} %slice.533), channel_id=1, source_target_pairs={{0,16},{2,18},{4,20},{6,22},{8,24},{10,26},{12,28},{14,30},{16,0},... | collective-permute-start | bytes 2162696 | tf_op jit(solution)/shard_map/ppermute | solution.py:39
  719.6 57.6 %collective-permute-start.49 = (bf16[384,2048]{1,0:T(8,128)(2,1)}, bf16[384,2048]{1,0:T(8,128)(2,1)}, u32[]{:S(2)}, u32[]{:S(2)}) collective-permute-start(bf16[384,2048]{1,0:T(8,128)(2,1)} %convolution_convert_fusion.5), channel_id=1, source_target_pairs={{0,1},{1,0},{2,3},{3,2},{4,5},{5,4},{6,7},{7,6},{8,9},{9,8},{10,11... | collective-permute-start | bytes 4718600 | tf_op jit(solution)/shard_map/ppermute | solution.py:43
  719.6 55.4 %collective-permute-start.59 = (bf16[2,2,2,1,128,640]{5,4,3,2,1,0:T(8,128)(2,1)S(1)}, bf16[2,2,2,1,128,640]{5,4,3,2,1,0:T(8,128)(2,1)S(1)}, u32[]{:S(2)}, u32[]{:S(2)}) collective-permute-start(bf16[2,2,2,1,128,640]{5,4,3,2,1,0:T(8,128)(2,1)S(1)} %slice.480), channel_id=1, source_target_pairs={{0,2},{2,0},{4,6},{6,4},{8,10},{10,8},{12,14},{14,12},{16,18},{18,... | collective-permute-start | bytes 3932168 | tf_op jit(solution)/shard_map/ppermute | solution.py:39
  719.9 53.3 %collective-permute-start.73 = (bf16[2,2,2,1,128,512]{5,4,3,2,1,0:T(8,128)(2,1)}, bf16[2,2,2,1,128,512]{5,4,3,2,1,0:T(8,128)(2,1)S(1)}, u32[]{:S(2)}, u32[]{:S(2)}) collective-permute-start(bf16[2,2,2,1,128,512]{5,4,3,2,1,0:T(8,128)(2,1)} %slice.505), channel_id=1, source_target_pairs={{0,2},{2,0},{4,6},{6,4},{8,10},{10,8},{12,14},{14,12},{16,18},{18,... | collective-permute-start | bytes 3145736 | tf_op jit(solution)/shard_map/ppermute | solution.py:39
  721.6 52.5 %collective-permute-start.65 = (bf16[2,2,1,2,128,512]{5,4,3,2,1,0:T(8,128)(2,1)}, bf16[2,2,1,2,128,512]{5,4,3,2,1,0:T(8,128)(2,1)S(1)}, u32[]{:S(2)}, u32[]{:S(2)}) collective-permute-start(bf16[2,2,1,2,128,512]{5,4,3,2,1,0:T(8,128)(2,1)} %slice.491), channel_id=1, source_target_pairs={{0,4},{2,6},{4,0},{6,2},{8,12},{10,14},{12,8},{14,10},{16,20},{18,... | collective-permute-start | bytes 3145736 | tf_op jit(solution)/shard_map/ppermute | solution.py:39
  750.6 31.9 %collective-permute-start.55 = (bf16[2,2,1,2,128,640]{5,4,3,2,1,0:T(8,128)(2,1)}, bf16[2,2,1,2,128,640]{5,4,3,2,1,0:T(8,128)(2,1)S(1)}, u32[]{:S(2)}, u32[]{:S(2)}) collective-permute-start(bf16[2,2,1,2,128,640]{5,4,3,2,1,0:T(8,128)(2,1)} %slice.472), channel_id=1, source_target_pairs={{0,4},{2,6},{4,0},{6,2},{8,12},{10,14},{12,8},{14,10},{16,20},{18,... | collective-permute-start | bytes 3932168 | tf_op jit(solution)/shard_map/ppermute | solution.py:39
  773.7 20.1 %collective-permute-start.76 = (bf16[2,2,1,1,128,512]{5,4,3,2,1,0:T(8,128)(2,1)S(1)}, bf16[2,2,1,1,128,512]{5,4,3,2,1,0:T(8,128)(2,1)S(1)}, u32[]{:S(2)}, u32[]{:S(2)}) collective-permute-start(bf16[2,2,1,1,128,512]{5,4,3,2,1,0:T(8,128)(2,1)S(1)} %slice.509), channel_id=1, source_target_pairs={{0,4},{2,6},{4,0},{6,2},{8,12},{10,14},{12,8},{14,10},{16,20},{18,... | collective-permute-start | bytes 1572872 | tf_op jit(solution)/shard_map/ppermute | solution.py:39
  774.6 39.4 %collective-permute-start.68 = (bf16[2,2,1,1,128,512]{5,4,3,2,1,0:T(8,128)(2,1)S(1)}, bf16[2,2,1,1,128,512]{5,4,3,2,1,0:T(8,128)(2,1)S(1)}, u32[]{:S(2)}, u32[]{:S(2)}) collective-permute-start(bf16[2,2,1,1,128,512]{5,4,3,2,1,0:T(8,128)(2,1)S(1)} %slice.495), channel_id=1, source_target_pairs={{0,2},{2,0},{4,6},{6,4},{8,10},{10,8},{12,14},{14,12},{16,18},{18,... | collective-permute-start | bytes 1572872 | tf_op jit(solution)/shard_map/ppermute | solution.py:39
  775.5 52.3 %collective-permute-start.60 = (bf16[2,2,1,1,128,640]{5,4,3,2,1,0:T(8,128)(2,1)S(1)}, bf16[2,2,1,1,128,640]{5,4,3,2,1,0:T(8,128)(2,1)S(1)}, u32[]{:S(2)}, u32[]{:S(2)}) collective-permute-start(bf16[2,2,1,1,128,640]{5,4,3,2,1,0:T(8,128)(2,1)S(1)} %slice.482), channel_id=1, source_target_pairs={{0,4},{2,6},{4,0},{6,2},{8,12},{10,14},{12,8},{14,10},{16,20},{18,... | collective-permute-start | bytes 1966088 | tf_op jit(solution)/shard_map/ppermute | solution.py:39
  783.0 46.2 %collective-permute-start.56 = (bf16[2,2,1,1,128,640]{5,4,3,2,1,0:T(8,128)(2,1)S(1)}, bf16[2,2,1,1,128,640]{5,4,3,2,1,0:T(8,128)(2,1)S(1)}, u32[]{:S(2)}, u32[]{:S(2)}) collective-permute-start(bf16[2,2,1,1,128,640]{5,4,3,2,1,0:T(8,128)(2,1)S(1)} %slice.474), channel_id=1, source_target_pairs={{0,2},{2,0},{4,6},{6,4},{8,10},{10,8},{12,14},{14,12},{16,18},{18,... | collective-permute-start | bytes 1966088 | tf_op jit(solution)/shard_map/ppermute | solution.py:39
  783.9 20.9 %collective-permute-start.51 = (f32[2,2,1,2,1,128]{5,4,3,2,1,0:T(1,128)S(1)}, f32[2,2,1,2,1,128]{5,4,3,2,1,0:T(1,128)S(1)}, u32[]{:S(2)}, u32[]{:S(2)}) collective-permute-start(f32[2,2,1,2,1,128]{5,4,3,2,1,0:T(1,128)S(1)} %slice.464), channel_id=1, source_target_pairs={{0,4},{2,6},{4,0},{6,2},{8,12},{10,14},{12,8},{14,10},{16,20},{18,... | collective-permute-start | bytes 12296 | tf_op jit(solution)/shard_map/ppermute | solution.py:39
  805.2 13.5 %collective-permute-start.77 = (bf16[1,2,1,1,128,512]{5,4,3,2,1,0:T(8,128)(2,1)S(1)}, bf16[1,2,1,1,128,512]{5,4,3,2,1,0:T(8,128)(2,1)S(1)}, u32[]{:S(2)}, u32[]{:S(2)}) collective-permute-start(bf16[1,2,1,1,128,512]{5,4,3,2,1,0:T(8,128)(2,1)S(1)} %slice.515), channel_id=1, source_target_pairs={{0,8},{2,10},{4,12},{6,14},{8,0},{10,2},{12,4},{14,6},{16,24},{18,... | collective-permute-start | bytes 786440 | tf_op jit(solution)/shard_map/ppermute | solution.py:39
  829.4 16.7 %collective-permute-start.57 = (bf16[1,2,1,1,128,640]{5,4,3,2,1,0:T(8,128)(2,1)S(1)}, bf16[1,2,1,1,128,640]{5,4,3,2,1,0:T(8,128)(2,1)S(1)}, u32[]{:S(2)}, u32[]{:S(2)}) collective-permute-start(bf16[1,2,1,1,128,640]{5,4,3,2,1,0:T(8,128)(2,1)S(1)} %slice.476), channel_id=1, source_target_pairs={{0,8},{2,10},{4,12},{6,14},{8,0},{10,2},{12,4},{14,6},{16,24},{18,... | collective-permute-start | bytes 983048 | tf_op jit(solution)/shard_map/ppermute | solution.py:39
  (128 other events, 2073.3 us)

commit v2 on v1

v2 whole, which is shorter than its diff:
```python
import functools

import jax
import jax.numpy as jnp
from jax import lax
from jax.experimental import pallas as pl
from jax.experimental.layout import Layout, with_layout_constraint
from jax.experimental.pallas import tpu as pltpu
from jax.sharding import PartitionSpec as P

HEAD_DIM = 64
BLOCK = 128
LANES = 128

norm_epsilon = 1e-05
rope_base = 10000.0
masked_score = -1e30

bf16 = jnp.bfloat16
f32 = jnp.float32

X, Y, T, Z = 0, 1, 2, 3


def nbits():
    return lax.axis_size("dp").bit_length() - 1


def block_axes():
    return [T] + list(range(nbits() - 1, Z - 1, -1)) + [Y, X]


def rest_bits():
    return list(range(Z, nbits()))


def exchange(values, bit):
    size = lax.axis_size("dp")
    return lax.ppermute(values, "dp", [(i, i ^ (1 << bit)) for i in range(size)])


def core_exchange(values):
    return lax.ppermute(values, "tensor", [(0, 1), (1, 0)])


def as_block(values):
    return values.reshape((1,) * nbits() + values.shape)


def after(values, *others):
    return lax.optimization_barrier((values,) + others)[0] if others else values


def row_major(values):
    return with_layout_constraint(values, Layout(major_to_minor=tuple(range(values.ndim))))


def join(values, came, bit):
    return jnp.concatenate([values, came], axis=block_axes().index(bit))


def part(values, bit, index):
    return lax.slice_in_dim(values, index, index + 1, axis=block_axes().index(bit))


def columns(values, low, high):
    return lax.slice_in_dim(values, low, high, axis=values.ndim - 1)


def add(kept, came, kind=bf16):
    return row_major((kept.astype(f32) + came.astype(f32)).astype(kind))


def flat(blocks):
    return blocks.reshape(-1, blocks.shape[-1])


def as_blocks(rows):
    return rows.reshape((2,) * nbits() + (rows.shape[0] // lax.axis_size("dp"), rows.shape[1]))


def block_mask(place):
    axes = block_axes()
    mask = 0
    for level, bit in enumerate(axes):
        mask |= ((place >> (len(axes) - 1 - level)) & 1) << bit
    return mask


def block_place(mask):
    axes = block_axes()
    place = 0
    for level, bit in enumerate(axes):
        place = place + (((mask >> bit) & 1) << (len(axes) - 1 - level))
    return place


def reorder_kernel(count, offsets, *refs):
    half = len(refs) // 2
    for source, target in zip(refs[:half], refs[half:]):
        for place in range(count):
            start = pl.multiple_of(offsets[place], LANES)
            target[:, place * LANES : (place + 1) * LANES] = source[:, pl.ds(start, LANES)]


def reorder(arrays, places):
    count = len(places)
    rows, columns = arrays[0].shape
    width = columns // count
    if width % LANES:
        return [
            jnp.concatenate(
                [lax.dynamic_slice_in_dim(v, p * width, width, 1) for p in places], axis=1
            )
            for v in arrays
        ]
    spec = pl.BlockSpec((BLOCK, columns), lambda i, offsets: (i, 0))
    return pl.pallas_call(
        functools.partial(reorder_kernel, count),
        grid_spec=pltpu.PrefetchScalarGridSpec(
            num_scalar_prefetch=1,
            grid=(rows // BLOCK,),
            in_specs=[spec] * len(arrays),
            out_specs=[spec] * len(arrays),
        ),
        out_shape=[jax.ShapeDtypeStruct(v.shape, v.dtype) for v in arrays],
        compiler_params=pltpu.CompilerParams(vmem_limit_bytes=32 * 1024 * 1024),
        cost_estimate=no_cost(),
        name="reorder",
    )(jnp.stack(places).astype(jnp.int32) * width, *arrays)


def to_relative(*arrays):
    me = lax.axis_index("dp")
    return reorder(arrays, [me ^ block_mask(place) for place in range(lax.axis_size("dp"))])


def from_relative(*arrays):
    me = lax.axis_index("dp")
    return reorder(arrays, [block_place(me ^ index) for index in range(lax.axis_size("dp"))])


def swap_halves(values):
    half = values.shape[1] // 2
    return jnp.concatenate([values[:, half:], values[:, :half]], axis=1)


def pick_first(flag, first, second, axis):
    return jnp.concatenate(
        [jnp.where(flag, first, second), jnp.where(flag, second, first)], axis=axis
    )


def build_layout(lengths, total_rows):
    block_counts = (lengths + BLOCK - 1) // BLOCK
    seq_ends = jnp.cumsum(block_counts, dtype=jnp.int32) * BLOCK
    seq_starts = seq_ends - block_counts * BLOCK
    row_ids = jnp.arange(total_rows, dtype=jnp.int32)
    membership = (
        (row_ids[:, None] >= seq_starts[None, :]) & (row_ids[:, None] < seq_ends[None, :])
    ).astype(jnp.int32)
    slot_ids = jnp.arange(lengths.shape[0], dtype=jnp.int32)
    segment = jnp.sum(membership * (slot_ids[None, :] + 1), axis=1, dtype=jnp.int32) - 1
    first_row = jnp.sum(membership * seq_starts[None, :], axis=1, dtype=jnp.int32)
    seq_limit = jnp.sum(membership * lengths[None, :], axis=1, dtype=jnp.int32)
    position = row_ids - first_row
    is_valid = (segment >= 0) & (position < seq_limit)
    allowed = (
        (segment[:, None] == segment[None, :])
        & (segment[:, None] >= 0)
        & (position[:, None] <= position[None, :])
        & is_valid[:, None]
    )
    allowed = allowed | (row_ids[:, None] == row_ids[None, :])
    bias = jnp.where(allowed, 0.0, masked_score).astype(f32)
    return position, is_valid, bias


def rotation_tables(position):
    half_dim = HEAD_DIM // 2
    lane = jnp.arange(LANES, dtype=jnp.int32)
    frequency = rope_base ** (-2.0 * (lane % half_dim).astype(f32) / HEAD_DIM)
    angles = position.astype(f32)[:, None] * frequency[None, :]
    sign = jnp.where(lane % HEAD_DIM < half_dim, -1.0, 1.0).astype(f32)
    return jnp.cos(angles), jnp.sin(angles) * sign[None, :]


def matmul(left, right):
    return jnp.dot(left, right, preferred_element_type=f32)


def contract_rows(left, right):
    return lax.dot_general(left, right, (((0,), (0,)), ((), ())), preferred_element_type=f32)


def contract_cols(left, right):
    return lax.dot_general(left, right, (((1,), (1,)), ((), ())), preferred_element_type=f32)


def rms_scale(values):
    return lax.rsqrt(jnp.mean(values * values, axis=-1, keepdims=True) + norm_epsilon)


def norm_back(grad_normed, unit_rows, row_scale, gain):
    scaled = grad_normed * gain
    grad_gain = jnp.sum(grad_normed * unit_rows, axis=0)
    grad_rows = row_scale * (
        scaled - unit_rows * jnp.mean(scaled * unit_rows, axis=-1, keepdims=True)
    )
    return grad_gain, grad_rows


def turn(values, cosine, sine):
    lane = lax.broadcasted_iota(jnp.int32, values.shape, 1)
    half_dim = HEAD_DIM // 2
    partner = jnp.where(
        lane % HEAD_DIM < half_dim,
        pltpu.roll(values, LANES - half_dim, 1),
        pltpu.roll(values, half_dim, 1),
    )
    return values * cosine + partner * sine


def doubled(values, second):
    lane = lax.broadcasted_iota(jnp.int32, values.shape, 1)
    rolled = pltpu.roll(values, HEAD_DIM, 1)
    low = lane < HEAD_DIM
    return jnp.where(second, jnp.where(low, rolled, values), jnp.where(low, values, rolled))


def split_heads(pair):
    lane = lax.broadcasted_iota(jnp.int32, pair.shape, 1)
    zero = jnp.zeros_like(pair)
    return jnp.concatenate(
        [jnp.where(lane < HEAD_DIM, pair, zero), jnp.where(lane < HEAD_DIM, zero, pair)], axis=0
    )


def join_heads(wide):
    row = lax.broadcasted_iota(jnp.int32, (LANES, BLOCK), 0)
    return jnp.where(row < HEAD_DIM, wide[:, :BLOCK], wide[:, BLOCK:]).T


def forward_kernel(
    second, q_ref, k_ref, v_ref, bias_ref, cos_ref, sin_ref,
    out_ref, turned_ref, keys_ref, values_ref, total_ref, v2t,
):
    rows = q_ref.shape[0]
    cosine, sine = cos_ref[...], sin_ref[...]

    @pl.when(pl.program_id(0) == 0)
    def _():
        keys = turn(k_ref[...], cosine, sine).astype(bf16).astype(f32)
        keys_ref[...] = doubled(keys, second).astype(bf16)
        values = doubled(v_ref[...], second)
        values_ref[...] = values.astype(bf16)
        v2t[...] = values.T.astype(bf16)

    turned_ref[...] = (turn(q_ref[...], cosine, sine) * HEAD_DIM ** (-0.5)).astype(bf16)
    for index in range(rows // BLOCK):
        span = (index + 1) * BLOCK
        here = slice(index * BLOCK, span)
        queries = split_heads(turned_ref[here, :])
        scores = lax.dot_general(
            keys_ref[:span, :], queries, (((1,), (1,)), ((), ())), preferred_element_type=f32
        )
        bias = bias_ref[:span, here]
        scores = scores + jnp.concatenate([bias, bias], axis=1)
        top = jnp.max(scores, axis=0, keepdims=True)
        weights = jnp.exp(scores - top)
        total = jnp.sum(weights, axis=0, keepdims=True)
        weights = (weights * (1.0 / total)).astype(bf16)
        mixed = jnp.dot(v2t[:, :span], weights, preferred_element_type=f32)
        out_ref[here, :] = join_heads(mixed).astype(bf16)
        total_ref[:, 2 * index * BLOCK : 2 * span] = top + jnp.log(total)


def backward_kernel(
    q_ref, k_ref, v_ref, grad_ref, bias_ref, cos_ref, sin_ref, total_ref,
    dq_ref, dk_ref, dv_ref, k2t, dk_sum, dv_sum,
):
    pair = pl.program_id(0)
    rows = q_ref.shape[0]
    cosine, sine = cos_ref[...], sin_ref[...]

    @pl.when(pair == 0)
    def _():
        k2t[...] = k_ref[...].astype(f32).T.astype(bf16)
        dk_sum[...] = jnp.zeros_like(dk_sum)
        dv_sum[...] = jnp.zeros_like(dv_sum)

    for index in range(rows // BLOCK):
        span = (index + 1) * BLOCK
        here = slice(index * BLOCK, span)
        queries = split_heads(q_ref[here, :])
        grads = split_heads(grad_ref[here, :])
        scores = lax.dot_general(
            k_ref[:span, :], queries, (((1,), (1,)), ((), ())), preferred_element_type=f32
        )
        bias = bias_ref[:span, here]
        scores = scores + jnp.concatenate([bias, bias], axis=1)
        probs = jnp.exp(scores - total_ref[:, 2 * index * BLOCK : 2 * span])
        grad_prob = lax.dot_general(
            v_ref[:span, :], grads, (((1,), (1,)), ((), ())), preferred_element_type=f32
        )
        center = jnp.sum(probs * grad_prob, axis=0, keepdims=True)
        grad_score = (probs * (grad_prob - center)).astype(bf16)
        dv_sum[:span, :] += jnp.dot(probs.astype(bf16), grads, preferred_element_type=f32)
        dk_sum[:span, :] += jnp.dot(grad_score, queries, preferred_element_type=f32)
        wide = jnp.dot(k2t[:, :span], grad_score, preferred_element_type=f32)
        grad_query = join_heads(wide) * HEAD_DIM ** (-0.5)
        dq_ref[here, :] = turn(grad_query, cosine[here, :], -sine[here, :]).astype(bf16)

    @pl.when(pair == pl.num_programs(0) - 1)
    def _():
        keys = dk_sum[...] + pltpu.roll(dk_sum[...], HEAD_DIM, 1)
        dk_ref[...] = turn(keys, cosine, -sine).astype(bf16)
        dv_ref[...] = (dv_sum[...] + pltpu.roll(dv_sum[...], HEAD_DIM, 1)).astype(bf16)


def attend_forward(raw, heads_width, group, bias, cosine, sine):
    rows = raw.shape[0]
    pairs = heads_width // LANES
    own = pairs // 2
    whole = lambda shape: pl.BlockSpec(shape, lambda i: (0, 0))
    column = pl.BlockSpec((rows, LANES), lambda i: (0, i))
    wide = jax.ShapeDtypeStruct((rows, own * LANES), bf16)
    narrow = jax.ShapeDtypeStruct((rows, LANES), bf16)
    return pl.pallas_call(
        functools.partial(forward_kernel, group == 1),
        grid=(own,),
        in_specs=[
            pl.BlockSpec((rows, LANES), lambda i: (0, group * own + i)),
            pl.BlockSpec((rows, LANES), lambda i: (0, pairs)),
            pl.BlockSpec((rows, LANES), lambda i: (0, pairs + 1)),
            whole((rows, rows)),
            whole((rows, LANES)),
            whole((rows, LANES)),
        ],
        out_specs=[
            column,
            column,
            whole((rows, LANES)),
            whole((rows, LANES)),
            pl.BlockSpec((None, 1, 2 * rows), lambda i: (i, 0, 0)),
        ],
        out_shape=[wide, wide, narrow, narrow, jax.ShapeDtypeStruct((own, 1, 2 * rows), f32)],
        scratch_shapes=[pltpu.VMEM((LANES, rows), bf16)],
        compiler_params=pltpu.CompilerParams(vmem_limit_bytes=40 * 1024 * 1024),
        cost_estimate=no_cost(),
        name="attend_forward",
    )(raw, raw, raw, bias, cosine, sine)


def attend_backward(queries, keys, values, grads, bias, cosine, sine, totals):
    rows, width = queries.shape
    whole = lambda shape: pl.BlockSpec(shape, lambda i: (0, 0))
    column = pl.BlockSpec((rows, LANES), lambda i: (0, i))
    narrow = jax.ShapeDtypeStruct((rows, LANES), bf16)
    return pl.pallas_call(
        backward_kernel,
        grid=(width // LANES,),
        in_specs=[
            column,
            whole((rows, LANES)),
            whole((rows, LANES)),
            column,
            whole((rows, rows)),
            whole((rows, LANES)),
            whole((rows, LANES)),
            pl.BlockSpec((None, 1, 2 * rows), lambda i: (i, 0, 0)),
        ],
        out_specs=[column, whole((rows, LANES)), whole((rows, LANES))],
        out_shape=[jax.ShapeDtypeStruct((rows, width), bf16), narrow, narrow],
        scratch_shapes=[
            pltpu.VMEM((LANES, rows), bf16),
            pltpu.VMEM((rows, LANES), f32),
            pltpu.VMEM((rows, LANES), f32),
        ],
        compiler_params=pltpu.CompilerParams(vmem_limit_bytes=40 * 1024 * 1024),
        cost_estimate=no_cost(),
        name="attend_backward",
    )(queries, keys, values, grads, bias, cosine, sine, totals)


def no_cost():
    return pl.CostEstimate(flops=1000000, bytes_accessed=1000000, transcendentals=0)


def whole_block(shape):
    return pl.BlockSpec(shape, lambda i: (0,) * len(shape))


def stack_kernel(*refs):
    out, turned = refs[-2:]
    for index, ref in enumerate(refs[:-2]):

        @pl.when(pl.program_id(0) == index)
        def _():
            value = ref[...]
            out[...] = value
            turned[...] = value.T


def stack_rows(*pieces):
    rows, width = pieces[0].shape
    count = len(pieces)
    kind = pieces[0].dtype
    return pl.pallas_call(
        stack_kernel,
        grid=(count,),
        in_specs=[whole_block((rows, width))] * count,
        out_specs=[
            pl.BlockSpec((rows, width), lambda i: (i, 0)),
            pl.BlockSpec((width, rows), lambda i: (0, i)),
        ],
        out_shape=[
            jax.ShapeDtypeStruct((count * rows, width), kind),
            jax.ShapeDtypeStruct((width, count * rows), kind),
        ],
        compiler_params=pltpu.CompilerParams(vmem_limit_bytes=40 * 1024 * 1024),
        cost_estimate=no_cost(),
        name="stack_rows",
    )(*pieces)


def hidden_kernel(
    rows_ref, grads_ref, gate_ref, up_ref, down_a, down_b, hidden_out, gate_out, up_out
):
    rows, grads = rows_ref[...], grads_ref[...]
    at = down_a.shape[1]
    for down, where in ((down_a, slice(0, at)), (down_b, slice(at, at + down_b.shape[1]))):
        gate = jnp.dot(rows, gate_ref[:, where], preferred_element_type=f32)
        up = jnp.dot(rows, up_ref[:, where], preferred_element_type=f32)
        grad = jnp.dot(grads, down[...], preferred_element_type=f32)
        sigmoid = 1.0 / (1.0 + jnp.exp(-gate))
        silu = gate * sigmoid
        hidden_out[:, where] = (silu * up).astype(bf16)
        gate_out[:, where] = (grad * up * sigmoid * (1.0 + gate * (1.0 - sigmoid))).astype(bf16)
        up_out[:, where] = (grad * silu).astype(bf16)


def hidden_rows(rows, grads, gate, up, down_a, down_b, height):
    total, depth = rows.shape
    width = gate.shape[1]
    tall = pl.BlockSpec((height, depth), lambda i: (i, 0))
    tile = pl.BlockSpec((height, width), lambda i: (i, 0))
    return pl.pallas_call(
        hidden_kernel,
        grid=(total // height,),
        in_specs=[tall, tall] + [whole_block(v.shape) for v in (gate, up, down_a, down_b)],
        out_specs=[tile] * 3,
        out_shape=[jax.ShapeDtypeStruct((total, width), bf16)] * 3,
        compiler_params=pltpu.CompilerParams(vmem_limit_bytes=48 * 1024 * 1024),
        cost_estimate=no_cost(),
        name="hidden_rows",
    )(rows, grads, gate, up, down_a, down_b)


def weight_grad_kernel(
    inner, turned_near, turned_far, near_ref, far_ref,
    grads_near, grads_far, hidden_near, hidden_far, kept, sent,
):
    def product(*pairs):
        return sum(jnp.dot(l[...], r[...], preferred_element_type=f32) for l, r in pairs)

    both = jnp.concatenate(
        [
            product((turned_near, near_ref), (turned_far, far_ref)),
            product((grads_near, hidden_near), (grads_far, hidden_far)),
        ],
        axis=1,
    ).astype(bf16)
    block = kept.shape[-2] * (1 if inner else 2)
    both = both.reshape(-1, 2, block, both.shape[-1])
    kept[...] = both[:, 0].reshape(kept.shape)
    sent[...] = both[:, 1].reshape(sent.shape)


def weight_grads(turned, lefts, grads_turned, hiddens, inner):
    depth, total = turned[0].shape
    block = depth // lax.axis_size("dp")
    high = 512
    count = high // (2 * block)
    width = lefts[0].shape[1] + hiddens[0].shape[1]
    out = pl.BlockSpec((count, block, width), lambda i: (i, 0, 0))
    shape = jax.ShapeDtypeStruct((depth // (2 * block), block, width), bf16)
    tall = pl.BlockSpec((high, total), lambda i: (i, 0))
    kept, sent = pl.pallas_call(
        functools.partial(weight_grad_kernel, inner),
        grid=(depth // high,),
        in_specs=[tall, tall]
        + [whole_block(v.shape) for v in lefts]
        + [tall, tall]
        + [whole_block(v.shape) for v in hiddens],
        out_specs=[out, out],
        out_shape=[shape, shape],
        compiler_params=pltpu.CompilerParams(vmem_limit_bytes=48 * 1024 * 1024),
        cost_estimate=no_cost(),
        name="weight_grads",
    )(*turned, *lefts, *grads_turned, *hiddens)
    dims = [2] * nbits()
    dims[block_axes().index(X if inner else Y)] = 1
    return kept.reshape(*dims, block, width), sent.reshape(*dims, block, width)


def back_kernel(cuts, *refs):
    count = len(cuts)
    weights, (own, other) = refs[len(refs) - 2 - count : len(refs) - 2], refs[-2:]
    lefts = refs[: len(refs) - 2 - count]
    total = 0.0
    for (index, low, high), weight in zip(cuts, weights):
        total += lax.dot_general(
            lefts[index][:, low:high],
            weight[...],
            (((1,), (1,)), ((), ())),
            preferred_element_type=f32,
        )
    half = own.shape[0]
    own[...] = total[:half]
    other[...] = total[half:].astype(bf16)


def back_rows(lefts, weights, cuts):
    rows = lefts[0].shape[0]
    depth = weights[0].shape[0]
    high = 512
    return pl.pallas_call(
        functools.partial(back_kernel, cuts),
        grid=(depth // high,),
        in_specs=[whole_block(v.shape) for v in lefts]
        + [pl.BlockSpec((high, v.shape[1]), lambda i: (i, 0)) for v in weights],
        out_specs=[pl.BlockSpec((rows // 2, high), lambda i: (0, i))] * 2,
        out_shape=[
            jax.ShapeDtypeStruct((rows // 2, depth), f32),
            jax.ShapeDtypeStruct((rows // 2, depth), bf16),
        ],
        compiler_params=pltpu.CompilerParams(vmem_limit_bytes=48 * 1024 * 1024),
        cost_estimate=no_cost(),
        name="back_rows",
    )(*lefts, *weights)


def my_half():
    return (lax.axis_index("dp") >> T) & 1


class Chunks:
    def __init__(self, quarter):
        self.quarter = quarter
        middle = -(-quarter // (2 * LANES)) * LANES
        self.spans = ((0, middle), (middle, quarter))
        self.cuts = [low + (high - low) // (2 * LANES) * LANES for low, high in self.spans]

    def layout(self, index):
        (low, high), at = self.spans[index], self.cuts[index]
        width = high - low
        return (
            (0, low, high, 0),
            (2, low, at, width),
            (1, low, high, width + at - low),
            (2, at, high, 2 * width + at - low),
        )

    def width(self, index):
        low, high = self.spans[index]
        return 3 * (high - low)

    def turn(self, index):
        (low, high), at = self.spans[index], self.cuts[index]
        return high - low + at - low


def pack_kernel(chunks, t_ref, gate_ref, up_ref, down_ref, *outs):
    for side in (0, 1):
        start = jnp.where(side == 0, t_ref[0], 1 - t_ref[0]) * chunks.quarter
        for index in (0, 1):
            out = outs[2 * side + index]
            for matrix, low, high, place in chunks.layout(index):
                where = pl.ds(pl.multiple_of(start + low, LANES), high - low)
                if matrix == 2:
                    value = down_ref[where, :].astype(f32).T.astype(bf16)
                else:
                    value = (gate_ref, up_ref)[matrix][:, where]
                out[:, place : place + high - low] = value


def pack_columns(chunks, gate, up, down):
    rows = gate.shape[0]
    if rows % LANES:
        sides = []
        for side in (0, 1):
            start = jnp.where(side == 0, my_half(), 1 - my_half()) * chunks.quarter
            halves = [
                lax.dynamic_slice_in_dim(v, start, chunks.quarter, 1) for v in (gate, up, down.T)
            ]
            for index in (0, 1):
                parts = sorted(chunks.layout(index), key=lambda entry: entry[3])
                sides.append(jnp.concatenate([halves[m][:, l:h] for m, l, h, _ in parts], axis=1))
        return sides
    whole = pl.BlockSpec(memory_space=pltpu.VMEM)
    shapes = [jax.ShapeDtypeStruct((rows, chunks.width(i)), bf16) for i in (0, 1)]
    return pl.pallas_call(
        functools.partial(pack_kernel, chunks),
        in_specs=[pl.BlockSpec(memory_space=pltpu.SMEM), whole, whole, whole],
        out_specs=[whole] * 4,
        out_shape=shapes + shapes,
        compiler_params=pltpu.CompilerParams(vmem_limit_bytes=40 * 1024 * 1024),
        cost_estimate=no_cost(),
        name="pack_columns",
    )(my_half().reshape(1).astype(jnp.int32), gate, up, down)


def unpack_kernel(chunks, t_ref, *refs):
    outs = refs[4:]
    for side in (0, 1):
        start = jnp.where(side == 0, t_ref[0], 1 - t_ref[0]) * chunks.quarter
        for index in (0, 1):
            for matrix, low, high, place in chunks.layout(index):
                where = pl.ds(pl.multiple_of(start + low, LANES), high - low)
                value = refs[2 * side + index][:, place : place + high - low].astype(f32)
                if matrix == 2:
                    outs[2][where, :] = value.T
                else:
                    outs[matrix][:, where] = value


def unpack_columns(chunks, *bundles):
    rows = bundles[0].shape[0]
    if rows % LANES:
        halves = []
        for side in (0, 1):
            found = [[], [], []]
            for index in (0, 1):
                for matrix, low, high, place in chunks.layout(index):
                    value = bundles[2 * side + index][:, place : place + high - low].astype(f32)
                    found[matrix].append((low, value))
            halves.append(
                [jnp.concatenate([v for _, v in sorted(f, key=lambda e: e[0])], axis=1) for f in found]
            )
        gate, up, down = [
            pick_first(my_half() == 0, own, came, 1) for own, came in zip(*halves)
        ]
        return gate, up, down.T
    whole = pl.BlockSpec(memory_space=pltpu.VMEM)
    flat_shape = jax.ShapeDtypeStruct((rows, 2 * chunks.quarter), f32)
    return pl.pallas_call(
        functools.partial(unpack_kernel, chunks),
        in_specs=[pl.BlockSpec(memory_space=pltpu.SMEM)] + [whole] * 4,
        out_specs=[whole] * 3,
        out_shape=[flat_shape, flat_shape, jax.ShapeDtypeStruct((2 * chunks.quarter, rows), f32)],
        compiler_params=pltpu.CompilerParams(vmem_limit_bytes=40 * 1024 * 1024),
        cost_estimate=no_cost(),
        name="unpack_columns",
    )(my_half().reshape(1).astype(jnp.int32), *bundles)


def body(
    inputs, cotangent, seq_lengths, attn_gain, w_query, w_key, w_value, w_out,
    mlp_gain, w_gate, w_up, w_down,
):
    own_rows = inputs.shape[0]
    chip_rows = 2 * own_rows
    core = lax.axis_index("tensor")
    rest = rest_bits()
    heads_width = w_query.shape[1]
    kv_width = w_key.shape[1]
    cut = (heads_width + 2 * kv_width) // 2
    cut_out = heads_width // 2

    last = []

    def held(values, *others):
        values = after(values, *last, *others)
        last[:] = [values]
        return values

    def did(values):
        last[:] = [values]
        return values

    def send(values, bit, *others):
        return exchange(held(values, *others), bit)

    def swap(values, *others):
        return core_exchange(held(values, *others))

    def gather(values, bit, *others):
        came = send(values, bit, *others)
        return lambda: join(values, held(came), bit)

    def fold(values, bit, kind=bf16):
        came = send(row_major(part(values, bit, 1).astype(bf16)), bit)
        return lambda: add(part(values, bit, 0), held(came), kind)

    gains = as_block(jnp.stack([attn_gain, mlp_gain]))
    gains = gather(gains, rest[0])
    qkv = jnp.concatenate([w_query, w_key, w_value], axis=1)
    q = gather(as_block(qkv), rest[0])
    for bit in rest[1:] + [T]:
        gains = gather(gains(), bit)
    inputs_rel, cotangent_rel = to_relative(held(inputs), cotangent)
    did(inputs_rel)
    gains = gather(gains(), X)
    out_t = did(held(w_out.T))
    gains = gather(gains(), Y)
    o = gather(as_block(out_t), rest[0])
    for bit in rest[1:] + [T]:
        q = gather(q(), bit)
    chunks = Chunks(w_gate.shape[1] // 2)
    own_0, own_1, other_0, other_1 = pack_columns(chunks, held(w_gate), w_up, w_down)
    did(own_0)
    gains = flat(gains()).reshape(-1, 2, attn_gain.shape[0]).transpose(1, 0, 2)
    gains = gains.reshape(2, -1).astype(f32)
    gain_one, gain_two = gains[0], gains[1]
    inputs_wide = inputs_rel.astype(f32)
    scale_one = rms_scale(inputs_wide)
    unit_one = inputs_wide * scale_one
    normed_own = (unit_one * gain_one).astype(bf16)
    normed_other = swap(normed_own)
    for bit in rest[1:] + [T]:
        o = gather(o(), bit)
    position, is_valid, bias = build_layout(seq_lengths[0], chip_rows)
    cosine, sine = rotation_tables(position)
    own_valid = lax.dynamic_slice_in_dim(is_valid, core * own_rows, own_rows, 0)[:, None]
    grad_branch_own = jnp.where(own_valid, cotangent_rel, jnp.zeros_like(cotangent_rel))
    q = q()
    qa = gather(columns(q, 0, cut), X)
    qb = gather(columns(q, cut, 2 * cut), Y)
    w0_t = send(as_block(other_0), T)
    bias = did(held(bias))
    grad_branch_other = swap(grad_branch_own)
    qa = gather(qa(), Y)
    qb = gather(qb(), X)
    w0 = join(as_block(own_0), held(w0_t), T)
    w0 = gather(w0, rest[0])
    grad_far_own = send(swap_halves(grad_branch_own), T)
    qa, qb = qa(), qb()
    o = o()
    oa = gather(columns(o, 0, cut_out), X)
    ob = gather(columns(o, cut_out, heads_width), Y)
    query_w = jnp.concatenate([flat(qa), flat(qb)], axis=1)

    normed = pick_first(core == 0, normed_own, normed_other, 0)
    raw = did(matmul(held(normed), query_w))
    tables = (bias, cosine, sine)
    mixed_a, queries_a, keys_a, values_a, totals_a = attend_forward(raw, heads_width, 0, *tables)
    did(mixed_a)
    oa = gather(oa(), Y)
    ob = gather(ob(), X)
    mixed_b, queries_b, keys_b, values_b, totals_b = attend_forward(
        held(raw), heads_width, 1, *tables
    )
    did(mixed_b)
    for bit in rest[1:]:
        w0 = gather(w0(), bit)
    w0 = w0()
    grad_far_other = swap(grad_far_own)
    w1_t = send(as_block(other_1), T)
    oa, ob = flat(oa()), flat(ob())
    w0b = gather(columns(w0, chunks.turn(0), w0.shape[-1]), Y)
    w0a = gather(columns(w0, 0, chunks.turn(0)), X)

    def rows_of(values, which):
        return lax.dynamic_slice_in_dim(values, which * own_rows, own_rows, 0)

    def project(which, mixed_a):
        return contract_cols(rows_of(mixed_a, which), oa) + contract_cols(
            rows_of(mixed_b, which), ob
        )

    came = swap(project(1 - core, held(mixed_a)).astype(bf16))
    residual = did(inputs_wide + (project(core, held(mixed_a)) + held(came).astype(f32)))

    scale_two = rms_scale(residual)
    unit_two = residual * scale_two
    normed_mlp_own = (unit_two * gain_two).astype(bf16)
    far_own = send(swap_halves(normed_mlp_own), T)
    near_other = held(swap(normed_mlp_own))
    near, near_turned = stack_rows(normed_mlp_own, near_other)
    did(near)
    grad_near, grad_near_turned = stack_rows(held(grad_branch_own), grad_branch_other)
    did(grad_near)
    w1 = join(as_block(own_1), held(w1_t), T)
    w1 = gather(w1, rest[0])
    grad_far, grad_far_turned = stack_rows(grad_far_own, held(grad_far_other))
    did(grad_far)
    w0b, w0a = w0b(), w0a()
    w0b_x = send(w0b, X)
    w0a_y = send(w0a, Y)
    for bit in rest[1:]:
        w1 = gather(w1(), bit)
    w1 = w1()

    def weights_of(first_a, came_a, first_b, came_b, index):
        whole_a = lambda low, high: flat(
            join(columns(first_a, low, high), columns(came_a, low, high), Y)
        )
        whole_b = lambda low, high: flat(
            join(columns(first_b, low, high), columns(came_b, low, high), X)
        )
        width, at = chunks.width(index) // 3, chunks.turn(index)
        return (
            whole_a(0, width), whole_b(0, width),
            whole_a(width, at), whole_b(width, chunks.width(index) - at),
        )

    def hidden_layer(rows, grads, weights):
        hidden, grad_gate, grad_up = hidden_rows(held(rows), grads, *weights, own_rows)
        return did(hidden), grad_gate, grad_up

    def weight_grad(left, right):
        return did(as_blocks(contract_rows(left, held(right)).astype(bf16)))

    def bundle_grads(grads, hiddens, index, inner):
        width = chunks.width(index) // 3
        at = chunks.turn(index) - width
        low, high = (at, width) if inner else (0, at)
        kept, sent = weight_grads(
            (near_turned, far_turned), (held(grads[0]), grads[1]),
            (grad_near_turned, grad_far_turned), [v[:, low:high] for v in hiddens], inner,
        )
        did(sent)
        return kept, sent

    weights_0 = weights_of(w0a, held(w0a_y), w0b, held(w0b_x), 0)
    w1a = gather(columns(w1, 0, chunks.turn(1)), X)
    w1b = gather(columns(w1, chunks.turn(1), w1.shape[-1]), Y)
    far_other = swap(far_own)
    near_0 = hidden_layer(near, grad_near, weights_0)
    far, far_turned = stack_rows(far_own, held(far_other))
    did(far)
    w1a, w1b = w1a(), w1b()
    w1a_y = send(w1a, Y)
    w1b_x = send(w1b, X)
    far_0 = hidden_layer(far, grad_far, weights_0)
    both = lambda index: (near_0[index], far_0[index])
    r0a, r0a_sent = bundle_grads(both(1), both(0), 0, False)
    r0a_y = send(r0a_sent, Y)
    r0b, r0b_sent = bundle_grads(both(2), both(0), 0, True)
    r0b_x = send(r0b_sent, X)
    weights_1 = weights_of(w1a, held(w1a_y), w1b, held(w1b_x), 1)
    weights_hidden = [*weights_0[:2], *weights_1[:2]]
    weights_down = [*weights_0[2:], *weights_1[2:]]
    cuts_hidden = tuple((i, 0, v.shape[1]) for i, v in enumerate(weights_hidden))
    cuts_down = tuple(
        (i, low, high)
        for i in (0, 1)
        for low, high in (
            (0, weights_down[2 * i].shape[1]),
            (weights_down[2 * i].shape[1], weights_hidden[2 * i].shape[1]),
        )
    )

    def hidden_back(first, second):
        lefts = [held(first[1]), first[2], second[1], second[2]]
        own, other = back_rows(lefts, weights_hidden, cuts_hidden)
        return did(own), other

    def branch_back(first, second):
        own, other = back_rows([held(first[0]), second[0]], weights_down, cuts_down)
        return did(own), other

    far_1 = hidden_layer(far, grad_far, weights_1)
    far_part, far_sent = hidden_back(far_0, far_1)
    far_came = swap(far_sent)
    near_1 = hidden_layer(near, grad_near, weights_1)
    both_1 = lambda index: (near_1[index], far_1[index])
    r0a = add(r0a, held(r0a_y))
    r0b = add(r0b, held(r0b_x))
    r0a_x = send(row_major(part(r0a, X, 1)), X)
    r0b_y = send(row_major(part(r0b, Y, 1)), Y)
    far_sum = far_part + held(far_came).astype(f32)
    grad_z = send(swap_halves(far_sum.astype(bf16)), T)
    r1a, r1a_sent = bundle_grads(both_1(1), both_1(0), 1, False)
    r1a_y = send(r1a_sent, Y)
    r1b, r1b_sent = bundle_grads(both_1(2), both_1(0), 1, True)
    r1b_x = send(r1b_sent, X)
    near_part, near_sent = hidden_back(near_0, near_1)
    near_came = swap(near_sent)

    def joined(a, a_came, b, b_came):
        return jnp.concatenate(
            [add(part(a, X, 0), held(a_came)), add(part(b, Y, 0), held(b_came))], axis=-1
        )

    r0 = joined(r0a, r0a_x, r0b, r0b_y)
    for bit in rest[:0:-1]:
        r0 = fold(r0, bit)()
    r0 = fold(r0, rest[0], f32)

    grad_normed_mlp = near_part + held(near_came).astype(f32) + held(grad_z).astype(f32)
    grad_gain_two, grad_norm_two = norm_back(grad_normed_mlp, unit_two, scale_two, gain_two)
    grad_residual = grad_branch_own.astype(f32) + grad_norm_two
    grad_att_own = grad_residual.astype(bf16)
    grad_att_other = swap(grad_att_own)
    far_branch, far_branch_sent = branch_back(far_0, far_1)
    far_branch_came = swap(far_branch_sent)
    r1a = add(r1a, held(r1a_y))
    r1b = add(r1b, held(r1b_x))
    r1a_x = send(row_major(part(r1a, X, 1)), X)
    r1b_y = send(row_major(part(r1b, Y, 1)), Y)
    grad_attended = pick_first(core == 0, grad_att_own, held(grad_att_other), 0)
    grad_out_a = weight_grad(grad_attended, mixed_a)
    roa_y = send(row_major(part(grad_out_a, Y, 1)), Y)
    grad_out_b = weight_grad(grad_attended, mixed_b)
    rob_x = send(row_major(part(grad_out_b, X, 1)), X)
    branch_sum = far_branch + held(far_branch_came).astype(f32)
    branch_z = send(swap_halves(branch_sum.astype(bf16)), T)
    d_query_a, d_key_a, d_value_a = attend_backward(
        queries_a, keys_a, values_a, matmul(held(grad_attended), oa).astype(bf16), *tables, totals_a
    )
    did(d_query_a)
    r0 = r0()
    r0_t = send(row_major(part(r0, T, 1).astype(bf16)), T)
    r1 = joined(r1a, r1a_x, r1b, r1b_y)
    for bit in rest[:0:-1]:
        r1 = fold(r1, bit)()
    r1 = fold(r1, rest[0], f32)
    d_query_b, d_key_b, d_value_b = attend_backward(
        queries_b, keys_b, values_b, matmul(held(grad_attended), ob).astype(bf16), *tables, totals_b
    )
    did(d_query_b)
    out_a = add(part(grad_out_a, Y, 0), held(roa_y))
    out_b = add(part(grad_out_b, X, 0), held(rob_x))
    roa_x = send(row_major(part(out_a, X, 1)), X)
    rob_y = send(row_major(part(out_b, Y, 1)), Y)
    low = jnp.arange(kv_width) < HEAD_DIM
    d_qkv = jnp.concatenate(
        [
            d_query_a, d_query_b,
            jnp.where(low, d_key_a, d_key_b), jnp.where(low, d_value_a, d_value_b),
        ],
        axis=1,
    )
    grad_qkv = weight_grad(normed, d_qkv)
    qkv_a, qkv_b = columns(grad_qkv, 0, cut), columns(grad_qkv, cut, 2 * cut)
    rqa_y = send(row_major(part(qkv_a, Y, 1)), Y)
    rqb_x = send(row_major(part(qkv_b, X, 1)), X)
    r0_t = held(r0_t)
    d_came = swap(contract_cols(rows_of(held(d_qkv), 1 - core), query_w).astype(bf16))
    near_branch, near_branch_sent = branch_back(near_0, near_1)
    near_branch_came = swap(near_branch_sent)
    out = fold(joined(out_a, roa_x, out_b, rob_y), T)
    r1 = r1()
    r1_t = send(row_major(part(r1, T, 1).astype(bf16)), T)
    qkv_a = add(part(qkv_a, Y, 0), held(rqa_y))
    qkv_b = add(part(qkv_b, X, 0), held(rqb_x))
    rqa_x = send(row_major(part(qkv_a, X, 1)), X)
    rqb_y = send(row_major(part(qkv_b, Y, 1)), Y)
    grad_normed = contract_cols(rows_of(held(d_qkv), core), query_w) + held(d_came).astype(f32)
    grad_gain_one, grad_norm_one = norm_back(grad_normed, unit_one, scale_one, gain_one)
    grad_rows = did(grad_residual + grad_norm_one)
    grad_gains = jnp.stack([grad_gain_one, grad_gain_two])
    gains_came = swap(grad_gains)
    out = out()
    for bit in rest[:0:-1]:
        out = fold(out, bit)()
    out = fold(out, rest[0], f32)
    grad_gains = grad_gains + held(gains_came)
    gain_blocks = grad_gains.reshape(2, lax.axis_size("dp"), -1).transpose(1, 0, 2)
    gain_blocks = gain_blocks.reshape((2,) * nbits() + gain_blocks.shape[1:])

    def fold_gains(blocks, bit):
        came = send(part(blocks, bit, 1), bit)
        return lambda: part(blocks, bit, 0) + held(came)

    gain_blocks = fold_gains(gain_blocks, Y)
    grad_rows = did(from_relative(held(grad_rows))[0])
    sum_qkv = fold(joined(qkv_a, rqa_x, qkv_b, rqb_y), T)
    gain_blocks = fold_gains(gain_blocks(), X)
    branch = near_branch + held(near_branch_came).astype(f32) + held(branch_z).astype(f32)
    output = jnp.where(own_valid, residual + branch, 0.0).astype(bf16)
    output = did(from_relative(output)[0])
    sum_gate, sum_up, sum_down = unpack_columns(
        chunks, flat(part(r0, T, 0)), flat(part(r1, T, 0)), flat(r0_t), held(flat(r1_t))
    )
    did(sum_gate)
    gain_blocks = fold_gains(gain_blocks(), T)
    for bit in rest[:0:-1]:
        sum_qkv = fold(sum_qkv(), bit)
        gain_blocks = fold_gains(gain_blocks(), bit)
    sum_qkv = fold(sum_qkv(), rest[0], f32)
    gain_blocks = fold_gains(gain_blocks(), rest[0])
    out = out()
    sum_qkv = flat(sum_qkv())
    gain_sums = gain_blocks().reshape(2, -1)
    return (
        output,
        grad_rows,
        gain_sums[0],
        sum_qkv[:, :heads_width],
        sum_qkv[:, heads_width : heads_width + kv_width],
        sum_qkv[:, heads_width + kv_width :],
        flat(out).T,
        gain_sums[1],
        sum_gate,
        sum_up,
        sum_down,
    )


def solution(mesh):
    placed = (
        P(("dp", "tensor"), None),
        P(("dp", "tensor"), None),
        P("dp", None),
        P("dp"),
        P("dp", "tensor"),
        P("dp", "tensor"),
        P("dp", "tensor"),
        P("tensor", "dp"),
        P("dp"),
        P("dp", "tensor"),
        P("dp", "tensor"),
        P("tensor", "dp"),
    )
    return jax.shard_map(
        body,
        mesh=mesh,
        in_specs=placed,
        out_specs=(
            P(("dp", "tensor"), None),
            P(("dp", "tensor"), None),
            P("dp"),
            P("dp", "tensor"),
            P("dp", "tensor"),
            P("dp", "tensor"),
            P("tensor", "dp"),
            P("dp"),
            P("dp", "tensor"),
            P("dp", "tensor"),
            P("tensor", "dp"),
        ),
        check_vma=False,
    )
```

time: 865 us -> 664 us (0.77)
  waiting for transfers between devices: 369 us -> 186 us
  matrix products: 177 us -> 28 us
  Pallas kernels: 63.6 us -> 210 us
  starting transfers between devices: 93.1 us -> 64.4 us
  other arithmetic: 94 us -> 107 us
    ppermute x76 -> x60, waiting for transfers between devices: 368 us -> 184 us  [exchange(): return lax.ppermute(values, 'dp', [(i, i ^ 1 << bit) for i in range(size)])]
    pallas_call x5 -> x22, Pallas kernels: 56.9 us -> 203 us  [the longest x4 52 us: hidden_rows(): pl.pallas_call(hidden_kernel, grid=(total // height,), in_specs=[tall, ta...]
    dot_general x8 -> x3, matrix products: 64.3 us -> 7.84 us  [matmul(): return jnp.dot(left, right, preferred_element_type=f32)]
    dot_general x10 -> x6, matrix products: 58.6 us -> 11.9 us  [contract_cols(): lax.dot_general(left, right, (((1,), (1,)), ((), ())), preferred_element_...]
    dot_general x5 -> x3, matrix products: 53.7 us -> 8.36 us  [contract_rows(): lax.dot_general(left, right, (((0,), (0,)), ((), ())), preferred_element_...]
    ppermute x76 -> x60, starting transfers between devices: 91.6 us -> 62.7 us  [exchange(): return lax.ppermute(values, 'dp', [(i, i ^ 1 << bit) for i in range(size)])]
    convert_element_type x21 -> x22, other arithmetic: 16.3 us -> 33.4 us  [the longest x18 27.6 us: add(): return row_major((kept.astype(f32) + came.astype(f32)).astype(kind))]
    unnamed x211 -> x226, local copies, waits for them, and re-layouts: 27 us -> 35.8 us
  transfers between devices with their start and end apart: 90 -> 73, of which waited for: 36 -> 21; matrix products, arithmetic and copies ran while one was open for 36% -> 22% of each run, Pallas kernels for 7% -> 32%
where the time goes in v2:
time: 664 us; the launch traced here: 659 us
  Pallas kernels  210 us (32%)
  waiting for transfers between devices  186 us (28%)
  other arithmetic  107 us (16%)
  starting transfers between devices  64.4 us (10%)
  local copies, waits for them, and re-layouts  60.3 us (9%)
  matrix products  28 us (4%)
    ppermute x60, waiting for transfers between devices, exchange(): return lax.ppermute(values, 'dp', [(i, i ^ 1 << bit) for i in range(size)])  184 us
    ppermute x60, starting transfers between devices, exchange(): return lax.ppermute(values, 'dp', [(i, i ^ 1 << bit) for i in range(size)])  62.7 us
    pallas_call x4, Pallas kernels, hidden_rows(): pl.pallas_call(hidden_kernel, grid=(total // height,), in_specs=[tall, ta...  52 us
    pallas_call x4, Pallas kernels, weight_grads(): pl.pallas_call(functools.partial(weight_grad_kernel, inner), grid=(depth...  45.1 us
    pallas_call x4, Pallas kernels, back_rows(): pl.pallas_call(functools.partial(back_kernel, cuts), grid=(depth // high,...  44.6 us
    concatenate x39, other arithmetic, join(): return jnp.concatenate([values, came], axis=block_axes().index(bit))  39.9 us
    unnamed x226, local copies, waits for them, and re-layouts  35.8 us
    convert_element_type x18, other arithmetic, add(): return row_major((kept.astype(f32) + came.astype(f32)).astype(kind))  27.6 us
  transfers between devices with their start and end apart: 73, of which 21 were waited for; matrix products, arithmetic and copies ran while one was open for 22% of the time, Pallas kernels for 32%

profile of v2, /device:TPU:0, one launch (start us, length us, event | category | flops | bytes accessed | tf_op | source)
XLA Modules:
  0.0 659.2 jit_solution(461050292549386799)
XLA Ops:
  1.3 4.0 collective-permute-start
  13.7 2.0 collective-permute-start.1
  22.1 2.2 collective-permute-done.2
  25.8 2.6 collective-permute-start.6
  30.9 7.5 %collective-permute-done.6 = bf16[1,1,1,1,128,1024]{5,4,3,2,1,0:T(8,128)(2,1)S(1)} collective-permute-done((bf16[1,1,1,1,128,1024]{5,4,3,2,1,0:T(8,128)(2,1)S(1)}, bf16[1,1,1,1,128,1024]{5,4,3,2,1,0:T(8,128)(2,1)S(1)}, u32[]{:S(2)}, u32[]{:S(2)}) %collective-permute-start.6) | collective-permute-done | bytes 262176 | tf_op jit(solution)/shard_map/ppermute | solution.py:39
  38.5 10.5 %collective-permute-done.8 = bf16[1,2,1,1,128,1280]{5,4,3,2,1,0:T(8,128)(2,1)S(1)} collective-permute-done((bf16[1,2,1,1,128,1280]{5,4,3,2,1,0:T(8,128)(2,1)S(1)}, bf16[1,2,1,1,128,1280]{5,4,3,2,1,0:T(8,128)(2,1)S(1)}, u32[]{:S(2)}, u32[]{:S(2)}) %collective-permute-start.8) | collective-permute-done | bytes 655392 | tf_op jit(solution)/shard_map/ppermute | solution.py:39
  53.3 11.6 %collective-permute-done.10 = bf16[2,2,1,1,128,640]{5,4,3,2,1,0:T(8,128)(2,1)S(1)} collective-permute-done((bf16[2,2,1,1,128,640]{5,4,3,2,1,0:T(8,128)(2,1)S(1)}, bf16[2,2,1,1,128,640]{5,4,3,2,1,0:T(8,128)(2,1)S(1)}, u32[]{:S(2)}, u32[]{:S(2)}) %collective-permute-start.10) | collective-permute-done | bytes 655392 | tf_op jit(solution)/shard_map/ppermute | solution.py:39
  65.5 1.9 collective-permute-done.9
  74.7 19.5 %collective-permute-done.12 = bf16[2,2,1,2,128,640]{5,4,3,2,1,0:T(8,128)(2,1)S(1)} collective-permute-done((bf16[2,2,1,2,128,640]{5,4,3,2,1,0:T(8,128)(2,1)S(1)}, bf16[2,2,1,2,128,640]{5,4,3,2,1,0:T(8,128)(2,1)S(1)}, u32[]{:S(2)}, u32[]{:S(2)}) %collective-permute-start.12) | collective-permute-done | bytes 1310752 | tf_op jit(solution)/shard_map/ppermute | solution.py:39
  97.3 4.2 fusion.20.q_ref.k_ref.v_ref
  101.5 13.1 %attend_forward.2 = (bf16[768,512]{1,0:T(8,128)(2,1)S(1)}, bf16[768,512]{1,0:T(8,128)(2,1)S(1)}, bf16[768,128]{1,0:T(8,128)(2,1)S(1)}, bf16[768,128]{1,0:T(8,128)(2,1)S(1)}, f32[4,1,1536]{2,1,0:T(1,128)S(1)}) custom-call(f32[768,1280]{1,0:T(8,128)S(1)} %fusion.20.q_ref.k_ref.v_ref, f32[768,1280]{1,0:T(8,128)S(1)} %fusion.20.q_ref.k_ref.v_ref, ...), custom_call_target="tpu_custom_call" | custom-call | flops 1000000 | bytes 1000000 | tf_op jit(solution)/shard_map/attend_forward/pallas_call | solution.py:329
  117.9 13.4 %attend_forward.3 = (bf16[768,512]{1,0:T(8,128)(2,1)S(1)}, bf16[768,512]{1,0:T(8,128)(2,1)S(1)}, bf16[768,128]{1,0:T(8,128)(2,1)S(1)}, bf16[768,128]{1,0:T(8,128)(2,1)S(1)}, f32[4,1,1536]{2,1,0:T(1,128)S(1)}) custom-call(f32[768,1280]{1,0:T(8,128)S(1)} %fusion.20.q_ref.k_ref.v_ref, f32[768,1280]{1,0:T(8,128)S(1)} %fusion.20.q_ref.k_ref.v_ref, ...), custom_call_target="tpu_custom_call" | custom-call | flops 1000000 | bytes 1000000 | tf_op jit(solution)/shard_map/attend_forward/pallas_call | solution.py:329
  131.4 6.6 collective-permute-done.19.refs_0_
  142.2 2.2 pad_maximum_fusion.15
  167.4 3.4 collective-permute-done.23
  174.4 8.8 %collective-permute-done.27 = bf16[2,2,1,1,128,1152]{5,4,3,2,1,0:T(8,128)(2,1)} collective-permute-done((bf16[2,2,1,1,128,1152]{5,4,3,2,1,0:T(8,128)(2,1)S(1)}, bf16[2,2,1,1,128,1152]{5,4,3,2,1,0:T(8,128)(2,1)}, u32[]{:S(2)}, u32[]{:S(2)}) %collective-permute-start.27) | collective-permute-done | bytes 1179680 | tf_op jit(solution)/shard_map/ppermute | solution.py:39
  184.7 2.0 pad_maximum_fusion.5
  189.1 53.9 %collective-permute-done.25 = bf16[2,1,1,1,128,1920]{5,4,3,2,1,0:T(8,128)(2,1)S(1)} collective-permute-done((bf16[2,1,1,1,128,1920]{5,4,3,2,1,0:T(8,128)(2,1)S(1)}, bf16[2,1,1,1,128,1920]{5,4,3,2,1,0:T(8,128)(2,1)S(1)}, u32[]{:S(2)}, u32[]{:S(2)}) %collective-permute-start.25) | collective-permute-done | bytes 983072 | tf_op jit(solution)/shard_map/ppermute | solution.py:39
  255.4 2.0 pad_maximum_fusion.2
  257.4 2.0 pad_maximum_fusion.3
  259.3 14.5 %hidden_rows.4 = (bf16[768,768]{1,0:T(8,128)(2,1)S(1)}, bf16[768,768]{1,0:T(8,128)(2,1)S(1)}, bf16[768,768]{1,0:T(8,128)(2,1)S(1)}) custom-call(bf16[768,2048]{1,0:T(8,128)(2,1)} %copy-done.8, bf16[768,2048]{1,0:T(8,128)(2,1)} %copy-done.9, bf16[2048,768]{1,0:T(8,128)(2,1)} %bitcast.156, bf16[2048,768]{1,0:T(8,128)(2,1)} %bitcast.160, ...), custom_call_target="tpu_custom_call" | custom-call | flops 1000000 | bytes 1000000 | tf_op jit(solution)/shard_map/hidden_rows/pallas_call | solution.py:448
  276.3 3.3 pad_maximum_fusion.13
  279.6 2.8 pad_maximum_fusion.7
  284.4 14.7 %hidden_rows.5 = (bf16[768,768]{1,0:T(8,128)(2,1)S(1)}, bf16[768,768]{1,0:T(8,128)(2,1)S(1)}, bf16[768,768]{1,0:T(8,128)(2,1)S(1)}) custom-call(bf16[768,2048]{1,0:T(8,128)(2,1)} %copy-done.11, bf16[768,2048]{1,0:T(8,128)(2,1)} %copy-done.10, bf16[2048,768]{1,0:T(8,128)(2,1)} %bitcast.157, bf16[2048,768]{1,0:T(8,128)(2,1)} %bitcast.161, ...), custom_call_target="tpu_custom_call" | custom-call | flops 1000000 | bytes 1000000 | tf_op jit(solution)/shard_map/hidden_rows/pallas_call | solution.py:448
  300.2 11.6 %weight_grads.4 = (bf16[8,128,1152]{2,1,0:T(8,128)(2,1)S(1)}, bf16[8,128,1152]{2,1,0:T(8,128)(2,1)}) custom-call(bf16[2048,768]{1,0:T(8,128)(2,1)} %copy-done, bf16[2048,768]{1,0:T(8,128)(2,1)} %copy-done.3, bf16[768,768]{1,0:T(8,128)(2,1)S(1)} %get-tuple-element.369.near_ref.refs_0_, bf16[768,768]{1,0:T(8,128)(2,1)S(1)} %get-tuple-element.347.far_ref.refs_0_, ...), custom_call_target="tpu_custom_call" | custom-call | flops 1000000 | bytes 1000000 | tf_op jit(solution)/shard_map/weight_grads/pallas_call | solution.py:489
  314.2 11.7 %weight_grads.5 = (bf16[8,128,1152]{2,1,0:T(8,128)(2,1)S(1)}, bf16[8,128,1152]{2,1,0:T(8,128)(2,1)}) custom-call(bf16[2048,768]{1,0:T(8,128)(2,1)} %copy-done, bf16[2048,768]{1,0:T(8,128)(2,1)} %copy-done.3, bf16[768,768]{1,0:T(8,128)(2,1)S(1)} %get-tuple-element.340.near_ref.refs_1_, bf16[768,768]{1,0:T(8,128)(2,1)S(1)} %get-tuple-element.341.far_ref.refs_1_, ...), custom_call_target="tpu_custom_call" | custom-call | flops 1000000 | bytes 1000000 | tf_op jit(solution)/shard_map/weight_grads/pallas_call | solution.py:489
  338.8 1.9 pad_maximum_fusion.11
  340.7 11.3 %hidden_rows.6 = (bf16[768,640]{1,0:T(8,128)(2,1)S(1)}, bf16[768,640]{1,0:T(8,128)(2,1)S(1)}, bf16[768,640]{1,0:T(8,128)(2,1)S(1)}) custom-call(bf16[768,2048]{1,0:T(8,128)(2,1)} %copy-done.11, bf16[768,2048]{1,0:T(8,128)(2,1)} %copy-done.10, bf16[2048,640]{1,0:T(8,128)(2,1)} %bitcast.164, bf16[2048,640]{1,0:T(8,128)(2,1)} %bitcast.168, ...), custom_call_target="tpu_custom_call" | custom-call | flops 1000000 | bytes 1000000 | tf_op jit(solution)/shard_map/hidden_rows/pallas_call | solution.py:448
  356.8 13.6 %back_rows.4 = (f32[384,2048]{1,0:T(8,128)}, bf16[384,2048]{1,0:T(8,128)(2,1)S(1)}) custom-call(bf16[768,768]{1,0:T(8,128)(2,1)S(1)} %get-tuple-element.347.far_ref.refs_0_, bf16[768,768]{1,0:T(8,128)(2,1)S(1)} %get-tuple-element.341.far_ref.refs_1_, bf16[768,640]{1,0:T(8,128)(2,1)S(1)} %copy-done.32, bf16[768,640]{1,0:T(8,128)(2,1)S(1)} %copy-done.25, ...), custom_call_target="tpu_custom_call" | custom-call | flops 1000000 | bytes 1000000 | tf_op jit(solution)/shard_map/back_rows/pallas_call | solution.py:528
  371.5 11.5 %hidden_rows.7 = (bf16[768,640]{1,0:T(8,128)(2,1)S(1)}, bf16[768,640]{1,0:T(8,128)(2,1)S(1)}, bf16[768,640]{1,0:T(8,128)(2,1)S(1)}) custom-call(bf16[768,2048]{1,0:T(8,128)(2,1)} %copy-done.8, bf16[768,2048]{1,0:T(8,128)(2,1)} %copy-done.9, bf16[2048,640]{1,0:T(8,128)(2,1)} %bitcast.166, bf16[2048,640]{1,0:T(8,128)(2,1)} %bitcast.170, ...), custom_call_target="tpu_custom_call" | custom-call | flops 1000000 | bytes 1000000 | tf_op jit(solution)/shard_map/hidden_rows/pallas_call | solution.py:448
  383.0 3.3 fusion.4
  389.3 2.3 fusion.5
  395.7 2.0 add_convert_fusion.1
  399.4 10.2 %weight_grads.6 = (bf16[8,128,896]{2,1,0:T(8,128)(2,1)S(1)}, bf16[8,128,896]{2,1,0:T(8,128)(2,1)}) custom-call(bf16[2048,768]{1,0:T(8,128)(2,1)} %copy-done, bf16[2048,768]{1,0:T(8,128)(2,1)} %copy-done.3, bf16[768,640]{1,0:T(8,128)(2,1)S(1)} %get-tuple-element.365.near_ref.refs_2_, bf16[768,640]{1,0:T(8,128)(2,1)S(1)} %copy-done.33, ...), custom_call_target="tpu_custom_call" | custom-call | flops 1000000 | bytes 1000000 | tf_op jit(solution)/shard_map/weight_grads/pallas_call | solution.py:489
  412.1 11.6 %weight_grads.7 = (bf16[8,128,1024]{2,1,0:T(8,128)(2,1)S(1)}, bf16[8,128,1024]{2,1,0:T(8,128)(2,1)}) custom-call(bf16[2048,768]{1,0:T(8,128)(2,1)} %copy-done, bf16[2048,768]{1,0:T(8,128)(2,1)} %copy-done.3, bf16[768,640]{1,0:T(8,128)(2,1)S(1)} %copy-done.30, bf16[768,640]{1,0:T(8,128)(2,1)S(1)} %copy-done.26, bf16[2048,768]{1,0:T(8,128)(2,1)} %copy-done.1, ...), custom_call_target="tpu_custom_call" | custom-call | flops 1000000 | bytes 1000000 | tf_op jit(solution)/shard_map/weight_grads/pallas_call | solution.py:489
  425.1 13.4 %back_rows.5 = (f32[384,2048]{1,0:T(8,128)}, bf16[384,2048]{1,0:T(8,128)(2,1)S(1)}) custom-call(bf16[768,768]{1,0:T(8,128)(2,1)S(1)} %get-tuple-element.369.near_ref.refs_0_, bf16[768,768]{1,0:T(8,128)(2,1)S(1)} %get-tuple-element.340.near_ref.refs_1_, bf16[768,640]{1,0:T(8,128)(2,1)S(1)} %copy-done.28, bf16[768,640]{1,0:T(8,128)(2,1)S(1)} %copy-done.30, ...), custom_call_target="tpu_custom_call" | custom-call | flops 1000000 | bytes 1000000 | tf_op jit(solution)/shard_map/back_rows/pallas_call | solution.py:528
  440.6 2.0 add_convert_fusion.5
  445.5 3.3 multiply_reduce_fusion
  448.8 4.5 fusion.57
  453.7 2.5 collective-permute-start.48
  458.6 8.7 %back_rows.6 = (f32[384,2048]{1,0:T(8,128)}, bf16[384,2048]{1,0:T(8,128)(2,1)S(1)}) custom-call(bf16[768,768]{1,0:T(8,128)(2,1)S(1)} %copy-done.19, bf16[768,640]{1,0:T(8,128)(2,1)S(1)} %copy-done.23, bf16[2048,384]{1,0:T(8,128)(2,1)} %bitcast.137, bf16[2048,384]{1,0:T(8,128)(2,1)} %bitcast.174, bf16[2048,256]{1,0:T(8,128)(2,1)S(1)} %bitcast.141, ...), custom_call_target="tpu_custom_call" | custom-call | flops 1000000 | bytes 1000000 | tf_op jit(solution)/shard_map/back_rows/pallas_call | solution.py:528
  467.4 2.1 fusion.7
  471.6 2.5 fusion.6
  476.9 2.1 broadcast_select_fusion.2
  492.8 13.2 %attend_backward.2 = (bf16[768,512]{1,0:T(8,128)(2,1)S(1)}, bf16[768,128]{1,0:T(8,128)(2,1)S(1)}, bf16[768,128]{1,0:T(8,128)(2,1)S(1)}) custom-call(bf16[768,512]{1,0:T(8,128)(2,1)S(1)} %copy-done.47, bf16[768,128]{1,0:T(8,128)(2,1)S(1)} %copy-done.60, bf16[768,128]{1,0:T(8,128)(2,1)S(1)} %copy-done.62, ...), custom_call_target="tpu_custom_call" | custom-call | flops 1000000 | bytes 1000000 | tf_op jit(solution)/shard_map/attend_backward/pallas_call | solution.py:360
  506.0 2.4 collective-permute-done.48
  514.7 3.4 collective-permute-start.56
  519.9 13.0 %attend_backward.3 = (bf16[768,512]{1,0:T(8,128)(2,1)S(1)}, bf16[768,128]{1,0:T(8,128)(2,1)S(1)}, bf16[768,128]{1,0:T(8,128)(2,1)S(1)}) custom-call(bf16[768,512]{1,0:T(8,128)(2,1)S(1)} %copy-done.45, bf16[768,128]{1,0:T(8,128)(2,1)S(1)} %copy-done.56, bf16[768,128]{1,0:T(8,128)(2,1)S(1)} %copy-done.58, ...), custom_call_target="tpu_custom_call" | custom-call | flops 1000000 | bytes 1000000 | tf_op jit(solution)/shard_map/attend_backward/pallas_call | solution.py:360
  533.2 2.2 add_convert_fusion.7
  535.7 2.1 add_convert_fusion.8
  541.4 4.6 convolution_convert_fusion
  549.5 3.4 convolution_convert_fusion.3
  552.9 8.9 %back_rows.7 = (f32[384,2048]{1,0:T(8,128)}, bf16[384,2048]{1,0:T(8,128)(2,1)S(1)}) custom-call(bf16[768,768]{1,0:T(8,128)(2,1)S(1)} %copy-done.17, bf16[768,640]{1,0:T(8,128)(2,1)S(1)} %copy-done.21, bf16[2048,384]{1,0:T(8,128)(2,1)} %bitcast.138, bf16[2048,384]{1,0:T(8,128)(2,1)} %bitcast.175, bf16[2048,256]{1,0:T(8,128)(2,1)S(1)} %bitcast.142, ...), custom_call_target="tpu_custom_call" | custom-call | flops 1000000 | bytes 1000000 | tf_op jit(solution)/shard_map/back_rows/pallas_call | solution.py:528
  569.6 22.1 %collective-permute-done.55 = bf16[2,2,1,2,128,640]{5,4,3,2,1,0:T(8,128)(2,1)S(1)} collective-permute-done((bf16[2,2,1,2,128,640]{5,4,3,2,1,0:T(8,128)(2,1)}, bf16[2,2,1,2,128,640]{5,4,3,2,1,0:T(8,128)(2,1)S(1)}, u32[]{:S(2)}, u32[]{:S(2)}) %collective-permute-start.55) | collective-permute-done | bytes 1310752 | tf_op jit(solution)/shard_map/ppermute | solution.py:39
  598.9 4.4 fusion.10
  606.7 2.8 reorder.4
  609.5 2.7 collective-permute-done.63
  613.7 2.7 collective-permute-done.62
  618.3 3.2 select_convert_fusion.refs_0_
  621.5 2.5 reorder.5
  625.6 2.5 unpack_columns.1
  628.2 11.0 %collective-permute-done.69 = bf16[1,2,1,1,128,1280]{5,4,3,2,1,0:T(8,128)(2,1)S(1)} collective-permute-done((bf16[1,2,1,1,128,1280]{5,4,3,2,1,0:T(8,128)(2,1)S(1)}, bf16[1,2,1,1,128,1280]{5,4,3,2,1,0:T(8,128)(2,1)S(1)}, u32[]{:S(2)}, u32[]{:S(2)}) %collective-permute-start.69) | collective-permute-done | bytes 655392 | tf_op jit(solution)/shard_map/ppermute | solution.py:39
  640.1 2.4 collective-permute-start.70
  643.5 13.1 %collective-permute-done.71 = bf16[1,1,1,1,128,1280]{5,4,3,2,1,0:T(8,128)(2,1)S(1)} collective-permute-done((bf16[1,1,1,1,128,1280]{5,4,3,2,1,0:T(8,128)(2,1)S(1)}, bf16[1,1,1,1,128,1280]{5,4,3,2,1,0:T(8,128)(2,1)S(1)}, u32[]{:S(2)}, u32[]{:S(2)}) %collective-permute-start.71) | collective-permute-done | bytes 327712 | tf_op jit(solution)/shard_map/ppermute | solution.py:39
  (515 shorter events, 192.8 us)
Async XLA Ops:
  1.3 12.4 %collective-permute-start = (bf16[1,1,1,1,2,128]{5,4,3,2,1,0:T(2,128)(2,1)S(1)}, bf16[1,1,1,1,2,128]{5,4,3,2,1,0:T(2,128)(2,1)S(1)}, u32[]{:S(2)}, u32[]{:S(2)}) collective-permute-start(bf16[1,1,1,1,2,128]{5,4,3,2,1,0:T(2,128)(2,1)S(1)} %maximum_bitcast_fusion.1), channel_id=1, source_target_pairs={{0,16},{2,18},{4,20},{6,22},{8,24},{10,26},{12,28},{14,30},{16,0},... | collective-permute-start | bytes 1544 | tf_op jit(solution)/shard_map/ppermute | solution.py:39
  6.4 22.0 %collective-permute-start.4 = (bf16[1,1,1,1,128,1280]{5,4,3,2,1,0:T(8,128)(2,1)S(1)}, bf16[1,1,1,1,128,1280]{5,4,3,2,1,0:T(8,128)(2,1)}, u32[]{:S(2)}, u32[]{:S(2)}) collective-permute-start(bf16[1,1,1,1,128,1280]{5,4,3,2,1,0:T(8,128)(2,1)S(1)} %maximum_bitcast_fusion), channel_id=1, source_target_pairs={{0,16},{2,18},{4,20},{6,22},{8,24},{10,26},{12,28},{14,30},{16,0},... | collective-permute-start | bytes 983048 | tf_op jit(solution)/shard_map/ppermute | solution.py:39
  25.8 12.6 %collective-permute-start.6 = (bf16[1,1,1,1,128,1024]{5,4,3,2,1,0:T(8,128)(2,1)S(1)}, bf16[1,1,1,1,128,1024]{5,4,3,2,1,0:T(8,128)(2,1)S(1)}, u32[]{:S(2)}, u32[]{:S(2)}) collective-permute-start(bf16[1,1,1,1,128,1024]{5,4,3,2,1,0:T(8,128)(2,1)S(1)} %bitcast.192), channel_id=1, source_target_pairs={{0,16},{2,18},{4,20},{6,22},{8,24},{10,26},{12,28},{14,30},{16,0},... | collective-permute-start | bytes 786440 | tf_op jit(solution)/shard_map/ppermute | solution.py:39
  29.4 19.5 %collective-permute-start.8 = (bf16[1,2,1,1,128,1280]{5,4,3,2,1,0:T(8,128)(2,1)S(1)}, bf16[1,2,1,1,128,1280]{5,4,3,2,1,0:T(8,128)(2,1)S(1)}, u32[]{:S(2)}, u32[]{:S(2)}) collective-permute-start(bf16[1,2,1,1,128,1280]{5,4,3,2,1,0:T(8,128)(2,1)S(1)} %pad_maximum_fusion.41), channel_id=1, source_target_pairs={{0,8},{2,10},{4,12},{6,14},{8,0},{10,2},{12,4},{14,6},{16,24},{18,... | collective-permute-start | bytes 1966088 | tf_op jit(solution)/shard_map/ppermute | solution.py:39
  30.8 40.2 %collective-permute-start.5 = (bf16[384,2048]{1,0:T(8,128)(2,1)S(1)}, bf16[384,2048]{1,0:T(8,128)(2,1)S(1)}, u32[]{:S(2)}, u32[]{:S(2)}) collective-permute-start(bf16[384,2048]{1,0:T(8,128)(2,1)S(1)} %fusion.8), channel_id=1, source_target_pairs={{0,1},{1,0},{2,3},{3,2},{4,5},{5,4},{6,7},{7,6},{8,9},{9,8},{10,11... | collective-permute-start | bytes 4718600 | tf_op jit(solution)/shard_map/ppermute | solution.py:43
  50.2 14.7 %collective-permute-start.10 = (bf16[2,2,1,1,128,640]{5,4,3,2,1,0:T(8,128)(2,1)S(1)}, bf16[2,2,1,1,128,640]{5,4,3,2,1,0:T(8,128)(2,1)S(1)}, u32[]{:S(2)}, u32[]{:S(2)}) collective-permute-start(bf16[2,2,1,1,128,640]{5,4,3,2,1,0:T(8,128)(2,1)S(1)} %get-tuple-element.258), channel_id=1, source_target_pairs={{0,2},{2,0},{4,6},{6,4},{8,10},{10,8},{12,14},{14,12},{16,18},{18,... | collective-permute-start | bytes 1966088 | tf_op jit(solution)/shard_map/ppermute | solution.py:39
  51.8 15.6 %collective-permute-start.9 = (bf16[2,2,1,1,128,640]{5,4,3,2,1,0:T(8,128)(2,1)S(1)}, bf16[2,2,1,1,128,640]{5,4,3,2,1,0:T(8,128)(2,1)S(1)}, u32[]{:S(2)}, u32[]{:S(2)}) collective-permute-start(bf16[2,2,1,1,128,640]{5,4,3,2,1,0:T(8,128)(2,1)S(1)} %get-tuple-element.259), channel_id=1, source_target_pairs={{0,4},{2,6},{4,0},{6,2},{8,12},{10,14},{12,8},{14,10},{16,20},{18,... | collective-permute-start | bytes 1966088 | tf_op jit(solution)/shard_map/ppermute | solution.py:39
  53.1 15.8 %collective-permute-start.13 = (bf16[1,1,1,1,128,2304]{5,4,3,2,1,0:T(8,128)(2,1)S(1)}, bf16[1,1,1,1,128,2304]{5,4,3,2,1,0:T(8,128)(2,1)S(1)}, u32[]{:S(2)}, u32[]{:S(2)}) collective-permute-start(bf16[1,1,1,1,128,2304]{5,4,3,2,1,0:T(8,128)(2,1)S(1)} %bitcast.154), channel_id=1, source_target_pairs={{0,8},{2,10},{4,12},{6,14},{8,0},{10,2},{12,4},{14,6},{16,24},{18,... | collective-permute-start | bytes 1769480 | tf_op jit(solution)/shard_map/ppermute | solution.py:39
  65.0 29.2 %collective-permute-start.12 = (bf16[2,2,1,2,128,640]{5,4,3,2,1,0:T(8,128)(2,1)S(1)}, bf16[2,2,1,2,128,640]{5,4,3,2,1,0:T(8,128)(2,1)S(1)}, u32[]{:S(2)}, u32[]{:S(2)}) collective-permute-start(bf16[2,2,1,2,128,640]{5,4,3,2,1,0:T(8,128)(2,1)S(1)} %pad_maximum_fusion.29), channel_id=1, source_target_pairs={{0,4},{2,6},{4,0},{6,2},{8,12},{10,14},{12,8},{14,10},{16,20},{18,... | collective-permute-start | bytes 3932168 | tf_op jit(solution)/shard_map/ppermute | solution.py:39
  67.5 26.7 %collective-permute-start.11 = (bf16[2,2,2,1,128,640]{5,4,3,2,1,0:T(8,128)(2,1)S(1)}, bf16[2,2,2,1,128,640]{5,4,3,2,1,0:T(8,128)(2,1)S(1)}, u32[]{:S(2)}, u32[]{:S(2)}) collective-permute-start(bf16[2,2,2,1,128,640]{5,4,3,2,1,0:T(8,128)(2,1)S(1)} %pad_maximum_fusion.30), channel_id=1, source_target_pairs={{0,2},{2,0},{4,6},{6,4},{8,10},{10,8},{12,14},{14,12},{16,18},{18,... | collective-permute-start | bytes 3932168 | tf_op jit(solution)/shard_map/ppermute | solution.py:39
  68.9 26.0 %collective-permute-start.7 = (bf16[1,2,1,1,128,1024]{5,4,3,2,1,0:T(8,128)(2,1)S(1)}, bf16[1,2,1,1,128,1024]{5,4,3,2,1,0:T(8,128)(2,1)S(1)}, u32[]{:S(2)}, u32[]{:S(2)}) collective-permute-start(bf16[1,2,1,1,128,1024]{5,4,3,2,1,0:T(8,128)(2,1)S(1)} %pad_maximum_fusion.43), channel_id=1, source_target_pairs={{0,8},{2,10},{4,12},{6,14},{8,0},{10,2},{12,4},{14,6},{16,24},{18,... | collective-permute-start | bytes 1572872 | tf_op jit(solution)/shard_map/ppermute | solution.py:39
  70.0 61.3 %collective-permute-start.14 = (bf16[2,1,1,1,128,2304]{5,4,3,2,1,0:T(8,128)(2,1)}, bf16[2,1,1,1,128,2304]{5,4,3,2,1,0:T(8,128)(2,1)}, u32[]{:S(2)}, u32[]{:S(2)}) collective-permute-start(bf16[2,1,1,1,128,2304]{5,4,3,2,1,0:T(8,128)(2,1)} %pad_maximum_fusion.32), channel_id=1, source_target_pairs={{0,16},{2,18},{4,20},{6,22},{8,24},{10,26},{12,28},{14,30},{16,0},... | collective-permute-start | bytes 3538952 | tf_op jit(solution)/shard_map/ppermute | solution.py:39
  71.0 66.9 %collective-permute-start.19 = (bf16[384,2048]{1,0:T(8,128)(2,1)}, bf16[384,2048]{1,0:T(8,128)(2,1)S(1)}, u32[]{:S(2)}, u32[]{:S(2)}) collective-permute-start(bf16[384,2048]{1,0:T(8,128)(2,1)} %pad_maximum_fusion.18), channel_id=1, source_target_pairs={{0,8},{2,10},{4,12},{6,14},{8,0},{10,2},{12,4},{14,6},{16,24},{18,... | collective-permute-start | bytes 4718600 | tf_op jit(solution)/shard_map/ppermute | solution.py:39
  95.1 19.6 %collective-permute-start.16 = (bf16[2,2,1,1,128,512]{5,4,3,2,1,0:T(8,128)(2,1)S(1)}, bf16[2,2,1,1,128,512]{5,4,3,2,1,0:T(8,128)(2,1)S(1)}, u32[]{:S(2)}, u32[]{:S(2)}) collective-permute-start(bf16[2,2,1,1,128,512]{5,4,3,2,1,0:T(8,128)(2,1)S(1)} %get-tuple-element.275), channel_id=1, source_target_pairs={{0,2},{2,0},{4,6},{6,4},{8,10},{10,8},{12,14},{14,12},{16,18},{18,... | collective-permute-start | bytes 1572872 | tf_op jit(solution)/shard_map/ppermute | solution.py:39
  95.7 19.6 %collective-permute-start.15 = (bf16[2,2,1,1,128,512]{5,4,3,2,1,0:T(8,128)(2,1)S(1)}, bf16[2,2,1,1,128,512]{5,4,3,2,1,0:T(8,128)(2,1)S(1)}, u32[]{:S(2)}, u32[]{:S(2)}) collective-permute-start(bf16[2,2,1,1,128,512]{5,4,3,2,1,0:T(8,128)(2,1)S(1)} %get-tuple-element.531), channel_id=1, source_target_pairs={{0,4},{2,6},{4,0},{6,2},{8,12},{10,14},{12,8},{14,10},{16,20},{18,... | collective-permute-start | bytes 1572872 | tf_op jit(solution)/shard_map/ppermute | solution.py:39
  114.8 25.9 %collective-permute-start.18 = (bf16[2,2,1,2,128,512]{5,4,3,2,1,0:T(8,128)(2,1)S(1)}, bf16[2,2,1,2,128,512]{5,4,3,2,1,0:T(8,128)(2,1)}, u32[]{:S(2)}, u32[]{:S(2)}) collective-permute-start(bf16[2,2,1,2,128,512]{5,4,3,2,1,0:T(8,128)(2,1)S(1)} %pad_maximum_fusion.34), channel_id=1, source_target_pairs={{0,4},{2,6},{4,0},{6,2},{8,12},{10,14},{12,8},{14,10},{16,20},{18,... | collective-permute-start | bytes 3145736 | tf_op jit(solution)/shard_map/ppermute | solution.py:39
  116.4 25.7 %collective-permute-start.17 = (bf16[2,2,2,1,128,512]{5,4,3,2,1,0:T(8,128)(2,1)}, bf16[2,2,2,1,128,512]{5,4,3,2,1,0:T(8,128)(2,1)}, u32[]{:S(2)}, u32[]{:S(2)}) collective-permute-start(bf16[2,2,2,1,128,512]{5,4,3,2,1,0:T(8,128)(2,1)} %pad_maximum_fusion.35), channel_id=1, source_target_pairs={{0,2},{2,0},{4,6},{6,4},{8,10},{10,8},{12,14},{14,12},{16,18},{18,... | collective-permute-start | bytes 3145736 | tf_op jit(solution)/shard_map/ppermute | solution.py:39
  154.7 16.3 %collective-permute-start.28 = (bf16[384,2048]{1,0:T(8,128)(2,1)S(1)}, bf16[384,2048]{1,0:T(8,128)(2,1)S(1)}, u32[]{:S(2)}, u32[]{:S(2)}) collective-permute-start(bf16[384,2048]{1,0:T(8,128)(2,1)S(1)} %collective-permute-done.19.refs_0_), channel_id=1, source_target_pairs={{0,1},{1,0},{2,3},{3,2},{4,5},{5,4},{6,7},{7,6},{8,9},{9,8},{10,11... | collective-permute-start | bytes 4718600 | tf_op jit(solution)/shard_map/ppermute | solution.py:43
  154.8 28.4 %collective-permute-start.27 = (bf16[2,2,1,1,128,1152]{5,4,3,2,1,0:T(8,128)(2,1)S(1)}, bf16[2,2,1,1,128,1152]{5,4,3,2,1,0:T(8,128)(2,1)}, u32[]{:S(2)}, u32[]{:S(2)}) collective-permute-start(bf16[2,2,1,1,128,1152]{5,4,3,2,1,0:T(8,128)(2,1)S(1)} %get-tuple-element.291), channel_id=1, source_target_pairs={{0,4},{2,6},{4,0},{6,2},{8,12},{10,14},{12,8},{14,10},{16,20},{18,... | collective-permute-start | bytes 3538952 | tf_op jit(solution)/shard_map/ppermute | solution.py:39
  156.3 28.4 %collective-permute-start.26 = (bf16[2,2,1,1,128,1152]{5,4,3,2,1,0:T(8,128)(2,1)}, bf16[2,2,1,1,128,1152]{5,4,3,2,1,0:T(8,128)(2,1)}, u32[]{:S(2)}, u32[]{:S(2)}) collective-permute-start(bf16[2,2,1,1,128,1152]{5,4,3,2,1,0:T(8,128)(2,1)} %get-tuple-element.292), channel_id=1, source_target_pairs={{0,2},{2,0},{4,6},{6,4},{8,10},{10,8},{12,14},{14,12},{16,18},{18,... | collective-permute-start | bytes 3538952 | tf_op jit(solution)/shard_map/ppermute | solution.py:39
  157.6 13.3 %collective-permute-start.23 = (bf16[1,1,1,1,128,1920]{5,4,3,2,1,0:T(8,128)(2,1)S(1)}, bf16[1,1,1,1,128,1920]{5,4,3,2,1,0:T(8,128)(2,1)S(1)}, u32[]{:S(2)}, u32[]{:S(2)}) collective-permute-start(bf16[1,1,1,1,128,1920]{5,4,3,2,1,0:T(8,128)(2,1)S(1)} %bitcast.155), channel_id=1, source_target_pairs={{0,8},{2,10},{4,12},{6,14},{8,0},{10,2},{12,4},{14,6},{16,24},{18,... | collective-permute-start | bytes 1474568 | tf_op jit(solution)/shard_map/ppermute | solution.py:39
  186.7 56.8 %collective-permute-start.30 = (bf16[2,2,1,2,128,1152]{5,4,3,2,1,0:T(8,128)(2,1)S(1)}, bf16[2,2,1,2,128,1152]{5,4,3,2,1,0:T(8,128)(2,1)S(1)}, u32[]{:S(2)}, u32[]{:S(2)}) collective-permute-start(bf16[2,2,1,2,128,1152]{5,4,3,2,1,0:T(8,128)(2,1)S(1)} %pad_maximum_fusion.5), channel_id=1, source_target_pairs={{0,4},{2,6},{4,0},{6,2},{8,12},{10,14},{12,8},{14,10},{16,20},{18,... | collective-permute-start | bytes 7077896 | tf_op jit(solution)/shard_map/ppermute | solution.py:39
  188.3 55.3 %collective-permute-start.29 = (bf16[2,2,2,1,128,1152]{5,4,3,2,1,0:T(8,128)(2,1)S(1)}, bf16[2,2,2,1,128,1152]{5,4,3,2,1,0:T(8,128)(2,1)S(1)}, u32[]{:S(2)}, u32[]{:S(2)}) collective-permute-start(bf16[2,2,2,1,128,1152]{5,4,3,2,1,0:T(8,128)(2,1)S(1)} %pad_maximum_fusion.6), channel_id=1, source_target_pairs={{0,2},{2,0},{4,6},{6,4},{8,10},{10,8},{12,14},{14,12},{16,18},{18,... | collective-permute-start | bytes 7077896 | tf_op jit(solution)/shard_map/ppermute | solution.py:39
  188.8 56.4 %collective-permute-start.22 = (bf16[384,2048]{1,0:T(8,128)(2,1)S(1)}, bf16[384,2048]{1,0:T(8,128)(2,1)S(1)}, u32[]{:S(2)}, u32[]{:S(2)}) collective-permute-start(bf16[384,2048]{1,0:T(8,128)(2,1)S(1)} %copy-done.104), channel_id=1, source_target_pairs={{0,8},{2,10},{4,12},{6,14},{8,0},{10,2},{12,4},{14,6},{16,24},{18,... | collective-permute-start | bytes 4718600 | tf_op jit(solution)/shard_map/ppermute | solution.py:39
  189.1 53.9 %collective-permute-start.25 = (bf16[2,1,1,1,128,1920]{5,4,3,2,1,0:T(8,128)(2,1)S(1)}, bf16[2,1,1,1,128,1920]{5,4,3,2,1,0:T(8,128)(2,1)S(1)}, u32[]{:S(2)}, u32[]{:S(2)}) collective-permute-start(bf16[2,1,1,1,128,1920]{5,4,3,2,1,0:T(8,128)(2,1)S(1)} %pad_maximum_fusion.38), channel_id=1, source_target_pairs={{0,16},{2,18},{4,20},{6,22},{8,24},{10,26},{12,28},{14,30},{16,0},... | collective-permute-start | bytes 2949128 | tf_op jit(solution)/shard_map/ppermute | solution.py:39
  245.2 29.7 %collective-permute-start.31 = (bf16[384,2048]{1,0:T(8,128)(2,1)S(1)}, bf16[384,2048]{1,0:T(8,128)(2,1)S(1)}, u32[]{:S(2)}, u32[]{:S(2)}) collective-permute-start(bf16[384,2048]{1,0:T(8,128)(2,1)S(1)} %collective-permute-done.22.refs_0_), channel_id=1, source_target_pairs={{0,1},{1,0},{2,3},{3,2},{4,5},{5,4},{6,7},{7,6},{8,9},{9,8},{10,11... | collective-permute-start | bytes 4718600 | tf_op jit(solution)/shard_map/ppermute | solution.py:43
  250.6 25.7 %collective-permute-start.33 = (bf16[2,2,1,1,128,896]{5,4,3,2,1,0:T(8,128)(2,1)S(1)}, bf16[2,2,1,1,128,896]{5,4,3,2,1,0:T(8,128)(2,1)}, u32[]{:S(2)}, u32[]{:S(2)}) collective-permute-start(bf16[2,2,1,1,128,896]{5,4,3,2,1,0:T(8,128)(2,1)S(1)} %pad_maximum_fusion.39), channel_id=1, source_target_pairs={{0,2},{2,0},{4,6},{6,4},{8,10},{10,8},{12,14},{14,12},{16,18},{18,... | collective-permute-start | bytes 2752520 | tf_op jit(solution)/shard_map/ppermute | solution.py:39
  252.2 27.4 %collective-permute-start.32 = (bf16[2,2,1,1,128,1024]{5,4,3,2,1,0:T(8,128)(2,1)S(1)}, bf16[2,2,1,1,128,1024]{5,4,3,2,1,0:T(8,128)(2,1)}, u32[]{:S(2)}, u32[]{:S(2)}) collective-permute-start(bf16[2,2,1,1,128,1024]{5,4,3,2,1,0:T(8,128)(2,1)S(1)} %slice.404), channel_id=1, source_target_pairs={{0,4},{2,6},{4,0},{6,2},{8,12},{10,14},{12,8},{14,10},{16,20},{18,... | collective-permute-start | bytes 3145736 | tf_op jit(solution)/shard_map/ppermute | solution.py:39
  282.3 49.1 %collective-permute-start.35 = (bf16[2,2,1,2,128,896]{5,4,3,2,1,0:T(8,128)(2,1)}, bf16[2,2,1,2,128,896]{5,4,3,2,1,0:T(8,128)(2,1)}, u32[]{:S(2)}, u32[]{:S(2)}) collective-permute-start(bf16[2,2,1,2,128,896]{5,4,3,2,1,0:T(8,128)(2,1)} %pad_maximum_fusion.13), channel_id=1, source_target_pairs={{0,4},{2,6},{4,0},{6,2},{8,12},{10,14},{12,8},{14,10},{16,20},{18,... | collective-permute-start | bytes 5505032 | tf_op jit(solution)/shard_map/ppermute | solution.py:39
  283.9 52.1 %collective-permute-start.34 = (bf16[2,2,2,1,128,1024]{5,4,3,2,1,0:T(8,128)(2,1)}, bf16[2,2,2,1,128,1024]{5,4,3,2,1,0:T(8,128)(2,1)}, u32[]{:S(2)}, u32[]{:S(2)}) collective-permute-start(bf16[2,2,2,1,128,1024]{5,4,3,2,1,0:T(8,128)(2,1)} %pad_maximum_fusion.7), channel_id=1, source_target_pairs={{0,2},{2,0},{4,6},{6,4},{8,10},{10,8},{12,14},{14,12},{16,18},{18,... | collective-permute-start | bytes 6291464 | tf_op jit(solution)/shard_map/ppermute | solution.py:39
  313.2 69.8 %collective-permute-start.38 = (bf16[2,2,1,2,128,1152]{5,4,3,2,1,0:T(8,128)(2,1)}, bf16[2,2,1,2,128,1152]{5,4,3,2,1,0:T(8,128)(2,1)}, u32[]{:S(2)}, u32[]{:S(2)}) collective-permute-start(bf16[2,2,1,2,128,1152]{5,4,3,2,1,0:T(8,128)(2,1)} %bitcast.213), channel_id=1, source_target_pairs={{0,4},{2,6},{4,0},{6,2},{8,12},{10,14},{12,8},{14,10},{16,20},{18,... | collective-permute-start | bytes 7077896 | tf_op jit(solution)/shard_map/ppermute | solution.py:39
  325.9 61.6 %collective-permute-start.37 = (bf16[2,2,2,1,128,1152]{5,4,3,2,1,0:T(8,128)(2,1)}, bf16[2,2,2,1,128,1152]{5,4,3,2,1,0:T(8,128)(2,1)}, u32[]{:S(2)}, u32[]{:S(2)}) collective-permute-start(bf16[2,2,2,1,128,1152]{5,4,3,2,1,0:T(8,128)(2,1)} %bitcast.214), channel_id=1, source_target_pairs={{0,2},{2,0},{4,6},{6,4},{8,10},{10,8},{12,14},{14,12},{16,18},{18,... | collective-permute-start | bytes 7077896 | tf_op jit(solution)/shard_map/ppermute | solution.py:39
  371.5 23.8 %collective-permute-start.36 = (bf16[384,2048]{1,0:T(8,128)(2,1)}, bf16[384,2048]{1,0:T(8,128)(2,1)}, u32[]{:S(2)}, u32[]{:S(2)}) collective-permute-start(bf16[384,2048]{1,0:T(8,128)(2,1)} %copy-done.63), channel_id=1, source_target_pairs={{0,1},{1,0},{2,3},{3,2},{4,5},{5,4},{6,7},{7,6},{8,9},{9,8},{10,11... | collective-permute-start | bytes 4718600 | tf_op jit(solution)/shard_map/ppermute | solution.py:43
  391.6 46.9 %collective-permute-start.40 = (bf16[2,2,1,1,128,1152]{5,4,3,2,1,0:T(8,128)(2,1)}, bf16[2,2,1,1,128,1152]{5,4,3,2,1,0:T(8,128)(2,1)}, u32[]{:S(2)}, u32[]{:S(2)}) collective-permute-start(bf16[2,2,1,1,128,1152]{5,4,3,2,1,0:T(8,128)(2,1)} %slice.422), channel_id=1, source_target_pairs={{0,2},{2,0},{4,6},{6,4},{8,10},{10,8},{12,14},{14,12},{16,18},{18,... | collective-permute-start | bytes 3538952 | tf_op jit(solution)/shard_map/ppermute | solution.py:39
  393.9 44.8 %collective-permute-start.41 = (bf16[2,2,1,1,128,1152]{5,4,3,2,1,0:T(8,128)(2,1)}, bf16[2,2,1,1,128,1152]{5,4,3,2,1,0:T(8,128)(2,1)}, u32[]{:S(2)}, u32[]{:S(2)}) collective-permute-start(bf16[2,2,1,1,128,1152]{5,4,3,2,1,0:T(8,128)(2,1)} %slice.421), channel_id=1, source_target_pairs={{0,4},{2,6},{4,0},{6,2},{8,12},{10,14},{12,8},{14,10},{16,20},{18,... | collective-permute-start | bytes 3538952 | tf_op jit(solution)/shard_map/ppermute | solution.py:39
  399.2 44.5 %collective-permute-start.42 = (bf16[384,2048]{1,0:T(8,128)(2,1)}, bf16[384,2048]{1,0:T(8,128)(2,1)}, u32[]{:S(2)}, u32[]{:S(2)}) collective-permute-start(bf16[384,2048]{1,0:T(8,128)(2,1)} %pad_maximum_fusion.23), channel_id=1, source_target_pairs={{0,8},{2,10},{4,12},{6,14},{8,0},{10,2},{12,4},{14,6},{16,24},{18,... | collective-permute-start | bytes 4718600 | tf_op jit(solution)/shard_map/ppermute | solution.py:39
  410.9 56.5 %collective-permute-start.45 = (bf16[2,2,1,2,128,896]{5,4,3,2,1,0:T(8,128)(2,1)}, bf16[2,2,1,2,128,896]{5,4,3,2,1,0:T(8,128)(2,1)}, u32[]{:S(2)}, u32[]{:S(2)}) collective-permute-start(bf16[2,2,1,2,128,896]{5,4,3,2,1,0:T(8,128)(2,1)} %bitcast.216), channel_id=1, source_target_pairs={{0,4},{2,6},{4,0},{6,2},{8,12},{10,14},{12,8},{14,10},{16,20},{18,... | collective-permute-start | bytes 5505032 | tf_op jit(solution)/shard_map/ppermute | solution.py:39
  423.7 47.9 %collective-permute-start.44 = (bf16[2,2,2,1,128,1024]{5,4,3,2,1,0:T(8,128)(2,1)}, bf16[2,2,2,1,128,1024]{5,4,3,2,1,0:T(8,128)(2,1)}, u32[]{:S(2)}, u32[]{:S(2)}) collective-permute-start(bf16[2,2,2,1,128,1024]{5,4,3,2,1,0:T(8,128)(2,1)} %bitcast.215), channel_id=1, source_target_pairs={{0,2},{2,0},{4,6},{6,4},{8,10},{10,8},{12,14},{14,12},{16,18},{18,... | collective-permute-start | bytes 6291464 | tf_op jit(solution)/shard_map/ppermute | solution.py:39
  453.3 23.6 %collective-permute-start.43 = (bf16[384,2048]{1,0:T(8,128)(2,1)}, bf16[384,2048]{1,0:T(8,128)(2,1)}, u32[]{:S(2)}, u32[]{:S(2)}) collective-permute-start(bf16[384,2048]{1,0:T(8,128)(2,1)} %get-tuple-element.378), channel_id=1, source_target_pairs={{0,1},{1,0},{2,3},{3,2},{4,5},{5,4},{6,7},{7,6},{8,9},{9,8},{10,11... | collective-permute-start | bytes 4718600 | tf_op jit(solution)/shard_map/ppermute | solution.py:43
  453.7 54.7 %collective-permute-start.48 = (bf16[2,1,1,1,128,2304]{5,4,3,2,1,0:T(8,128)(2,1)}, bf16[2,1,1,1,128,2304]{5,4,3,2,1,0:T(8,128)(2,1)}, u32[]{:S(2)}, u32[]{:S(2)}) collective-permute-start(bf16[2,1,1,1,128,2304]{5,4,3,2,1,0:T(8,128)(2,1)} %fusion.23), channel_id=1, source_target_pairs={{0,16},{2,18},{4,20},{6,22},{8,24},{10,26},{12,28},{14,30},{16,0},... | collective-permute-start | bytes 3538952 | tf_op jit(solution)/shard_map/ppermute | solution.py:39
  467.4 19.1 %collective-permute-start.46 = (bf16[384,2048]{1,0:T(8,128)(2,1)S(1)}, bf16[384,2048]{1,0:T(8,128)(2,1)S(1)}, u32[]{:S(2)}, u32[]{:S(2)}) collective-permute-start(bf16[384,2048]{1,0:T(8,128)(2,1)S(1)} %get-tuple-element.383), channel_id=1, source_target_pairs={{0,1},{1,0},{2,3},{3,2},{4,5},{5,4},{6,7},{7,6},{8,9},{9,8},{10,11... | collective-permute-start | bytes 4718600 | tf_op jit(solution)/shard_map/ppermute | solution.py:43
  474.1 36.5 %collective-permute-start.47 = (bf16[2,2,1,1,128,896]{5,4,3,2,1,0:T(8,128)(2,1)}, bf16[2,2,1,1,128,896]{5,4,3,2,1,0:T(8,128)(2,1)}, u32[]{:S(2)}, u32[]{:S(2)}) collective-permute-start(bf16[2,2,1,1,128,896]{5,4,3,2,1,0:T(8,128)(2,1)} %slice.430), channel_id=1, source_target_pairs={{0,2},{2,0},{4,6},{6,4},{8,10},{10,8},{12,14},{14,12},{16,18},{18,... | collective-permute-start | bytes 2752520 | tf_op jit(solution)/shard_map/ppermute | solution.py:39
  476.4 35.6 %collective-permute-start.49 = (bf16[2,2,1,1,128,1024]{5,4,3,2,1,0:T(8,128)(2,1)}, bf16[2,2,1,1,128,1024]{5,4,3,2,1,0:T(8,128)(2,1)}, u32[]{:S(2)}, u32[]{:S(2)}) collective-permute-start(bf16[2,2,1,1,128,1024]{5,4,3,2,1,0:T(8,128)(2,1)} %slice.429), channel_id=1, source_target_pairs={{0,4},{2,6},{4,0},{6,2},{8,12},{10,14},{12,8},{14,10},{16,20},{18,... | collective-permute-start | bytes 3145736 | tf_op jit(solution)/shard_map/ppermute | solution.py:39
  481.9 51.3 %collective-permute-start.52 = (bf16[2,2,1,2,128,512]{5,4,3,2,1,0:T(8,128)(2,1)}, bf16[2,2,1,2,128,512]{5,4,3,2,1,0:T(8,128)(2,1)}, u32[]{:S(2)}, u32[]{:S(2)}) collective-permute-start(bf16[2,2,1,2,128,512]{5,4,3,2,1,0:T(8,128)(2,1)} %slice.431), channel_id=1, source_target_pairs={{0,4},{2,6},{4,0},{6,2},{8,12},{10,14},{12,8},{14,10},{16,20},{18,... | collective-permute-start | bytes 3145736 | tf_op jit(solution)/shard_map/ppermute | solution.py:39
  486.4 49.0 %collective-permute-start.51 = (bf16[2,2,2,1,128,512]{5,4,3,2,1,0:T(8,128)(2,1)}, bf16[2,2,2,1,128,512]{5,4,3,2,1,0:T(8,128)(2,1)}, u32[]{:S(2)}, u32[]{:S(2)}) collective-permute-start(bf16[2,2,2,1,128,512]{5,4,3,2,1,0:T(8,128)(2,1)} %slice.432), channel_id=1, source_target_pairs={{0,2},{2,0},{4,6},{6,4},{8,10},{10,8},{12,14},{14,12},{16,18},{18,... | collective-permute-start | bytes 3145736 | tf_op jit(solution)/shard_map/ppermute | solution.py:39
  510.0 38.4 %collective-permute-start.50 = (bf16[1,1,1,1,128,2304]{5,4,3,2,1,0:T(8,128)(2,1)S(1)}, bf16[1,1,1,1,128,2304]{5,4,3,2,1,0:T(8,128)(2,1)S(1)}, u32[]{:S(2)}, u32[]{:S(2)}) collective-permute-start(bf16[1,1,1,1,128,2304]{5,4,3,2,1,0:T(8,128)(2,1)S(1)} %slice.572), channel_id=1, source_target_pairs={{0,8},{2,10},{4,12},{6,14},{8,0},{10,2},{12,4},{14,6},{16,24},{18,... | collective-permute-start | bytes 1769480 | tf_op jit(solution)/shard_map/ppermute | solution.py:39
  514.7 52.1 %collective-permute-start.56 = (bf16[2,1,1,1,128,1920]{5,4,3,2,1,0:T(8,128)(2,1)}, bf16[2,1,1,1,128,1920]{5,4,3,2,1,0:T(8,128)(2,1)}, u32[]{:S(2)}, u32[]{:S(2)}) collective-permute-start(bf16[2,1,1,1,128,1920]{5,4,3,2,1,0:T(8,128)(2,1)} %fusion.24), channel_id=1, source_target_pairs={{0,16},{2,18},{4,20},{6,22},{8,24},{10,26},{12,28},{14,30},{16,0},... | collective-permute-start | bytes 2949128 | tf_op jit(solution)/shard_map/ppermute | solution.py:39
  518.1 100.2 %collective-permute-start.65 = (bf16[384,2048]{1,0:T(8,128)(2,1)}, bf16[384,2048]{1,0:T(8,128)(2,1)}, u32[]{:S(2)}, u32[]{:S(2)}) collective-permute-start(bf16[384,2048]{1,0:T(8,128)(2,1)} %pad_maximum_fusion.24), channel_id=1, source_target_pairs={{0,8},{2,10},{4,12},{6,14},{8,0},{10,2},{12,4},{14,6},{16,24},{18,... | collective-permute-start | bytes 4718600 | tf_op jit(solution)/shard_map/ppermute | solution.py:39
  539.5 22.2 %collective-permute-start.57 = (bf16[2,2,1,1,128,512]{5,4,3,2,1,0:T(8,128)(2,1)}, bf16[2,2,1,1,128,512]{5,4,3,2,1,0:T(8,128)(2,1)S(1)}, u32[]{:S(2)}, u32[]{:S(2)}) collective-permute-start(bf16[2,2,1,1,128,512]{5,4,3,2,1,0:T(8,128)(2,1)} %slice.443), channel_id=1, source_target_pairs={{0,2},{2,0},{4,6},{6,4},{8,10},{10,8},{12,14},{14,12},{16,18},{18,... | collective-permute-start | bytes 1572872 | tf_op jit(solution)/shard_map/ppermute | solution.py:39
  540.8 22.5 %collective-permute-start.58 = (bf16[2,2,1,1,128,512]{5,4,3,2,1,0:T(8,128)(2,1)}, bf16[2,2,1,1,128,512]{5,4,3,2,1,0:T(8,128)(2,1)}, u32[]{:S(2)}, u32[]{:S(2)}) collective-permute-start(bf16[2,2,1,1,128,512]{5,4,3,2,1,0:T(8,128)(2,1)} %slice.441), channel_id=1, source_target_pairs={{0,4},{2,6},{4,0},{6,2},{8,12},{10,14},{12,8},{14,10},{16,20},{18,... | collective-permute-start | bytes 1572872 | tf_op jit(solution)/shard_map/ppermute | solution.py:39
  548.4 45.0 %collective-permute-start.54 = (bf16[2,2,2,1,128,640]{5,4,3,2,1,0:T(8,128)(2,1)}, bf16[2,2,2,1,128,640]{5,4,3,2,1,0:T(8,128)(2,1)}, u32[]{:S(2)}, u32[]{:S(2)}) collective-permute-start(bf16[2,2,2,1,128,640]{5,4,3,2,1,0:T(8,128)(2,1)} %slice.444), channel_id=1, source_target_pairs={{0,2},{2,0},{4,6},{6,4},{8,10},{10,8},{12,14},{14,12},{16,18},{18,... | collective-permute-start | bytes 3932168 | tf_op jit(solution)/shard_map/ppermute | solution.py:39
  561.8 29.9 %collective-permute-start.55 = (bf16[2,2,1,2,128,640]{5,4,3,2,1,0:T(8,128)(2,1)}, bf16[2,2,1,2,128,640]{5,4,3,2,1,0:T(8,128)(2,1)S(1)}, u32[]{:S(2)}, u32[]{:S(2)}) collective-permute-start(bf16[2,2,1,2,128,640]{5,4,3,2,1,0:T(8,128)(2,1)} %slice.445), channel_id=1, source_target_pairs={{0,4},{2,6},{4,0},{6,2},{8,12},{10,14},{12,8},{14,10},{16,20},{18,... | collective-permute-start | bytes 3932168 | tf_op jit(solution)/shard_map/ppermute | solution.py:39
  563.4 54.4 %collective-permute-start.53 = (bf16[384,2048]{1,0:T(8,128)(2,1)S(1)}, bf16[384,2048]{1,0:T(8,128)(2,1)}, u32[]{:S(2)}, u32[]{:S(2)}) collective-permute-start(bf16[384,2048]{1,0:T(8,128)(2,1)S(1)} %get-tuple-element.427), channel_id=1, source_target_pairs={{0,1},{1,0},{2,3},{3,2},{4,5},{5,4},{6,7},{7,6},{8,9},{9,8},{10,11... | collective-permute-start | bytes 4718600 | tf_op jit(solution)/shard_map/ppermute | solution.py:43
  566.8 31.4 %collective-permute-start.59 = (bf16[384,2048]{1,0:T(8,128)(2,1)S(1)}, bf16[384,2048]{1,0:T(8,128)(2,1)S(1)}, u32[]{:S(2)}, u32[]{:S(2)}) collective-permute-start(bf16[384,2048]{1,0:T(8,128)(2,1)S(1)} %copy-done.111), channel_id=1, source_target_pairs={{0,1},{1,0},{2,3},{3,2},{4,5},{5,4},{6,7},{7,6},{8,9},{9,8},{10,11... | collective-permute-start | bytes 4718600 | tf_op jit(solution)/shard_map/ppermute | solution.py:43
  591.7 12.8 %collective-permute-start.61 = (bf16[1,2,1,1,128,1024]{5,4,3,2,1,0:T(8,128)(2,1)}, bf16[1,2,1,1,128,1024]{5,4,3,2,1,0:T(8,128)(2,1)}, u32[]{:S(2)}, u32[]{:S(2)}) collective-permute-start(bf16[1,2,1,1,128,1024]{5,4,3,2,1,0:T(8,128)(2,1)} %fusion.31), channel_id=1, source_target_pairs={{0,8},{2,10},{4,12},{6,14},{8,0},{10,2},{12,4},{14,6},{16,24},{18,... | collective-permute-start | bytes 1572872 | tf_op jit(solution)/shard_map/ppermute | solution.py:39
  596.6 16.3 %collective-permute-start.64 = (bf16[2,2,1,1,128,640]{5,4,3,2,1,0:T(8,128)(2,1)S(1)}, bf16[2,2,1,1,128,640]{5,4,3,2,1,0:T(8,128)(2,1)S(1)}, u32[]{:S(2)}, u32[]{:S(2)}) collective-permute-start(bf16[2,2,1,1,128,640]{5,4,3,2,1,0:T(8,128)(2,1)S(1)} %slice.452), channel_id=1, source_target_pairs={{0,4},{2,6},{4,0},{6,2},{8,12},{10,14},{12,8},{14,10},{16,20},{18,... | collective-permute-start | bytes 1966088 | tf_op jit(solution)/shard_map/ppermute | solution.py:39
  598.2 14.0 %collective-permute-start.63 = (bf16[2,2,1,1,128,640]{5,4,3,2,1,0:T(8,128)(2,1)}, bf16[2,2,1,1,128,640]{5,4,3,2,1,0:T(8,128)(2,1)S(1)}, u32[]{:S(2)}, u32[]{:S(2)}) collective-permute-start(bf16[2,2,1,1,128,640]{5,4,3,2,1,0:T(8,128)(2,1)} %slice.454), channel_id=1, source_target_pairs={{0,2},{2,0},{4,6},{6,4},{8,10},{10,8},{12,14},{14,12},{16,18},{18,... | collective-permute-start | bytes 1966088 | tf_op jit(solution)/shard_map/ppermute | solution.py:39
  605.9 19.7 %collective-permute-start.67 = (bf16[1,1,1,1,128,1920]{5,4,3,2,1,0:T(8,128)(2,1)S(1)}, bf16[1,1,1,1,128,1920]{5,4,3,2,1,0:T(8,128)(2,1)S(1)}, u32[]{:S(2)}, u32[]{:S(2)}) collective-permute-start(bf16[1,1,1,1,128,1920]{5,4,3,2,1,0:T(8,128)(2,1)S(1)} %copy-done.105), channel_id=1, source_target_pairs={{0,8},{2,10},{4,12},{6,14},{8,0},{10,2},{12,4},{14,6},{16,24},{18,... | collective-permute-start | bytes 1474568 | tf_op jit(solution)/shard_map/ppermute | solution.py:39
  612.2 30.3 %collective-permute-start.72 = (bf16[1,1,1,1,128,1024]{5,4,3,2,1,0:T(8,128)(2,1)S(1)}, bf16[1,1,1,1,128,1024]{5,4,3,2,1,0:T(8,128)(2,1)S(1)}, u32[]{:S(2)}, u32[]{:S(2)}) collective-permute-start(bf16[1,1,1,1,128,1024]{5,4,3,2,1,0:T(8,128)(2,1)S(1)} %slice.455), channel_id=1, source_target_pairs={{0,16},{2,18},{4,20},{6,22},{8,24},{10,26},{12,28},{14,30},{16,0},... | collective-permute-start | bytes 786440 | tf_op jit(solution)/shard_map/ppermute | solution.py:39
  616.5 22.7 %collective-permute-start.69 = (bf16[1,2,1,1,128,1280]{5,4,3,2,1,0:T(8,128)(2,1)S(1)}, bf16[1,2,1,1,128,1280]{5,4,3,2,1,0:T(8,128)(2,1)S(1)}, u32[]{:S(2)}, u32[]{:S(2)}) collective-permute-start(bf16[1,2,1,1,128,1280]{5,4,3,2,1,0:T(8,128)(2,1)S(1)} %fusion.30), channel_id=1, source_target_pairs={{0,8},{2,10},{4,12},{6,14},{8,0},{10,2},{12,4},{14,6},{16,24},{18,... | collective-permute-start | bytes 1966088 | tf_op jit(solution)/shard_map/ppermute | solution.py:39
  617.8 10.3 %collective-permute-start.66 = (f32[2,2,1,1,2,128]{5,4,3,2,1,0:T(2,128)S(1)}, f32[2,2,1,1,2,128]{5,4,3,2,1,0:T(2,128)S(1)}, u32[]{:S(2)}, u32[]{:S(2)}) collective-permute-start(f32[2,2,1,1,2,128]{5,4,3,2,1,0:T(2,128)S(1)} %slice.462), channel_id=1, source_target_pairs={{0,2},{2,0},{4,6},{6,4},{8,10},{10,8},{12,14},{14,12},{16,18},{18,... | collective-permute-start | bytes 12296 | tf_op jit(solution)/shard_map/ppermute | solution.py:39
  628.1 12.0 %collective-permute-start.68 = (f32[1,2,1,1,2,128]{5,4,3,2,1,0:T(2,128)S(1)}, f32[1,2,1,1,2,128]{5,4,3,2,1,0:T(2,128)S(1)}, u32[]{:S(2)}, u32[]{:S(2)}) collective-permute-start(f32[1,2,1,1,2,128]{5,4,3,2,1,0:T(2,128)S(1)} %slice.467), channel_id=1, source_target_pairs={{0,8},{2,10},{4,12},{6,14},{8,0},{10,2},{12,4},{14,6},{16,24},{18,... | collective-permute-start | bytes 6152 | tf_op jit(solution)/shard_map/ppermute | solution.py:39
  639.4 17.3 %collective-permute-start.71 = (bf16[1,1,1,1,128,1280]{5,4,3,2,1,0:T(8,128)(2,1)S(1)}, bf16[1,1,1,1,128,1280]{5,4,3,2,1,0:T(8,128)(2,1)S(1)}, u32[]{:S(2)}, u32[]{:S(2)}) collective-permute-start(bf16[1,1,1,1,128,1280]{5,4,3,2,1,0:T(8,128)(2,1)S(1)} %slice.468), channel_id=1, source_target_pairs={{0,16},{2,18},{4,20},{6,22},{8,24},{10,26},{12,28},{14,30},{16,0},... | collective-permute-start | bytes 983048 | tf_op jit(solution)/shard_map/ppermute | solution.py:39
  640.1 18.2 %collective-permute-start.70 = (f32[1,1,1,1,2,128]{5,4,3,2,1,0:T(2,128)S(1)}, f32[1,1,1,1,2,128]{5,4,3,2,1,0:T(2,128)S(1)}, u32[]{:S(2)}, u32[]{:S(2)}) collective-permute-start(f32[1,1,1,1,2,128]{5,4,3,2,1,0:T(2,128)S(1)} %slice.470), channel_id=1, source_target_pairs={{0,16},{2,18},{4,20},{6,22},{8,24},{10,26},{12,28},{14,30},{16,0},... | collective-permute-start | bytes 3080 | tf_op jit(solution)/shard_map/ppermute | solution.py:39
  (125 other events, 1181.2 us)

commit v3 on v2

--- a/solution.py
+++ b/solution.py
@@ -734,6 +734,8 @@
     qb = gather(qb(), X)
     w0 = join(as_block(own_0), held(w0_t), T)
     w0 = gather(w0, rest[0])
+    for bit in rest[1:]:
+        w0 = gather(w0(), bit)
     grad_far_own = send(swap_halves(grad_branch_own), T)
     qa, qb = qa(), qb()
     o = o()
@@ -748,18 +750,18 @@
     did(mixed_a)
     oa = gather(oa(), Y)
     ob = gather(ob(), X)
+    w0 = w0()
+    w1_t = send(as_block(other_1), T)
     mixed_b, queries_b, keys_b, values_b, totals_b = attend_forward(
         held(raw), heads_width, 1, *tables
     )
     did(mixed_b)
-    for bit in rest[1:]:
-        w0 = gather(w0(), bit)
-    w0 = w0()
     grad_far_other = swap(grad_far_own)
-    w1_t = send(as_block(other_1), T)
     oa, ob = flat(oa()), flat(ob())
     w0b = gather(columns(w0, chunks.turn(0), w0.shape[-1]), Y)
     w0a = gather(columns(w0, 0, chunks.turn(0)), X)
+    w1 = join(as_block(own_1), held(w1_t), T)
+    w1 = gather(w1, rest[0])
 
     def rows_of(values, which):
         return lax.dynamic_slice_in_dim(values, which * own_rows, own_rows, 0)
@@ -770,24 +772,21 @@
         )
 
     came = swap(project(1 - core, held(mixed_a)).astype(bf16))
-    residual = did(inputs_wide + (project(core, held(mixed_a)) + held(came).astype(f32)))
+    projected = did(project(core, held(mixed_a)))
+    w0b, w0a = w0b(), w0a()
+    w0b_x = send(w0b, X)
+    w0a_y = send(w0a, Y)
+    residual = did(inputs_wide + (projected + held(came).astype(f32)))
 
     scale_two = rms_scale(residual)
     unit_two = residual * scale_two
     normed_mlp_own = (unit_two * gain_two).astype(bf16)
     far_own = send(swap_halves(normed_mlp_own), T)
-    near_other = held(swap(normed_mlp_own))
-    near, near_turned = stack_rows(normed_mlp_own, near_other)
-    did(near)
+    near_other = swap(normed_mlp_own)
     grad_near, grad_near_turned = stack_rows(held(grad_branch_own), grad_branch_other)
     did(grad_near)
-    w1 = join(as_block(own_1), held(w1_t), T)
-    w1 = gather(w1, rest[0])
     grad_far, grad_far_turned = stack_rows(grad_far_own, held(grad_far_other))
     did(grad_far)
-    w0b, w0a = w0b(), w0a()
-    w0b_x = send(w0b, X)
-    w0a_y = send(w0a, Y)
     for bit in rest[1:]:
         w1 = gather(w1(), bit)
     w1 = w1()
@@ -827,6 +826,8 @@
     w1a = gather(columns(w1, 0, chunks.turn(1)), X)
     w1b = gather(columns(w1, chunks.turn(1), w1.shape[-1]), Y)
     far_other = swap(far_own)
+    near, near_turned = stack_rows(normed_mlp_own, held(near_other))
+    did(near)
     near_0 = hidden_layer(near, grad_near, weights_0)
     far, far_turned = stack_rows(far_own, held(far_other))
     did(far)
@@ -861,15 +862,25 @@
         own, other = back_rows([held(first[0]), second[0]], weights_down, cuts_down)
         return did(own), other
 
+    def pass_on(kept, came, bit):
+        came = held(came)
+        sent = add(part(kept, bit, 1), part(came, bit, 1))
+        return send(sent, bit), (part(kept, bit, 0), part(came, bit, 0))
+
+    def joined(a, a_came, b, b_came):
+        totals = [
+            sum(v.astype(f32) for v in (*terms, held(came))).astype(bf16)
+            for terms, came in ((a, a_came), (b, b_came))
+        ]
+        return row_major(jnp.concatenate(totals, axis=-1))
+
     far_1 = hidden_layer(far, grad_far, weights_1)
     far_part, far_sent = hidden_back(far_0, far_1)
     far_came = swap(far_sent)
     near_1 = hidden_layer(near, grad_near, weights_1)
     both_1 = lambda index: (near_1[index], far_1[index])
-    r0a = add(r0a, held(r0a_y))
-    r0b = add(r0b, held(r0b_x))
-    r0a_x = send(row_major(part(r0a, X, 1)), X)
-    r0b_y = send(row_major(part(r0b, Y, 1)), Y)
+    r0a_x, r0a = pass_on(r0a, r0a_y, X)
+    r0b_y, r0b = pass_on(r0b, r0b_x, Y)
     far_sum = far_part + held(far_came).astype(f32)
     grad_z = send(swap_halves(far_sum.astype(bf16)), T)
     r1a, r1a_sent = bundle_grads(both_1(1), both_1(0), 1, False)
@@ -879,11 +890,6 @@
     near_part, near_sent = hidden_back(near_0, near_1)
     near_came = swap(near_sent)
 
-    def joined(a, a_came, b, b_came):
-        return jnp.concatenate(
-            [add(part(a, X, 0), held(a_came)), add(part(b, Y, 0), held(b_came))], axis=-1
-        )
-
     r0 = joined(r0a, r0a_x, r0b, r0b_y)
     for bit in rest[:0:-1]:
         r0 = fold(r0, bit)()
@@ -896,10 +902,8 @@
     grad_att_other = swap(grad_att_own)
     far_branch, far_branch_sent = branch_back(far_0, far_1)
     far_branch_came = swap(far_branch_sent)
-    r1a = add(r1a, held(r1a_y))
-    r1b = add(r1b, held(r1b_x))
-    r1a_x = send(row_major(part(r1a, X, 1)), X)
-    r1b_y = send(row_major(part(r1b, Y, 1)), Y)
+    r1a_x, r1a = pass_on(r1a, r1a_y, X)
+    r1b_y, r1b = pass_on(r1b, r1b_x, Y)
     grad_attended = pick_first(core == 0, grad_att_own, held(grad_att_other), 0)
     grad_out_a = weight_grad(grad_attended, mixed_a)
     roa_y = send(row_major(part(grad_out_a, Y, 1)), Y)
@@ -917,14 +921,13 @@
     for bit in rest[:0:-1]:
         r1 = fold(r1, bit)()
     r1 = fold(r1, rest[0], f32)
+    out_a, out_b = part(grad_out_a, Y, 0), part(grad_out_b, X, 0)
+    roa_x, out_a = pass_on(out_a, roa_y, X)
+    rob_y, out_b = pass_on(out_b, rob_x, Y)
     d_query_b, d_key_b, d_value_b = attend_backward(
         queries_b, keys_b, values_b, matmul(held(grad_attended), ob).astype(bf16), *tables, totals_b
     )
     did(d_query_b)
-    out_a = add(part(grad_out_a, Y, 0), held(roa_y))
-    out_b = add(part(grad_out_b, X, 0), held(rob_x))
-    roa_x = send(row_major(part(out_a, X, 1)), X)
-    rob_y = send(row_major(part(out_b, Y, 1)), Y)
     low = jnp.arange(kv_width) < HEAD_DIM
     d_qkv = jnp.concatenate(
         [
@@ -937,17 +940,12 @@
     qkv_a, qkv_b = columns(grad_qkv, 0, cut), columns(grad_qkv, cut, 2 * cut)
     rqa_y = send(row_major(part(qkv_a, Y, 1)), Y)
     rqb_x = send(row_major(part(qkv_b, X, 1)), X)
-    r0_t = held(r0_t)
+    out = fold(joined(out_a, roa_x, out_b, rob_y), T)
     d_came = swap(contract_cols(rows_of(held(d_qkv), 1 - core), query_w).astype(bf16))
-    near_branch, near_branch_sent = branch_back(near_0, near_1)
-    near_branch_came = swap(near_branch_sent)
-    out = fold(joined(out_a, roa_x, out_b, rob_y), T)
     r1 = r1()
     r1_t = send(row_major(part(r1, T, 1).astype(bf16)), T)
-    qkv_a = add(part(qkv_a, Y, 0), held(rqa_y))
-    qkv_b = add(part(qkv_b, X, 0), held(rqb_x))
-    rqa_x = send(row_major(part(qkv_a, X, 1)), X)
-    rqb_y = send(row_major(part(qkv_b, Y, 1)), Y)
+    rqa_x, qkv_a = pass_on(part(qkv_a, Y, 0), rqa_y, X)
+    rqb_y, qkv_b = pass_on(part(qkv_b, X, 0), rqb_x, Y)
     grad_normed = contract_cols(rows_of(held(d_qkv), core), query_w) + held(d_came).astype(f32)
     grad_gain_one, grad_norm_one = norm_back(grad_normed, unit_one, scale_one, gain_one)
     grad_rows = did(grad_residual + grad_norm_one)
@@ -957,6 +955,9 @@
     for bit in rest[:0:-1]:
         out = fold(out, bit)()
     out = fold(out, rest[0], f32)
+    near_branch, near_branch_sent = branch_back(near_0, near_1)
+    near_branch_came = swap(near_branch_sent)
+    r1_t = held(r1_t)
     grad_gains = grad_gains + held(gains_came)
     gain_blocks = grad_gains.reshape(2, lax.axis_size("dp"), -1).transpose(1, 0, 2)
     gain_blocks = gain_blocks.reshape((2,) * nbits() + gain_blocks.shape[1:])

time: 664 us -> 632 us (0.952)
  waiting for transfers between devices: 186 us -> 163 us
  other arithmetic: 107 us -> 98.7 us
    ppermute x60, waiting for transfers between devices: 184 us -> 163 us  [exchange(): return lax.ppermute(values, 'dp', [(i, i ^ 1 << bit) for i in range(size)])]
    convert_element_type x0 -> x7, other arithmetic: none -> 13.8 us  [joined(): sum((v.astype(f32) for v in (*terms, held(came)))).astype(bf16)]
    convert_element_type x18 -> x10, other arithmetic: 27.6 us -> 14.7 us  [add(): return row_major((kept.astype(f32) + came.astype(f32)).astype(kind))]
    slice x20 -> x12, local copies, waits for them, and re-layouts: 12.4 us -> 5.29 us  [part(): lax.slice_in_dim(values, index, index + 1, axis=block_axes().index(bit))]
    unnamed x226 -> x254, local copies, waits for them, and re-layouts: 35.8 us -> 34.4 us
  transfers between devices with their start and end apart: 73 -> 73, of which waited for: 21 -> 21; matrix products, arithmetic and copies ran while one was open for 22% -> 23% of each run, Pallas kernels for 32% -> 34%
where the time goes in v3:
time: 632 us; the launch traced here: 628 us
  Pallas kernels  212 us (34%)
  waiting for transfers between devices  163 us (26%)
  other arithmetic  98.7 us (16%)
  starting transfers between devices  69.9 us (11%)
  local copies, waits for them, and re-layouts  54.3 us (9%)
  matrix products  26.7 us (4%)
    ppermute x60, waiting for transfers between devices, exchange(): return lax.ppermute(values, 'dp', [(i, i ^ 1 << bit) for i in range(size)])  163 us
    ppermute x60, starting transfers between devices, exchange(): return lax.ppermute(values, 'dp', [(i, i ^ 1 << bit) for i in range(size)])  68.5 us
    pallas_call x4, Pallas kernels, hidden_rows(): pl.pallas_call(hidden_kernel, grid=(total // height,), in_specs=[tall, ta...  52.1 us
    pallas_call x4, Pallas kernels, back_rows(): pl.pallas_call(functools.partial(back_kernel, cuts), grid=(depth // high,...  44.9 us
    pallas_call x4, Pallas kernels, weight_grads(): pl.pallas_call(functools.partial(weight_grad_kernel, inner), grid=(depth...  44.9 us
    concatenate x39, other arithmetic, join(): return jnp.concatenate([values, came], axis=block_axes().index(bit))  34.8 us
    unnamed x254, local copies, waits for them, and re-layouts  34.4 us
    pallas_call x2, Pallas kernels, attend_forward(): pl.pallas_call(functools.partial(forward_kernel, group == 1), grid=(own,)...  26.6 us
  transfers between devices with their start and end apart: 73, of which 21 were waited for; matrix products, arithmetic and copies ran while one was open for 23% of the time, Pallas kernels for 34%

profile of v3, /device:TPU:0, one launch (start us, length us, event | category | flops | bytes accessed | tf_op | source)
XLA Modules:
  0.0 627.9 jit_solution(12222839144304973881)
XLA Ops:
  1.3 4.0 collective-permute-start
  13.1 2.0 collective-permute-start.1
  21.5 2.2 collective-permute-done.2
  25.2 2.6 collective-permute-start.6
  30.4 7.4 %collective-permute-done.6 = bf16[1,1,1,1,128,1024]{5,4,3,2,1,0:T(8,128)(2,1)S(1)} collective-permute-done((bf16[1,1,1,1,128,1024]{5,4,3,2,1,0:T(8,128)(2,1)S(1)}, bf16[1,1,1,1,128,1024]{5,4,3,2,1,0:T(8,128)(2,1)S(1)}, u32[]{:S(2)}, u32[]{:S(2)}) %collective-permute-start.6) | collective-permute-done | bytes 262176 | tf_op jit(solution)/shard_map/ppermute | solution.py:39
  37.9 10.6 %collective-permute-done.8 = bf16[1,2,1,1,128,1280]{5,4,3,2,1,0:T(8,128)(2,1)S(1)} collective-permute-done((bf16[1,2,1,1,128,1280]{5,4,3,2,1,0:T(8,128)(2,1)S(1)}, bf16[1,2,1,1,128,1280]{5,4,3,2,1,0:T(8,128)(2,1)S(1)}, u32[]{:S(2)}, u32[]{:S(2)}) %collective-permute-start.8) | collective-permute-done | bytes 655392 | tf_op jit(solution)/shard_map/ppermute | solution.py:39
  52.3 12.3 %collective-permute-done.10 = bf16[2,2,1,1,128,640]{5,4,3,2,1,0:T(8,128)(2,1)S(1)} collective-permute-done((bf16[2,2,1,1,128,640]{5,4,3,2,1,0:T(8,128)(2,1)S(1)}, bf16[2,2,1,1,128,640]{5,4,3,2,1,0:T(8,128)(2,1)S(1)}, u32[]{:S(2)}, u32[]{:S(2)}) %collective-permute-start.10) | collective-permute-done | bytes 655392 | tf_op jit(solution)/shard_map/ppermute | solution.py:39
  74.4 19.4 %collective-permute-done.12 = bf16[2,2,1,2,128,640]{5,4,3,2,1,0:T(8,128)(2,1)S(1)} collective-permute-done((bf16[2,2,1,2,128,640]{5,4,3,2,1,0:T(8,128)(2,1)S(1)}, bf16[2,2,1,2,128,640]{5,4,3,2,1,0:T(8,128)(2,1)S(1)}, u32[]{:S(2)}, u32[]{:S(2)}) %collective-permute-start.12) | collective-permute-done | bytes 1310752 | tf_op jit(solution)/shard_map/ppermute | solution.py:39
  97.0 4.2 fusion.16.q_ref.k_ref.v_ref
  101.3 13.5 %attend_forward.2 = (bf16[768,512]{1,0:T(8,128)(2,1)S(1)}, bf16[768,512]{1,0:T(8,128)(2,1)S(1)}, bf16[768,128]{1,0:T(8,128)(2,1)S(1)}, bf16[768,128]{1,0:T(8,128)(2,1)S(1)}, f32[4,1,1536]{2,1,0:T(1,128)S(1)}) custom-call(f32[768,1280]{1,0:T(8,128)S(1)} %fusion.16.q_ref.k_ref.v_ref, f32[768,1280]{1,0:T(8,128)S(1)} %fusion.16.q_ref.k_ref.v_ref, ...), custom_call_target="tpu_custom_call" | custom-call | flops 1000000 | bytes 1000000 | tf_op jit(solution)/shard_map/attend_forward/pallas_call | solution.py:329
  124.5 13.1 %attend_forward.3 = (bf16[768,512]{1,0:T(8,128)(2,1)S(1)}, bf16[768,512]{1,0:T(8,128)(2,1)S(1)}, bf16[768,128]{1,0:T(8,128)(2,1)S(1)}, bf16[768,128]{1,0:T(8,128)(2,1)S(1)}, f32[4,1,1536]{2,1,0:T(1,128)S(1)}) custom-call(f32[768,1280]{1,0:T(8,128)S(1)} %copy-done.1, f32[768,1280]{1,0:T(8,128)S(1)} %copy-done.1, f32[768,1280]{1,0:T(8,128)S(1)} %copy-done.1, ...), custom_call_target="tpu_custom_call" | custom-call | flops 1000000 | bytes 1000000 | tf_op jit(solution)/shard_map/attend_forward/pallas_call | solution.py:329
  137.6 2.6 collective-permute-done.20.refs_0_
  144.2 2.2 pad_maximum_fusion.14
  153.4 9.8 %collective-permute-done.23 = bf16[2,2,1,1,128,1152]{5,4,3,2,1,0:T(8,128)(2,1)S(1)} collective-permute-done((bf16[2,2,1,1,128,1152]{5,4,3,2,1,0:T(8,128)(2,1)S(1)}, bf16[2,2,1,1,128,1152]{5,4,3,2,1,0:T(8,128)(2,1)S(1)}, u32[]{:S(2)}, u32[]{:S(2)}) %collective-permute-start.23) | collective-permute-done | bytes 1179680 | tf_op jit(solution)/shard_map/ppermute | solution.py:39
  163.2 2.1 collective-permute-done.22
  182.1 2.9 stack_rows.5
  186.7 37.5 %collective-permute-done.26 = bf16[2,1,1,1,128,1920]{5,4,3,2,1,0:T(8,128)(2,1)} collective-permute-done((bf16[2,1,1,1,128,1920]{5,4,3,2,1,0:T(8,128)(2,1)S(1)}, bf16[2,1,1,1,128,1920]{5,4,3,2,1,0:T(8,128)(2,1)}, u32[]{:S(2)}, u32[]{:S(2)}) %collective-permute-start.26) | collective-permute-done | bytes 983072 | tf_op jit(solution)/shard_map/ppermute | solution.py:39
  243.9 1.9 pad_maximum_fusion.2
  246.5 2.0 pad_maximum_fusion.3
  248.4 14.5 %hidden_rows.4 = (bf16[768,768]{1,0:T(8,128)(2,1)S(1)}, bf16[768,768]{1,0:T(8,128)(2,1)S(1)}, bf16[768,768]{1,0:T(8,128)(2,1)S(1)}) custom-call(bf16[768,2048]{1,0:T(8,128)(2,1)} %copy-done.15, bf16[768,2048]{1,0:T(8,128)(2,1)} %copy-done.13, bf16[2048,768]{1,0:T(8,128)(2,1)} %bitcast.156, bf16[2048,768]{1,0:T(8,128)(2,1)} %bitcast.160, ...), custom_call_target="tpu_custom_call" | custom-call | flops 1000000 | bytes 1000000 | tf_op jit(solution)/shard_map/hidden_rows/pallas_call | solution.py:448
  266.0 2.1 pad_maximum_fusion.7
  270.7 14.8 %hidden_rows.5 = (bf16[768,768]{1,0:T(8,128)(2,1)S(1)}, bf16[768,768]{1,0:T(8,128)(2,1)S(1)}, bf16[768,768]{1,0:T(8,128)(2,1)S(1)}) custom-call(bf16[768,2048]{1,0:T(8,128)(2,1)} %copy-done.16, bf16[768,2048]{1,0:T(8,128)(2,1)} %copy-done.14, bf16[2048,768]{1,0:T(8,128)(2,1)} %bitcast.157, bf16[2048,768]{1,0:T(8,128)(2,1)} %bitcast.161, ...), custom_call_target="tpu_custom_call" | custom-call | flops 1000000 | bytes 1000000 | tf_op jit(solution)/shard_map/hidden_rows/pallas_call | solution.py:448
  286.6 11.6 %weight_grads.4 = (bf16[8,128,1152]{2,1,0:T(8,128)(2,1)S(1)}, bf16[8,128,1152]{2,1,0:T(8,128)(2,1)}) custom-call(bf16[2048,768]{1,0:T(8,128)(2,1)} %copy-done.4, bf16[2048,768]{1,0:T(8,128)(2,1)} %copy-done.5, bf16[768,768]{1,0:T(8,128)(2,1)S(1)} %get-tuple-element.366.near_ref.refs_0_, bf16[768,768]{1,0:T(8,128)(2,1)S(1)} %get-tuple-element.344.far_ref.refs_0_, ...), custom_call_target="tpu_custom_call" | custom-call | flops 1000000 | bytes 1000000 | tf_op jit(solution)/shard_map/weight_grads/pallas_call | solution.py:489
  301.4 11.6 %weight_grads.5 = (bf16[8,128,1152]{2,1,0:T(8,128)(2,1)S(1)}, bf16[8,128,1152]{2,1,0:T(8,128)(2,1)}) custom-call(bf16[2048,768]{1,0:T(8,128)(2,1)} %copy-done.4, bf16[2048,768]{1,0:T(8,128)(2,1)} %copy-done.5, bf16[768,768]{1,0:T(8,128)(2,1)S(1)} %get-tuple-element.337.near_ref.refs_1_, bf16[768,768]{1,0:T(8,128)(2,1)S(1)} %get-tuple-element.338.far_ref.refs_1_, ...), custom_call_target="tpu_custom_call" | custom-call | flops 1000000 | bytes 1000000 | tf_op jit(solution)/shard_map/weight_grads/pallas_call | solution.py:489
  322.1 2.1 pad_maximum_fusion.11
  324.2 11.3 %hidden_rows.6 = (bf16[768,640]{1,0:T(8,128)(2,1)S(1)}, bf16[768,640]{1,0:T(8,128)(2,1)S(1)}, bf16[768,640]{1,0:T(8,128)(2,1)S(1)}) custom-call(bf16[768,2048]{1,0:T(8,128)(2,1)} %copy-done.16, bf16[768,2048]{1,0:T(8,128)(2,1)} %copy-done.14, bf16[2048,640]{1,0:T(8,128)(2,1)} %bitcast.164, bf16[2048,640]{1,0:T(8,128)(2,1)} %bitcast.168, ...), custom_call_target="tpu_custom_call" | custom-call | flops 1000000 | bytes 1000000 | tf_op jit(solution)/shard_map/hidden_rows/pallas_call | solution.py:448
  335.5 14.2 %back_rows.4 = (f32[384,2048]{1,0:T(8,128)}, bf16[384,2048]{1,0:T(8,128)(2,1)S(1)}) custom-call(bf16[768,768]{1,0:T(8,128)(2,1)S(1)} %get-tuple-element.344.far_ref.refs_0_, bf16[768,768]{1,0:T(8,128)(2,1)S(1)} %get-tuple-element.338.far_ref.refs_1_, bf16[768,640]{1,0:T(8,128)(2,1)S(1)} %get-tuple-element.345.refs_2_.far_ref, ...), custom_call_target="tpu_custom_call" | custom-call | flops 1000000 | bytes 1000000 | tf_op jit(solution)/shard_map/back_rows/pallas_call | solution.py:528
  350.9 11.5 %hidden_rows.7 = (bf16[768,640]{1,0:T(8,128)(2,1)S(1)}, bf16[768,640]{1,0:T(8,128)(2,1)S(1)}, bf16[768,640]{1,0:T(8,128)(2,1)S(1)}) custom-call(bf16[768,2048]{1,0:T(8,128)(2,1)} %copy-done.15, bf16[768,2048]{1,0:T(8,128)(2,1)} %copy-done.13, bf16[2048,640]{1,0:T(8,128)(2,1)} %bitcast.166, bf16[2048,640]{1,0:T(8,128)(2,1)} %bitcast.170, ...), custom_call_target="tpu_custom_call" | custom-call | flops 1000000 | bytes 1000000 | tf_op jit(solution)/shard_map/hidden_rows/pallas_call | solution.py:448
  362.4 2.9 add_convert_fusion.6
  366.1 2.0 collective-permute-done.37
  368.1 2.6 add_convert_fusion.5
  375.0 10.2 %weight_grads.6 = (bf16[8,128,896]{2,1,0:T(8,128)(2,1)S(1)}, bf16[8,128,896]{2,1,0:T(8,128)(2,1)}) custom-call(bf16[2048,768]{1,0:T(8,128)(2,1)} %copy-done.4, bf16[2048,768]{1,0:T(8,128)(2,1)} %copy-done.5, bf16[768,640]{1,0:T(8,128)(2,1)S(1)} %get-tuple-element.362.near_ref.refs_2_, bf16[768,640]{1,0:T(8,128)(2,1)S(1)} %copy-done.36, ...), custom_call_target="tpu_custom_call" | custom-call | flops 1000000 | bytes 1000000 | tf_op jit(solution)/shard_map/weight_grads/pallas_call | solution.py:489
  386.9 11.5 %weight_grads.7 = (bf16[8,128,1024]{2,1,0:T(8,128)(2,1)S(1)}, bf16[8,128,1024]{2,1,0:T(8,128)(2,1)}) custom-call(bf16[2048,768]{1,0:T(8,128)(2,1)} %copy-done.4, bf16[2048,768]{1,0:T(8,128)(2,1)} %copy-done.5, bf16[768,640]{1,0:T(8,128)(2,1)S(1)} %get-tuple-element.364.near_ref.refs_3_, bf16[768,640]{1,0:T(8,128)(2,1)S(1)} %copy-done.34, ...), custom_call_target="tpu_custom_call" | custom-call | flops 1000000 | bytes 1000000 | tf_op jit(solution)/shard_map/weight_grads/pallas_call | solution.py:489
  400.2 13.3 %back_rows.5 = (f32[384,2048]{1,0:T(8,128)}, bf16[384,2048]{1,0:T(8,128)(2,1)S(1)}) custom-call(bf16[768,768]{1,0:T(8,128)(2,1)S(1)} %get-tuple-element.366.near_ref.refs_0_, bf16[768,768]{1,0:T(8,128)(2,1)S(1)} %get-tuple-element.337.near_ref.refs_1_, bf16[768,640]{1,0:T(8,128)(2,1)S(1)} %get-tuple-element.362.near_ref.refs_2_, ...), custom_call_target="tpu_custom_call" | custom-call | flops 1000000 | bytes 1000000 | tf_op jit(solution)/shard_map/back_rows/pallas_call | solution.py:528
  413.6 2.2 add_convert_fusion.4
  415.9 2.5 add_convert_fusion.3
  421.3 2.7 multiply_reduce_fusion
  424.0 4.3 fusion.52
  428.7 3.5 collective-permute-start.48
  434.7 8.7 %back_rows.6 = (f32[384,2048]{1,0:T(8,128)}, bf16[384,2048]{1,0:T(8,128)(2,1)S(1)}) custom-call(bf16[768,768]{1,0:T(8,128)(2,1)S(1)} %copy-done.26, bf16[768,640]{1,0:T(8,128)(2,1)S(1)} %copy-done.32, bf16[2048,384]{1,0:T(8,128)(2,1)} %bitcast.133, bf16[2048,384]{1,0:T(8,128)(2,1)} %bitcast.174, bf16[2048,256]{1,0:T(8,128)(2,1)S(1)} %bitcast.137, ...), custom_call_target="tpu_custom_call" | custom-call | flops 1000000 | bytes 1000000 | tf_op jit(solution)/shard_map/back_rows/pallas_call | solution.py:528
  443.5 2.5 add_convert_fusion.10
  449.6 2.1 broadcast_select_fusion.2
  465.2 13.2 %attend_backward.2 = (bf16[768,512]{1,0:T(8,128)(2,1)S(1)}, bf16[768,128]{1,0:T(8,128)(2,1)S(1)}, bf16[768,128]{1,0:T(8,128)(2,1)S(1)}) custom-call(bf16[768,512]{1,0:T(8,128)(2,1)S(1)} %copy-done.54, bf16[768,128]{1,0:T(8,128)(2,1)S(1)} %copy-done.66, bf16[768,128]{1,0:T(8,128)(2,1)S(1)} %copy-done.68, ...), custom_call_target="tpu_custom_call" | custom-call | flops 1000000 | bytes 1000000 | tf_op jit(solution)/shard_map/attend_backward/pallas_call | solution.py:360
  478.4 5.7 collective-permute-done.48
  487.9 2.2 add_convert_fusion.7
  491.1 3.3 collective-permute-start.57
  497.4 2.0 add_convert_fusion.19
  503.0 13.0 %attend_backward.3 = (bf16[768,512]{1,0:T(8,128)(2,1)S(1)}, bf16[768,128]{1,0:T(8,128)(2,1)S(1)}, bf16[768,128]{1,0:T(8,128)(2,1)S(1)}) custom-call(bf16[768,512]{1,0:T(8,128)(2,1)S(1)} %copy-done.52, bf16[768,128]{1,0:T(8,128)(2,1)S(1)} %copy-done.62, bf16[768,128]{1,0:T(8,128)(2,1)S(1)} %copy-done.64, ...), custom_call_target="tpu_custom_call" | custom-call | flops 1000000 | bytes 1000000 | tf_op jit(solution)/shard_map/attend_backward/pallas_call | solution.py:360
  517.9 4.9 convolution_convert_fusion
  531.4 3.4 convolution_convert_fusion.3
  534.9 5.3 collective-permute-done.57
  540.2 3.9 collective-permute-start.54
  545.1 8.8 %collective-permute-done.56 = bf16[2,2,1,2,128,640]{5,4,3,2,1,0:T(8,128)(2,1)S(1)} collective-permute-done((bf16[2,2,1,2,128,640]{5,4,3,2,1,0:T(8,128)(2,1)}, bf16[2,2,1,2,128,640]{5,4,3,2,1,0:T(8,128)(2,1)S(1)}, u32[]{:S(2)}, u32[]{:S(2)}) %collective-permute-start.56) | collective-permute-done | bytes 1310752 | tf_op jit(solution)/shard_map/ppermute | solution.py:39
  558.3 2.6 fusion.6
  563.8 8.7 %back_rows.7 = (f32[384,2048]{1,0:T(8,128)}, bf16[384,2048]{1,0:T(8,128)(2,1)S(1)}) custom-call(bf16[768,768]{1,0:T(8,128)(2,1)S(1)} %copy-done.24, bf16[768,640]{1,0:T(8,128)(2,1)S(1)} %copy-done.30, bf16[2048,384]{1,0:T(8,128)(2,1)} %bitcast.134, bf16[2048,384]{1,0:T(8,128)(2,1)} %bitcast.175, bf16[2048,256]{1,0:T(8,128)(2,1)S(1)} %bitcast.138, ...), custom_call_target="tpu_custom_call" | custom-call | flops 1000000 | bytes 1000000 | tf_op jit(solution)/shard_map/back_rows/pallas_call | solution.py:528
  574.1 3.0 reorder.4
  578.2 2.0 add_convert_fusion.12
  583.2 2.7 select_convert_fusion.refs_0_
  585.8 2.5 reorder.5
  588.3 6.3 collective-permute-done.67
  594.6 2.5 unpack_columns.1
  597.1 10.9 %collective-permute-done.69 = bf16[1,2,1,1,128,1280]{5,4,3,2,1,0:T(8,128)(2,1)S(1)} collective-permute-done((bf16[1,2,1,1,128,1280]{5,4,3,2,1,0:T(8,128)(2,1)S(1)}, bf16[1,2,1,1,128,1280]{5,4,3,2,1,0:T(8,128)(2,1)S(1)}, u32[]{:S(2)}, u32[]{:S(2)}) %collective-permute-start.69) | collective-permute-done | bytes 655392 | tf_op jit(solution)/shard_map/ppermute | solution.py:39
  608.3 3.0 collective-permute-start.70
  612.4 13.0 %collective-permute-done.71 = bf16[1,1,1,1,128,1280]{5,4,3,2,1,0:T(8,128)(2,1)S(1)} collective-permute-done((bf16[1,1,1,1,128,1280]{5,4,3,2,1,0:T(8,128)(2,1)S(1)}, bf16[1,1,1,1,128,1280]{5,4,3,2,1,0:T(8,128)(2,1)S(1)}, u32[]{:S(2)}, u32[]{:S(2)}) %collective-permute-start.71) | collective-permute-done | bytes 327712 | tf_op jit(solution)/shard_map/ppermute | solution.py:39
  (530 shorter events, 184.8 us)
Async XLA Ops:
  7.1 20.7 %collective-permute-start.4 = (bf16[1,1,1,1,128,1280]{5,4,3,2,1,0:T(8,128)(2,1)}, bf16[1,1,1,1,128,1280]{5,4,3,2,1,0:T(8,128)(2,1)}, u32[]{:S(2)}, u32[]{:S(2)}) collective-permute-start(bf16[1,1,1,1,128,1280]{5,4,3,2,1,0:T(8,128)(2,1)} %maximum_bitcast_fusion), channel_id=1, source_target_pairs={{0,16},{2,18},{4,20},{6,22},{8,24},{10,26},{12,28},{14,30},{16,0},... | collective-permute-start | bytes 983048 | tf_op jit(solution)/shard_map/ppermute | solution.py:39
  25.2 12.6 %collective-permute-start.6 = (bf16[1,1,1,1,128,1024]{5,4,3,2,1,0:T(8,128)(2,1)S(1)}, bf16[1,1,1,1,128,1024]{5,4,3,2,1,0:T(8,128)(2,1)S(1)}, u32[]{:S(2)}, u32[]{:S(2)}) collective-permute-start(bf16[1,1,1,1,128,1024]{5,4,3,2,1,0:T(8,128)(2,1)S(1)} %bitcast.193), channel_id=1, source_target_pairs={{0,16},{2,18},{4,20},{6,22},{8,24},{10,26},{12,28},{14,30},{16,0},... | collective-permute-start | bytes 786440 | tf_op jit(solution)/shard_map/ppermute | solution.py:39
  28.9 19.5 %collective-permute-start.8 = (bf16[1,2,1,1,128,1280]{5,4,3,2,1,0:T(8,128)(2,1)S(1)}, bf16[1,2,1,1,128,1280]{5,4,3,2,1,0:T(8,128)(2,1)S(1)}, u32[]{:S(2)}, u32[]{:S(2)}) collective-permute-start(bf16[1,2,1,1,128,1280]{5,4,3,2,1,0:T(8,128)(2,1)S(1)} %pad_maximum_fusion.41), channel_id=1, source_target_pairs={{0,8},{2,10},{4,12},{6,14},{8,0},{10,2},{12,4},{14,6},{16,24},{18,... | collective-permute-start | bytes 1966088 | tf_op jit(solution)/shard_map/ppermute | solution.py:39
  30.3 40.6 %collective-permute-start.5 = (bf16[384,2048]{1,0:T(8,128)(2,1)S(1)}, bf16[384,2048]{1,0:T(8,128)(2,1)S(1)}, u32[]{:S(2)}, u32[]{:S(2)}) collective-permute-start(bf16[384,2048]{1,0:T(8,128)(2,1)S(1)} %fusion.4), channel_id=1, source_target_pairs={{0,1},{1,0},{2,3},{3,2},{4,5},{5,4},{6,7},{7,6},{8,9},{9,8},{10,11... | collective-permute-start | bytes 4718600 | tf_op jit(solution)/shard_map/ppermute | solution.py:43
  49.8 14.8 %collective-permute-start.10 = (bf16[2,2,1,1,128,640]{5,4,3,2,1,0:T(8,128)(2,1)S(1)}, bf16[2,2,1,1,128,640]{5,4,3,2,1,0:T(8,128)(2,1)S(1)}, u32[]{:S(2)}, u32[]{:S(2)}) collective-permute-start(bf16[2,2,1,1,128,640]{5,4,3,2,1,0:T(8,128)(2,1)S(1)} %get-tuple-element.258), channel_id=1, source_target_pairs={{0,2},{2,0},{4,6},{6,4},{8,10},{10,8},{12,14},{14,12},{16,18},{18,... | collective-permute-start | bytes 1966088 | tf_op jit(solution)/shard_map/ppermute | solution.py:39
  51.3 15.6 %collective-permute-start.9 = (bf16[2,2,1,1,128,640]{5,4,3,2,1,0:T(8,128)(2,1)S(1)}, bf16[2,2,1,1,128,640]{5,4,3,2,1,0:T(8,128)(2,1)S(1)}, u32[]{:S(2)}, u32[]{:S(2)}) collective-permute-start(bf16[2,2,1,1,128,640]{5,4,3,2,1,0:T(8,128)(2,1)S(1)} %get-tuple-element.259), channel_id=1, source_target_pairs={{0,4},{2,6},{4,0},{6,2},{8,12},{10,14},{12,8},{14,10},{16,20},{18,... | collective-permute-start | bytes 1966088 | tf_op jit(solution)/shard_map/ppermute | solution.py:39
  52.0 16.4 %collective-permute-start.13 = (bf16[1,1,1,1,128,2304]{5,4,3,2,1,0:T(8,128)(2,1)S(1)}, bf16[1,1,1,1,128,2304]{5,4,3,2,1,0:T(8,128)(2,1)S(1)}, u32[]{:S(2)}, u32[]{:S(2)}) collective-permute-start(bf16[1,1,1,1,128,2304]{5,4,3,2,1,0:T(8,128)(2,1)S(1)} %bitcast.154), channel_id=1, source_target_pairs={{0,8},{2,10},{4,12},{6,14},{8,0},{10,2},{12,4},{14,6},{16,24},{18,... | collective-permute-start | bytes 1769480 | tf_op jit(solution)/shard_map/ppermute | solution.py:39
  64.7 29.1 %collective-permute-start.12 = (bf16[2,2,1,2,128,640]{5,4,3,2,1,0:T(8,128)(2,1)S(1)}, bf16[2,2,1,2,128,640]{5,4,3,2,1,0:T(8,128)(2,1)S(1)}, u32[]{:S(2)}, u32[]{:S(2)}) collective-permute-start(bf16[2,2,1,2,128,640]{5,4,3,2,1,0:T(8,128)(2,1)S(1)} %pad_maximum_fusion.29), channel_id=1, source_target_pairs={{0,4},{2,6},{4,0},{6,2},{8,12},{10,14},{12,8},{14,10},{16,20},{18,... | collective-permute-start | bytes 3932168 | tf_op jit(solution)/shard_map/ppermute | solution.py:39
  67.1 26.7 %collective-permute-start.11 = (bf16[2,2,2,1,128,640]{5,4,3,2,1,0:T(8,128)(2,1)S(1)}, bf16[2,2,2,1,128,640]{5,4,3,2,1,0:T(8,128)(2,1)S(1)}, u32[]{:S(2)}, u32[]{:S(2)}) collective-permute-start(bf16[2,2,2,1,128,640]{5,4,3,2,1,0:T(8,128)(2,1)S(1)} %pad_maximum_fusion.30), channel_id=1, source_target_pairs={{0,2},{2,0},{4,6},{6,4},{8,10},{10,8},{12,14},{14,12},{16,18},{18,... | collective-permute-start | bytes 3932168 | tf_op jit(solution)/shard_map/ppermute | solution.py:39
  68.4 26.1 %collective-permute-start.7 = (bf16[1,2,1,1,128,1024]{5,4,3,2,1,0:T(8,128)(2,1)S(1)}, bf16[1,2,1,1,128,1024]{5,4,3,2,1,0:T(8,128)(2,1)S(1)}, u32[]{:S(2)}, u32[]{:S(2)}) collective-permute-start(bf16[1,2,1,1,128,1024]{5,4,3,2,1,0:T(8,128)(2,1)S(1)} %pad_maximum_fusion.43), channel_id=1, source_target_pairs={{0,8},{2,10},{4,12},{6,14},{8,0},{10,2},{12,4},{14,6},{16,24},{18,... | collective-permute-start | bytes 1572872 | tf_op jit(solution)/shard_map/ppermute | solution.py:39
  69.7 50.9 %collective-permute-start.14 = (bf16[2,1,1,1,128,2304]{5,4,3,2,1,0:T(8,128)(2,1)}, bf16[2,1,1,1,128,2304]{5,4,3,2,1,0:T(8,128)(2,1)}, u32[]{:S(2)}, u32[]{:S(2)}) collective-permute-start(bf16[2,1,1,1,128,2304]{5,4,3,2,1,0:T(8,128)(2,1)} %pad_maximum_fusion.32), channel_id=1, source_target_pairs={{0,16},{2,18},{4,20},{6,22},{8,24},{10,26},{12,28},{14,30},{16,0},... | collective-permute-start | bytes 3538952 | tf_op jit(solution)/shard_map/ppermute | solution.py:39
  70.9 69.3 %collective-permute-start.20 = (bf16[384,2048]{1,0:T(8,128)(2,1)}, bf16[384,2048]{1,0:T(8,128)(2,1)}, u32[]{:S(2)}, u32[]{:S(2)}) collective-permute-start(bf16[384,2048]{1,0:T(8,128)(2,1)} %pad_maximum_fusion.18), channel_id=1, source_target_pairs={{0,8},{2,10},{4,12},{6,14},{8,0},{10,2},{12,4},{14,6},{16,24},{18,... | collective-permute-start | bytes 4718600 | tf_op jit(solution)/shard_map/ppermute | solution.py:39
  94.8 20.1 %collective-permute-start.16 = (bf16[2,2,1,1,128,512]{5,4,3,2,1,0:T(8,128)(2,1)S(1)}, bf16[2,2,1,1,128,512]{5,4,3,2,1,0:T(8,128)(2,1)S(1)}, u32[]{:S(2)}, u32[]{:S(2)}) collective-permute-start(bf16[2,2,1,1,128,512]{5,4,3,2,1,0:T(8,128)(2,1)S(1)} %get-tuple-element.275), channel_id=1, source_target_pairs={{0,2},{2,0},{4,6},{6,4},{8,10},{10,8},{12,14},{14,12},{16,18},{18,... | collective-permute-start | bytes 1572872 | tf_op jit(solution)/shard_map/ppermute | solution.py:39
  95.5 21.1 %collective-permute-start.15 = (bf16[2,2,1,1,128,512]{5,4,3,2,1,0:T(8,128)(2,1)S(1)}, bf16[2,2,1,1,128,512]{5,4,3,2,1,0:T(8,128)(2,1)S(1)}, u32[]{:S(2)}, u32[]{:S(2)}) collective-permute-start(bf16[2,2,1,1,128,512]{5,4,3,2,1,0:T(8,128)(2,1)S(1)} %get-tuple-element.533), channel_id=1, source_target_pairs={{0,4},{2,6},{4,0},{6,2},{8,12},{10,14},{12,8},{14,10},{16,20},{18,... | collective-permute-start | bytes 1572872 | tf_op jit(solution)/shard_map/ppermute | solution.py:39
  116.1 24.1 %collective-permute-start.19 = (bf16[2,2,1,2,128,512]{5,4,3,2,1,0:T(8,128)(2,1)}, bf16[2,2,1,2,128,512]{5,4,3,2,1,0:T(8,128)(2,1)}, u32[]{:S(2)}, u32[]{:S(2)}) collective-permute-start(bf16[2,2,1,2,128,512]{5,4,3,2,1,0:T(8,128)(2,1)} %pad_maximum_fusion.34), channel_id=1, source_target_pairs={{0,4},{2,6},{4,0},{6,2},{8,12},{10,14},{12,8},{14,10},{16,20},{18,... | collective-permute-start | bytes 3145736 | tf_op jit(solution)/shard_map/ppermute | solution.py:39
  117.8 22.4 %collective-permute-start.18 = (bf16[2,2,2,1,128,512]{5,4,3,2,1,0:T(8,128)(2,1)}, bf16[2,2,2,1,128,512]{5,4,3,2,1,0:T(8,128)(2,1)}, u32[]{:S(2)}, u32[]{:S(2)}) collective-permute-start(bf16[2,2,2,1,128,512]{5,4,3,2,1,0:T(8,128)(2,1)} %pad_maximum_fusion.35), channel_id=1, source_target_pairs={{0,2},{2,0},{4,6},{6,4},{8,10},{10,8},{12,14},{14,12},{16,18},{18,... | collective-permute-start | bytes 3145736 | tf_op jit(solution)/shard_map/ppermute | solution.py:39
  120.5 27.6 %collective-permute-start.17 = (bf16[1,1,1,1,128,1920]{5,4,3,2,1,0:T(8,128)(2,1)}, bf16[1,1,1,1,128,1920]{5,4,3,2,1,0:T(8,128)(2,1)S(1)}, u32[]{:S(2)}, u32[]{:S(2)}) collective-permute-start(bf16[1,1,1,1,128,1920]{5,4,3,2,1,0:T(8,128)(2,1)} %bitcast.155), channel_id=1, source_target_pairs={{0,8},{2,10},{4,12},{6,14},{8,0},{10,2},{12,4},{14,6},{16,24},{18,... | collective-permute-start | bytes 1474568 | tf_op jit(solution)/shard_map/ppermute | solution.py:39
  140.2 23.0 %collective-permute-start.23 = (bf16[2,2,1,1,128,1152]{5,4,3,2,1,0:T(8,128)(2,1)S(1)}, bf16[2,2,1,1,128,1152]{5,4,3,2,1,0:T(8,128)(2,1)S(1)}, u32[]{:S(2)}, u32[]{:S(2)}) collective-permute-start(bf16[2,2,1,1,128,1152]{5,4,3,2,1,0:T(8,128)(2,1)S(1)} %get-tuple-element.292), channel_id=1, source_target_pairs={{0,4},{2,6},{4,0},{6,2},{8,12},{10,14},{12,8},{14,10},{16,20},{18,... | collective-permute-start | bytes 3538952 | tf_op jit(solution)/shard_map/ppermute | solution.py:39
  142.1 23.2 %collective-permute-start.22 = (bf16[2,2,1,1,128,1152]{5,4,3,2,1,0:T(8,128)(2,1)S(1)}, bf16[2,2,1,1,128,1152]{5,4,3,2,1,0:T(8,128)(2,1)S(1)}, u32[]{:S(2)}, u32[]{:S(2)}) collective-permute-start(bf16[2,2,1,1,128,1152]{5,4,3,2,1,0:T(8,128)(2,1)S(1)} %get-tuple-element.293), channel_id=1, source_target_pairs={{0,2},{2,0},{4,6},{6,4},{8,10},{10,8},{12,14},{14,12},{16,18},{18,... | collective-permute-start | bytes 3538952 | tf_op jit(solution)/shard_map/ppermute | solution.py:39
  150.4 21.3 %collective-permute-start.21 = (bf16[384,2048]{1,0:T(8,128)(2,1)S(1)}, bf16[384,2048]{1,0:T(8,128)(2,1)S(1)}, u32[]{:S(2)}, u32[]{:S(2)}) collective-permute-start(bf16[384,2048]{1,0:T(8,128)(2,1)S(1)} %add_convert_fusion.2), channel_id=1, source_target_pairs={{0,1},{1,0},{2,3},{3,2},{4,5},{5,4},{6,7},{7,6},{8,9},{9,8},{10,11... | collective-permute-start | bytes 4718600 | tf_op jit(solution)/shard_map/ppermute | solution.py:43
  150.7 26.5 %collective-permute-start.28 = (bf16[384,2048]{1,0:T(8,128)(2,1)S(1)}, bf16[384,2048]{1,0:T(8,128)(2,1)S(1)}, u32[]{:S(2)}, u32[]{:S(2)}) collective-permute-start(bf16[384,2048]{1,0:T(8,128)(2,1)S(1)} %copy-done.12), channel_id=1, source_target_pairs={{0,1},{1,0},{2,3},{3,2},{4,5},{5,4},{6,7},{7,6},{8,9},{9,8},{10,11... | collective-permute-start | bytes 4718600 | tf_op jit(solution)/shard_map/ppermute | solution.py:43
  151.0 26.3 %collective-permute-start.27 = (bf16[384,2048]{1,0:T(8,128)(2,1)}, bf16[384,2048]{1,0:T(8,128)(2,1)S(1)}, u32[]{:S(2)}, u32[]{:S(2)}) collective-permute-start(bf16[384,2048]{1,0:T(8,128)(2,1)} %collective-permute-done.20.refs_0_), channel_id=1, source_target_pairs={{0,1},{1,0},{2,3},{3,2},{4,5},{5,4},{6,7},{7,6},{8,9},{9,8},{10,11... | collective-permute-start | bytes 4718600 | tf_op jit(solution)/shard_map/ppermute | solution.py:43
  167.2 59.9 %collective-permute-start.29 = (bf16[2,2,2,1,128,1152]{5,4,3,2,1,0:T(8,128)(2,1)}, bf16[2,2,2,1,128,1152]{5,4,3,2,1,0:T(8,128)(2,1)}, u32[]{:S(2)}, u32[]{:S(2)}) collective-permute-start(bf16[2,2,2,1,128,1152]{5,4,3,2,1,0:T(8,128)(2,1)} %pad_maximum_fusion.6), channel_id=1, source_target_pairs={{0,2},{2,0},{4,6},{6,4},{8,10},{10,8},{12,14},{14,12},{16,18},{18,... | collective-permute-start | bytes 7077896 | tf_op jit(solution)/shard_map/ppermute | solution.py:39
  170.3 56.7 %collective-permute-start.30 = (bf16[2,2,1,2,128,1152]{5,4,3,2,1,0:T(8,128)(2,1)}, bf16[2,2,1,2,128,1152]{5,4,3,2,1,0:T(8,128)(2,1)}, u32[]{:S(2)}, u32[]{:S(2)}) collective-permute-start(bf16[2,2,1,2,128,1152]{5,4,3,2,1,0:T(8,128)(2,1)} %pad_maximum_fusion.5), channel_id=1, source_target_pairs={{0,4},{2,6},{4,0},{6,2},{8,12},{10,14},{12,8},{14,10},{16,20},{18,... | collective-permute-start | bytes 7077896 | tf_op jit(solution)/shard_map/ppermute | solution.py:39
  175.8 51.2 %collective-permute-start.25 = (bf16[384,2048]{1,0:T(8,128)(2,1)}, bf16[384,2048]{1,0:T(8,128)(2,1)S(1)}, u32[]{:S(2)}, u32[]{:S(2)}) collective-permute-start(bf16[384,2048]{1,0:T(8,128)(2,1)} %pad_maximum_fusion.19), channel_id=1, source_target_pairs={{0,8},{2,10},{4,12},{6,14},{8,0},{10,2},{12,4},{14,6},{16,24},{18,... | collective-permute-start | bytes 4718600 | tf_op jit(solution)/shard_map/ppermute | solution.py:39
  177.2 47.0 %collective-permute-start.26 = (bf16[2,1,1,1,128,1920]{5,4,3,2,1,0:T(8,128)(2,1)S(1)}, bf16[2,1,1,1,128,1920]{5,4,3,2,1,0:T(8,128)(2,1)}, u32[]{:S(2)}, u32[]{:S(2)}) collective-permute-start(bf16[2,1,1,1,128,1920]{5,4,3,2,1,0:T(8,128)(2,1)S(1)} %pad_maximum_fusion.38), channel_id=1, source_target_pairs={{0,16},{2,18},{4,20},{6,22},{8,24},{10,26},{12,28},{14,30},{16,0},... | collective-permute-start | bytes 2949128 | tf_op jit(solution)/shard_map/ppermute | solution.py:39
  177.2 61.0 %collective-permute-start.24 = (bf16[384,2048]{1,0:T(8,128)(2,1)S(1)}, bf16[384,2048]{1,0:T(8,128)(2,1)S(1)}, u32[]{:S(2)}, u32[]{:S(2)}) collective-permute-start(bf16[384,2048]{1,0:T(8,128)(2,1)S(1)} %multiply_convert_fusion.refs_0_), channel_id=1, source_target_pairs={{0,1},{1,0},{2,3},{3,2},{4,5},{5,4},{6,7},{7,6},{8,9},{9,8},{10,11... | collective-permute-start | bytes 4718600 | tf_op jit(solution)/shard_map/ppermute | solution.py:43
  227.0 35.9 %collective-permute-start.31 = (bf16[384,2048]{1,0:T(8,128)(2,1)S(1)}, bf16[384,2048]{1,0:T(8,128)(2,1)S(1)}, u32[]{:S(2)}, u32[]{:S(2)}) collective-permute-start(bf16[384,2048]{1,0:T(8,128)(2,1)S(1)} %collective-permute-done.25.refs_0_), channel_id=1, source_target_pairs={{0,1},{1,0},{2,3},{3,2},{4,5},{5,4},{6,7},{7,6},{8,9},{9,8},{10,11... | collective-permute-start | bytes 4718600 | tf_op jit(solution)/shard_map/ppermute | solution.py:43
  229.4 35.0 %collective-permute-start.33 = (bf16[2,2,1,1,128,896]{5,4,3,2,1,0:T(8,128)(2,1)S(1)}, bf16[2,2,1,1,128,896]{5,4,3,2,1,0:T(8,128)(2,1)S(1)}, u32[]{:S(2)}, u32[]{:S(2)}) collective-permute-start(bf16[2,2,1,1,128,896]{5,4,3,2,1,0:T(8,128)(2,1)S(1)} %pad_maximum_fusion.39), channel_id=1, source_target_pairs={{0,2},{2,0},{4,6},{6,4},{8,10},{10,8},{12,14},{14,12},{16,18},{18,... | collective-permute-start | bytes 2752520 | tf_op jit(solution)/shard_map/ppermute | solution.py:39
  230.9 35.1 %collective-permute-start.32 = (bf16[2,2,1,1,128,1024]{5,4,3,2,1,0:T(8,128)(2,1)S(1)}, bf16[2,2,1,1,128,1024]{5,4,3,2,1,0:T(8,128)(2,1)S(1)}, u32[]{:S(2)}, u32[]{:S(2)}) collective-permute-start(bf16[2,2,1,1,128,1024]{5,4,3,2,1,0:T(8,128)(2,1)S(1)} %slice.464), channel_id=1, source_target_pairs={{0,4},{2,6},{4,0},{6,2},{8,12},{10,14},{12,8},{14,10},{16,20},{18,... | collective-permute-start | bytes 3145736 | tf_op jit(solution)/shard_map/ppermute | solution.py:39
  268.5 46.2 %collective-permute-start.35 = (bf16[2,2,1,2,128,896]{5,4,3,2,1,0:T(8,128)(2,1)}, bf16[2,2,1,2,128,896]{5,4,3,2,1,0:T(8,128)(2,1)}, u32[]{:S(2)}, u32[]{:S(2)}) collective-permute-start(bf16[2,2,1,2,128,896]{5,4,3,2,1,0:T(8,128)(2,1)} %pad_maximum_fusion.13), channel_id=1, source_target_pairs={{0,4},{2,6},{4,0},{6,2},{8,12},{10,14},{12,8},{14,10},{16,20},{18,... | collective-permute-start | bytes 5505032 | tf_op jit(solution)/shard_map/ppermute | solution.py:39
  270.1 49.1 %collective-permute-start.34 = (bf16[2,2,2,1,128,1024]{5,4,3,2,1,0:T(8,128)(2,1)}, bf16[2,2,2,1,128,1024]{5,4,3,2,1,0:T(8,128)(2,1)}, u32[]{:S(2)}, u32[]{:S(2)}) collective-permute-start(bf16[2,2,2,1,128,1024]{5,4,3,2,1,0:T(8,128)(2,1)} %pad_maximum_fusion.7), channel_id=1, source_target_pairs={{0,2},{2,0},{4,6},{6,4},{8,10},{10,8},{12,14},{14,12},{16,18},{18,... | collective-permute-start | bytes 6291464 | tf_op jit(solution)/shard_map/ppermute | solution.py:39
  299.6 62.8 %collective-permute-start.38 = (bf16[2,2,1,2,128,1152]{5,4,3,2,1,0:T(8,128)(2,1)}, bf16[2,2,1,2,128,1152]{5,4,3,2,1,0:T(8,128)(2,1)}, u32[]{:S(2)}, u32[]{:S(2)}) collective-permute-start(bf16[2,2,1,2,128,1152]{5,4,3,2,1,0:T(8,128)(2,1)} %bitcast.216), channel_id=1, source_target_pairs={{0,4},{2,6},{4,0},{6,2},{8,12},{10,14},{12,8},{14,10},{16,20},{18,... | collective-permute-start | bytes 7077896 | tf_op jit(solution)/shard_map/ppermute | solution.py:39
  313.0 55.1 %collective-permute-start.37 = (bf16[2,2,2,1,128,1152]{5,4,3,2,1,0:T(8,128)(2,1)}, bf16[2,2,2,1,128,1152]{5,4,3,2,1,0:T(8,128)(2,1)}, u32[]{:S(2)}, u32[]{:S(2)}) collective-permute-start(bf16[2,2,2,1,128,1152]{5,4,3,2,1,0:T(8,128)(2,1)} %bitcast.217), channel_id=1, source_target_pairs={{0,2},{2,0},{4,6},{6,4},{8,10},{10,8},{12,14},{14,12},{16,18},{18,... | collective-permute-start | bytes 7077896 | tf_op jit(solution)/shard_map/ppermute | solution.py:39
  350.9 20.6 %collective-permute-start.36 = (bf16[384,2048]{1,0:T(8,128)(2,1)}, bf16[384,2048]{1,0:T(8,128)(2,1)S(1)}, u32[]{:S(2)}, u32[]{:S(2)}) collective-permute-start(bf16[384,2048]{1,0:T(8,128)(2,1)} %copy-done.69), channel_id=1, source_target_pairs={{0,1},{1,0},{2,3},{3,2},{4,5},{5,4},{6,7},{7,6},{8,9},{9,8},{10,11... | collective-permute-start | bytes 4718600 | tf_op jit(solution)/shard_map/ppermute | solution.py:43
  365.3 48.2 %collective-permute-start.40 = (bf16[2,2,1,1,128,1152]{5,4,3,2,1,0:T(8,128)(2,1)}, bf16[2,2,1,1,128,1152]{5,4,3,2,1,0:T(8,128)(2,1)}, u32[]{:S(2)}, u32[]{:S(2)}) collective-permute-start(bf16[2,2,1,1,128,1152]{5,4,3,2,1,0:T(8,128)(2,1)} %add_convert_fusion.6), channel_id=1, source_target_pairs={{0,2},{2,0},{4,6},{6,4},{8,10},{10,8},{12,14},{14,12},{16,18},{18,... | collective-permute-start | bytes 3538952 | tf_op jit(solution)/shard_map/ppermute | solution.py:39
  370.8 42.9 %collective-permute-start.41 = (bf16[2,2,1,1,128,1152]{5,4,3,2,1,0:T(8,128)(2,1)}, bf16[2,2,1,1,128,1152]{5,4,3,2,1,0:T(8,128)(2,1)}, u32[]{:S(2)}, u32[]{:S(2)}) collective-permute-start(bf16[2,2,1,1,128,1152]{5,4,3,2,1,0:T(8,128)(2,1)} %add_convert_fusion.5), channel_id=1, source_target_pairs={{0,4},{2,6},{4,0},{6,2},{8,12},{10,14},{12,8},{14,10},{16,20},{18,... | collective-permute-start | bytes 3538952 | tf_op jit(solution)/shard_map/ppermute | solution.py:39
  374.7 45.2 %collective-permute-start.42 = (bf16[384,2048]{1,0:T(8,128)(2,1)}, bf16[384,2048]{1,0:T(8,128)(2,1)}, u32[]{:S(2)}, u32[]{:S(2)}) collective-permute-start(bf16[384,2048]{1,0:T(8,128)(2,1)} %pad_maximum_fusion.23), channel_id=1, source_target_pairs={{0,8},{2,10},{4,12},{6,14},{8,0},{10,2},{12,4},{14,6},{16,24},{18,... | collective-permute-start | bytes 4718600 | tf_op jit(solution)/shard_map/ppermute | solution.py:39
  386.5 57.0 %collective-permute-start.45 = (bf16[2,2,1,2,128,896]{5,4,3,2,1,0:T(8,128)(2,1)}, bf16[2,2,1,2,128,896]{5,4,3,2,1,0:T(8,128)(2,1)}, u32[]{:S(2)}, u32[]{:S(2)}) collective-permute-start(bf16[2,2,1,2,128,896]{5,4,3,2,1,0:T(8,128)(2,1)} %bitcast.219), channel_id=1, source_target_pairs={{0,4},{2,6},{4,0},{6,2},{8,12},{10,14},{12,8},{14,10},{16,20},{18,... | collective-permute-start | bytes 5505032 | tf_op jit(solution)/shard_map/ppermute | solution.py:39
  398.4 48.3 %collective-permute-start.44 = (bf16[2,2,2,1,128,1024]{5,4,3,2,1,0:T(8,128)(2,1)}, bf16[2,2,2,1,128,1024]{5,4,3,2,1,0:T(8,128)(2,1)}, u32[]{:S(2)}, u32[]{:S(2)}) collective-permute-start(bf16[2,2,2,1,128,1024]{5,4,3,2,1,0:T(8,128)(2,1)} %bitcast.218), channel_id=1, source_target_pairs={{0,2},{2,0},{4,6},{6,4},{8,10},{10,8},{12,14},{14,12},{16,18},{18,... | collective-permute-start | bytes 6291464 | tf_op jit(solution)/shard_map/ppermute | solution.py:39
  428.3 21.3 %collective-permute-start.43 = (bf16[384,2048]{1,0:T(8,128)(2,1)}, bf16[384,2048]{1,0:T(8,128)(2,1)}, u32[]{:S(2)}, u32[]{:S(2)}) collective-permute-start(bf16[384,2048]{1,0:T(8,128)(2,1)} %get-tuple-element.375), channel_id=1, source_target_pairs={{0,1},{1,0},{2,3},{3,2},{4,5},{5,4},{6,7},{7,6},{8,9},{9,8},{10,11... | collective-permute-start | bytes 4718600 | tf_op jit(solution)/shard_map/ppermute | solution.py:43
  428.7 55.4 %collective-permute-start.48 = (bf16[2,1,1,1,128,2304]{5,4,3,2,1,0:T(8,128)(2,1)}, bf16[2,1,1,1,128,2304]{5,4,3,2,1,0:T(8,128)(2,1)S(1)}, u32[]{:S(2)}, u32[]{:S(2)}) collective-permute-start(bf16[2,1,1,1,128,2304]{5,4,3,2,1,0:T(8,128)(2,1)} %fusion.19), channel_id=1, source_target_pairs={{0,16},{2,18},{4,20},{6,22},{8,24},{10,26},{12,28},{14,30},{16,0},... | collective-permute-start | bytes 3538952 | tf_op jit(solution)/shard_map/ppermute | solution.py:39
  443.5 15.0 %collective-permute-start.49 = (bf16[384,2048]{1,0:T(8,128)(2,1)S(1)}, bf16[384,2048]{1,0:T(8,128)(2,1)S(1)}, u32[]{:S(2)}, u32[]{:S(2)}) collective-permute-start(bf16[384,2048]{1,0:T(8,128)(2,1)S(1)} %get-tuple-element.381), channel_id=1, source_target_pairs={{0,1},{1,0},{2,3},{3,2},{4,5},{5,4},{6,7},{7,6},{8,9},{9,8},{10,11... | collective-permute-start | bytes 4718600 | tf_op jit(solution)/shard_map/ppermute | solution.py:43
  446.0 40.1 %collective-permute-start.47 = (bf16[2,2,1,1,128,896]{5,4,3,2,1,0:T(8,128)(2,1)}, bf16[2,2,1,1,128,896]{5,4,3,2,1,0:T(8,128)(2,1)}, u32[]{:S(2)}, u32[]{:S(2)}) collective-permute-start(bf16[2,2,1,1,128,896]{5,4,3,2,1,0:T(8,128)(2,1)} %add_convert_fusion.10), channel_id=1, source_target_pairs={{0,2},{2,0},{4,6},{6,4},{8,10},{10,8},{12,14},{14,12},{16,18},{18,... | collective-permute-start | bytes 2752520 | tf_op jit(solution)/shard_map/ppermute | solution.py:39
  448.4 37.7 %collective-permute-start.50 = (bf16[2,2,1,1,128,1024]{5,4,3,2,1,0:T(8,128)(2,1)S(1)}, bf16[2,2,1,1,128,1024]{5,4,3,2,1,0:T(8,128)(2,1)}, u32[]{:S(2)}, u32[]{:S(2)}) collective-permute-start(bf16[2,2,1,1,128,1024]{5,4,3,2,1,0:T(8,128)(2,1)S(1)} %add_convert_fusion.8), channel_id=1, source_target_pairs={{0,4},{2,6},{4,0},{6,2},{8,12},{10,14},{12,8},{14,10},{16,20},{18,... | collective-permute-start | bytes 3145736 | tf_op jit(solution)/shard_map/ppermute | solution.py:39
  454.6 41.6 %collective-permute-start.46 = (bf16[2,2,1,2,128,512]{5,4,3,2,1,0:T(8,128)(2,1)}, bf16[2,2,1,2,128,512]{5,4,3,2,1,0:T(8,128)(2,1)}, u32[]{:S(2)}, u32[]{:S(2)}) collective-permute-start(bf16[2,2,1,2,128,512]{5,4,3,2,1,0:T(8,128)(2,1)} %slice.492), channel_id=1, source_target_pairs={{0,4},{2,6},{4,0},{6,2},{8,12},{10,14},{12,8},{14,10},{16,20},{18,... | collective-permute-start | bytes 3145736 | tf_op jit(solution)/shard_map/ppermute | solution.py:39
  458.4 39.0 %collective-permute-start.52 = (bf16[2,2,2,1,128,512]{5,4,3,2,1,0:T(8,128)(2,1)}, bf16[2,2,2,1,128,512]{5,4,3,2,1,0:T(8,128)(2,1)}, u32[]{:S(2)}, u32[]{:S(2)}) collective-permute-start(bf16[2,2,2,1,128,512]{5,4,3,2,1,0:T(8,128)(2,1)} %slice.494), channel_id=1, source_target_pairs={{0,2},{2,0},{4,6},{6,4},{8,10},{10,8},{12,14},{14,12},{16,18},{18,... | collective-permute-start | bytes 3145736 | tf_op jit(solution)/shard_map/ppermute | solution.py:39
  484.1 99.1 %collective-permute-start.65 = (bf16[384,2048]{1,0:T(8,128)(2,1)}, bf16[384,2048]{1,0:T(8,128)(2,1)}, u32[]{:S(2)}, u32[]{:S(2)}) collective-permute-start(bf16[384,2048]{1,0:T(8,128)(2,1)} %pad_maximum_fusion.24), channel_id=1, source_target_pairs={{0,8},{2,10},{4,12},{6,14},{8,0},{10,2},{12,4},{14,6},{16,24},{18,... | collective-permute-start | bytes 4718600 | tf_op jit(solution)/shard_map/ppermute | solution.py:39
  491.1 49.0 %collective-permute-start.57 = (bf16[2,1,1,1,128,1920]{5,4,3,2,1,0:T(8,128)(2,1)}, bf16[2,1,1,1,128,1920]{5,4,3,2,1,0:T(8,128)(2,1)S(1)}, u32[]{:S(2)}, u32[]{:S(2)}) collective-permute-start(bf16[2,1,1,1,128,1920]{5,4,3,2,1,0:T(8,128)(2,1)} %fusion.20), channel_id=1, source_target_pairs={{0,16},{2,18},{4,20},{6,22},{8,24},{10,26},{12,28},{14,30},{16,0},... | collective-permute-start | bytes 2949128 | tf_op jit(solution)/shard_map/ppermute | solution.py:39
  499.4 29.6 %collective-permute-start.53 = (bf16[2,2,1,1,128,512]{5,4,3,2,1,0:T(8,128)(2,1)}, bf16[2,2,1,1,128,512]{5,4,3,2,1,0:T(8,128)(2,1)}, u32[]{:S(2)}, u32[]{:S(2)}) collective-permute-start(bf16[2,2,1,1,128,512]{5,4,3,2,1,0:T(8,128)(2,1)} %add_convert_fusion.19), channel_id=1, source_target_pairs={{0,4},{2,6},{4,0},{6,2},{8,12},{10,14},{12,8},{14,10},{16,20},{18,... | collective-permute-start | bytes 1572872 | tf_op jit(solution)/shard_map/ppermute | solution.py:39
  500.5 25.4 %collective-permute-start.51 = (bf16[2,2,1,1,128,512]{5,4,3,2,1,0:T(8,128)(2,1)S(1)}, bf16[2,2,1,1,128,512]{5,4,3,2,1,0:T(8,128)(2,1)S(1)}, u32[]{:S(2)}, u32[]{:S(2)}) collective-permute-start(bf16[2,2,1,1,128,512]{5,4,3,2,1,0:T(8,128)(2,1)S(1)} %add_convert_fusion.20), channel_id=1, source_target_pairs={{0,2},{2,0},{4,6},{6,4},{8,10},{10,8},{12,14},{14,12},{16,18},{18,... | collective-permute-start | bytes 1572872 | tf_op jit(solution)/shard_map/ppermute | solution.py:39
  524.3 29.6 %collective-permute-start.56 = (bf16[2,2,1,2,128,640]{5,4,3,2,1,0:T(8,128)(2,1)}, bf16[2,2,1,2,128,640]{5,4,3,2,1,0:T(8,128)(2,1)S(1)}, u32[]{:S(2)}, u32[]{:S(2)}) collective-permute-start(bf16[2,2,1,2,128,640]{5,4,3,2,1,0:T(8,128)(2,1)} %slice.504), channel_id=1, source_target_pairs={{0,4},{2,6},{4,0},{6,2},{8,12},{10,14},{12,8},{14,10},{16,20},{18,... | collective-permute-start | bytes 3932168 | tf_op jit(solution)/shard_map/ppermute | solution.py:39
  526.6 29.1 %collective-permute-start.55 = (bf16[2,2,2,1,128,640]{5,4,3,2,1,0:T(8,128)(2,1)S(1)}, bf16[2,2,2,1,128,640]{5,4,3,2,1,0:T(8,128)(2,1)S(1)}, u32[]{:S(2)}, u32[]{:S(2)}) collective-permute-start(bf16[2,2,2,1,128,640]{5,4,3,2,1,0:T(8,128)(2,1)S(1)} %slice.503), channel_id=1, source_target_pairs={{0,2},{2,0},{4,6},{6,4},{8,10},{10,8},{12,14},{14,12},{16,18},{18,... | collective-permute-start | bytes 3932168 | tf_op jit(solution)/shard_map/ppermute | solution.py:39
  534.8 22.7 %collective-permute-start.58 = (bf16[384,2048]{1,0:T(8,128)(2,1)}, bf16[384,2048]{1,0:T(8,128)(2,1)S(1)}, u32[]{:S(2)}, u32[]{:S(2)}) collective-permute-start(bf16[384,2048]{1,0:T(8,128)(2,1)} %convolution_convert_fusion.3), channel_id=1, source_target_pairs={{0,1},{1,0},{2,3},{3,2},{4,5},{5,4},{6,7},{7,6},{8,9},{9,8},{10,11... | collective-permute-start | bytes 4718600 | tf_op jit(solution)/shard_map/ppermute | solution.py:43
  540.2 21.9 %collective-permute-start.54 = (bf16[1,2,1,1,128,1024]{5,4,3,2,1,0:T(8,128)(2,1)}, bf16[1,2,1,1,128,1024]{5,4,3,2,1,0:T(8,128)(2,1)}, u32[]{:S(2)}, u32[]{:S(2)}) collective-permute-start(bf16[1,2,1,1,128,1024]{5,4,3,2,1,0:T(8,128)(2,1)} %pad_maximum_fusion.42), channel_id=1, source_target_pairs={{0,8},{2,10},{4,12},{6,14},{8,0},{10,2},{12,4},{14,6},{16,24},{18,... | collective-permute-start | bytes 1572872 | tf_op jit(solution)/shard_map/ppermute | solution.py:39
  553.9 18.5 %collective-permute-start.61 = (bf16[1,1,1,1,128,1920]{5,4,3,2,1,0:T(8,128)(2,1)}, bf16[1,1,1,1,128,1920]{5,4,3,2,1,0:T(8,128)(2,1)S(1)}, u32[]{:S(2)}, u32[]{:S(2)}) collective-permute-start(bf16[1,1,1,1,128,1920]{5,4,3,2,1,0:T(8,128)(2,1)} %slice.651), channel_id=1, source_target_pairs={{0,8},{2,10},{4,12},{6,14},{8,0},{10,2},{12,4},{14,6},{16,24},{18,... | collective-permute-start | bytes 1474568 | tf_op jit(solution)/shard_map/ppermute | solution.py:39
  556.0 21.2 %collective-permute-start.64 = (bf16[2,2,1,1,128,640]{5,4,3,2,1,0:T(8,128)(2,1)S(1)}, bf16[2,2,1,1,128,640]{5,4,3,2,1,0:T(8,128)(2,1)S(1)}, u32[]{:S(2)}, u32[]{:S(2)}) collective-permute-start(bf16[2,2,1,1,128,640]{5,4,3,2,1,0:T(8,128)(2,1)S(1)} %add_convert_fusion.14), channel_id=1, source_target_pairs={{0,4},{2,6},{4,0},{6,2},{8,12},{10,14},{12,8},{14,10},{16,20},{18,... | collective-permute-start | bytes 1966088 | tf_op jit(solution)/shard_map/ppermute | solution.py:39
  557.5 19.6 %collective-permute-start.63 = (bf16[2,2,1,1,128,640]{5,4,3,2,1,0:T(8,128)(2,1)S(1)}, bf16[2,2,1,1,128,640]{5,4,3,2,1,0:T(8,128)(2,1)S(1)}, u32[]{:S(2)}, u32[]{:S(2)}) collective-permute-start(bf16[2,2,1,1,128,640]{5,4,3,2,1,0:T(8,128)(2,1)S(1)} %add_convert_fusion.15), channel_id=1, source_target_pairs={{0,2},{2,0},{4,6},{6,4},{8,10},{10,8},{12,14},{14,12},{16,18},{18,... | collective-permute-start | bytes 1966088 | tf_op jit(solution)/shard_map/ppermute | solution.py:39
  572.7 21.8 %collective-permute-start.67 = (bf16[1,1,1,1,128,2304]{5,4,3,2,1,0:T(8,128)(2,1)S(1)}, bf16[1,1,1,1,128,2304]{5,4,3,2,1,0:T(8,128)(2,1)S(1)}, u32[]{:S(2)}, u32[]{:S(2)}) collective-permute-start(bf16[1,1,1,1,128,2304]{5,4,3,2,1,0:T(8,128)(2,1)S(1)} %copy-done.120), channel_id=1, source_target_pairs={{0,8},{2,10},{4,12},{6,14},{8,0},{10,2},{12,4},{14,6},{16,24},{18,... | collective-permute-start | bytes 1769480 | tf_op jit(solution)/shard_map/ppermute | solution.py:39
  577.1 34.2 %collective-permute-start.72 = (bf16[1,1,1,1,128,1024]{5,4,3,2,1,0:T(8,128)(2,1)S(1)}, bf16[1,1,1,1,128,1024]{5,4,3,2,1,0:T(8,128)(2,1)S(1)}, u32[]{:S(2)}, u32[]{:S(2)}) collective-permute-start(bf16[1,1,1,1,128,1024]{5,4,3,2,1,0:T(8,128)(2,1)S(1)} %slice.511), channel_id=1, source_target_pairs={{0,16},{2,18},{4,20},{6,22},{8,24},{10,26},{12,28},{14,30},{16,0},... | collective-permute-start | bytes 786440 | tf_op jit(solution)/shard_map/ppermute | solution.py:39
  580.9 27.1 %collective-permute-start.69 = (bf16[1,2,1,1,128,1280]{5,4,3,2,1,0:T(8,128)(2,1)S(1)}, bf16[1,2,1,1,128,1280]{5,4,3,2,1,0:T(8,128)(2,1)S(1)}, u32[]{:S(2)}, u32[]{:S(2)}) collective-permute-start(bf16[1,2,1,1,128,1280]{5,4,3,2,1,0:T(8,128)(2,1)S(1)} %fusion.26), channel_id=1, source_target_pairs={{0,8},{2,10},{4,12},{6,14},{8,0},{10,2},{12,4},{14,6},{16,24},{18,... | collective-permute-start | bytes 1966088 | tf_op jit(solution)/shard_map/ppermute | solution.py:39
  581.8 15.3 %collective-permute-start.66 = (f32[2,2,1,1,2,128]{5,4,3,2,1,0:T(2,128)S(1)}, f32[2,2,1,1,2,128]{5,4,3,2,1,0:T(2,128)S(1)}, u32[]{:S(2)}, u32[]{:S(2)}) collective-permute-start(f32[2,2,1,1,2,128]{5,4,3,2,1,0:T(2,128)S(1)} %slice.518), channel_id=1, source_target_pairs={{0,2},{2,0},{4,6},{6,4},{8,10},{10,8},{12,14},{14,12},{16,18},{18,... | collective-permute-start | bytes 12296 | tf_op jit(solution)/shard_map/ppermute | solution.py:39
  608.2 17.1 %collective-permute-start.71 = (bf16[1,1,1,1,128,1280]{5,4,3,2,1,0:T(8,128)(2,1)S(1)}, bf16[1,1,1,1,128,1280]{5,4,3,2,1,0:T(8,128)(2,1)S(1)}, u32[]{:S(2)}, u32[]{:S(2)}) collective-permute-start(bf16[1,1,1,1,128,1280]{5,4,3,2,1,0:T(8,128)(2,1)S(1)} %slice.524), channel_id=1, source_target_pairs={{0,16},{2,18},{4,20},{6,22},{8,24},{10,26},{12,28},{14,30},{16,0},... | collective-permute-start | bytes 983048 | tf_op jit(solution)/shard_map/ppermute | solution.py:39
  608.3 18.6 %collective-permute-start.70 = (f32[1,1,1,1,2,128]{5,4,3,2,1,0:T(2,128)S(1)}, f32[1,1,1,1,2,128]{5,4,3,2,1,0:T(2,128)S(1)}, u32[]{:S(2)}, u32[]{:S(2)}) collective-permute-start(f32[1,1,1,1,2,128]{5,4,3,2,1,0:T(2,128)S(1)} %slice.526), channel_id=1, source_target_pairs={{0,16},{2,18},{4,20},{6,22},{8,24},{10,26},{12,28},{14,30},{16,0},... | collective-permute-start | bytes 3080 | tf_op jit(solution)/shard_map/ppermute | solution.py:39
  (135 other events, 1308.8 us)

commit v4 on v3

--- a/solution.py
+++ b/solution.py
@@ -383,8 +383,8 @@
     )(queries, keys, values, grads, bias, cosine, sine, totals)
 
 
-def no_cost():
-    return pl.CostEstimate(flops=1000000, bytes_accessed=1000000, transcendentals=0)
+def no_cost(hint=1):
+    return pl.CostEstimate(flops=hint * 1000000, bytes_accessed=1000000, transcendentals=0)
 
 
 def whole_block(shape):
@@ -422,6 +422,38 @@
         cost_estimate=no_cost(),
         name="stack_rows",
     )(*pieces)
+
+
+def join_kernel(block, first_a, came_a, first_b, came_b, gate, up, down_a, down_b):
+    def whole(first, came, size):
+        shape = (-1, size, first.shape[1])
+        both = jnp.concatenate([first[...].reshape(shape), came[...].reshape(shape)], axis=1)
+        return both.reshape(-1, first.shape[1])
+
+    width = gate.shape[1]
+    both_a = whole(first_a, came_a, 2 * block)
+    gate[...] = both_a[:, :width]
+    down_a[...] = both_a[:, width:]
+    both_b = whole(first_b, came_b, block)
+    up[...] = both_b[:, :width]
+    down_b[...] = both_b[:, width:]
+
+
+def join_weights(first_a, came_a, first_b, came_b, width):
+    high = 512
+    arrays = [flat(v) for v in (first_a, came_a, first_b, came_b)]
+    depth = 2 * arrays[0].shape[0]
+    widths = (width, width, arrays[0].shape[1] - width, arrays[2].shape[1] - width)
+    return pl.pallas_call(
+        functools.partial(join_kernel, depth // lax.axis_size("dp")),
+        grid=(depth // high,),
+        in_specs=[pl.BlockSpec((high // 2, v.shape[1]), lambda i: (i, 0)) for v in arrays],
+        out_specs=[pl.BlockSpec((high, w), lambda i: (i, 0)) for w in widths],
+        out_shape=[jax.ShapeDtypeStruct((depth, w), bf16) for w in widths],
+        compiler_params=pltpu.CompilerParams(vmem_limit_bytes=40 * 1024 * 1024),
+        cost_estimate=no_cost(20000),
+        name="join_weights",
+    )(*arrays)
 
 
 def hidden_kernel(
@@ -792,17 +824,8 @@
     w1 = w1()
 
     def weights_of(first_a, came_a, first_b, came_b, index):
-        whole_a = lambda low, high: flat(
-            join(columns(first_a, low, high), columns(came_a, low, high), Y)
-        )
-        whole_b = lambda low, high: flat(
-            join(columns(first_b, low, high), columns(came_b, low, high), X)
-        )
-        width, at = chunks.width(index) // 3, chunks.turn(index)
-        return (
-            whole_a(0, width), whole_b(0, width),
-            whole_a(width, at), whole_b(width, chunks.width(index) - at),
-        )
+        width = chunks.width(index) // 3
+        return join_weights(first_a, came_a, first_b, held(came_b), width)
 
     def hidden_layer(rows, grads, weights):
         hidden, grad_gate, grad_up = hidden_rows(held(rows), grads, *weights, own_rows)
@@ -822,7 +845,7 @@
         did(sent)
         return kept, sent
 
-    weights_0 = weights_of(w0a, held(w0a_y), w0b, held(w0b_x), 0)
+    weights_0 = weights_of(w0a, held(w0a_y), w0b, w0b_x, 0)
     w1a = gather(columns(w1, 0, chunks.turn(1)), X)
     w1b = gather(columns(w1, chunks.turn(1), w1.shape[-1]), Y)
     far_other = swap(far_own)
@@ -840,7 +863,8 @@
     r0a_y = send(r0a_sent, Y)
     r0b, r0b_sent = bundle_grads(both(2), both(0), 0, True)
     r0b_x = send(r0b_sent, X)
-    weights_1 = weights_of(w1a, held(w1a_y), w1b, held(w1b_x), 1)
+    w1a_y, w1b_x = held(w1a_y), held(w1b_x)
+    weights_1 = weights_of(w1a, w1a_y, w1b, w1b_x, 1)
     weights_hidden = [*weights_0[:2], *weights_1[:2]]
     weights_down = [*weights_0[2:], *weights_1[2:]]
     cuts_hidden = tuple((i, 0, v.shape[1]) for i, v in enumerate(weights_hidden))
@@ -921,13 +945,13 @@
     for bit in rest[:0:-1]:
         r1 = fold(r1, bit)()
     r1 = fold(r1, rest[0], f32)
+    d_query_b, d_key_b, d_value_b = attend_backward(
+        queries_b, keys_b, values_b, matmul(held(grad_attended), ob).astype(bf16), *tables, totals_b
+    )
+    did(d_query_b)
     out_a, out_b = part(grad_out_a, Y, 0), part(grad_out_b, X, 0)
     roa_x, out_a = pass_on(out_a, roa_y, X)
     rob_y, out_b = pass_on(out_b, rob_x, Y)
-    d_query_b, d_key_b, d_value_b = attend_backward(
-        queries_b, keys_b, values_b, matmul(held(grad_attended), ob).astype(bf16), *tables, totals_b
-    )
-    did(d_query_b)
     low = jnp.arange(kv_width) < HEAD_DIM
     d_qkv = jnp.concatenate(
         [

time: 632 us -> 627 us (level)
  Pallas kernels: 212 us -> 227 us
  other arithmetic: 98.7 us -> 84.7 us
  local copies, waits for them, and re-layouts: 54.3 us -> 42.5 us
  waiting for transfers between devices: 163 us -> 172 us
    concatenate x39 -> x23, other arithmetic: 34.8 us -> 19.5 us  [join(): return jnp.concatenate([values, came], axis=block_axes().index(bit))]
    pallas_call x0 -> x2, Pallas kernels: none -> 10.8 us  [join_weights(): pl.pallas_call(functools.partial(join_kernel, depth // lax.axis_size('dp'...]
    slice x12 -> x4, local copies, waits for them, and re-layouts: 11.2 us -> 1.58 us  [columns(): return lax.slice_in_dim(values, low, high, axis=values.ndim - 1)]
    ppermute x60, waiting for transfers between devices: 163 us -> 172 us  [exchange(): return lax.ppermute(values, 'dp', [(i, i ^ 1 << bit) for i in range(size)])]
    unnamed x254 -> x236, local copies, waits for them, and re-layouts: 34.4 us -> 29.9 us
  transfers between devices with their start and end apart: 73 -> 73, of which waited for: 21 -> 26; matrix products, arithmetic and copies ran while one was open for 23% -> 19% of each run, Pallas kernels for 34% -> 36%
where the time goes in v4:
time: 627 us; the launch traced here: 623 us
  Pallas kernels  227 us (36%)
  waiting for transfers between devices  172 us (27%)
  other arithmetic  84.7 us (14%)
  starting transfers between devices  67.1 us (11%)
  local copies, waits for them, and re-layouts  42.5 us (7%)
  matrix products  26.7 us (4%)
    ppermute x60, waiting for transfers between devices, exchange(): return lax.ppermute(values, 'dp', [(i, i ^ 1 << bit) for i in range(size)])  172 us
    ppermute x60, starting transfers between devices, exchange(): return lax.ppermute(values, 'dp', [(i, i ^ 1 << bit) for i in range(size)])  65.8 us
    pallas_call x4, Pallas kernels, hidden_rows(): pl.pallas_call(hidden_kernel, grid=(total // height,), in_specs=[tall, ta...  52.7 us
    pallas_call x4, Pallas kernels, back_rows(): pl.pallas_call(functools.partial(back_kernel, cuts), grid=(depth // high,...  44.9 us
    pallas_call x4, Pallas kernels, weight_grads(): pl.pallas_call(functools.partial(weight_grad_kernel, inner), grid=(depth...  44.8 us
    unnamed x236, local copies, waits for them, and re-layouts  29.9 us
    pallas_call x2, Pallas kernels, attend_forward(): pl.pallas_call(functools.partial(forward_kernel, group == 1), grid=(own,)...  26.4 us
    pallas_call x2, Pallas kernels, attend_backward(): pl.pallas_call(backward_kernel, grid=(width // LANES,), in_specs=[column,...  26.1 us
  transfers between devices with their start and end apart: 73, of which 26 were waited for; matrix products, arithmetic and copies ran while one was open for 19% of the time, Pallas kernels for 36%

profile of v4, /device:TPU:0, one launch (start us, length us, event | category | flops | bytes accessed | tf_op | source)
XLA Modules:
  0.0 622.9 jit_solution(8527047947233247391)
XLA Ops:
  1.3 4.0 collective-permute-start
  21.5 2.2 collective-permute-done.2
  25.2 2.6 collective-permute-start.6
  30.4 7.4 %collective-permute-done.6 = bf16[1,1,1,1,128,1024]{5,4,3,2,1,0:T(8,128)(2,1)S(1)} collective-permute-done((bf16[1,1,1,1,128,1024]{5,4,3,2,1,0:T(8,128)(2,1)S(1)}, bf16[1,1,1,1,128,1024]{5,4,3,2,1,0:T(8,128)(2,1)S(1)}, u32[]{:S(2)}, u32[]{:S(2)}) %collective-permute-start.6) | collective-permute-done | bytes 262176 | tf_op jit(solution)/shard_map/ppermute | solution.py:39
  37.8 10.6 %collective-permute-done.8 = bf16[1,2,1,1,128,1280]{5,4,3,2,1,0:T(8,128)(2,1)S(1)} collective-permute-done((bf16[1,2,1,1,128,1280]{5,4,3,2,1,0:T(8,128)(2,1)S(1)}, bf16[1,2,1,1,128,1280]{5,4,3,2,1,0:T(8,128)(2,1)S(1)}, u32[]{:S(2)}, u32[]{:S(2)}) %collective-permute-start.8) | collective-permute-done | bytes 655392 | tf_op jit(solution)/shard_map/ppermute | solution.py:39
  52.2 12.3 %collective-permute-done.10 = bf16[2,2,1,1,128,640]{5,4,3,2,1,0:T(8,128)(2,1)S(1)} collective-permute-done((bf16[2,2,1,1,128,640]{5,4,3,2,1,0:T(8,128)(2,1)S(1)}, bf16[2,2,1,1,128,640]{5,4,3,2,1,0:T(8,128)(2,1)S(1)}, u32[]{:S(2)}, u32[]{:S(2)}) %collective-permute-start.10) | collective-permute-done | bytes 655392 | tf_op jit(solution)/shard_map/ppermute | solution.py:39
  74.4 19.4 %collective-permute-done.12 = bf16[2,2,1,2,128,640]{5,4,3,2,1,0:T(8,128)(2,1)S(1)} collective-permute-done((bf16[2,2,1,2,128,640]{5,4,3,2,1,0:T(8,128)(2,1)S(1)}, bf16[2,2,1,2,128,640]{5,4,3,2,1,0:T(8,128)(2,1)S(1)}, u32[]{:S(2)}, u32[]{:S(2)}) %collective-permute-start.12) | collective-permute-done | bytes 1310752 | tf_op jit(solution)/shard_map/ppermute | solution.py:39
  96.9 4.3 fusion.14.q_ref.k_ref.v_ref
  101.2 13.3 %attend_forward.2 = (bf16[768,512]{1,0:T(8,128)(2,1)S(1)}, bf16[768,512]{1,0:T(8,128)(2,1)S(1)}, bf16[768,128]{1,0:T(8,128)(2,1)S(1)}, bf16[768,128]{1,0:T(8,128)(2,1)S(1)}, f32[4,1,1536]{2,1,0:T(1,128)S(1)}) custom-call(f32[768,1280]{1,0:T(8,128)S(1)} %fusion.14.q_ref.k_ref.v_ref, f32[768,1280]{1,0:T(8,128)S(1)} %fusion.14.q_ref.k_ref.v_ref, ...), custom_call_target="tpu_custom_call" | custom-call | flops 1000000 | bytes 1000000 | tf_op jit(solution)/shard_map/attend_forward/pallas_call | solution.py:329
  124.4 13.1 %attend_forward.3 = (bf16[768,512]{1,0:T(8,128)(2,1)S(1)}, bf16[768,512]{1,0:T(8,128)(2,1)S(1)}, bf16[768,128]{1,0:T(8,128)(2,1)S(1)}, bf16[768,128]{1,0:T(8,128)(2,1)S(1)}, f32[4,1,1536]{2,1,0:T(1,128)S(1)}) custom-call(f32[768,1280]{1,0:T(8,128)S(1)} %copy-done.1, f32[768,1280]{1,0:T(8,128)S(1)} %copy-done.1, f32[768,1280]{1,0:T(8,128)S(1)} %copy-done.1, ...), custom_call_target="tpu_custom_call" | custom-call | flops 1000000 | bytes 1000000 | tf_op jit(solution)/shard_map/attend_forward/pallas_call | solution.py:329
  137.6 2.6 collective-permute-done.20.refs_0_
  144.2 2.2 pad_maximum_fusion.9
  154.2 8.9 %collective-permute-done.23 = bf16[2,2,1,1,128,1152]{5,4,3,2,1,0:T(8,128)(2,1)S(1)} collective-permute-done((bf16[2,2,1,1,128,1152]{5,4,3,2,1,0:T(8,128)(2,1)S(1)}, bf16[2,2,1,1,128,1152]{5,4,3,2,1,0:T(8,128)(2,1)S(1)}, u32[]{:S(2)}, u32[]{:S(2)}) %collective-permute-start.23) | collective-permute-done | bytes 1179680 | tf_op jit(solution)/shard_map/ppermute | solution.py:39
  163.2 3.8 collective-permute-done.22
  180.7 3.1 stack_rows.5
  185.5 35.6 %collective-permute-done.26 = bf16[2,1,1,1,128,1920]{5,4,3,2,1,0:T(8,128)(2,1)S(1)} collective-permute-done((bf16[2,1,1,1,128,1920]{5,4,3,2,1,0:T(8,128)(2,1)}, bf16[2,1,1,1,128,1920]{5,4,3,2,1,0:T(8,128)(2,1)S(1)}, u32[]{:S(2)}, u32[]{:S(2)}) %collective-permute-start.26) | collective-permute-done | bytes 983072 | tf_op jit(solution)/shard_map/ppermute | solution.py:39
  224.7 5.5 join_weights.2
  230.2 3.9 stack_rows.6
  237.4 14.5 %hidden_rows.4 = (bf16[768,768]{1,0:T(8,128)(2,1)S(1)}, bf16[768,768]{1,0:T(8,128)(2,1)S(1)}, bf16[768,768]{1,0:T(8,128)(2,1)S(1)}) custom-call(bf16[768,2048]{1,0:T(8,128)(2,1)} %copy-done.17, bf16[768,2048]{1,0:T(8,128)(2,1)} %copy-done.15, bf16[2048,768]{1,0:T(8,128)(2,1)} %get-tuple-element.327.gate_ref.refs_4_, ...), custom_call_target="tpu_custom_call" | custom-call | flops 1000000 | bytes 1000000 | tf_op jit(solution)/shard_map/hidden_rows/pallas_call | solution.py:480
  251.9 3.2 stack_rows.7
  256.8 3.6 pad_maximum_fusion.10
  262.6 14.7 %hidden_rows.5 = (bf16[768,768]{1,0:T(8,128)(2,1)S(1)}, bf16[768,768]{1,0:T(8,128)(2,1)S(1)}, bf16[768,768]{1,0:T(8,128)(2,1)S(1)}) custom-call(bf16[768,2048]{1,0:T(8,128)(2,1)} %copy-done.18, bf16[768,2048]{1,0:T(8,128)(2,1)} %copy-done.16, bf16[2048,768]{1,0:T(8,128)(2,1)} %get-tuple-element.327.gate_ref.refs_4_, ...), custom_call_target="tpu_custom_call" | custom-call | flops 1000000 | bytes 1000000 | tf_op jit(solution)/shard_map/hidden_rows/pallas_call | solution.py:480
  278.4 11.5 %weight_grads.4 = (bf16[8,128,1152]{2,1,0:T(8,128)(2,1)S(1)}, bf16[8,128,1152]{2,1,0:T(8,128)(2,1)}) custom-call(bf16[2048,768]{1,0:T(8,128)(2,1)} %copy-done.4, bf16[2048,768]{1,0:T(8,128)(2,1)} %copy-done.5, bf16[768,768]{1,0:T(8,128)(2,1)S(1)} %get-tuple-element.382.near_ref.refs_0_, bf16[768,768]{1,0:T(8,128)(2,1)S(1)} %get-tuple-element.360.far_ref.refs_0_, ...), custom_call_target="tpu_custom_call" | custom-call | flops 1000000 | bytes 1000000 | tf_op jit(solution)/shard_map/weight_grads/pallas_call | solution.py:521
  291.7 11.6 %weight_grads.5 = (bf16[8,128,1152]{2,1,0:T(8,128)(2,1)S(1)}, bf16[8,128,1152]{2,1,0:T(8,128)(2,1)}) custom-call(bf16[2048,768]{1,0:T(8,128)(2,1)} %copy-done.4, bf16[2048,768]{1,0:T(8,128)(2,1)} %copy-done.5, bf16[768,768]{1,0:T(8,128)(2,1)S(1)} %get-tuple-element.349.near_ref.refs_1_, bf16[768,768]{1,0:T(8,128)(2,1)S(1)} %get-tuple-element.350.far_ref.refs_1_, ...), custom_call_target="tpu_custom_call" | custom-call | flops 1000000 | bytes 1000000 | tf_op jit(solution)/shard_map/weight_grads/pallas_call | solution.py:521
  305.3 3.9 collective-permute-done.34
  309.1 5.3 join_weights.3
  316.0 11.9 %hidden_rows.6 = (bf16[768,640]{1,0:T(8,128)(2,1)S(1)}, bf16[768,640]{1,0:T(8,128)(2,1)S(1)}, bf16[768,640]{1,0:T(8,128)(2,1)S(1)}) custom-call(bf16[768,2048]{1,0:T(8,128)(2,1)} %copy-done.18, bf16[768,2048]{1,0:T(8,128)(2,1)} %copy-done.16, bf16[2048,640]{1,0:T(8,128)(2,1)} %copy-done.6, bf16[2048,640]{1,0:T(8,128)(2,1)} %get-tuple-element.356.up_ref.refs_7_, ...), custom_call_target="tpu_custom_call" | custom-call | flops 1000000 | bytes 1000000 | tf_op jit(solution)/shard_map/hidden_rows/pallas_call | solution.py:480
  327.9 14.3 %back_rows.4 = (f32[384,2048]{1,0:T(8,128)}, bf16[384,2048]{1,0:T(8,128)(2,1)}) custom-call(bf16[768,768]{1,0:T(8,128)(2,1)S(1)} %get-tuple-element.360.far_ref.refs_0_, bf16[768,768]{1,0:T(8,128)(2,1)S(1)} %get-tuple-element.350.far_ref.refs_1_, bf16[768,640]{1,0:T(8,128)(2,1)S(1)} %get-tuple-element.361.refs_2_.far_ref, ...), custom_call_target="tpu_custom_call" | custom-call | flops 1000000 | bytes 1000000 | tf_op jit(solution)/shard_map/back_rows/pallas_call | solution.py:560
  342.4 11.6 %hidden_rows.7 = (bf16[768,640]{1,0:T(8,128)(2,1)S(1)}, bf16[768,640]{1,0:T(8,128)(2,1)S(1)}, bf16[768,640]{1,0:T(8,128)(2,1)S(1)}) custom-call(bf16[768,2048]{1,0:T(8,128)(2,1)} %copy-done.17, bf16[768,2048]{1,0:T(8,128)(2,1)} %copy-done.15, bf16[2048,640]{1,0:T(8,128)(2,1)} %copy-done.6, bf16[2048,640]{1,0:T(8,128)(2,1)} %get-tuple-element.356.up_ref.refs_7_, ...), custom_call_target="tpu_custom_call" | custom-call | flops 1000000 | bytes 1000000 | tf_op jit(solution)/shard_map/hidden_rows/pallas_call | solution.py:480
  355.1 2.6 add_convert_fusion.6
  359.3 2.6 add_convert_fusion.5
  367.0 10.2 %weight_grads.6 = (bf16[8,128,896]{2,1,0:T(8,128)(2,1)S(1)}, bf16[8,128,896]{2,1,0:T(8,128)(2,1)}) custom-call(bf16[2048,768]{1,0:T(8,128)(2,1)} %copy-done.4, bf16[2048,768]{1,0:T(8,128)(2,1)} %copy-done.5, bf16[768,640]{1,0:T(8,128)(2,1)S(1)} %get-tuple-element.378.near_ref.refs_2_, bf16[768,640]{1,0:T(8,128)(2,1)S(1)} %copy-done.38, ...), custom_call_target="tpu_custom_call" | custom-call | flops 1000000 | bytes 1000000 | tf_op jit(solution)/shard_map/weight_grads/pallas_call | solution.py:521
  378.5 11.5 %weight_grads.7 = (bf16[8,128,1024]{2,1,0:T(8,128)(2,1)S(1)}, bf16[8,128,1024]{2,1,0:T(8,128)(2,1)}) custom-call(bf16[2048,768]{1,0:T(8,128)(2,1)} %copy-done.4, bf16[2048,768]{1,0:T(8,128)(2,1)} %copy-done.5, bf16[768,640]{1,0:T(8,128)(2,1)S(1)} %get-tuple-element.380.near_ref.refs_3_, bf16[768,640]{1,0:T(8,128)(2,1)S(1)} %copy-done.36, ...), custom_call_target="tpu_custom_call" | custom-call | flops 1000000 | bytes 1000000 | tf_op jit(solution)/shard_map/weight_grads/pallas_call | solution.py:521
  392.2 13.2 %back_rows.5 = (f32[384,2048]{1,0:T(8,128)}, bf16[384,2048]{1,0:T(8,128)(2,1)S(1)}) custom-call(bf16[768,768]{1,0:T(8,128)(2,1)S(1)} %get-tuple-element.382.near_ref.refs_0_, bf16[768,768]{1,0:T(8,128)(2,1)S(1)} %get-tuple-element.349.near_ref.refs_1_, bf16[768,640]{1,0:T(8,128)(2,1)S(1)} %get-tuple-element.378.near_ref.refs_2_, ...), custom_call_target="tpu_custom_call" | custom-call | flops 1000000 | bytes 1000000 | tf_op jit(solution)/shard_map/back_rows/pallas_call | solution.py:560
  405.5 2.2 add_convert_fusion.4
  407.8 2.5 add_convert_fusion.3
  413.2 2.7 multiply_reduce_fusion
  415.9 4.7 fusion.44
  421.0 3.3 collective-permute-start.48
  426.8 8.7 %back_rows.6 = (f32[384,2048]{1,0:T(8,128)}, bf16[384,2048]{1,0:T(8,128)(2,1)S(1)}) custom-call(bf16[768,768]{1,0:T(8,128)(2,1)S(1)} %copy-done.28, bf16[768,640]{1,0:T(8,128)(2,1)S(1)} %copy-done.34, bf16[2048,384]{1,0:T(8,128)(2,1)} %copy-done.11, bf16[2048,384]{1,0:T(8,128)(2,1)} %copy-done.12, bf16[2048,256]{1,0:T(8,128)(2,1)S(1)} %get-tuple-element.357.down_a.refs_4_, ...), custom_call_target="tpu_custom_call" | custom-call | flops 1000000 | bytes 1000000 | tf_op jit(solution)/shard_map/back_rows/pallas_call | solution.py:560
  435.6 2.5 add_convert_fusion.10
  441.6 2.1 broadcast_select_fusion.2
  455.9 13.1 %attend_backward.2 = (bf16[768,512]{1,0:T(8,128)(2,1)S(1)}, bf16[768,128]{1,0:T(8,128)(2,1)S(1)}, bf16[768,128]{1,0:T(8,128)(2,1)S(1)}) custom-call(bf16[768,512]{1,0:T(8,128)(2,1)S(1)} %copy-done.53, bf16[768,128]{1,0:T(8,128)(2,1)S(1)} %copy-done.63, bf16[768,128]{1,0:T(8,128)(2,1)S(1)} %copy-done.65, ...), custom_call_target="tpu_custom_call" | custom-call | flops 1000000 | bytes 1000000 | tf_op jit(solution)/shard_map/attend_backward/pallas_call | solution.py:360
  469.1 7.3 %collective-permute-done.48 = bf16[2,1,1,1,128,2304]{5,4,3,2,1,0:T(8,128)(2,1)} collective-permute-done((bf16[2,1,1,1,128,2304]{5,4,3,2,1,0:T(8,128)(2,1)}, bf16[2,1,1,1,128,2304]{5,4,3,2,1,0:T(8,128)(2,1)}, u32[]{:S(2)}, u32[]{:S(2)}) %collective-permute-start.48) | collective-permute-done | bytes 1179680 | tf_op jit(solution)/shard_map/ppermute | solution.py:39
  481.7 2.2 add_convert_fusion.7
  487.6 13.0 %attend_backward.3 = (bf16[768,512]{1,0:T(8,128)(2,1)S(1)}, bf16[768,128]{1,0:T(8,128)(2,1)S(1)}, bf16[768,128]{1,0:T(8,128)(2,1)S(1)}) custom-call(bf16[768,512]{1,0:T(8,128)(2,1)S(1)} %copy-done.55, bf16[768,128]{1,0:T(8,128)(2,1)S(1)} %copy-done.67, bf16[768,128]{1,0:T(8,128)(2,1)S(1)} %copy-done.69, ...), custom_call_target="tpu_custom_call" | custom-call | flops 1000000 | bytes 1000000 | tf_op jit(solution)/shard_map/attend_backward/pallas_call | solution.py:360
  501.4 2.2 add_convert_fusion.20
  506.8 4.9 convolution_convert_fusion
  521.6 3.4 convolution_convert_fusion.3
  525.1 5.3 collective-permute-done.57
  532.7 13.2 %collective-permute-done.56 = bf16[2,2,1,2,128,640]{5,4,3,2,1,0:T(8,128)(2,1)S(1)} collective-permute-done((bf16[2,2,1,2,128,640]{5,4,3,2,1,0:T(8,128)(2,1)}, bf16[2,2,1,2,128,640]{5,4,3,2,1,0:T(8,128)(2,1)S(1)}, u32[]{:S(2)}, u32[]{:S(2)}) %collective-permute-start.56) | collective-permute-done | bytes 1310752 | tf_op jit(solution)/shard_map/ppermute | solution.py:39
  545.9 3.1 collective-permute-start.61
  553.5 2.6 fusion.6
  558.9 8.7 %back_rows.7 = (f32[384,2048]{1,0:T(8,128)}, bf16[384,2048]{1,0:T(8,128)(2,1)S(1)}) custom-call(bf16[768,768]{1,0:T(8,128)(2,1)S(1)} %copy-done.26, bf16[768,640]{1,0:T(8,128)(2,1)S(1)} %copy-done.32, bf16[2048,384]{1,0:T(8,128)(2,1)} %copy-done.11, bf16[2048,384]{1,0:T(8,128)(2,1)} %copy-done.12, bf16[2048,256]{1,0:T(8,128)(2,1)S(1)} %get-tuple-element.357.down_a.refs_4_, ...), custom_call_target="tpu_custom_call" | custom-call | flops 1000000 | bytes 1000000 | tf_op jit(solution)/shard_map/back_rows/pallas_call | solution.py:560
  568.1 3.0 reorder.4
  571.2 2.0 collective-permute-start.72
  574.1 2.3 add_convert_fusion.12
  579.5 2.7 select_convert_fusion.refs_0_
  582.2 2.5 reorder.5
  584.6 5.3 collective-permute-done.67
  589.9 2.5 unpack_columns.1
  592.5 10.9 %collective-permute-done.69 = bf16[1,2,1,1,128,1280]{5,4,3,2,1,0:T(8,128)(2,1)S(1)} collective-permute-done((bf16[1,2,1,1,128,1280]{5,4,3,2,1,0:T(8,128)(2,1)S(1)}, bf16[1,2,1,1,128,1280]{5,4,3,2,1,0:T(8,128)(2,1)S(1)}, u32[]{:S(2)}, u32[]{:S(2)}) %collective-permute-start.69) | collective-permute-done | bytes 655392 | tf_op jit(solution)/shard_map/ppermute | solution.py:39
  603.5 2.0 collective-permute-start.71
  607.7 12.8 %collective-permute-done.71 = bf16[1,1,1,1,128,1280]{5,4,3,2,1,0:T(8,128)(2,1)S(1)} collective-permute-done((bf16[1,1,1,1,128,1280]{5,4,3,2,1,0:T(8,128)(2,1)S(1)}, bf16[1,1,1,1,128,1280]{5,4,3,2,1,0:T(8,128)(2,1)S(1)}, u32[]{:S(2)}, u32[]{:S(2)}) %collective-permute-start.71) | collective-permute-done | bytes 327712 | tf_op jit(solution)/shard_map/ppermute | solution.py:39
  (490 shorter events, 165.4 us)
Async XLA Ops:
  7.1 20.7 %collective-permute-start.4 = (bf16[1,1,1,1,128,1280]{5,4,3,2,1,0:T(8,128)(2,1)}, bf16[1,1,1,1,128,1280]{5,4,3,2,1,0:T(8,128)(2,1)}, u32[]{:S(2)}, u32[]{:S(2)}) collective-permute-start(bf16[1,1,1,1,128,1280]{5,4,3,2,1,0:T(8,128)(2,1)} %maximum_bitcast_fusion), channel_id=1, source_target_pairs={{0,16},{2,18},{4,20},{6,22},{8,24},{10,26},{12,28},{14,30},{16,0},... | collective-permute-start | bytes 983048 | tf_op jit(solution)/shard_map/ppermute | solution.py:39
  25.2 12.6 %collective-permute-start.6 = (bf16[1,1,1,1,128,1024]{5,4,3,2,1,0:T(8,128)(2,1)S(1)}, bf16[1,1,1,1,128,1024]{5,4,3,2,1,0:T(8,128)(2,1)S(1)}, u32[]{:S(2)}, u32[]{:S(2)}) collective-permute-start(bf16[1,1,1,1,128,1024]{5,4,3,2,1,0:T(8,128)(2,1)S(1)} %bitcast.163), channel_id=1, source_target_pairs={{0,16},{2,18},{4,20},{6,22},{8,24},{10,26},{12,28},{14,30},{16,0},... | collective-permute-start | bytes 786440 | tf_op jit(solution)/shard_map/ppermute | solution.py:39
  28.9 19.5 %collective-permute-start.8 = (bf16[1,2,1,1,128,1280]{5,4,3,2,1,0:T(8,128)(2,1)S(1)}, bf16[1,2,1,1,128,1280]{5,4,3,2,1,0:T(8,128)(2,1)S(1)}, u32[]{:S(2)}, u32[]{:S(2)}) collective-permute-start(bf16[1,2,1,1,128,1280]{5,4,3,2,1,0:T(8,128)(2,1)S(1)} %pad_maximum_fusion.33), channel_id=1, source_target_pairs={{0,8},{2,10},{4,12},{6,14},{8,0},{10,2},{12,4},{14,6},{16,24},{18,... | collective-permute-start | bytes 1966088 | tf_op jit(solution)/shard_map/ppermute | solution.py:39
  30.3 40.6 %collective-permute-start.5 = (bf16[384,2048]{1,0:T(8,128)(2,1)S(1)}, bf16[384,2048]{1,0:T(8,128)(2,1)S(1)}, u32[]{:S(2)}, u32[]{:S(2)}) collective-permute-start(bf16[384,2048]{1,0:T(8,128)(2,1)S(1)} %fusion.4), channel_id=1, source_target_pairs={{0,1},{1,0},{2,3},{3,2},{4,5},{5,4},{6,7},{7,6},{8,9},{9,8},{10,11... | collective-permute-start | bytes 4718600 | tf_op jit(solution)/shard_map/ppermute | solution.py:43
  49.7 14.8 %collective-permute-start.10 = (bf16[2,2,1,1,128,640]{5,4,3,2,1,0:T(8,128)(2,1)S(1)}, bf16[2,2,1,1,128,640]{5,4,3,2,1,0:T(8,128)(2,1)S(1)}, u32[]{:S(2)}, u32[]{:S(2)}) collective-permute-start(bf16[2,2,1,1,128,640]{5,4,3,2,1,0:T(8,128)(2,1)S(1)} %get-tuple-element.266), channel_id=1, source_target_pairs={{0,2},{2,0},{4,6},{6,4},{8,10},{10,8},{12,14},{14,12},{16,18},{18,... | collective-permute-start | bytes 1966088 | tf_op jit(solution)/shard_map/ppermute | solution.py:39
  51.3 15.6 %collective-permute-start.9 = (bf16[2,2,1,1,128,640]{5,4,3,2,1,0:T(8,128)(2,1)S(1)}, bf16[2,2,1,1,128,640]{5,4,3,2,1,0:T(8,128)(2,1)S(1)}, u32[]{:S(2)}, u32[]{:S(2)}) collective-permute-start(bf16[2,2,1,1,128,640]{5,4,3,2,1,0:T(8,128)(2,1)S(1)} %get-tuple-element.267), channel_id=1, source_target_pairs={{0,4},{2,6},{4,0},{6,2},{8,12},{10,14},{12,8},{14,10},{16,20},{18,... | collective-permute-start | bytes 1966088 | tf_op jit(solution)/shard_map/ppermute | solution.py:39
  52.0 16.4 %collective-permute-start.13 = (bf16[1,1,1,1,128,2304]{5,4,3,2,1,0:T(8,128)(2,1)S(1)}, bf16[1,1,1,1,128,2304]{5,4,3,2,1,0:T(8,128)(2,1)S(1)}, u32[]{:S(2)}, u32[]{:S(2)}) collective-permute-start(bf16[1,1,1,1,128,2304]{5,4,3,2,1,0:T(8,128)(2,1)S(1)} %bitcast.144), channel_id=1, source_target_pairs={{0,8},{2,10},{4,12},{6,14},{8,0},{10,2},{12,4},{14,6},{16,24},{18,... | collective-permute-start | bytes 1769480 | tf_op jit(solution)/shard_map/ppermute | solution.py:39
  64.6 29.1 %collective-permute-start.12 = (bf16[2,2,1,2,128,640]{5,4,3,2,1,0:T(8,128)(2,1)S(1)}, bf16[2,2,1,2,128,640]{5,4,3,2,1,0:T(8,128)(2,1)S(1)}, u32[]{:S(2)}, u32[]{:S(2)}) collective-permute-start(bf16[2,2,1,2,128,640]{5,4,3,2,1,0:T(8,128)(2,1)S(1)} %pad_maximum_fusion.22), channel_id=1, source_target_pairs={{0,4},{2,6},{4,0},{6,2},{8,12},{10,14},{12,8},{14,10},{16,20},{18,... | collective-permute-start | bytes 3932168 | tf_op jit(solution)/shard_map/ppermute | solution.py:39
  67.0 26.7 %collective-permute-start.11 = (bf16[2,2,2,1,128,640]{5,4,3,2,1,0:T(8,128)(2,1)S(1)}, bf16[2,2,2,1,128,640]{5,4,3,2,1,0:T(8,128)(2,1)S(1)}, u32[]{:S(2)}, u32[]{:S(2)}) collective-permute-start(bf16[2,2,2,1,128,640]{5,4,3,2,1,0:T(8,128)(2,1)S(1)} %pad_maximum_fusion.23), channel_id=1, source_target_pairs={{0,2},{2,0},{4,6},{6,4},{8,10},{10,8},{12,14},{14,12},{16,18},{18,... | collective-permute-start | bytes 3932168 | tf_op jit(solution)/shard_map/ppermute | solution.py:39
  68.4 26.1 %collective-permute-start.7 = (bf16[1,2,1,1,128,1024]{5,4,3,2,1,0:T(8,128)(2,1)S(1)}, bf16[1,2,1,1,128,1024]{5,4,3,2,1,0:T(8,128)(2,1)S(1)}, u32[]{:S(2)}, u32[]{:S(2)}) collective-permute-start(bf16[1,2,1,1,128,1024]{5,4,3,2,1,0:T(8,128)(2,1)S(1)} %pad_maximum_fusion.35), channel_id=1, source_target_pairs={{0,8},{2,10},{4,12},{6,14},{8,0},{10,2},{12,4},{14,6},{16,24},{18,... | collective-permute-start | bytes 1572872 | tf_op jit(solution)/shard_map/ppermute | solution.py:39
  69.6 50.9 %collective-permute-start.14 = (bf16[2,1,1,1,128,2304]{5,4,3,2,1,0:T(8,128)(2,1)}, bf16[2,1,1,1,128,2304]{5,4,3,2,1,0:T(8,128)(2,1)}, u32[]{:S(2)}, u32[]{:S(2)}) collective-permute-start(bf16[2,1,1,1,128,2304]{5,4,3,2,1,0:T(8,128)(2,1)} %pad_maximum_fusion.25), channel_id=1, source_target_pairs={{0,16},{2,18},{4,20},{6,22},{8,24},{10,26},{12,28},{14,30},{16,0},... | collective-permute-start | bytes 3538952 | tf_op jit(solution)/shard_map/ppermute | solution.py:39
  70.9 69.2 %collective-permute-start.20 = (bf16[384,2048]{1,0:T(8,128)(2,1)}, bf16[384,2048]{1,0:T(8,128)(2,1)}, u32[]{:S(2)}, u32[]{:S(2)}) collective-permute-start(bf16[384,2048]{1,0:T(8,128)(2,1)} %pad_maximum_fusion.14), channel_id=1, source_target_pairs={{0,8},{2,10},{4,12},{6,14},{8,0},{10,2},{12,4},{14,6},{16,24},{18,... | collective-permute-start | bytes 4718600 | tf_op jit(solution)/shard_map/ppermute | solution.py:39
  94.7 19.9 %collective-permute-start.16 = (bf16[2,2,1,1,128,512]{5,4,3,2,1,0:T(8,128)(2,1)S(1)}, bf16[2,2,1,1,128,512]{5,4,3,2,1,0:T(8,128)(2,1)S(1)}, u32[]{:S(2)}, u32[]{:S(2)}) collective-permute-start(bf16[2,2,1,1,128,512]{5,4,3,2,1,0:T(8,128)(2,1)S(1)} %get-tuple-element.283), channel_id=1, source_target_pairs={{0,2},{2,0},{4,6},{6,4},{8,10},{10,8},{12,14},{14,12},{16,18},{18,... | collective-permute-start | bytes 1572872 | tf_op jit(solution)/shard_map/ppermute | solution.py:39
  95.4 21.0 %collective-permute-start.15 = (bf16[2,2,1,1,128,512]{5,4,3,2,1,0:T(8,128)(2,1)S(1)}, bf16[2,2,1,1,128,512]{5,4,3,2,1,0:T(8,128)(2,1)S(1)}, u32[]{:S(2)}, u32[]{:S(2)}) collective-permute-start(bf16[2,2,1,1,128,512]{5,4,3,2,1,0:T(8,128)(2,1)S(1)} %get-tuple-element.549), channel_id=1, source_target_pairs={{0,4},{2,6},{4,0},{6,2},{8,12},{10,14},{12,8},{14,10},{16,20},{18,... | collective-permute-start | bytes 1572872 | tf_op jit(solution)/shard_map/ppermute | solution.py:39
  115.9 24.3 %collective-permute-start.19 = (bf16[2,2,1,2,128,512]{5,4,3,2,1,0:T(8,128)(2,1)}, bf16[2,2,1,2,128,512]{5,4,3,2,1,0:T(8,128)(2,1)}, u32[]{:S(2)}, u32[]{:S(2)}) collective-permute-start(bf16[2,2,1,2,128,512]{5,4,3,2,1,0:T(8,128)(2,1)} %pad_maximum_fusion.27), channel_id=1, source_target_pairs={{0,4},{2,6},{4,0},{6,2},{8,12},{10,14},{12,8},{14,10},{16,20},{18,... | collective-permute-start | bytes 3145736 | tf_op jit(solution)/shard_map/ppermute | solution.py:39
  117.6 22.6 %collective-permute-start.18 = (bf16[2,2,2,1,128,512]{5,4,3,2,1,0:T(8,128)(2,1)}, bf16[2,2,2,1,128,512]{5,4,3,2,1,0:T(8,128)(2,1)}, u32[]{:S(2)}, u32[]{:S(2)}) collective-permute-start(bf16[2,2,2,1,128,512]{5,4,3,2,1,0:T(8,128)(2,1)} %pad_maximum_fusion.28), channel_id=1, source_target_pairs={{0,2},{2,0},{4,6},{6,4},{8,10},{10,8},{12,14},{14,12},{16,18},{18,... | collective-permute-start | bytes 3145736 | tf_op jit(solution)/shard_map/ppermute | solution.py:39
  120.5 27.6 %collective-permute-start.17 = (bf16[1,1,1,1,128,1920]{5,4,3,2,1,0:T(8,128)(2,1)}, bf16[1,1,1,1,128,1920]{5,4,3,2,1,0:T(8,128)(2,1)S(1)}, u32[]{:S(2)}, u32[]{:S(2)}) collective-permute-start(bf16[1,1,1,1,128,1920]{5,4,3,2,1,0:T(8,128)(2,1)} %bitcast.145), channel_id=1, source_target_pairs={{0,8},{2,10},{4,12},{6,14},{8,0},{10,2},{12,4},{14,6},{16,24},{18,... | collective-permute-start | bytes 1474568 | tf_op jit(solution)/shard_map/ppermute | solution.py:39
  140.2 23.0 %collective-permute-start.23 = (bf16[2,2,1,1,128,1152]{5,4,3,2,1,0:T(8,128)(2,1)S(1)}, bf16[2,2,1,1,128,1152]{5,4,3,2,1,0:T(8,128)(2,1)S(1)}, u32[]{:S(2)}, u32[]{:S(2)}) collective-permute-start(bf16[2,2,1,1,128,1152]{5,4,3,2,1,0:T(8,128)(2,1)S(1)} %get-tuple-element.300), channel_id=1, source_target_pairs={{0,4},{2,6},{4,0},{6,2},{8,12},{10,14},{12,8},{14,10},{16,20},{18,... | collective-permute-start | bytes 3538952 | tf_op jit(solution)/shard_map/ppermute | solution.py:39
  141.7 25.3 %collective-permute-start.22 = (bf16[2,2,1,1,128,1152]{5,4,3,2,1,0:T(8,128)(2,1)S(1)}, bf16[2,2,1,1,128,1152]{5,4,3,2,1,0:T(8,128)(2,1)S(1)}, u32[]{:S(2)}, u32[]{:S(2)}) collective-permute-start(bf16[2,2,1,1,128,1152]{5,4,3,2,1,0:T(8,128)(2,1)S(1)} %get-tuple-element.301), channel_id=1, source_target_pairs={{0,2},{2,0},{4,6},{6,4},{8,10},{10,8},{12,14},{14,12},{16,18},{18,... | collective-permute-start | bytes 3538952 | tf_op jit(solution)/shard_map/ppermute | solution.py:39
  151.3 19.2 %collective-permute-start.21 = (bf16[384,2048]{1,0:T(8,128)(2,1)S(1)}, bf16[384,2048]{1,0:T(8,128)(2,1)S(1)}, u32[]{:S(2)}, u32[]{:S(2)}) collective-permute-start(bf16[384,2048]{1,0:T(8,128)(2,1)S(1)} %add_convert_fusion.2), channel_id=1, source_target_pairs={{0,1},{1,0},{2,3},{3,2},{4,5},{5,4},{6,7},{7,6},{8,9},{9,8},{10,11... | collective-permute-start | bytes 4718600 | tf_op jit(solution)/shard_map/ppermute | solution.py:43
  151.6 24.3 %collective-permute-start.28 = (bf16[384,2048]{1,0:T(8,128)(2,1)S(1)}, bf16[384,2048]{1,0:T(8,128)(2,1)S(1)}, u32[]{:S(2)}, u32[]{:S(2)}) collective-permute-start(bf16[384,2048]{1,0:T(8,128)(2,1)S(1)} %copy-done.14), channel_id=1, source_target_pairs={{0,1},{1,0},{2,3},{3,2},{4,5},{5,4},{6,7},{7,6},{8,9},{9,8},{10,11... | collective-permute-start | bytes 4718600 | tf_op jit(solution)/shard_map/ppermute | solution.py:43
  151.9 28.8 %collective-permute-start.27 = (bf16[384,2048]{1,0:T(8,128)(2,1)}, bf16[384,2048]{1,0:T(8,128)(2,1)S(1)}, u32[]{:S(2)}, u32[]{:S(2)}) collective-permute-start(bf16[384,2048]{1,0:T(8,128)(2,1)} %collective-permute-done.20.refs_0_), channel_id=1, source_target_pairs={{0,1},{1,0},{2,3},{3,2},{4,5},{5,4},{6,7},{7,6},{8,9},{9,8},{10,11... | collective-permute-start | bytes 4718600 | tf_op jit(solution)/shard_map/ppermute | solution.py:43
  167.2 55.3 %collective-permute-start.29 = (bf16[2,2,2,1,128,1152]{5,4,3,2,1,0:T(8,128)(2,1)S(1)}, bf16[2,2,2,1,128,1152]{5,4,3,2,1,0:T(8,128)(2,1)}, u32[]{:S(2)}, u32[]{:S(2)}) collective-permute-start(bf16[2,2,2,1,128,1152]{5,4,3,2,1,0:T(8,128)(2,1)S(1)} %pad_maximum_fusion.7), channel_id=1, source_target_pairs={{0,2},{2,0},{4,6},{6,4},{8,10},{10,8},{12,14},{14,12},{16,18},{18,... | collective-permute-start | bytes 7077896 | tf_op jit(solution)/shard_map/ppermute | solution.py:39
  169.0 53.5 %collective-permute-start.30 = (bf16[2,2,1,2,128,1152]{5,4,3,2,1,0:T(8,128)(2,1)S(1)}, bf16[2,2,1,2,128,1152]{5,4,3,2,1,0:T(8,128)(2,1)}, u32[]{:S(2)}, u32[]{:S(2)}) collective-permute-start(bf16[2,2,1,2,128,1152]{5,4,3,2,1,0:T(8,128)(2,1)S(1)} %pad_maximum_fusion.6), channel_id=1, source_target_pairs={{0,4},{2,6},{4,0},{6,2},{8,12},{10,14},{12,8},{14,10},{16,20},{18,... | collective-permute-start | bytes 7077896 | tf_op jit(solution)/shard_map/ppermute | solution.py:39
  174.6 50.0 %collective-permute-start.25 = (bf16[384,2048]{1,0:T(8,128)(2,1)}, bf16[384,2048]{1,0:T(8,128)(2,1)S(1)}, u32[]{:S(2)}, u32[]{:S(2)}) collective-permute-start(bf16[384,2048]{1,0:T(8,128)(2,1)} %pad_maximum_fusion.15), channel_id=1, source_target_pairs={{0,8},{2,10},{4,12},{6,14},{8,0},{10,2},{12,4},{14,6},{16,24},{18,... | collective-permute-start | bytes 4718600 | tf_op jit(solution)/shard_map/ppermute | solution.py:39
  175.9 45.2 %collective-permute-start.26 = (bf16[2,1,1,1,128,1920]{5,4,3,2,1,0:T(8,128)(2,1)}, bf16[2,1,1,1,128,1920]{5,4,3,2,1,0:T(8,128)(2,1)S(1)}, u32[]{:S(2)}, u32[]{:S(2)}) collective-permute-start(bf16[2,1,1,1,128,1920]{5,4,3,2,1,0:T(8,128)(2,1)} %pad_maximum_fusion.30), channel_id=1, source_target_pairs={{0,16},{2,18},{4,20},{6,22},{8,24},{10,26},{12,28},{14,30},{16,0},... | collective-permute-start | bytes 2949128 | tf_op jit(solution)/shard_map/ppermute | solution.py:39
  180.7 49.5 %collective-permute-start.24 = (bf16[384,2048]{1,0:T(8,128)(2,1)S(1)}, bf16[384,2048]{1,0:T(8,128)(2,1)}, u32[]{:S(2)}, u32[]{:S(2)}) collective-permute-start(bf16[384,2048]{1,0:T(8,128)(2,1)S(1)} %multiply_convert_fusion.refs_0_), channel_id=1, source_target_pairs={{0,1},{1,0},{2,3},{3,2},{4,5},{5,4},{6,7},{7,6},{8,9},{9,8},{10,11... | collective-permute-start | bytes 4718600 | tf_op jit(solution)/shard_map/ppermute | solution.py:43
  222.6 32.6 %collective-permute-start.33 = (bf16[2,2,1,1,128,896]{5,4,3,2,1,0:T(8,128)(2,1)S(1)}, bf16[2,2,1,1,128,896]{5,4,3,2,1,0:T(8,128)(2,1)S(1)}, u32[]{:S(2)}, u32[]{:S(2)}) collective-permute-start(bf16[2,2,1,1,128,896]{5,4,3,2,1,0:T(8,128)(2,1)S(1)} %pad_maximum_fusion.31), channel_id=1, source_target_pairs={{0,2},{2,0},{4,6},{6,4},{8,10},{10,8},{12,14},{14,12},{16,18},{18,... | collective-permute-start | bytes 2752520 | tf_op jit(solution)/shard_map/ppermute | solution.py:39
  224.1 32.7 %collective-permute-start.32 = (bf16[2,2,1,1,128,1024]{5,4,3,2,1,0:T(8,128)(2,1)}, bf16[2,2,1,1,128,1024]{5,4,3,2,1,0:T(8,128)(2,1)S(1)}, u32[]{:S(2)}, u32[]{:S(2)}) collective-permute-start(bf16[2,2,1,1,128,1024]{5,4,3,2,1,0:T(8,128)(2,1)} %slice.400), channel_id=1, source_target_pairs={{0,4},{2,6},{4,0},{6,2},{8,12},{10,14},{12,8},{14,10},{16,20},{18,... | collective-permute-start | bytes 3145736 | tf_op jit(solution)/shard_map/ppermute | solution.py:39
  224.7 27.3 %collective-permute-start.31 = (bf16[384,2048]{1,0:T(8,128)(2,1)S(1)}, bf16[384,2048]{1,0:T(8,128)(2,1)}, u32[]{:S(2)}, u32[]{:S(2)}) collective-permute-start(bf16[384,2048]{1,0:T(8,128)(2,1)S(1)} %collective-permute-done.25.refs_0_), channel_id=1, source_target_pairs={{0,1},{1,0},{2,3},{3,2},{4,5},{5,4},{6,7},{7,6},{8,9},{9,8},{10,11... | collective-permute-start | bytes 4718600 | tf_op jit(solution)/shard_map/ppermute | solution.py:43
  260.4 48.7 %collective-permute-start.34 = (bf16[2,2,2,1,128,1024]{5,4,3,2,1,0:T(8,128)(2,1)}, bf16[2,2,2,1,128,1024]{5,4,3,2,1,0:T(8,128)(2,1)}, u32[]{:S(2)}, u32[]{:S(2)}) collective-permute-start(bf16[2,2,2,1,128,1024]{5,4,3,2,1,0:T(8,128)(2,1)} %pad_maximum_fusion.10), channel_id=1, source_target_pairs={{0,2},{2,0},{4,6},{6,4},{8,10},{10,8},{12,14},{14,12},{16,18},{18,... | collective-permute-start | bytes 6291464 | tf_op jit(solution)/shard_map/ppermute | solution.py:39
  262.1 43.2 %collective-permute-start.35 = (bf16[2,2,1,2,128,896]{5,4,3,2,1,0:T(8,128)(2,1)}, bf16[2,2,1,2,128,896]{5,4,3,2,1,0:T(8,128)(2,1)}, u32[]{:S(2)}, u32[]{:S(2)}) collective-permute-start(bf16[2,2,1,2,128,896]{5,4,3,2,1,0:T(8,128)(2,1)} %pad_maximum_fusion.13), channel_id=1, source_target_pairs={{0,4},{2,6},{4,0},{6,2},{8,12},{10,14},{12,8},{14,10},{16,20},{18,... | collective-permute-start | bytes 5505032 | tf_op jit(solution)/shard_map/ppermute | solution.py:39
  290.0 65.2 %collective-permute-start.38 = (bf16[2,2,1,2,128,1152]{5,4,3,2,1,0:T(8,128)(2,1)}, bf16[2,2,1,2,128,1152]{5,4,3,2,1,0:T(8,128)(2,1)}, u32[]{:S(2)}, u32[]{:S(2)}) collective-permute-start(bf16[2,2,1,2,128,1152]{5,4,3,2,1,0:T(8,128)(2,1)} %bitcast.186), channel_id=1, source_target_pairs={{0,4},{2,6},{4,0},{6,2},{8,12},{10,14},{12,8},{14,10},{16,20},{18,... | collective-permute-start | bytes 7077896 | tf_op jit(solution)/shard_map/ppermute | solution.py:39
  304.7 54.6 %collective-permute-start.37 = (bf16[2,2,2,1,128,1152]{5,4,3,2,1,0:T(8,128)(2,1)}, bf16[2,2,2,1,128,1152]{5,4,3,2,1,0:T(8,128)(2,1)}, u32[]{:S(2)}, u32[]{:S(2)}) collective-permute-start(bf16[2,2,2,1,128,1152]{5,4,3,2,1,0:T(8,128)(2,1)} %bitcast.187), channel_id=1, source_target_pairs={{0,2},{2,0},{4,6},{6,4},{8,10},{10,8},{12,14},{14,12},{16,18},{18,... | collective-permute-start | bytes 7077896 | tf_op jit(solution)/shard_map/ppermute | solution.py:39
  342.3 22.2 %collective-permute-start.36 = (bf16[384,2048]{1,0:T(8,128)(2,1)}, bf16[384,2048]{1,0:T(8,128)(2,1)S(1)}, u32[]{:S(2)}, u32[]{:S(2)}) collective-permute-start(bf16[384,2048]{1,0:T(8,128)(2,1)} %get-tuple-element.365), channel_id=1, source_target_pairs={{0,1},{1,0},{2,3},{3,2},{4,5},{5,4},{6,7},{7,6},{8,9},{9,8},{10,11... | collective-permute-start | bytes 4718600 | tf_op jit(solution)/shard_map/ppermute | solution.py:43
  357.7 47.7 %collective-permute-start.40 = (bf16[2,2,1,1,128,1152]{5,4,3,2,1,0:T(8,128)(2,1)}, bf16[2,2,1,1,128,1152]{5,4,3,2,1,0:T(8,128)(2,1)}, u32[]{:S(2)}, u32[]{:S(2)}) collective-permute-start(bf16[2,2,1,1,128,1152]{5,4,3,2,1,0:T(8,128)(2,1)} %add_convert_fusion.6), channel_id=1, source_target_pairs={{0,2},{2,0},{4,6},{6,4},{8,10},{10,8},{12,14},{14,12},{16,18},{18,... | collective-permute-start | bytes 3538952 | tf_op jit(solution)/shard_map/ppermute | solution.py:39
  361.9 43.6 %collective-permute-start.41 = (bf16[2,2,1,1,128,1152]{5,4,3,2,1,0:T(8,128)(2,1)}, bf16[2,2,1,1,128,1152]{5,4,3,2,1,0:T(8,128)(2,1)}, u32[]{:S(2)}, u32[]{:S(2)}) collective-permute-start(bf16[2,2,1,1,128,1152]{5,4,3,2,1,0:T(8,128)(2,1)} %add_convert_fusion.5), channel_id=1, source_target_pairs={{0,4},{2,6},{4,0},{6,2},{8,12},{10,14},{12,8},{14,10},{16,20},{18,... | collective-permute-start | bytes 3538952 | tf_op jit(solution)/shard_map/ppermute | solution.py:39
  366.5 45.3 %collective-permute-start.42 = (bf16[384,2048]{1,0:T(8,128)(2,1)}, bf16[384,2048]{1,0:T(8,128)(2,1)}, u32[]{:S(2)}, u32[]{:S(2)}) collective-permute-start(bf16[384,2048]{1,0:T(8,128)(2,1)} %pad_maximum_fusion.16), channel_id=1, source_target_pairs={{0,8},{2,10},{4,12},{6,14},{8,0},{10,2},{12,4},{14,6},{16,24},{18,... | collective-permute-start | bytes 4718600 | tf_op jit(solution)/shard_map/ppermute | solution.py:39
  390.0 48.9 %collective-permute-start.44 = (bf16[2,2,2,1,128,1024]{5,4,3,2,1,0:T(8,128)(2,1)}, bf16[2,2,2,1,128,1024]{5,4,3,2,1,0:T(8,128)(2,1)}, u32[]{:S(2)}, u32[]{:S(2)}) collective-permute-start(bf16[2,2,2,1,128,1024]{5,4,3,2,1,0:T(8,128)(2,1)} %bitcast.188), channel_id=1, source_target_pairs={{0,2},{2,0},{4,6},{6,4},{8,10},{10,8},{12,14},{14,12},{16,18},{18,... | collective-permute-start | bytes 6291464 | tf_op jit(solution)/shard_map/ppermute | solution.py:39
  391.3 44.3 %collective-permute-start.45 = (bf16[2,2,1,2,128,896]{5,4,3,2,1,0:T(8,128)(2,1)}, bf16[2,2,1,2,128,896]{5,4,3,2,1,0:T(8,128)(2,1)}, u32[]{:S(2)}, u32[]{:S(2)}) collective-permute-start(bf16[2,2,1,2,128,896]{5,4,3,2,1,0:T(8,128)(2,1)} %bitcast.189), channel_id=1, source_target_pairs={{0,4},{2,6},{4,0},{6,2},{8,12},{10,14},{12,8},{14,10},{16,20},{18,... | collective-permute-start | bytes 5505032 | tf_op jit(solution)/shard_map/ppermute | solution.py:39
  420.6 21.0 %collective-permute-start.43 = (bf16[384,2048]{1,0:T(8,128)(2,1)}, bf16[384,2048]{1,0:T(8,128)(2,1)}, u32[]{:S(2)}, u32[]{:S(2)}) collective-permute-start(bf16[384,2048]{1,0:T(8,128)(2,1)} %get-tuple-element.391), channel_id=1, source_target_pairs={{0,1},{1,0},{2,3},{3,2},{4,5},{5,4},{6,7},{7,6},{8,9},{9,8},{10,11... | collective-permute-start | bytes 4718600 | tf_op jit(solution)/shard_map/ppermute | solution.py:43
  421.0 55.4 %collective-permute-start.48 = (bf16[2,1,1,1,128,2304]{5,4,3,2,1,0:T(8,128)(2,1)}, bf16[2,1,1,1,128,2304]{5,4,3,2,1,0:T(8,128)(2,1)}, u32[]{:S(2)}, u32[]{:S(2)}) collective-permute-start(bf16[2,1,1,1,128,2304]{5,4,3,2,1,0:T(8,128)(2,1)} %fusion.15), channel_id=1, source_target_pairs={{0,16},{2,18},{4,20},{6,22},{8,24},{10,26},{12,28},{14,30},{16,0},... | collective-permute-start | bytes 3538952 | tf_op jit(solution)/shard_map/ppermute | solution.py:39
  435.5 15.7 %collective-permute-start.49 = (bf16[384,2048]{1,0:T(8,128)(2,1)S(1)}, bf16[384,2048]{1,0:T(8,128)(2,1)S(1)}, u32[]{:S(2)}, u32[]{:S(2)}) collective-permute-start(bf16[384,2048]{1,0:T(8,128)(2,1)S(1)} %get-tuple-element.397), channel_id=1, source_target_pairs={{0,1},{1,0},{2,3},{3,2},{4,5},{5,4},{6,7},{7,6},{8,9},{9,8},{10,11... | collective-permute-start | bytes 4718600 | tf_op jit(solution)/shard_map/ppermute | solution.py:43
  438.1 41.8 %collective-permute-start.47 = (bf16[2,2,1,1,128,896]{5,4,3,2,1,0:T(8,128)(2,1)}, bf16[2,2,1,1,128,896]{5,4,3,2,1,0:T(8,128)(2,1)}, u32[]{:S(2)}, u32[]{:S(2)}) collective-permute-start(bf16[2,2,1,1,128,896]{5,4,3,2,1,0:T(8,128)(2,1)} %add_convert_fusion.10), channel_id=1, source_target_pairs={{0,2},{2,0},{4,6},{6,4},{8,10},{10,8},{12,14},{14,12},{16,18},{18,... | collective-permute-start | bytes 2752520 | tf_op jit(solution)/shard_map/ppermute | solution.py:39
  440.6 41.1 %collective-permute-start.50 = (bf16[2,2,1,1,128,1024]{5,4,3,2,1,0:T(8,128)(2,1)S(1)}, bf16[2,2,1,1,128,1024]{5,4,3,2,1,0:T(8,128)(2,1)}, u32[]{:S(2)}, u32[]{:S(2)}) collective-permute-start(bf16[2,2,1,1,128,1024]{5,4,3,2,1,0:T(8,128)(2,1)S(1)} %add_convert_fusion.8), channel_id=1, source_target_pairs={{0,4},{2,6},{4,0},{6,2},{8,12},{10,14},{12,8},{14,10},{16,20},{18,... | collective-permute-start | bytes 3145736 | tf_op jit(solution)/shard_map/ppermute | solution.py:39
  450.0 54.5 %collective-permute-start.52 = (bf16[2,2,2,1,128,512]{5,4,3,2,1,0:T(8,128)(2,1)}, bf16[2,2,2,1,128,512]{5,4,3,2,1,0:T(8,128)(2,1)}, u32[]{:S(2)}, u32[]{:S(2)}) collective-permute-start(bf16[2,2,2,1,128,512]{5,4,3,2,1,0:T(8,128)(2,1)} %slice.414), channel_id=1, source_target_pairs={{0,2},{2,0},{4,6},{6,4},{8,10},{10,8},{12,14},{14,12},{16,18},{18,... | collective-permute-start | bytes 3145736 | tf_op jit(solution)/shard_map/ppermute | solution.py:39
  452.1 127.4 %collective-permute-start.65 = (bf16[384,2048]{1,0:T(8,128)(2,1)S(1)}, bf16[384,2048]{1,0:T(8,128)(2,1)}, u32[]{:S(2)}, u32[]{:S(2)}) collective-permute-start(bf16[384,2048]{1,0:T(8,128)(2,1)S(1)} %pad_maximum_fusion.17), channel_id=1, source_target_pairs={{0,8},{2,10},{4,12},{6,14},{8,0},{10,2},{12,4},{14,6},{16,24},{18,... | collective-permute-start | bytes 4718600 | tf_op jit(solution)/shard_map/ppermute | solution.py:39
  476.4 25.0 %collective-permute-start.46 = (bf16[2,2,1,2,128,512]{5,4,3,2,1,0:T(8,128)(2,1)}, bf16[2,2,1,2,128,512]{5,4,3,2,1,0:T(8,128)(2,1)}, u32[]{:S(2)}, u32[]{:S(2)}) collective-permute-start(bf16[2,2,1,2,128,512]{5,4,3,2,1,0:T(8,128)(2,1)} %slice.412), channel_id=1, source_target_pairs={{0,4},{2,6},{4,0},{6,2},{8,12},{10,14},{12,8},{14,10},{16,20},{18,... | collective-permute-start | bytes 3145736 | tf_op jit(solution)/shard_map/ppermute | solution.py:39
  485.0 45.5 %collective-permute-start.57 = (bf16[2,1,1,1,128,1920]{5,4,3,2,1,0:T(8,128)(2,1)}, bf16[2,1,1,1,128,1920]{5,4,3,2,1,0:T(8,128)(2,1)}, u32[]{:S(2)}, u32[]{:S(2)}) collective-permute-start(bf16[2,1,1,1,128,1920]{5,4,3,2,1,0:T(8,128)(2,1)} %fusion.16), channel_id=1, source_target_pairs={{0,16},{2,18},{4,20},{6,22},{8,24},{10,26},{12,28},{14,30},{16,0},... | collective-permute-start | bytes 2949128 | tf_op jit(solution)/shard_map/ppermute | solution.py:39
  505.7 14.6 %collective-permute-start.53 = (bf16[2,2,1,1,128,512]{5,4,3,2,1,0:T(8,128)(2,1)S(1)}, bf16[2,2,1,1,128,512]{5,4,3,2,1,0:T(8,128)(2,1)S(1)}, u32[]{:S(2)}, u32[]{:S(2)}) collective-permute-start(bf16[2,2,1,1,128,512]{5,4,3,2,1,0:T(8,128)(2,1)S(1)} %add_convert_fusion.19), channel_id=1, source_target_pairs={{0,4},{2,6},{4,0},{6,2},{8,12},{10,14},{12,8},{14,10},{16,20},{18,... | collective-permute-start | bytes 1572872 | tf_op jit(solution)/shard_map/ppermute | solution.py:39
  514.7 31.2 %collective-permute-start.56 = (bf16[2,2,1,2,128,640]{5,4,3,2,1,0:T(8,128)(2,1)}, bf16[2,2,1,2,128,640]{5,4,3,2,1,0:T(8,128)(2,1)S(1)}, u32[]{:S(2)}, u32[]{:S(2)}) collective-permute-start(bf16[2,2,1,2,128,640]{5,4,3,2,1,0:T(8,128)(2,1)} %slice.424), channel_id=1, source_target_pairs={{0,4},{2,6},{4,0},{6,2},{8,12},{10,14},{12,8},{14,10},{16,20},{18,... | collective-permute-start | bytes 3932168 | tf_op jit(solution)/shard_map/ppermute | solution.py:39
  515.9 34.2 %collective-permute-start.55 = (bf16[2,2,2,1,128,640]{5,4,3,2,1,0:T(8,128)(2,1)}, bf16[2,2,2,1,128,640]{5,4,3,2,1,0:T(8,128)(2,1)S(1)}, u32[]{:S(2)}, u32[]{:S(2)}) collective-permute-start(bf16[2,2,2,1,128,640]{5,4,3,2,1,0:T(8,128)(2,1)} %slice.423), channel_id=1, source_target_pairs={{0,2},{2,0},{4,6},{6,4},{8,10},{10,8},{12,14},{14,12},{16,18},{18,... | collective-permute-start | bytes 3932168 | tf_op jit(solution)/shard_map/ppermute | solution.py:39
  525.0 27.2 %collective-permute-start.58 = (bf16[384,2048]{1,0:T(8,128)(2,1)}, bf16[384,2048]{1,0:T(8,128)(2,1)S(1)}, u32[]{:S(2)}, u32[]{:S(2)}) collective-permute-start(bf16[384,2048]{1,0:T(8,128)(2,1)} %convolution_convert_fusion.3), channel_id=1, source_target_pairs={{0,1},{1,0},{2,3},{3,2},{4,5},{5,4},{6,7},{7,6},{8,9},{9,8},{10,11... | collective-permute-start | bytes 4718600 | tf_op jit(solution)/shard_map/ppermute | solution.py:43
  530.5 26.8 %collective-permute-start.54 = (bf16[1,2,1,1,128,1024]{5,4,3,2,1,0:T(8,128)(2,1)S(1)}, bf16[1,2,1,1,128,1024]{5,4,3,2,1,0:T(8,128)(2,1)}, u32[]{:S(2)}, u32[]{:S(2)}) collective-permute-start(bf16[1,2,1,1,128,1024]{5,4,3,2,1,0:T(8,128)(2,1)S(1)} %pad_maximum_fusion.34), channel_id=1, source_target_pairs={{0,8},{2,10},{4,12},{6,14},{8,0},{10,2},{12,4},{14,6},{16,24},{18,... | collective-permute-start | bytes 1572872 | tf_op jit(solution)/shard_map/ppermute | solution.py:39
  545.9 21.6 %collective-permute-start.61 = (bf16[1,1,1,1,128,1920]{5,4,3,2,1,0:T(8,128)(2,1)}, bf16[1,1,1,1,128,1920]{5,4,3,2,1,0:T(8,128)(2,1)S(1)}, u32[]{:S(2)}, u32[]{:S(2)}) collective-permute-start(bf16[1,1,1,1,128,1920]{5,4,3,2,1,0:T(8,128)(2,1)} %slice.523), channel_id=1, source_target_pairs={{0,8},{2,10},{4,12},{6,14},{8,0},{10,2},{12,4},{14,6},{16,24},{18,... | collective-permute-start | bytes 1474568 | tf_op jit(solution)/shard_map/ppermute | solution.py:39
  551.2 21.9 %collective-permute-start.64 = (bf16[2,2,1,1,128,640]{5,4,3,2,1,0:T(8,128)(2,1)}, bf16[2,2,1,1,128,640]{5,4,3,2,1,0:T(8,128)(2,1)}, u32[]{:S(2)}, u32[]{:S(2)}) collective-permute-start(bf16[2,2,1,1,128,640]{5,4,3,2,1,0:T(8,128)(2,1)} %add_convert_fusion.14), channel_id=1, source_target_pairs={{0,4},{2,6},{4,0},{6,2},{8,12},{10,14},{12,8},{14,10},{16,20},{18,... | collective-permute-start | bytes 1966088 | tf_op jit(solution)/shard_map/ppermute | solution.py:39
  552.3 18.9 %collective-permute-start.63 = (bf16[2,2,1,1,128,640]{5,4,3,2,1,0:T(8,128)(2,1)}, bf16[2,2,1,1,128,640]{5,4,3,2,1,0:T(8,128)(2,1)}, u32[]{:S(2)}, u32[]{:S(2)}) collective-permute-start(bf16[2,2,1,1,128,640]{5,4,3,2,1,0:T(8,128)(2,1)} %add_convert_fusion.15), channel_id=1, source_target_pairs={{0,2},{2,0},{4,6},{6,4},{8,10},{10,8},{12,14},{14,12},{16,18},{18,... | collective-permute-start | bytes 1966088 | tf_op jit(solution)/shard_map/ppermute | solution.py:39
  567.8 22.0 %collective-permute-start.67 = (bf16[1,1,1,1,128,2304]{5,4,3,2,1,0:T(8,128)(2,1)}, bf16[1,1,1,1,128,2304]{5,4,3,2,1,0:T(8,128)(2,1)S(1)}, u32[]{:S(2)}, u32[]{:S(2)}) collective-permute-start(bf16[1,1,1,1,128,2304]{5,4,3,2,1,0:T(8,128)(2,1)} %slice.522), channel_id=1, source_target_pairs={{0,8},{2,10},{4,12},{6,14},{8,0},{10,2},{12,4},{14,6},{16,24},{18,... | collective-permute-start | bytes 1769480 | tf_op jit(solution)/shard_map/ppermute | solution.py:39
  571.2 35.5 %collective-permute-start.72 = (bf16[1,1,1,1,128,1024]{5,4,3,2,1,0:T(8,128)(2,1)S(1)}, bf16[1,1,1,1,128,1024]{5,4,3,2,1,0:T(8,128)(2,1)S(1)}, u32[]{:S(2)}, u32[]{:S(2)}) collective-permute-start(bf16[1,1,1,1,128,1024]{5,4,3,2,1,0:T(8,128)(2,1)S(1)} %slice.431), channel_id=1, source_target_pairs={{0,16},{2,18},{4,20},{6,22},{8,24},{10,26},{12,28},{14,30},{16,0},... | collective-permute-start | bytes 786440 | tf_op jit(solution)/shard_map/ppermute | solution.py:39
  576.8 26.6 %collective-permute-start.69 = (bf16[1,2,1,1,128,1280]{5,4,3,2,1,0:T(8,128)(2,1)S(1)}, bf16[1,2,1,1,128,1280]{5,4,3,2,1,0:T(8,128)(2,1)S(1)}, u32[]{:S(2)}, u32[]{:S(2)}) collective-permute-start(bf16[1,2,1,1,128,1280]{5,4,3,2,1,0:T(8,128)(2,1)S(1)} %fusion.19), channel_id=1, source_target_pairs={{0,8},{2,10},{4,12},{6,14},{8,0},{10,2},{12,4},{14,6},{16,24},{18,... | collective-permute-start | bytes 1966088 | tf_op jit(solution)/shard_map/ppermute | solution.py:39
  578.7 13.7 %collective-permute-start.66 = (f32[2,2,1,1,2,128]{5,4,3,2,1,0:T(2,128)S(1)}, f32[2,2,1,1,2,128]{5,4,3,2,1,0:T(2,128)S(1)}, u32[]{:S(2)}, u32[]{:S(2)}) collective-permute-start(f32[2,2,1,1,2,128]{5,4,3,2,1,0:T(2,128)S(1)} %slice.438), channel_id=1, source_target_pairs={{0,2},{2,0},{4,6},{6,4},{8,10},{10,8},{12,14},{14,12},{16,18},{18,... | collective-permute-start | bytes 12296 | tf_op jit(solution)/shard_map/ppermute | solution.py:39
  592.4 13.1 %collective-permute-start.68 = (f32[1,2,1,1,2,128]{5,4,3,2,1,0:T(2,128)S(1)}, f32[1,2,1,1,2,128]{5,4,3,2,1,0:T(2,128)S(1)}, u32[]{:S(2)}, u32[]{:S(2)}) collective-permute-start(f32[1,2,1,1,2,128]{5,4,3,2,1,0:T(2,128)S(1)} %slice.443), channel_id=1, source_target_pairs={{0,8},{2,10},{4,12},{6,14},{8,0},{10,2},{12,4},{14,6},{16,24},{18,... | collective-permute-start | bytes 6152 | tf_op jit(solution)/shard_map/ppermute | solution.py:39
  603.5 17.0 %collective-permute-start.71 = (bf16[1,1,1,1,128,1280]{5,4,3,2,1,0:T(8,128)(2,1)S(1)}, bf16[1,1,1,1,128,1280]{5,4,3,2,1,0:T(8,128)(2,1)S(1)}, u32[]{:S(2)}, u32[]{:S(2)}) collective-permute-start(bf16[1,1,1,1,128,1280]{5,4,3,2,1,0:T(8,128)(2,1)S(1)} %slice.444), channel_id=1, source_target_pairs={{0,16},{2,18},{4,20},{6,22},{8,24},{10,26},{12,28},{14,30},{16,0},... | collective-permute-start | bytes 983048 | tf_op jit(solution)/shard_map/ppermute | solution.py:39
  605.5 16.6 %collective-permute-start.70 = (f32[1,1,1,1,2,128]{5,4,3,2,1,0:T(2,128)S(1)}, f32[1,1,1,1,2,128]{5,4,3,2,1,0:T(2,128)S(1)}, u32[]{:S(2)}, u32[]{:S(2)}) collective-permute-start(f32[1,1,1,1,2,128]{5,4,3,2,1,0:T(2,128)S(1)} %slice.446), channel_id=1, source_target_pairs={{0,16},{2,18},{4,20},{6,22},{8,24},{10,26},{12,28},{14,30},{16,0},... | collective-permute-start | bytes 3080 | tf_op jit(solution)/shard_map/ppermute | solution.py:39
  (126 other events, 1366.4 us)

commit v5 on v4

--- a/solution.py
+++ b/solution.py
@@ -939,8 +939,6 @@
         queries_a, keys_a, values_a, matmul(held(grad_attended), oa).astype(bf16), *tables, totals_a
     )
     did(d_query_a)
-    r0 = r0()
-    r0_t = send(row_major(part(r0, T, 1).astype(bf16)), T)
     r1 = joined(r1a, r1a_x, r1b, r1b_y)
     for bit in rest[:0:-1]:
         r1 = fold(r1, bit)()
@@ -964,6 +962,8 @@
     qkv_a, qkv_b = columns(grad_qkv, 0, cut), columns(grad_qkv, cut, 2 * cut)
     rqa_y = send(row_major(part(qkv_a, Y, 1)), Y)
     rqb_x = send(row_major(part(qkv_b, X, 1)), X)
+    r0 = r0()
+    r0_t = send(row_major(part(r0, T, 1).astype(bf16)), T)
     out = fold(joined(out_a, roa_x, out_b, rob_y), T)
     d_came = swap(contract_cols(rows_of(held(d_qkv), 1 - core), query_w).astype(bf16))
     r1 = r1()

time: 627 us -> 620 us (0.989)
  transfers between devices with their start and end apart: 73 -> 73, of which waited for: 26 -> 23; matrix products, arithmetic and copies ran while one was open for 19% -> 20% of each run, Pallas kernels for 36% -> 37%
where the time goes in v5:
time: 620 us; the launch traced here: 616 us
  Pallas kernels  227 us (37%)
  waiting for transfers between devices  166 us (27%)
  other arithmetic  86.7 us (14%)
  starting transfers between devices  65.3 us (11%)
  local copies, waits for them, and re-layouts  42.7 us (7%)
  matrix products  25.6 us (4%)
    ppermute x60, waiting for transfers between devices, exchange(): return lax.ppermute(values, 'dp', [(i, i ^ 1 << bit) for i in range(size)])  166 us
    ppermute x60, starting transfers between devices, exchange(): return lax.ppermute(values, 'dp', [(i, i ^ 1 << bit) for i in range(size)])  63.8 us
    pallas_call x4, Pallas kernels, hidden_rows(): pl.pallas_call(hidden_kernel, grid=(total // height,), in_specs=[tall, ta...  52.7 us
    pallas_call x4, Pallas kernels, back_rows(): pl.pallas_call(functools.partial(back_kernel, cuts), grid=(depth // high,...  45 us
    pallas_call x4, Pallas kernels, weight_grads(): pl.pallas_call(functools.partial(weight_grad_kernel, inner), grid=(depth...  44.8 us
    unnamed x236, local copies, waits for them, and re-layouts  30.8 us
    pallas_call x2, Pallas kernels, attend_forward(): pl.pallas_call(functools.partial(forward_kernel, group == 1), grid=(own,)...  26.4 us
    pallas_call x2, Pallas kernels, attend_backward(): pl.pallas_call(backward_kernel, grid=(width // LANES,), in_specs=[column,...  26.1 us
  transfers between devices with their start and end apart: 73, of which 23 were waited for; matrix products, arithmetic and copies ran while one was open for 20% of the time, Pallas kernels for 37%

profile of v5, /device:TPU:0, one launch (start us, length us, event | category | flops | bytes accessed | tf_op | source)
XLA Modules:
  0.0 616.0 jit_solution(17653786975191028714)
XLA Ops:
  1.3 4.0 collective-permute-start
  13.1 2.0 collective-permute-start.1
  21.5 2.2 collective-permute-done.2
  25.2 2.6 collective-permute-start.6
  30.4 7.4 %collective-permute-done.6 = bf16[1,1,1,1,128,1024]{5,4,3,2,1,0:T(8,128)(2,1)S(1)} collective-permute-done((bf16[1,1,1,1,128,1024]{5,4,3,2,1,0:T(8,128)(2,1)S(1)}, bf16[1,1,1,1,128,1024]{5,4,3,2,1,0:T(8,128)(2,1)S(1)}, u32[]{:S(2)}, u32[]{:S(2)}) %collective-permute-start.6) | collective-permute-done | bytes 262176 | tf_op jit(solution)/shard_map/ppermute | solution.py:39
  37.8 10.6 %collective-permute-done.8 = bf16[1,2,1,1,128,1280]{5,4,3,2,1,0:T(8,128)(2,1)S(1)} collective-permute-done((bf16[1,2,1,1,128,1280]{5,4,3,2,1,0:T(8,128)(2,1)S(1)}, bf16[1,2,1,1,128,1280]{5,4,3,2,1,0:T(8,128)(2,1)S(1)}, u32[]{:S(2)}, u32[]{:S(2)}) %collective-permute-start.8) | collective-permute-done | bytes 655392 | tf_op jit(solution)/shard_map/ppermute | solution.py:39
  52.2 12.3 %collective-permute-done.10 = bf16[2,2,1,1,128,640]{5,4,3,2,1,0:T(8,128)(2,1)S(1)} collective-permute-done((bf16[2,2,1,1,128,640]{5,4,3,2,1,0:T(8,128)(2,1)S(1)}, bf16[2,2,1,1,128,640]{5,4,3,2,1,0:T(8,128)(2,1)S(1)}, u32[]{:S(2)}, u32[]{:S(2)}) %collective-permute-start.10) | collective-permute-done | bytes 655392 | tf_op jit(solution)/shard_map/ppermute | solution.py:39
  65.0 1.9 collective-permute-done.9
  74.4 19.4 %collective-permute-done.12 = bf16[2,2,1,2,128,640]{5,4,3,2,1,0:T(8,128)(2,1)S(1)} collective-permute-done((bf16[2,2,1,2,128,640]{5,4,3,2,1,0:T(8,128)(2,1)S(1)}, bf16[2,2,1,2,128,640]{5,4,3,2,1,0:T(8,128)(2,1)S(1)}, u32[]{:S(2)}, u32[]{:S(2)}) %collective-permute-start.12) | collective-permute-done | bytes 1310752 | tf_op jit(solution)/shard_map/ppermute | solution.py:39
  96.9 4.3 fusion.14.q_ref.k_ref.v_ref
  101.2 13.3 %attend_forward.2 = (bf16[768,512]{1,0:T(8,128)(2,1)S(1)}, bf16[768,512]{1,0:T(8,128)(2,1)S(1)}, bf16[768,128]{1,0:T(8,128)(2,1)S(1)}, bf16[768,128]{1,0:T(8,128)(2,1)S(1)}, f32[4,1,1536]{2,1,0:T(1,128)S(1)}) custom-call(f32[768,1280]{1,0:T(8,128)S(1)} %fusion.14.q_ref.k_ref.v_ref, f32[768,1280]{1,0:T(8,128)S(1)} %fusion.14.q_ref.k_ref.v_ref, ...), custom_call_target="tpu_custom_call" | custom-call | flops 1000000 | bytes 1000000 | tf_op jit(solution)/shard_map/attend_forward/pallas_call | solution.py:329
  124.4 13.1 %attend_forward.3 = (bf16[768,512]{1,0:T(8,128)(2,1)S(1)}, bf16[768,512]{1,0:T(8,128)(2,1)S(1)}, bf16[768,128]{1,0:T(8,128)(2,1)S(1)}, bf16[768,128]{1,0:T(8,128)(2,1)S(1)}, f32[4,1,1536]{2,1,0:T(1,128)S(1)}) custom-call(f32[768,1280]{1,0:T(8,128)S(1)} %copy-done.1, f32[768,1280]{1,0:T(8,128)S(1)} %copy-done.1, f32[768,1280]{1,0:T(8,128)S(1)} %copy-done.1, ...), custom_call_target="tpu_custom_call" | custom-call | flops 1000000 | bytes 1000000 | tf_op jit(solution)/shard_map/attend_forward/pallas_call | solution.py:329
  137.6 2.6 collective-permute-done.20.refs_0_
  144.2 2.2 pad_maximum_fusion.9
  154.2 8.9 %collective-permute-done.23 = bf16[2,2,1,1,128,1152]{5,4,3,2,1,0:T(8,128)(2,1)S(1)} collective-permute-done((bf16[2,2,1,1,128,1152]{5,4,3,2,1,0:T(8,128)(2,1)S(1)}, bf16[2,2,1,1,128,1152]{5,4,3,2,1,0:T(8,128)(2,1)S(1)}, u32[]{:S(2)}, u32[]{:S(2)}) %collective-permute-start.23) | collective-permute-done | bytes 1179680 | tf_op jit(solution)/shard_map/ppermute | solution.py:39
  163.2 3.9 collective-permute-done.22
  180.5 3.1 stack_rows.5
  185.3 35.7 %collective-permute-done.26 = bf16[2,1,1,1,128,1920]{5,4,3,2,1,0:T(8,128)(2,1)S(1)} collective-permute-done((bf16[2,1,1,1,128,1920]{5,4,3,2,1,0:T(8,128)(2,1)}, bf16[2,1,1,1,128,1920]{5,4,3,2,1,0:T(8,128)(2,1)S(1)}, u32[]{:S(2)}, u32[]{:S(2)}) %collective-permute-start.26) | collective-permute-done | bytes 983072 | tf_op jit(solution)/shard_map/ppermute | solution.py:39
  224.6 5.6 join_weights.2
  230.1 3.9 stack_rows.6
  237.4 14.5 %hidden_rows.4 = (bf16[768,768]{1,0:T(8,128)(2,1)S(1)}, bf16[768,768]{1,0:T(8,128)(2,1)S(1)}, bf16[768,768]{1,0:T(8,128)(2,1)S(1)}) custom-call(bf16[768,2048]{1,0:T(8,128)(2,1)} %copy-done.17, bf16[768,2048]{1,0:T(8,128)(2,1)} %copy-done.15, bf16[2048,768]{1,0:T(8,128)(2,1)} %get-tuple-element.327.gate_ref.refs_4_, ...), custom_call_target="tpu_custom_call" | custom-call | flops 1000000 | bytes 1000000 | tf_op jit(solution)/shard_map/hidden_rows/pallas_call | solution.py:480
  252.0 3.2 stack_rows.7
  256.8 3.5 pad_maximum_fusion.10
  262.4 14.7 %hidden_rows.5 = (bf16[768,768]{1,0:T(8,128)(2,1)S(1)}, bf16[768,768]{1,0:T(8,128)(2,1)S(1)}, bf16[768,768]{1,0:T(8,128)(2,1)S(1)}) custom-call(bf16[768,2048]{1,0:T(8,128)(2,1)} %copy-done.18, bf16[768,2048]{1,0:T(8,128)(2,1)} %copy-done.16, bf16[2048,768]{1,0:T(8,128)(2,1)} %get-tuple-element.327.gate_ref.refs_4_, ...), custom_call_target="tpu_custom_call" | custom-call | flops 1000000 | bytes 1000000 | tf_op jit(solution)/shard_map/hidden_rows/pallas_call | solution.py:480
  278.3 11.6 %weight_grads.4 = (bf16[8,128,1152]{2,1,0:T(8,128)(2,1)S(1)}, bf16[8,128,1152]{2,1,0:T(8,128)(2,1)}) custom-call(bf16[2048,768]{1,0:T(8,128)(2,1)} %copy-done.4, bf16[2048,768]{1,0:T(8,128)(2,1)} %copy-done.5, bf16[768,768]{1,0:T(8,128)(2,1)S(1)} %get-tuple-element.382.near_ref.refs_0_, bf16[768,768]{1,0:T(8,128)(2,1)S(1)} %get-tuple-element.360.far_ref.refs_0_, ...), custom_call_target="tpu_custom_call" | custom-call | flops 1000000 | bytes 1000000 | tf_op jit(solution)/shard_map/weight_grads/pallas_call | solution.py:521
  291.6 11.6 %weight_grads.5 = (bf16[8,128,1152]{2,1,0:T(8,128)(2,1)S(1)}, bf16[8,128,1152]{2,1,0:T(8,128)(2,1)}) custom-call(bf16[2048,768]{1,0:T(8,128)(2,1)} %copy-done.4, bf16[2048,768]{1,0:T(8,128)(2,1)} %copy-done.5, bf16[768,768]{1,0:T(8,128)(2,1)S(1)} %get-tuple-element.349.near_ref.refs_1_, bf16[768,768]{1,0:T(8,128)(2,1)S(1)} %get-tuple-element.350.far_ref.refs_1_, ...), custom_call_target="tpu_custom_call" | custom-call | flops 1000000 | bytes 1000000 | tf_op jit(solution)/shard_map/weight_grads/pallas_call | solution.py:521
  305.2 3.9 collective-permute-done.34
  309.0 5.2 join_weights.3
  315.8 11.9 %hidden_rows.6 = (bf16[768,640]{1,0:T(8,128)(2,1)S(1)}, bf16[768,640]{1,0:T(8,128)(2,1)S(1)}, bf16[768,640]{1,0:T(8,128)(2,1)S(1)}) custom-call(bf16[768,2048]{1,0:T(8,128)(2,1)} %copy-done.18, bf16[768,2048]{1,0:T(8,128)(2,1)} %copy-done.16, bf16[2048,640]{1,0:T(8,128)(2,1)} %copy-done.6, bf16[2048,640]{1,0:T(8,128)(2,1)} %get-tuple-element.356.up_ref.refs_7_, ...), custom_call_target="tpu_custom_call" | custom-call | flops 1000000 | bytes 1000000 | tf_op jit(solution)/shard_map/hidden_rows/pallas_call | solution.py:480
  327.7 14.4 %back_rows.4 = (f32[384,2048]{1,0:T(8,128)}, bf16[384,2048]{1,0:T(8,128)(2,1)}) custom-call(bf16[768,768]{1,0:T(8,128)(2,1)S(1)} %get-tuple-element.360.far_ref.refs_0_, bf16[768,768]{1,0:T(8,128)(2,1)S(1)} %get-tuple-element.350.far_ref.refs_1_, bf16[768,640]{1,0:T(8,128)(2,1)S(1)} %get-tuple-element.361.refs_2_.far_ref, ...), custom_call_target="tpu_custom_call" | custom-call | flops 1000000 | bytes 1000000 | tf_op jit(solution)/shard_map/back_rows/pallas_call | solution.py:560
  342.2 11.6 %hidden_rows.7 = (bf16[768,640]{1,0:T(8,128)(2,1)S(1)}, bf16[768,640]{1,0:T(8,128)(2,1)S(1)}, bf16[768,640]{1,0:T(8,128)(2,1)S(1)}) custom-call(bf16[768,2048]{1,0:T(8,128)(2,1)} %copy-done.17, bf16[768,2048]{1,0:T(8,128)(2,1)} %copy-done.15, bf16[2048,640]{1,0:T(8,128)(2,1)} %copy-done.6, bf16[2048,640]{1,0:T(8,128)(2,1)} %get-tuple-element.356.up_ref.refs_7_, ...), custom_call_target="tpu_custom_call" | custom-call | flops 1000000 | bytes 1000000 | tf_op jit(solution)/shard_map/hidden_rows/pallas_call | solution.py:480
  355.0 2.6 add_convert_fusion.6
  359.2 2.7 add_convert_fusion.5
  367.1 10.2 %weight_grads.6 = (bf16[8,128,896]{2,1,0:T(8,128)(2,1)S(1)}, bf16[8,128,896]{2,1,0:T(8,128)(2,1)}) custom-call(bf16[2048,768]{1,0:T(8,128)(2,1)} %copy-done.4, bf16[2048,768]{1,0:T(8,128)(2,1)} %copy-done.5, bf16[768,640]{1,0:T(8,128)(2,1)S(1)} %get-tuple-element.378.near_ref.refs_2_, bf16[768,640]{1,0:T(8,128)(2,1)S(1)} %copy-done.38, ...), custom_call_target="tpu_custom_call" | custom-call | flops 1000000 | bytes 1000000 | tf_op jit(solution)/shard_map/weight_grads/pallas_call | solution.py:521
  378.5 11.5 %weight_grads.7 = (bf16[8,128,1024]{2,1,0:T(8,128)(2,1)S(1)}, bf16[8,128,1024]{2,1,0:T(8,128)(2,1)}) custom-call(bf16[2048,768]{1,0:T(8,128)(2,1)} %copy-done.4, bf16[2048,768]{1,0:T(8,128)(2,1)} %copy-done.5, bf16[768,640]{1,0:T(8,128)(2,1)S(1)} %get-tuple-element.380.near_ref.refs_3_, bf16[768,640]{1,0:T(8,128)(2,1)S(1)} %copy-done.36, ...), custom_call_target="tpu_custom_call" | custom-call | flops 1000000 | bytes 1000000 | tf_op jit(solution)/shard_map/weight_grads/pallas_call | solution.py:521
  392.1 13.2 %back_rows.5 = (f32[384,2048]{1,0:T(8,128)}, bf16[384,2048]{1,0:T(8,128)(2,1)S(1)}) custom-call(bf16[768,768]{1,0:T(8,128)(2,1)S(1)} %get-tuple-element.382.near_ref.refs_0_, bf16[768,768]{1,0:T(8,128)(2,1)S(1)} %get-tuple-element.349.near_ref.refs_1_, bf16[768,640]{1,0:T(8,128)(2,1)S(1)} %get-tuple-element.378.near_ref.refs_2_, ...), custom_call_target="tpu_custom_call" | custom-call | flops 1000000 | bytes 1000000 | tf_op jit(solution)/shard_map/back_rows/pallas_call | solution.py:560
  405.4 2.2 add_convert_fusion.4
  407.7 2.5 add_convert_fusion.3
  413.1 2.7 multiply_reduce_fusion
  415.8 4.7 fusion.44
  421.4 3.3 collective-permute-start.51
  427.2 8.7 %back_rows.6 = (f32[384,2048]{1,0:T(8,128)}, bf16[384,2048]{1,0:T(8,128)(2,1)S(1)}) custom-call(bf16[768,768]{1,0:T(8,128)(2,1)S(1)} %copy-done.28, bf16[768,640]{1,0:T(8,128)(2,1)S(1)} %copy-done.34, bf16[2048,384]{1,0:T(8,128)(2,1)} %copy-done.11, bf16[2048,384]{1,0:T(8,128)(2,1)} %copy-done.12, bf16[2048,256]{1,0:T(8,128)(2,1)S(1)} %get-tuple-element.357.down_a.refs_4_, ...), custom_call_target="tpu_custom_call" | custom-call | flops 1000000 | bytes 1000000 | tf_op jit(solution)/shard_map/back_rows/pallas_call | solution.py:560
  435.9 2.5 add_convert_fusion.10
  442.1 2.1 broadcast_select_fusion.2
  457.3 13.1 %attend_backward.2 = (bf16[768,512]{1,0:T(8,128)(2,1)S(1)}, bf16[768,128]{1,0:T(8,128)(2,1)S(1)}, bf16[768,128]{1,0:T(8,128)(2,1)S(1)}) custom-call(bf16[768,512]{1,0:T(8,128)(2,1)S(1)} %copy-done.53, bf16[768,128]{1,0:T(8,128)(2,1)S(1)} %copy-done.63, bf16[768,128]{1,0:T(8,128)(2,1)S(1)} %copy-done.65, ...), custom_call_target="tpu_custom_call" | custom-call | flops 1000000 | bytes 1000000 | tf_op jit(solution)/shard_map/attend_backward/pallas_call | solution.py:360
  473.3 1.9 add_convert_fusion.7
  479.4 13.0 %attend_backward.3 = (bf16[768,512]{1,0:T(8,128)(2,1)S(1)}, bf16[768,128]{1,0:T(8,128)(2,1)S(1)}, bf16[768,128]{1,0:T(8,128)(2,1)S(1)}) custom-call(bf16[768,512]{1,0:T(8,128)(2,1)S(1)} %copy-done.55, bf16[768,128]{1,0:T(8,128)(2,1)S(1)} %copy-done.67, bf16[768,128]{1,0:T(8,128)(2,1)S(1)} %copy-done.69, ...), custom_call_target="tpu_custom_call" | custom-call | flops 1000000 | bytes 1000000 | tf_op jit(solution)/shard_map/attend_backward/pallas_call | solution.py:360
  492.6 2.6 collective-permute-done.46
  499.7 4.8 convolution_convert_fusion
  516.1 2.5 convolution_convert_fusion.3
  518.7 2.5 collective-permute-done.57
  524.4 15.5 %collective-permute-done.56 = bf16[2,2,1,2,128,640]{5,4,3,2,1,0:T(8,128)(2,1)} collective-permute-done((bf16[2,2,1,2,128,640]{5,4,3,2,1,0:T(8,128)(2,1)}, bf16[2,2,1,2,128,640]{5,4,3,2,1,0:T(8,128)(2,1)}, u32[]{:S(2)}, u32[]{:S(2)}) %collective-permute-start.56) | collective-permute-done | bytes 1310752 | tf_op jit(solution)/shard_map/ppermute | solution.py:39
  541.6 2.1 add_convert_fusion.15
  546.8 2.7 fusion.6
  552.3 8.7 %back_rows.7 = (f32[384,2048]{1,0:T(8,128)}, bf16[384,2048]{1,0:T(8,128)(2,1)S(1)}) custom-call(bf16[768,768]{1,0:T(8,128)(2,1)S(1)} %copy-done.26, bf16[768,640]{1,0:T(8,128)(2,1)S(1)} %copy-done.32, bf16[2048,384]{1,0:T(8,128)(2,1)} %copy-done.11, bf16[2048,384]{1,0:T(8,128)(2,1)} %copy-done.12, bf16[2048,256]{1,0:T(8,128)(2,1)S(1)} %get-tuple-element.357.down_a.refs_4_, ...), custom_call_target="tpu_custom_call" | custom-call | flops 1000000 | bytes 1000000 | tf_op jit(solution)/shard_map/back_rows/pallas_call | solution.py:560
  561.7 2.8 reorder.4
  565.7 2.2 add_convert_fusion.12
  571.3 2.7 select_convert_fusion.refs_0_
  574.0 2.5 reorder.5
  576.4 6.8 %collective-permute-done.67 = bf16[1,1,1,1,128,2304]{5,4,3,2,1,0:T(8,128)(2,1)S(1)} collective-permute-done((bf16[1,1,1,1,128,2304]{5,4,3,2,1,0:T(8,128)(2,1)S(1)}, bf16[1,1,1,1,128,2304]{5,4,3,2,1,0:T(8,128)(2,1)S(1)}, u32[]{:S(2)}, u32[]{:S(2)}) %collective-permute-start.67) | collective-permute-done | bytes 589856 | tf_op jit(solution)/shard_map/ppermute | solution.py:39
  583.2 2.5 unpack_columns.1
  585.7 10.9 %collective-permute-done.69 = bf16[1,2,1,1,128,1280]{5,4,3,2,1,0:T(8,128)(2,1)S(1)} collective-permute-done((bf16[1,2,1,1,128,1280]{5,4,3,2,1,0:T(8,128)(2,1)S(1)}, bf16[1,2,1,1,128,1280]{5,4,3,2,1,0:T(8,128)(2,1)S(1)}, u32[]{:S(2)}, u32[]{:S(2)}) %collective-permute-start.69) | collective-permute-done | bytes 655392 | tf_op jit(solution)/shard_map/ppermute | solution.py:39
  596.9 3.0 collective-permute-start.70
  601.0 12.7 %collective-permute-done.71 = bf16[1,1,1,1,128,1280]{5,4,3,2,1,0:T(8,128)(2,1)S(1)} collective-permute-done((bf16[1,1,1,1,128,1280]{5,4,3,2,1,0:T(8,128)(2,1)S(1)}, bf16[1,1,1,1,128,1280]{5,4,3,2,1,0:T(8,128)(2,1)S(1)}, u32[]{:S(2)}, u32[]{:S(2)}) %collective-permute-start.71) | collective-permute-done | bytes 327712 | tf_op jit(solution)/shard_map/ppermute | solution.py:39
  (490 shorter events, 164.2 us)
Async XLA Ops:
  7.1 20.7 %collective-permute-start.4 = (bf16[1,1,1,1,128,1280]{5,4,3,2,1,0:T(8,128)(2,1)}, bf16[1,1,1,1,128,1280]{5,4,3,2,1,0:T(8,128)(2,1)}, u32[]{:S(2)}, u32[]{:S(2)}) collective-permute-start(bf16[1,1,1,1,128,1280]{5,4,3,2,1,0:T(8,128)(2,1)} %maximum_bitcast_fusion), channel_id=1, source_target_pairs={{0,16},{2,18},{4,20},{6,22},{8,24},{10,26},{12,28},{14,30},{16,0},... | collective-permute-start | bytes 983048 | tf_op jit(solution)/shard_map/ppermute | solution.py:39
  25.2 12.6 %collective-permute-start.6 = (bf16[1,1,1,1,128,1024]{5,4,3,2,1,0:T(8,128)(2,1)S(1)}, bf16[1,1,1,1,128,1024]{5,4,3,2,1,0:T(8,128)(2,1)S(1)}, u32[]{:S(2)}, u32[]{:S(2)}) collective-permute-start(bf16[1,1,1,1,128,1024]{5,4,3,2,1,0:T(8,128)(2,1)S(1)} %bitcast.163), channel_id=1, source_target_pairs={{0,16},{2,18},{4,20},{6,22},{8,24},{10,26},{12,28},{14,30},{16,0},... | collective-permute-start | bytes 786440 | tf_op jit(solution)/shard_map/ppermute | solution.py:39
  28.9 19.5 %collective-permute-start.8 = (bf16[1,2,1,1,128,1280]{5,4,3,2,1,0:T(8,128)(2,1)S(1)}, bf16[1,2,1,1,128,1280]{5,4,3,2,1,0:T(8,128)(2,1)S(1)}, u32[]{:S(2)}, u32[]{:S(2)}) collective-permute-start(bf16[1,2,1,1,128,1280]{5,4,3,2,1,0:T(8,128)(2,1)S(1)} %pad_maximum_fusion.33), channel_id=1, source_target_pairs={{0,8},{2,10},{4,12},{6,14},{8,0},{10,2},{12,4},{14,6},{16,24},{18,... | collective-permute-start | bytes 1966088 | tf_op jit(solution)/shard_map/ppermute | solution.py:39
  30.3 40.6 %collective-permute-start.5 = (bf16[384,2048]{1,0:T(8,128)(2,1)S(1)}, bf16[384,2048]{1,0:T(8,128)(2,1)S(1)}, u32[]{:S(2)}, u32[]{:S(2)}) collective-permute-start(bf16[384,2048]{1,0:T(8,128)(2,1)S(1)} %fusion.4), channel_id=1, source_target_pairs={{0,1},{1,0},{2,3},{3,2},{4,5},{5,4},{6,7},{7,6},{8,9},{9,8},{10,11... | collective-permute-start | bytes 4718600 | tf_op jit(solution)/shard_map/ppermute | solution.py:43
  49.7 14.8 %collective-permute-start.10 = (bf16[2,2,1,1,128,640]{5,4,3,2,1,0:T(8,128)(2,1)S(1)}, bf16[2,2,1,1,128,640]{5,4,3,2,1,0:T(8,128)(2,1)S(1)}, u32[]{:S(2)}, u32[]{:S(2)}) collective-permute-start(bf16[2,2,1,1,128,640]{5,4,3,2,1,0:T(8,128)(2,1)S(1)} %get-tuple-element.266), channel_id=1, source_target_pairs={{0,2},{2,0},{4,6},{6,4},{8,10},{10,8},{12,14},{14,12},{16,18},{18,... | collective-permute-start | bytes 1966088 | tf_op jit(solution)/shard_map/ppermute | solution.py:39
  51.3 15.6 %collective-permute-start.9 = (bf16[2,2,1,1,128,640]{5,4,3,2,1,0:T(8,128)(2,1)S(1)}, bf16[2,2,1,1,128,640]{5,4,3,2,1,0:T(8,128)(2,1)S(1)}, u32[]{:S(2)}, u32[]{:S(2)}) collective-permute-start(bf16[2,2,1,1,128,640]{5,4,3,2,1,0:T(8,128)(2,1)S(1)} %get-tuple-element.267), channel_id=1, source_target_pairs={{0,4},{2,6},{4,0},{6,2},{8,12},{10,14},{12,8},{14,10},{16,20},{18,... | collective-permute-start | bytes 1966088 | tf_op jit(solution)/shard_map/ppermute | solution.py:39
  52.0 16.4 %collective-permute-start.13 = (bf16[1,1,1,1,128,2304]{5,4,3,2,1,0:T(8,128)(2,1)S(1)}, bf16[1,1,1,1,128,2304]{5,4,3,2,1,0:T(8,128)(2,1)S(1)}, u32[]{:S(2)}, u32[]{:S(2)}) collective-permute-start(bf16[1,1,1,1,128,2304]{5,4,3,2,1,0:T(8,128)(2,1)S(1)} %bitcast.144), channel_id=1, source_target_pairs={{0,8},{2,10},{4,12},{6,14},{8,0},{10,2},{12,4},{14,6},{16,24},{18,... | collective-permute-start | bytes 1769480 | tf_op jit(solution)/shard_map/ppermute | solution.py:39
  64.6 29.1 %collective-permute-start.12 = (bf16[2,2,1,2,128,640]{5,4,3,2,1,0:T(8,128)(2,1)S(1)}, bf16[2,2,1,2,128,640]{5,4,3,2,1,0:T(8,128)(2,1)S(1)}, u32[]{:S(2)}, u32[]{:S(2)}) collective-permute-start(bf16[2,2,1,2,128,640]{5,4,3,2,1,0:T(8,128)(2,1)S(1)} %pad_maximum_fusion.22), channel_id=1, source_target_pairs={{0,4},{2,6},{4,0},{6,2},{8,12},{10,14},{12,8},{14,10},{16,20},{18,... | collective-permute-start | bytes 3932168 | tf_op jit(solution)/shard_map/ppermute | solution.py:39
  67.0 26.7 %collective-permute-start.11 = (bf16[2,2,2,1,128,640]{5,4,3,2,1,0:T(8,128)(2,1)S(1)}, bf16[2,2,2,1,128,640]{5,4,3,2,1,0:T(8,128)(2,1)S(1)}, u32[]{:S(2)}, u32[]{:S(2)}) collective-permute-start(bf16[2,2,2,1,128,640]{5,4,3,2,1,0:T(8,128)(2,1)S(1)} %pad_maximum_fusion.23), channel_id=1, source_target_pairs={{0,2},{2,0},{4,6},{6,4},{8,10},{10,8},{12,14},{14,12},{16,18},{18,... | collective-permute-start | bytes 3932168 | tf_op jit(solution)/shard_map/ppermute | solution.py:39
  68.4 26.1 %collective-permute-start.7 = (bf16[1,2,1,1,128,1024]{5,4,3,2,1,0:T(8,128)(2,1)S(1)}, bf16[1,2,1,1,128,1024]{5,4,3,2,1,0:T(8,128)(2,1)S(1)}, u32[]{:S(2)}, u32[]{:S(2)}) collective-permute-start(bf16[1,2,1,1,128,1024]{5,4,3,2,1,0:T(8,128)(2,1)S(1)} %pad_maximum_fusion.35), channel_id=1, source_target_pairs={{0,8},{2,10},{4,12},{6,14},{8,0},{10,2},{12,4},{14,6},{16,24},{18,... | collective-permute-start | bytes 1572872 | tf_op jit(solution)/shard_map/ppermute | solution.py:39
  69.6 50.9 %collective-permute-start.14 = (bf16[2,1,1,1,128,2304]{5,4,3,2,1,0:T(8,128)(2,1)}, bf16[2,1,1,1,128,2304]{5,4,3,2,1,0:T(8,128)(2,1)}, u32[]{:S(2)}, u32[]{:S(2)}) collective-permute-start(bf16[2,1,1,1,128,2304]{5,4,3,2,1,0:T(8,128)(2,1)} %pad_maximum_fusion.25), channel_id=1, source_target_pairs={{0,16},{2,18},{4,20},{6,22},{8,24},{10,26},{12,28},{14,30},{16,0},... | collective-permute-start | bytes 3538952 | tf_op jit(solution)/shard_map/ppermute | solution.py:39
  70.9 69.2 %collective-permute-start.20 = (bf16[384,2048]{1,0:T(8,128)(2,1)}, bf16[384,2048]{1,0:T(8,128)(2,1)}, u32[]{:S(2)}, u32[]{:S(2)}) collective-permute-start(bf16[384,2048]{1,0:T(8,128)(2,1)} %pad_maximum_fusion.14), channel_id=1, source_target_pairs={{0,8},{2,10},{4,12},{6,14},{8,0},{10,2},{12,4},{14,6},{16,24},{18,... | collective-permute-start | bytes 4718600 | tf_op jit(solution)/shard_map/ppermute | solution.py:39
  94.7 19.9 %collective-permute-start.16 = (bf16[2,2,1,1,128,512]{5,4,3,2,1,0:T(8,128)(2,1)S(1)}, bf16[2,2,1,1,128,512]{5,4,3,2,1,0:T(8,128)(2,1)S(1)}, u32[]{:S(2)}, u32[]{:S(2)}) collective-permute-start(bf16[2,2,1,1,128,512]{5,4,3,2,1,0:T(8,128)(2,1)S(1)} %get-tuple-element.283), channel_id=1, source_target_pairs={{0,2},{2,0},{4,6},{6,4},{8,10},{10,8},{12,14},{14,12},{16,18},{18,... | collective-permute-start | bytes 1572872 | tf_op jit(solution)/shard_map/ppermute | solution.py:39
  95.4 20.9 %collective-permute-start.15 = (bf16[2,2,1,1,128,512]{5,4,3,2,1,0:T(8,128)(2,1)S(1)}, bf16[2,2,1,1,128,512]{5,4,3,2,1,0:T(8,128)(2,1)S(1)}, u32[]{:S(2)}, u32[]{:S(2)}) collective-permute-start(bf16[2,2,1,1,128,512]{5,4,3,2,1,0:T(8,128)(2,1)S(1)} %get-tuple-element.549), channel_id=1, source_target_pairs={{0,4},{2,6},{4,0},{6,2},{8,12},{10,14},{12,8},{14,10},{16,20},{18,... | collective-permute-start | bytes 1572872 | tf_op jit(solution)/shard_map/ppermute | solution.py:39
  115.9 24.3 %collective-permute-start.19 = (bf16[2,2,1,2,128,512]{5,4,3,2,1,0:T(8,128)(2,1)}, bf16[2,2,1,2,128,512]{5,4,3,2,1,0:T(8,128)(2,1)}, u32[]{:S(2)}, u32[]{:S(2)}) collective-permute-start(bf16[2,2,1,2,128,512]{5,4,3,2,1,0:T(8,128)(2,1)} %pad_maximum_fusion.27), channel_id=1, source_target_pairs={{0,4},{2,6},{4,0},{6,2},{8,12},{10,14},{12,8},{14,10},{16,20},{18,... | collective-permute-start | bytes 3145736 | tf_op jit(solution)/shard_map/ppermute | solution.py:39
  117.5 22.6 %collective-permute-start.18 = (bf16[2,2,2,1,128,512]{5,4,3,2,1,0:T(8,128)(2,1)}, bf16[2,2,2,1,128,512]{5,4,3,2,1,0:T(8,128)(2,1)}, u32[]{:S(2)}, u32[]{:S(2)}) collective-permute-start(bf16[2,2,2,1,128,512]{5,4,3,2,1,0:T(8,128)(2,1)} %pad_maximum_fusion.28), channel_id=1, source_target_pairs={{0,2},{2,0},{4,6},{6,4},{8,10},{10,8},{12,14},{14,12},{16,18},{18,... | collective-permute-start | bytes 3145736 | tf_op jit(solution)/shard_map/ppermute | solution.py:39
  120.5 27.6 %collective-permute-start.17 = (bf16[1,1,1,1,128,1920]{5,4,3,2,1,0:T(8,128)(2,1)}, bf16[1,1,1,1,128,1920]{5,4,3,2,1,0:T(8,128)(2,1)S(1)}, u32[]{:S(2)}, u32[]{:S(2)}) collective-permute-start(bf16[1,1,1,1,128,1920]{5,4,3,2,1,0:T(8,128)(2,1)} %bitcast.145), channel_id=1, source_target_pairs={{0,8},{2,10},{4,12},{6,14},{8,0},{10,2},{12,4},{14,6},{16,24},{18,... | collective-permute-start | bytes 1474568 | tf_op jit(solution)/shard_map/ppermute | solution.py:39
  140.2 23.0 %collective-permute-start.23 = (bf16[2,2,1,1,128,1152]{5,4,3,2,1,0:T(8,128)(2,1)S(1)}, bf16[2,2,1,1,128,1152]{5,4,3,2,1,0:T(8,128)(2,1)S(1)}, u32[]{:S(2)}, u32[]{:S(2)}) collective-permute-start(bf16[2,2,1,1,128,1152]{5,4,3,2,1,0:T(8,128)(2,1)S(1)} %get-tuple-element.300), channel_id=1, source_target_pairs={{0,4},{2,6},{4,0},{6,2},{8,12},{10,14},{12,8},{14,10},{16,20},{18,... | collective-permute-start | bytes 3538952 | tf_op jit(solution)/shard_map/ppermute | solution.py:39
  141.8 25.3 %collective-permute-start.22 = (bf16[2,2,1,1,128,1152]{5,4,3,2,1,0:T(8,128)(2,1)S(1)}, bf16[2,2,1,1,128,1152]{5,4,3,2,1,0:T(8,128)(2,1)S(1)}, u32[]{:S(2)}, u32[]{:S(2)}) collective-permute-start(bf16[2,2,1,1,128,1152]{5,4,3,2,1,0:T(8,128)(2,1)S(1)} %get-tuple-element.301), channel_id=1, source_target_pairs={{0,2},{2,0},{4,6},{6,4},{8,10},{10,8},{12,14},{14,12},{16,18},{18,... | collective-permute-start | bytes 3538952 | tf_op jit(solution)/shard_map/ppermute | solution.py:39
  151.3 19.1 %collective-permute-start.21 = (bf16[384,2048]{1,0:T(8,128)(2,1)S(1)}, bf16[384,2048]{1,0:T(8,128)(2,1)S(1)}, u32[]{:S(2)}, u32[]{:S(2)}) collective-permute-start(bf16[384,2048]{1,0:T(8,128)(2,1)S(1)} %add_convert_fusion.2), channel_id=1, source_target_pairs={{0,1},{1,0},{2,3},{3,2},{4,5},{5,4},{6,7},{7,6},{8,9},{9,8},{10,11... | collective-permute-start | bytes 4718600 | tf_op jit(solution)/shard_map/ppermute | solution.py:43
  151.6 24.2 %collective-permute-start.28 = (bf16[384,2048]{1,0:T(8,128)(2,1)S(1)}, bf16[384,2048]{1,0:T(8,128)(2,1)S(1)}, u32[]{:S(2)}, u32[]{:S(2)}) collective-permute-start(bf16[384,2048]{1,0:T(8,128)(2,1)S(1)} %copy-done.14), channel_id=1, source_target_pairs={{0,1},{1,0},{2,3},{3,2},{4,5},{5,4},{6,7},{7,6},{8,9},{9,8},{10,11... | collective-permute-start | bytes 4718600 | tf_op jit(solution)/shard_map/ppermute | solution.py:43
  151.9 28.6 %collective-permute-start.27 = (bf16[384,2048]{1,0:T(8,128)(2,1)}, bf16[384,2048]{1,0:T(8,128)(2,1)S(1)}, u32[]{:S(2)}, u32[]{:S(2)}) collective-permute-start(bf16[384,2048]{1,0:T(8,128)(2,1)} %collective-permute-done.20.refs_0_), channel_id=1, source_target_pairs={{0,1},{1,0},{2,3},{3,2},{4,5},{5,4},{6,7},{7,6},{8,9},{9,8},{10,11... | collective-permute-start | bytes 4718600 | tf_op jit(solution)/shard_map/ppermute | solution.py:43
  167.4 55.1 %collective-permute-start.29 = (bf16[2,2,2,1,128,1152]{5,4,3,2,1,0:T(8,128)(2,1)S(1)}, bf16[2,2,2,1,128,1152]{5,4,3,2,1,0:T(8,128)(2,1)}, u32[]{:S(2)}, u32[]{:S(2)}) collective-permute-start(bf16[2,2,2,1,128,1152]{5,4,3,2,1,0:T(8,128)(2,1)S(1)} %pad_maximum_fusion.7), channel_id=1, source_target_pairs={{0,2},{2,0},{4,6},{6,4},{8,10},{10,8},{12,14},{14,12},{16,18},{18,... | collective-permute-start | bytes 7077896 | tf_op jit(solution)/shard_map/ppermute | solution.py:39
  169.0 53.4 %collective-permute-start.30 = (bf16[2,2,1,2,128,1152]{5,4,3,2,1,0:T(8,128)(2,1)S(1)}, bf16[2,2,1,2,128,1152]{5,4,3,2,1,0:T(8,128)(2,1)}, u32[]{:S(2)}, u32[]{:S(2)}) collective-permute-start(bf16[2,2,1,2,128,1152]{5,4,3,2,1,0:T(8,128)(2,1)S(1)} %pad_maximum_fusion.6), channel_id=1, source_target_pairs={{0,4},{2,6},{4,0},{6,2},{8,12},{10,14},{12,8},{14,10},{16,20},{18,... | collective-permute-start | bytes 7077896 | tf_op jit(solution)/shard_map/ppermute | solution.py:39
  174.4 50.1 %collective-permute-start.25 = (bf16[384,2048]{1,0:T(8,128)(2,1)}, bf16[384,2048]{1,0:T(8,128)(2,1)S(1)}, u32[]{:S(2)}, u32[]{:S(2)}) collective-permute-start(bf16[384,2048]{1,0:T(8,128)(2,1)} %pad_maximum_fusion.15), channel_id=1, source_target_pairs={{0,8},{2,10},{4,12},{6,14},{8,0},{10,2},{12,4},{14,6},{16,24},{18,... | collective-permute-start | bytes 4718600 | tf_op jit(solution)/shard_map/ppermute | solution.py:39
  175.8 45.2 %collective-permute-start.26 = (bf16[2,1,1,1,128,1920]{5,4,3,2,1,0:T(8,128)(2,1)}, bf16[2,1,1,1,128,1920]{5,4,3,2,1,0:T(8,128)(2,1)S(1)}, u32[]{:S(2)}, u32[]{:S(2)}) collective-permute-start(bf16[2,1,1,1,128,1920]{5,4,3,2,1,0:T(8,128)(2,1)} %pad_maximum_fusion.30), channel_id=1, source_target_pairs={{0,16},{2,18},{4,20},{6,22},{8,24},{10,26},{12,28},{14,30},{16,0},... | collective-permute-start | bytes 2949128 | tf_op jit(solution)/shard_map/ppermute | solution.py:39
  180.5 49.7 %collective-permute-start.24 = (bf16[384,2048]{1,0:T(8,128)(2,1)S(1)}, bf16[384,2048]{1,0:T(8,128)(2,1)}, u32[]{:S(2)}, u32[]{:S(2)}) collective-permute-start(bf16[384,2048]{1,0:T(8,128)(2,1)S(1)} %multiply_convert_fusion.refs_0_), channel_id=1, source_target_pairs={{0,1},{1,0},{2,3},{3,2},{4,5},{5,4},{6,7},{7,6},{8,9},{9,8},{10,11... | collective-permute-start | bytes 4718600 | tf_op jit(solution)/shard_map/ppermute | solution.py:43
  222.5 32.7 %collective-permute-start.33 = (bf16[2,2,1,1,128,896]{5,4,3,2,1,0:T(8,128)(2,1)S(1)}, bf16[2,2,1,1,128,896]{5,4,3,2,1,0:T(8,128)(2,1)S(1)}, u32[]{:S(2)}, u32[]{:S(2)}) collective-permute-start(bf16[2,2,1,1,128,896]{5,4,3,2,1,0:T(8,128)(2,1)S(1)} %pad_maximum_fusion.31), channel_id=1, source_target_pairs={{0,2},{2,0},{4,6},{6,4},{8,10},{10,8},{12,14},{14,12},{16,18},{18,... | collective-permute-start | bytes 2752520 | tf_op jit(solution)/shard_map/ppermute | solution.py:39
  224.2 32.6 %collective-permute-start.32 = (bf16[2,2,1,1,128,1024]{5,4,3,2,1,0:T(8,128)(2,1)}, bf16[2,2,1,1,128,1024]{5,4,3,2,1,0:T(8,128)(2,1)S(1)}, u32[]{:S(2)}, u32[]{:S(2)}) collective-permute-start(bf16[2,2,1,1,128,1024]{5,4,3,2,1,0:T(8,128)(2,1)} %slice.400), channel_id=1, source_target_pairs={{0,4},{2,6},{4,0},{6,2},{8,12},{10,14},{12,8},{14,10},{16,20},{18,... | collective-permute-start | bytes 3145736 | tf_op jit(solution)/shard_map/ppermute | solution.py:39
  224.6 27.4 %collective-permute-start.31 = (bf16[384,2048]{1,0:T(8,128)(2,1)S(1)}, bf16[384,2048]{1,0:T(8,128)(2,1)}, u32[]{:S(2)}, u32[]{:S(2)}) collective-permute-start(bf16[384,2048]{1,0:T(8,128)(2,1)S(1)} %collective-permute-done.25.refs_0_), channel_id=1, source_target_pairs={{0,1},{1,0},{2,3},{3,2},{4,5},{5,4},{6,7},{7,6},{8,9},{9,8},{10,11... | collective-permute-start | bytes 4718600 | tf_op jit(solution)/shard_map/ppermute | solution.py:43
  260.3 48.7 %collective-permute-start.34 = (bf16[2,2,2,1,128,1024]{5,4,3,2,1,0:T(8,128)(2,1)}, bf16[2,2,2,1,128,1024]{5,4,3,2,1,0:T(8,128)(2,1)}, u32[]{:S(2)}, u32[]{:S(2)}) collective-permute-start(bf16[2,2,2,1,128,1024]{5,4,3,2,1,0:T(8,128)(2,1)} %pad_maximum_fusion.10), channel_id=1, source_target_pairs={{0,2},{2,0},{4,6},{6,4},{8,10},{10,8},{12,14},{14,12},{16,18},{18,... | collective-permute-start | bytes 6291464 | tf_op jit(solution)/shard_map/ppermute | solution.py:39
  262.0 43.2 %collective-permute-start.35 = (bf16[2,2,1,2,128,896]{5,4,3,2,1,0:T(8,128)(2,1)}, bf16[2,2,1,2,128,896]{5,4,3,2,1,0:T(8,128)(2,1)}, u32[]{:S(2)}, u32[]{:S(2)}) collective-permute-start(bf16[2,2,1,2,128,896]{5,4,3,2,1,0:T(8,128)(2,1)} %pad_maximum_fusion.13), channel_id=1, source_target_pairs={{0,4},{2,6},{4,0},{6,2},{8,12},{10,14},{12,8},{14,10},{16,20},{18,... | collective-permute-start | bytes 5505032 | tf_op jit(solution)/shard_map/ppermute | solution.py:39
  289.9 65.1 %collective-permute-start.38 = (bf16[2,2,1,2,128,1152]{5,4,3,2,1,0:T(8,128)(2,1)}, bf16[2,2,1,2,128,1152]{5,4,3,2,1,0:T(8,128)(2,1)}, u32[]{:S(2)}, u32[]{:S(2)}) collective-permute-start(bf16[2,2,1,2,128,1152]{5,4,3,2,1,0:T(8,128)(2,1)} %bitcast.186), channel_id=1, source_target_pairs={{0,4},{2,6},{4,0},{6,2},{8,12},{10,14},{12,8},{14,10},{16,20},{18,... | collective-permute-start | bytes 7077896 | tf_op jit(solution)/shard_map/ppermute | solution.py:39
  304.6 54.6 %collective-permute-start.37 = (bf16[2,2,2,1,128,1152]{5,4,3,2,1,0:T(8,128)(2,1)}, bf16[2,2,2,1,128,1152]{5,4,3,2,1,0:T(8,128)(2,1)}, u32[]{:S(2)}, u32[]{:S(2)}) collective-permute-start(bf16[2,2,2,1,128,1152]{5,4,3,2,1,0:T(8,128)(2,1)} %bitcast.187), channel_id=1, source_target_pairs={{0,2},{2,0},{4,6},{6,4},{8,10},{10,8},{12,14},{14,12},{16,18},{18,... | collective-permute-start | bytes 7077896 | tf_op jit(solution)/shard_map/ppermute | solution.py:39
  342.1 22.4 %collective-permute-start.36 = (bf16[384,2048]{1,0:T(8,128)(2,1)}, bf16[384,2048]{1,0:T(8,128)(2,1)S(1)}, u32[]{:S(2)}, u32[]{:S(2)}) collective-permute-start(bf16[384,2048]{1,0:T(8,128)(2,1)} %get-tuple-element.365), channel_id=1, source_target_pairs={{0,1},{1,0},{2,3},{3,2},{4,5},{5,4},{6,7},{7,6},{8,9},{9,8},{10,11... | collective-permute-start | bytes 4718600 | tf_op jit(solution)/shard_map/ppermute | solution.py:43
  357.6 47.7 %collective-permute-start.40 = (bf16[2,2,1,1,128,1152]{5,4,3,2,1,0:T(8,128)(2,1)}, bf16[2,2,1,1,128,1152]{5,4,3,2,1,0:T(8,128)(2,1)}, u32[]{:S(2)}, u32[]{:S(2)}) collective-permute-start(bf16[2,2,1,1,128,1152]{5,4,3,2,1,0:T(8,128)(2,1)} %add_convert_fusion.6), channel_id=1, source_target_pairs={{0,2},{2,0},{4,6},{6,4},{8,10},{10,8},{12,14},{14,12},{16,18},{18,... | collective-permute-start | bytes 3538952 | tf_op jit(solution)/shard_map/ppermute | solution.py:39
  361.8 43.5 %collective-permute-start.41 = (bf16[2,2,1,1,128,1152]{5,4,3,2,1,0:T(8,128)(2,1)}, bf16[2,2,1,1,128,1152]{5,4,3,2,1,0:T(8,128)(2,1)}, u32[]{:S(2)}, u32[]{:S(2)}) collective-permute-start(bf16[2,2,1,1,128,1152]{5,4,3,2,1,0:T(8,128)(2,1)} %add_convert_fusion.5), channel_id=1, source_target_pairs={{0,4},{2,6},{4,0},{6,2},{8,12},{10,14},{12,8},{14,10},{16,20},{18,... | collective-permute-start | bytes 3538952 | tf_op jit(solution)/shard_map/ppermute | solution.py:39
  366.5 45.1 %collective-permute-start.42 = (bf16[384,2048]{1,0:T(8,128)(2,1)}, bf16[384,2048]{1,0:T(8,128)(2,1)}, u32[]{:S(2)}, u32[]{:S(2)}) collective-permute-start(bf16[384,2048]{1,0:T(8,128)(2,1)} %pad_maximum_fusion.16), channel_id=1, source_target_pairs={{0,8},{2,10},{4,12},{6,14},{8,0},{10,2},{12,4},{14,6},{16,24},{18,... | collective-permute-start | bytes 4718600 | tf_op jit(solution)/shard_map/ppermute | solution.py:39
  390.0 49.4 %collective-permute-start.44 = (bf16[2,2,2,1,128,1024]{5,4,3,2,1,0:T(8,128)(2,1)}, bf16[2,2,2,1,128,1024]{5,4,3,2,1,0:T(8,128)(2,1)}, u32[]{:S(2)}, u32[]{:S(2)}) collective-permute-start(bf16[2,2,2,1,128,1024]{5,4,3,2,1,0:T(8,128)(2,1)} %bitcast.188), channel_id=1, source_target_pairs={{0,2},{2,0},{4,6},{6,4},{8,10},{10,8},{12,14},{14,12},{16,18},{18,... | collective-permute-start | bytes 6291464 | tf_op jit(solution)/shard_map/ppermute | solution.py:39
  391.1 44.7 %collective-permute-start.45 = (bf16[2,2,1,2,128,896]{5,4,3,2,1,0:T(8,128)(2,1)}, bf16[2,2,1,2,128,896]{5,4,3,2,1,0:T(8,128)(2,1)}, u32[]{:S(2)}, u32[]{:S(2)}) collective-permute-start(bf16[2,2,1,2,128,896]{5,4,3,2,1,0:T(8,128)(2,1)} %bitcast.189), channel_id=1, source_target_pairs={{0,4},{2,6},{4,0},{6,2},{8,12},{10,14},{12,8},{14,10},{16,20},{18,... | collective-permute-start | bytes 5505032 | tf_op jit(solution)/shard_map/ppermute | solution.py:39
  420.5 21.6 %collective-permute-start.43 = (bf16[384,2048]{1,0:T(8,128)(2,1)}, bf16[384,2048]{1,0:T(8,128)(2,1)}, u32[]{:S(2)}, u32[]{:S(2)}) collective-permute-start(bf16[384,2048]{1,0:T(8,128)(2,1)} %get-tuple-element.391), channel_id=1, source_target_pairs={{0,1},{1,0},{2,3},{3,2},{4,5},{5,4},{6,7},{7,6},{8,9},{9,8},{10,11... | collective-permute-start | bytes 4718600 | tf_op jit(solution)/shard_map/ppermute | solution.py:43
  421.4 85.5 %collective-permute-start.51 = (bf16[2,1,1,1,128,2304]{5,4,3,2,1,0:T(8,128)(2,1)}, bf16[2,1,1,1,128,2304]{5,4,3,2,1,0:T(8,128)(2,1)S(1)}, u32[]{:S(2)}, u32[]{:S(2)}) collective-permute-start(bf16[2,1,1,1,128,2304]{5,4,3,2,1,0:T(8,128)(2,1)} %fusion.15), channel_id=1, source_target_pairs={{0,16},{2,18},{4,20},{6,22},{8,24},{10,26},{12,28},{14,30},{16,0},... | collective-permute-start | bytes 3538952 | tf_op jit(solution)/shard_map/ppermute | solution.py:39
  435.9 15.6 %collective-permute-start.48 = (bf16[384,2048]{1,0:T(8,128)(2,1)S(1)}, bf16[384,2048]{1,0:T(8,128)(2,1)S(1)}, u32[]{:S(2)}, u32[]{:S(2)}) collective-permute-start(bf16[384,2048]{1,0:T(8,128)(2,1)S(1)} %get-tuple-element.397), channel_id=1, source_target_pairs={{0,1},{1,0},{2,3},{3,2},{4,5},{5,4},{6,7},{7,6},{8,9},{9,8},{10,11... | collective-permute-start | bytes 4718600 | tf_op jit(solution)/shard_map/ppermute | solution.py:43
  438.4 32.1 %collective-permute-start.47 = (bf16[2,2,1,1,128,896]{5,4,3,2,1,0:T(8,128)(2,1)}, bf16[2,2,1,1,128,896]{5,4,3,2,1,0:T(8,128)(2,1)}, u32[]{:S(2)}, u32[]{:S(2)}) collective-permute-start(bf16[2,2,1,1,128,896]{5,4,3,2,1,0:T(8,128)(2,1)} %add_convert_fusion.10), channel_id=1, source_target_pairs={{0,2},{2,0},{4,6},{6,4},{8,10},{10,8},{12,14},{14,12},{16,18},{18,... | collective-permute-start | bytes 2752520 | tf_op jit(solution)/shard_map/ppermute | solution.py:39
  441.1 32.2 %collective-permute-start.49 = (bf16[2,2,1,1,128,1024]{5,4,3,2,1,0:T(8,128)(2,1)S(1)}, bf16[2,2,1,1,128,1024]{5,4,3,2,1,0:T(8,128)(2,1)S(1)}, u32[]{:S(2)}, u32[]{:S(2)}) collective-permute-start(bf16[2,2,1,1,128,1024]{5,4,3,2,1,0:T(8,128)(2,1)S(1)} %add_convert_fusion.8), channel_id=1, source_target_pairs={{0,4},{2,6},{4,0},{6,2},{8,12},{10,14},{12,8},{14,10},{16,20},{18,... | collective-permute-start | bytes 3145736 | tf_op jit(solution)/shard_map/ppermute | solution.py:39
  450.4 47.0 %collective-permute-start.52 = (bf16[2,2,2,1,128,512]{5,4,3,2,1,0:T(8,128)(2,1)}, bf16[2,2,2,1,128,512]{5,4,3,2,1,0:T(8,128)(2,1)}, u32[]{:S(2)}, u32[]{:S(2)}) collective-permute-start(bf16[2,2,2,1,128,512]{5,4,3,2,1,0:T(8,128)(2,1)} %slice.414), channel_id=1, source_target_pairs={{0,2},{2,0},{4,6},{6,4},{8,10},{10,8},{12,14},{14,12},{16,18},{18,... | collective-permute-start | bytes 3145736 | tf_op jit(solution)/shard_map/ppermute | solution.py:39
  453.5 117.7 %collective-permute-start.65 = (bf16[384,2048]{1,0:T(8,128)(2,1)}, bf16[384,2048]{1,0:T(8,128)(2,1)}, u32[]{:S(2)}, u32[]{:S(2)}) collective-permute-start(bf16[384,2048]{1,0:T(8,128)(2,1)} %pad_maximum_fusion.17), channel_id=1, source_target_pairs={{0,8},{2,10},{4,12},{6,14},{8,0},{10,2},{12,4},{14,6},{16,24},{18,... | collective-permute-start | bytes 4718600 | tf_op jit(solution)/shard_map/ppermute | solution.py:39
  470.5 24.7 %collective-permute-start.46 = (bf16[2,2,1,2,128,512]{5,4,3,2,1,0:T(8,128)(2,1)}, bf16[2,2,1,2,128,512]{5,4,3,2,1,0:T(8,128)(2,1)}, u32[]{:S(2)}, u32[]{:S(2)}) collective-permute-start(bf16[2,2,1,2,128,512]{5,4,3,2,1,0:T(8,128)(2,1)} %slice.412), channel_id=1, source_target_pairs={{0,4},{2,6},{4,0},{6,2},{8,12},{10,14},{12,8},{14,10},{16,20},{18,... | collective-permute-start | bytes 3145736 | tf_op jit(solution)/shard_map/ppermute | solution.py:39
  476.2 45.0 %collective-permute-start.57 = (bf16[2,1,1,1,128,1920]{5,4,3,2,1,0:T(8,128)(2,1)}, bf16[2,1,1,1,128,1920]{5,4,3,2,1,0:T(8,128)(2,1)S(1)}, u32[]{:S(2)}, u32[]{:S(2)}) collective-permute-start(bf16[2,1,1,1,128,1920]{5,4,3,2,1,0:T(8,128)(2,1)} %fusion.16), channel_id=1, source_target_pairs={{0,16},{2,18},{4,20},{6,22},{8,24},{10,26},{12,28},{14,30},{16,0},... | collective-permute-start | bytes 2949128 | tf_op jit(solution)/shard_map/ppermute | solution.py:39
  496.4 14.9 %collective-permute-start.50 = (bf16[2,2,1,1,128,512]{5,4,3,2,1,0:T(8,128)(2,1)S(1)}, bf16[2,2,1,1,128,512]{5,4,3,2,1,0:T(8,128)(2,1)S(1)}, u32[]{:S(2)}, u32[]{:S(2)}) collective-permute-start(bf16[2,2,1,1,128,512]{5,4,3,2,1,0:T(8,128)(2,1)S(1)} %add_convert_fusion.20), channel_id=1, source_target_pairs={{0,2},{2,0},{4,6},{6,4},{8,10},{10,8},{12,14},{14,12},{16,18},{18,... | collective-permute-start | bytes 1572872 | tf_op jit(solution)/shard_map/ppermute | solution.py:39
  498.5 15.3 %collective-permute-start.53 = (bf16[2,2,1,1,128,512]{5,4,3,2,1,0:T(8,128)(2,1)S(1)}, bf16[2,2,1,1,128,512]{5,4,3,2,1,0:T(8,128)(2,1)S(1)}, u32[]{:S(2)}, u32[]{:S(2)}) collective-permute-start(bf16[2,2,1,1,128,512]{5,4,3,2,1,0:T(8,128)(2,1)S(1)} %add_convert_fusion.19), channel_id=1, source_target_pairs={{0,4},{2,6},{4,0},{6,2},{8,12},{10,14},{12,8},{14,10},{16,20},{18,... | collective-permute-start | bytes 1572872 | tf_op jit(solution)/shard_map/ppermute | solution.py:39
  507.9 35.8 %collective-permute-start.55 = (bf16[2,2,2,1,128,640]{5,4,3,2,1,0:T(8,128)(2,1)}, bf16[2,2,2,1,128,640]{5,4,3,2,1,0:T(8,128)(2,1)S(1)}, u32[]{:S(2)}, u32[]{:S(2)}) collective-permute-start(bf16[2,2,2,1,128,640]{5,4,3,2,1,0:T(8,128)(2,1)} %slice.422), channel_id=1, source_target_pairs={{0,2},{2,0},{4,6},{6,4},{8,10},{10,8},{12,14},{14,12},{16,18},{18,... | collective-permute-start | bytes 3932168 | tf_op jit(solution)/shard_map/ppermute | solution.py:39
  511.3 28.5 %collective-permute-start.56 = (bf16[2,2,1,2,128,640]{5,4,3,2,1,0:T(8,128)(2,1)}, bf16[2,2,1,2,128,640]{5,4,3,2,1,0:T(8,128)(2,1)}, u32[]{:S(2)}, u32[]{:S(2)}) collective-permute-start(bf16[2,2,1,2,128,640]{5,4,3,2,1,0:T(8,128)(2,1)} %slice.423), channel_id=1, source_target_pairs={{0,4},{2,6},{4,0},{6,2},{8,12},{10,14},{12,8},{14,10},{16,20},{18,... | collective-permute-start | bytes 3932168 | tf_op jit(solution)/shard_map/ppermute | solution.py:39
  518.5 27.4 %collective-permute-start.58 = (bf16[384,2048]{1,0:T(8,128)(2,1)S(1)}, bf16[384,2048]{1,0:T(8,128)(2,1)S(1)}, u32[]{:S(2)}, u32[]{:S(2)}) collective-permute-start(bf16[384,2048]{1,0:T(8,128)(2,1)S(1)} %convolution_convert_fusion.3), channel_id=1, source_target_pairs={{0,1},{1,0},{2,3},{3,2},{4,5},{5,4},{6,7},{7,6},{8,9},{9,8},{10,11... | collective-permute-start | bytes 4718600 | tf_op jit(solution)/shard_map/ppermute | solution.py:43
  522.2 28.5 %collective-permute-start.54 = (bf16[1,2,1,1,128,1024]{5,4,3,2,1,0:T(8,128)(2,1)}, bf16[1,2,1,1,128,1024]{5,4,3,2,1,0:T(8,128)(2,1)}, u32[]{:S(2)}, u32[]{:S(2)}) collective-permute-start(bf16[1,2,1,1,128,1024]{5,4,3,2,1,0:T(8,128)(2,1)} %pad_maximum_fusion.34), channel_id=1, source_target_pairs={{0,8},{2,10},{4,12},{6,14},{8,0},{10,2},{12,4},{14,6},{16,24},{18,... | collective-permute-start | bytes 1572872 | tf_op jit(solution)/shard_map/ppermute | solution.py:39
  539.8 21.2 %collective-permute-start.61 = (bf16[1,1,1,1,128,1920]{5,4,3,2,1,0:T(8,128)(2,1)}, bf16[1,1,1,1,128,1920]{5,4,3,2,1,0:T(8,128)(2,1)S(1)}, u32[]{:S(2)}, u32[]{:S(2)}) collective-permute-start(bf16[1,1,1,1,128,1920]{5,4,3,2,1,0:T(8,128)(2,1)} %slice.523), channel_id=1, source_target_pairs={{0,8},{2,10},{4,12},{6,14},{8,0},{10,2},{12,4},{14,6},{16,24},{18,... | collective-permute-start | bytes 1474568 | tf_op jit(solution)/shard_map/ppermute | solution.py:39
  544.9 19.7 %collective-permute-start.64 = (bf16[2,2,1,1,128,640]{5,4,3,2,1,0:T(8,128)(2,1)}, bf16[2,2,1,1,128,640]{5,4,3,2,1,0:T(8,128)(2,1)S(1)}, u32[]{:S(2)}, u32[]{:S(2)}) collective-permute-start(bf16[2,2,1,1,128,640]{5,4,3,2,1,0:T(8,128)(2,1)} %add_convert_fusion.14), channel_id=1, source_target_pairs={{0,4},{2,6},{4,0},{6,2},{8,12},{10,14},{12,8},{14,10},{16,20},{18,... | collective-permute-start | bytes 1966088 | tf_op jit(solution)/shard_map/ppermute | solution.py:39
  545.9 18.6 %collective-permute-start.63 = (bf16[2,2,1,1,128,640]{5,4,3,2,1,0:T(8,128)(2,1)}, bf16[2,2,1,1,128,640]{5,4,3,2,1,0:T(8,128)(2,1)S(1)}, u32[]{:S(2)}, u32[]{:S(2)}) collective-permute-start(bf16[2,2,1,1,128,640]{5,4,3,2,1,0:T(8,128)(2,1)} %add_convert_fusion.15), channel_id=1, source_target_pairs={{0,2},{2,0},{4,6},{6,4},{8,10},{10,8},{12,14},{14,12},{16,18},{18,... | collective-permute-start | bytes 1966088 | tf_op jit(solution)/shard_map/ppermute | solution.py:39
  561.3 21.8 %collective-permute-start.67 = (bf16[1,1,1,1,128,2304]{5,4,3,2,1,0:T(8,128)(2,1)S(1)}, bf16[1,1,1,1,128,2304]{5,4,3,2,1,0:T(8,128)(2,1)S(1)}, u32[]{:S(2)}, u32[]{:S(2)}) collective-permute-start(bf16[1,1,1,1,128,2304]{5,4,3,2,1,0:T(8,128)(2,1)S(1)} %copy-done.109), channel_id=1, source_target_pairs={{0,8},{2,10},{4,12},{6,14},{8,0},{10,2},{12,4},{14,6},{16,24},{18,... | collective-permute-start | bytes 1769480 | tf_op jit(solution)/shard_map/ppermute | solution.py:39
  564.5 35.4 %collective-permute-start.72 = (bf16[1,1,1,1,128,1024]{5,4,3,2,1,0:T(8,128)(2,1)S(1)}, bf16[1,1,1,1,128,1024]{5,4,3,2,1,0:T(8,128)(2,1)S(1)}, u32[]{:S(2)}, u32[]{:S(2)}) collective-permute-start(bf16[1,1,1,1,128,1024]{5,4,3,2,1,0:T(8,128)(2,1)S(1)} %slice.431), channel_id=1, source_target_pairs={{0,16},{2,18},{4,20},{6,22},{8,24},{10,26},{12,28},{14,30},{16,0},... | collective-permute-start | bytes 786440 | tf_op jit(solution)/shard_map/ppermute | solution.py:39
  568.2 28.4 %collective-permute-start.69 = (bf16[1,2,1,1,128,1280]{5,4,3,2,1,0:T(8,128)(2,1)S(1)}, bf16[1,2,1,1,128,1280]{5,4,3,2,1,0:T(8,128)(2,1)S(1)}, u32[]{:S(2)}, u32[]{:S(2)}) collective-permute-start(bf16[1,2,1,1,128,1280]{5,4,3,2,1,0:T(8,128)(2,1)S(1)} %fusion.19), channel_id=1, source_target_pairs={{0,8},{2,10},{4,12},{6,14},{8,0},{10,2},{12,4},{14,6},{16,24},{18,... | collective-permute-start | bytes 1966088 | tf_op jit(solution)/shard_map/ppermute | solution.py:39
  570.0 15.6 %collective-permute-start.66 = (f32[2,2,1,1,2,128]{5,4,3,2,1,0:T(2,128)S(1)}, f32[2,2,1,1,2,128]{5,4,3,2,1,0:T(2,128)S(1)}, u32[]{:S(2)}, u32[]{:S(2)}) collective-permute-start(f32[2,2,1,1,2,128]{5,4,3,2,1,0:T(2,128)S(1)} %slice.438), channel_id=1, source_target_pairs={{0,2},{2,0},{4,6},{6,4},{8,10},{10,8},{12,14},{14,12},{16,18},{18,... | collective-permute-start | bytes 12296 | tf_op jit(solution)/shard_map/ppermute | solution.py:39
  596.8 16.9 %collective-permute-start.71 = (bf16[1,1,1,1,128,1280]{5,4,3,2,1,0:T(8,128)(2,1)S(1)}, bf16[1,1,1,1,128,1280]{5,4,3,2,1,0:T(8,128)(2,1)S(1)}, u32[]{:S(2)}, u32[]{:S(2)}) collective-permute-start(bf16[1,1,1,1,128,1280]{5,4,3,2,1,0:T(8,128)(2,1)S(1)} %slice.444), channel_id=1, source_target_pairs={{0,16},{2,18},{4,20},{6,22},{8,24},{10,26},{12,28},{14,30},{16,0},... | collective-permute-start | bytes 983048 | tf_op jit(solution)/shard_map/ppermute | solution.py:39
  596.9 18.3 %collective-permute-start.70 = (f32[1,1,1,1,2,128]{5,4,3,2,1,0:T(2,128)S(1)}, f32[1,1,1,1,2,128]{5,4,3,2,1,0:T(2,128)S(1)}, u32[]{:S(2)}, u32[]{:S(2)}) collective-permute-start(f32[1,1,1,1,2,128]{5,4,3,2,1,0:T(2,128)S(1)} %slice.446), channel_id=1, source_target_pairs={{0,16},{2,18},{4,20},{6,22},{8,24},{10,26},{12,28},{14,30},{16,0},... | collective-permute-start | bytes 3080 | tf_op jit(solution)/shard_map/ppermute | solution.py:39
  (126 other events, 1301.3 us)
